TPU v7x, 256 devices: a whole 4x4x8 slice. The times are simulated.
256 devices in a mesh: grp: 8 (over x, z_lo), att: 32 (over y, z_hi, core).
Axes of the slice: x: 4, y: 4, z: 8 (z_hi: 4, z_lo: 2; z = z_hi * 2 + z_lo), core: 2. Of those that a mesh axis runs over, the one named last changes fastest.
Arguments:
- hidden_in: bfloat16 [1024, 8192], P(None, 'grp'), may hold values from -20 to 20
- queries: bfloat16 [1024, 8192], P(('grp', 'att')), may hold values from -100 to 100
- cache_key: bfloat16 [1024, 256, 1024], P(('grp', 'att')), may hold values from -5 to 5
- cache_value: bfloat16 [1024, 256, 1024], P(('grp', 'att')), may hold values from -6 to 6
- new_key: bfloat16 [1024, 1024], P(('grp', 'att')), may hold values from -6 to 6
- new_value: bfloat16 [1024, 1024], P(('grp', 'att')), may hold values from -6 to 6
- lengths: int32 [1024], P(('grp', 'att')), may hold values from 1 to 256, as said below
- out_weight: bfloat16 [8192, 8192], P('att', 'grp'), may hold values from -0.0625 to 0.0625
- norm_gain: float32 [8192], P('grp'), may hold values from 0.1 to 1.9
- w_gate: bfloat16 [8192, 28672], P('grp', 'att'), may hold values from -0.0625 to 0.0625
- w_up: bfloat16 [8192, 28672], P('grp', 'att'), may hold values from -0.0625 to 0.0625
- w_down: bfloat16 [28672, 8192], P('att', 'grp'), may hold values from -0.03125 to 0.03125
Outputs:
- layer_out: bfloat16 [1024, 8192], P('att', 'grp')
Inputs may be any that keep to these rules, and one draw needn't show every extreme that they name: `lengths`: some row has 256 live slots and some row has one.
All inputs are finite; a program needn't handle non-finite values.
Results may differ from a plain program's by a relative error of at most 0.012.
Values may be sent and summed in bfloat16 or wider, within the bound.
No kernel may reach another device: no remote copies, remote signals or barrier semaphores. Data moves between devices by JAX's collectives and lax.ppermute only.
A program may use at most 128 MiB of HBM per device.

v0:
```python
import jax
import jax.numpy as jnp
from jax import lax
from jax.sharding import PartitionSpec as P

D = 8192
HQ = 64
KVH = 8
HD = 128


def attend(queries, cache_key, cache_value, new_key, new_value, lengths):
    row_count = queries.shape[0]
    slot_count = cache_key.shape[1]
    scale_factor = 1.0 / jnp.sqrt(jnp.float32(HD))
    query_heads = queries.reshape(row_count, KVH, HQ // KVH, HD)
    key_heads = cache_key.reshape(row_count, slot_count, KVH, HD)
    value_heads = cache_value.reshape(row_count, slot_count, KVH, HD)
    scores = (
        jnp.einsum("rkgd,rpkd->rkgp", query_heads, key_heads, preferred_element_type=jnp.float32)
        * scale_factor
    )
    score_new = (
        jnp.einsum(
            "rkgd,rkd->rkg",
            query_heads,
            new_key.reshape(row_count, KVH, HD),
            preferred_element_type=jnp.float32,
        )
        * scale_factor
    )
    valid = jnp.arange(slot_count, dtype=jnp.int32)[None, :] < lengths[:, None]
    scores = jnp.where(valid[:, None, None, :], scores, -jnp.inf)
    top_score = jnp.maximum(jnp.max(scores, axis=-1), score_new)
    weights = jnp.exp(scores - top_score[..., None])
    weight_new = jnp.exp(score_new - top_score)
    total = jnp.sum(weights, axis=-1) + weight_new
    summed = jnp.einsum(
        "rkgp,rpkd->rkgd",
        weights.astype(jnp.bfloat16),
        value_heads,
        preferred_element_type=jnp.float32,
    )
    new_low = weight_new.astype(jnp.bfloat16).astype(jnp.float32)
    summed = summed + new_low[..., None] * new_value.astype(jnp.float32).reshape(
        row_count, KVH, 1, HD
    )
    return (summed / total[..., None]).astype(jnp.bfloat16).reshape(row_count, HQ * HD)


def activate(gate_sum, up_sum, square_sum):
    inv_rms = lax.rsqrt(square_sum / D + 1e-05)
    gate = gate_sum * inv_rms[:, None]
    up_proj = up_sum * inv_rms[:, None]
    return (jax.nn.silu(gate) * up_proj).astype(jnp.bfloat16)


def body(
    hidden_in,
    queries,
    cache_key,
    cache_value,
    new_key,
    new_value,
    lengths,
    out_weight,
    norm_gain,
    w_gate,
    w_up,
    w_down,
):
    attended = attend(queries, cache_key, cache_value, new_key, new_value, lengths)
    head_block = lax.all_to_all(attended, "att", split_axis=1, concat_axis=0, tiled=True)
    partial_proj = jnp.dot(
        lax.all_gather(head_block, "grp", axis=0, tiled=True),
        out_weight,
        preferred_element_type=jnp.float32,
    )
    row_share = partial_proj.shape[0] // lax.axis_size("att")
    projected = lax.psum(partial_proj, "att")
    mixed_rows = hidden_in.astype(jnp.float32) + projected
    squares = jnp.sum(mixed_rows * mixed_rows, axis=1)
    normed = (mixed_rows * norm_gain).astype(jnp.bfloat16)
    own_rows = lax.dynamic_slice_in_dim(mixed_rows, lax.axis_index("att") * row_share, row_share, 0)
    gate_part = jnp.dot(normed, w_gate, preferred_element_type=jnp.float32)
    up_part = jnp.dot(normed, w_up, preferred_element_type=jnp.float32)
    gate_sum, up_sum, square_sum = lax.psum((gate_part, up_part, squares), "grp")
    hidden = activate(gate_sum, up_sum, square_sum)
    down_share = lax.psum_scatter(
        jnp.dot(hidden, w_down, preferred_element_type=jnp.float32),
        "att",
        scatter_dimension=0,
        tiled=True,
    )
    return (own_rows + down_share).astype(jnp.bfloat16)


def solution(mesh):
    in_specs = (
        P(None, "grp"),
        P(("grp", "att"), None),
        P(("grp", "att"), None, None),
        P(("grp", "att"), None, None),
        P(("grp", "att"), None),
        P(("grp", "att"), None),
        P(("grp", "att")),
        P("att", "grp"),
        P("grp"),
        P("grp", "att"),
        P("grp", "att"),
        P("att", "grp"),
    )
    out_specs = P("att", "grp")
    return jax.shard_map(body, mesh=mesh, in_specs=in_specs, out_specs=out_specs, check_vma=False)
```

profile of v0, /device:TPU:1, one launch (start us, length us, event | category | flops | bytes accessed | tf_op | source)
XLA Modules:
  0.0 794.9 jit_solution(11407416387820297404)
XLA Ops:
  6.5 0.0 copy-start
  6.5 0.0 copy-start.2
  6.5 0.0 all-reduce.4.cloned.1.call-start
  6.5 0.9 iota_compare_fusion
  7.4 0.7 reshape.49
  8.1 1.0 fusion.28
  9.1 0.0 copy-done
  9.1 1.6 fusion.35
  10.7 0.2 fusion.24
  11.0 0.7 convert_bitcast_fusion
  11.7 2.0 fusion.19
  13.7 0.1 copy.17
  13.8 22.4 %all_to_all.19 = bf16[4,32,256]{2,0,1:T(4,128)(2,1)S(1)} all-to-all(bf16[4,32,256]{2,0,1:T(4,128)(2,1)S(1)} %copy.17), channel_id=1, replica_groups=mesh['grp'=8,'att'=32] {'att'}, dimensions={1} | all-to-all | bytes 131072 | tf_op jit(solution)/shard_map/all_to_all | solution.py:73
  36.3 24.2 %all_gather.3 = bf16[1024,256]{1,0:T(8,128)(2,1)S(1)} all-gather(bf16[128,256]{1,0:T(8,128)(2,1)S(1)} %all_to_all.17), channel_id=1, replica_groups=mesh['grp'=8,'att'=32] {'grp'}, dimensions={0}, use_global_device_ids=true | all-gather | bytes 589824 | tf_op jit(solution)/shard_map/all_gather | solution.py:75
  60.4 0.0 copy-done.2
  60.4 2.7 fusion.36
  63.1 0.0 all-reduce.4.cloned.1.call-update
  63.1 0.0 copy-start.5
  63.1 0.0 all-reduce.6.cloned.1.call-start
  63.2 298.8 %all-reduce.4.cloned.1.call-done = f32[1024,1024]{1,0:T(8,128)} async-done(((f32[1024,1024]{1,0:T(8,128)}), f32[1024,1024]{1,0:T(8,128)}) %all-reduce.4.cloned.1.call-update) | async-done | bytes 4194320 | tf_op jit(solution)/shard_map/psum | solution.py:80
  362.0 0.0 copy-start.3
  362.0 3.6 multiply_reduce_fusion
  365.6 0.0 copy-start.1
  365.6 0.0 copy-done.5
  365.6 0.0 copy-done.3
  365.6 0.0 copy-start.4
  365.6 4.2 fusion.22
  369.8 0.0 copy-done.1
  369.8 0.0 copy-done.4
  369.8 4.2 fusion.23
  374.0 0.0 all-reduce.6.cloned.1.call-update
  374.0 0.0 reduce-scatter.2.cloned.1.call-start
  374.0 16.5 %psum.30 = f32[1024]{0:T(1024)S(1)} all-reduce(f32[1024]{0:T(1024)S(1)} %get-tuple-element.7), channel_id=1, replica_groups=mesh['grp'=8,'att'=32] {'grp'}, use_global_device_ids=true, to_apply=%region_5.6 | all-reduce | flops 1024 | bytes 8192 | tf_op jit(solution)/shard_map/psum | solution.py:87
  390.5 288.9 %all-reduce.6.cloned.1.call-done = (f32[1024,896]{1,0:T(8,128)}, f32[1024,896]{1,0:T(8,128)}) async-done(((f32[1024,896]{1,0:T(8,128)}, f32[1024,896]{1,0:T(8,128)}), (f32[1024,896]{1,0:T(8,128)}, f32[1024,896]{1,0:T(8,128)})) %all-reduce.6.cloned.1.call-update) | async-done | bytes 7340048 | tf_op jit(solution)/shard_map/psum | solution.py:87
  679.4 8.2 %fusion.6 = f32[1024,1024]{1,0:T(8,128)} fusion(bf16[896,1024]{1,0:T(8,128)(2,1)} %param.23, f32[1024,896]{1,0:T(8,128)} %get-tuple-element.5, f32[1024,896]{1,0:T(8,128)} %get-tuple-element.6, f32[1024]{0:T(1024)S(1)} %add_rsqrt_fusion), kind=kOutput, calls=%fused_computation.10 | convolution fusion | flops 1886388224 | bytes 13373440 | tf_op jit(solution)/shard_map/dot_general | solution.py:90
  687.6 0.0 reduce-scatter.2.cloned.1.call-update
  687.6 99.1 %reduce-scatter.2.cloned.1.call-done = f32[32,1024]{1,0:T(8,128)} async-done(((f32[1024,1024]{1,0:T(8,128)}), f32[32,1024]{1,0:T(8,128)}) %reduce-scatter.2.cloned.1.call-update) | async-done | bytes 131088 | tf_op jit(solution)/shard_map/reduce_scatter | solution.py:89
  786.7 1.6 add_convert_fusion
  (6 shorter events, 0.1 us)
Async XLA Ops:
  6.5 2.6 copy-start
  6.5 53.9 %copy-start.2 = (bf16[256,1024]{1,0:T(8,128)(2,1)S(1)}, bf16[256,1024]{1,0:T(8,128)(2,1)}, u32[]{:S(2)}) copy-start(bf16[256,1024]{1,0:T(8,128)(2,1)} %param.19) | copy-start | bytes 1572868
  6.5 355.4 %all-reduce.4.cloned.1.call-start = ((), (), s32[]{:S(2)}) async-start(), calls=%async_computation.2 | async-start | bytes 8388608 | tf_op jit(solution)/shard_map/psum | solution.py:80
  63.1 302.5 %copy-start.5 = (f32[1024]{0:T(1024)S(1)}, f32[1024]{0:T(1024)}, u32[]{:S(2)}) copy-start(f32[1024]{0:T(1024)} %param.20) | copy-start | bytes 12292
  63.1 616.3 %all-reduce.6.cloned.1.call-start = ((), (), s32[]{:S(2)}) async-start(), calls=%async_computation.4 | async-start | bytes 14680064 | tf_op jit(solution)/shard_map/psum | solution.py:87
  362.0 3.6 copy-start.3
  365.6 4.2 copy-start.1
  365.6 4.2 copy-start.4
  374.0 412.7 %reduce-scatter.2.cloned.1.call-start = ((), (), s32[]{:S(2)}) async-start(), calls=%async_computation.3 | async-start | bytes 4325376 | tf_op jit(solution)/shard_map/reduce_scatter | solution.py:89
Sparse Core Ops, SparseCore 0:
  63.2 298.6 all-reduce.3
  374.1 305.2 all-reduce.5
  687.7 98.9 reduce-scatter.1
where the time goes:
time: 796 us; the launch traced here: 795 us
  waiting for transfers between devices  687 us (86%)
  blocking collectives  63.1 us (8%)
  matrix products  23.8 us (3%)
  between operations  13.2 us (2%)
    psum x1, waiting for transfers between devices, body(): projected = lax.psum(partial_proj, 'att')  299 us
    psum x1, waiting for transfers between devices, body(): lax.psum((gate_part, up_part, squares), 'grp')  289 us
    reduce_scatter x1, waiting for transfers between devices, body(): lax.psum_scatter(jnp.dot(hidden, w_down, preferred_element_type=jnp.float...  99.1 us
    all_gather x1, blocking collectives, body(): lax.all_gather(head_block, 'grp', axis=0, tiled=True)  24.2 us
    all_to_all x1, blocking collectives, body(): lax.all_to_all(attended, 'att', split_axis=1, concat_axis=0, tiled=True)  22.4 us
    psum x1, blocking collectives, body(): lax.psum((gate_part, up_part, squares), 'grp')  16.5 us
  transfers between devices with their start and end apart: 3, of which 3 were waited for; matrix products, arithmetic and copies ran while one was open for 0% of the time, Pallas kernels for 0%

commit v1 on v0

v1 whole, which is shorter than its diff:
```python
import jax
import jax.numpy as jnp
import numpy as np
from jax import lax
from jax.experimental import pallas as pl
from jax.experimental.pallas import tpu as pltpu
from jax.sharding import Mesh
from jax.sharding import PartitionSpec as P

NAMES = ("x", "l", "y", "z", "core")
SIZES = (4, 2, 4, 4, 2)
GRP, ATT = ("x", "l"), ("y", "z", "core")
VMEM = pl.BlockSpec(memory_space=pltpu.VMEM)
SMEM = pl.BlockSpec(memory_space=pltpu.SMEM)
ANY = pl.BlockSpec(memory_space=pl.ANY)
STEP = 256

D = 8192
HQ = 64
KVH = 8
HD = 128


def attend(queries, cache_key, cache_value, new_key, new_value, lengths):
    row_count = queries.shape[0]
    slot_count = cache_key.shape[1]
    scale_factor = 1.0 / jnp.sqrt(jnp.float32(HD))
    query_heads = queries.reshape(row_count, KVH, HQ // KVH, HD)
    key_heads = cache_key.reshape(row_count, slot_count, KVH, HD)
    value_heads = cache_value.reshape(row_count, slot_count, KVH, HD)
    scores = (
        jnp.einsum("rkgd,rpkd->rkgp", query_heads, key_heads, preferred_element_type=jnp.float32)
        * scale_factor
    )
    score_new = (
        jnp.einsum(
            "rkgd,rkd->rkg",
            query_heads,
            new_key.reshape(row_count, KVH, HD),
            preferred_element_type=jnp.float32,
        )
        * scale_factor
    )
    valid = jnp.arange(slot_count, dtype=jnp.int32)[None, :] < lengths[:, None]
    scores = jnp.where(valid[:, None, None, :], scores, -jnp.inf)
    top_score = jnp.maximum(jnp.max(scores, axis=-1), score_new)
    weights = jnp.exp(scores - top_score[..., None])
    weight_new = jnp.exp(score_new - top_score)
    total = jnp.sum(weights, axis=-1) + weight_new
    summed = jnp.einsum(
        "rkgp,rpkd->rkgd",
        weights.astype(jnp.bfloat16),
        value_heads,
        preferred_element_type=jnp.float32,
    )
    new_low = weight_new.astype(jnp.bfloat16).astype(jnp.float32)
    summed = summed + new_low[..., None] * new_value.astype(jnp.float32).reshape(
        row_count, KVH, 1, HD
    )
    return (summed / total[..., None]).astype(jnp.bfloat16).reshape(row_count, HQ * HD)


def activate(gate_sum, up_sum, square_sum):
    inv_rms = lax.rsqrt(square_sum / D + 1e-05)
    gate = gate_sum * inv_rms[:, None]
    up_proj = up_sum * inv_rms[:, None]
    return (jax.nn.silu(gate) * up_proj).astype(jnp.bfloat16)


def places():
    table = np.zeros((256, 13), np.int32)
    for device in range(256):
        x, l, y, core = device >> 6, (device >> 5) & 1, (device >> 3) & 3, device & 1
        table[device, :8] = [(l ^ b) * 4 + (x ^ j) for j in range(4) for b in range(2)]
        table[device, 8:12] = [(y + t) % 4 for t in range(4)]
        table[device, 12] = core
    return table


def swap(block, axis):
    return lax.ppermute(block, axis, [(0, 1), (1, 0)])


def ring_from(block, axis, shift):
    return lax.ppermute(block, axis, [((i + shift) % 4, i) for i in range(4)])


def ring_to(block, axis, shift):
    return lax.ppermute(block, axis, [(i, (i + shift) % 4) for i in range(4)])


def spread(block, step):
    perm = []
    for x in range(4):
        for y in range(4):
            for core in range(2):
                target = (((y // 2) * 2 + core) ^ step, x, y % 2)
                perm.append(((x * 4 + y) * 2 + core, (target[0] * 4 + target[1]) * 2 + target[2]))
    return lax.ppermute(block, ("x", "y", "core"), perm)


def params(mebibytes, flops, nbytes):
    return dict(
        compiler_params=pltpu.CompilerParams(vmem_limit_bytes=mebibytes << 20),
        cost_estimate=pl.CostEstimate(flops=flops, bytes_accessed=nbytes, transcendentals=0),
    )


def steps(width):
    return [(n, min(STEP, width - n)) for n in range(0, width, STEP)]


def start_all(copies):
    for copy in copies:
        copy.start()
    return copies


def wait_all(copies):
    for copy in copies:
        copy.wait()


def project_kernel(place_ref, *refs):
    pieces, own, other, others = refs[:4], refs[4:8], refs[8], refs[9]
    out_ref, rows_ref, held_ref, row_sems, held_sems = refs[10:]
    step = pieces[0].shape[0] // 2
    row_copies = start_all(
        [
            pltpu.make_async_copy(
                pieces[j].at[pl.ds(b * step, step), :],
                rows_ref.at[pl.ds(pl.multiple_of(place_ref[2 * j + b] * step, step), step), :],
                row_sems.at[2 * j + b],
            )
            for j in range(4)
            for b in range(2)
        ]
    )
    depth, width = own[0].shape
    held_copies = []
    for t in range(4):
        for b in range(2):
            source = own[t] if b == 0 else (other if t == 0 else others.at[pl.ds((t - 1) * depth, depth), :])
            start = (2 * place_ref[8 + t] + (place_ref[12] if b == 0 else 1 - place_ref[12])) * depth
            held = held_ref.at[pl.ds(pl.multiple_of(start, depth), depth), :]
            held_copies.append(pltpu.make_async_copy(source, held, held_sems.at[2 * t + b]))
    start_all(held_copies)
    wait_all(row_copies)
    wait_all(held_copies)
    for n, size in steps(width):
        out_ref[:, n : n + size] = jnp.dot(
            rows_ref[...], held_ref[:, n : n + size], preferred_element_type=jnp.float32
        ).astype(out_ref.dtype)


def project(place, pieces, own, other, others):
    count, depth = 4 * pieces[0].shape[0], pieces[0].shape[1]
    width = other.shape[1]
    return pl.pallas_call(
        project_kernel,
        in_specs=[SMEM] + [ANY] * 10,
        out_specs=VMEM,
        out_shape=jax.ShapeDtypeStruct((count, width), jnp.bfloat16),
        scratch_shapes=[
            pltpu.VMEM((count, depth), jnp.bfloat16),
            pltpu.VMEM((depth, width), jnp.bfloat16),
            pltpu.SemaphoreType.DMA((8,)),
            pltpu.SemaphoreType.DMA((8,)),
        ],
        name="project",
        **params(12, 2 * count * depth * width, 2 * (depth * width + count * (depth + width))),
    )(place, *pieces, *own, other, others)


def gate_up_kernel(gain_ref, *refs):
    pieces, weights = refs[:-9], refs[-9:-5]
    out_ref, rows_ref, held_ref, row_sems, held_sems = refs[-5:]
    step = pieces[0].shape[0]
    width = weights[0].shape[1]
    row_copies = start_all(
        [
            pltpu.make_async_copy(piece, rows_ref.at[pl.ds(t * step, step), :], row_sems.at[t])
            for t, piece in enumerate(pieces)
        ]
    )
    held_copies = start_all(
        [pltpu.make_async_copy(weights[j], held_ref.at[j], held_sems.at[j]) for j in range(4)]
    )
    inverse = 1.0 / gain_ref[...]
    part = 64
    lane = lax.broadcasted_iota(jnp.int32, (part, 128), 1)
    wait_all(row_copies)
    for t in range(0, rows_ref.shape[0], part):
        mixed = rows_ref[t : t + part, :].astype(jnp.float32) * inverse
        squares = jnp.sum(mixed * mixed, axis=1, keepdims=True)
        high = squares.astype(jnp.bfloat16).astype(jnp.float32)
        columns = jnp.where(lane == 0, high, jnp.where(lane == 1, squares - high, 0.0))
        out_ref[t : t + part, 4 * width :] = columns.astype(out_ref.dtype)
    for j in range(4):
        held_copies[j].wait()
        for n, size in steps(width):
            product = jnp.dot(rows_ref[...], held_ref[j, :, n : n + size], preferred_element_type=jnp.float32)
            out_ref[:, j * width + n : j * width + n + size] = product.astype(out_ref.dtype)


def gate_up(gain, pieces, weights):
    count, depth = len(pieces) * pieces[0].shape[0], pieces[0].shape[1]
    width = weights[0].shape[1]
    return pl.pallas_call(
        gate_up_kernel,
        in_specs=[VMEM] + [ANY] * (len(pieces) + 4),
        out_specs=VMEM,
        out_shape=jax.ShapeDtypeStruct((count, 4 * width + 128), jnp.bfloat16),
        scratch_shapes=[
            pltpu.VMEM((count, depth), jnp.bfloat16),
            pltpu.VMEM((4, depth, width), jnp.bfloat16),
            pltpu.SemaphoreType.DMA((len(pieces),)),
            pltpu.SemaphoreType.DMA((4,)),
        ],
        name="gate_up",
        **params(20, 8 * count * depth * width, 2 * (count * depth + 4 * depth * width + 4 * count * width)),
    )(gain, *pieces, *weights)


def down_kernel(hidden_ref, own, other, *refs):
    outs, rows_ref, held_ref, row_sem, held_sems = refs[:4], refs[4], refs[5], refs[6], refs[7]
    depth, width = own.shape
    row_copy = pltpu.make_async_copy(hidden_ref, rows_ref, row_sem.at[0])
    row_copy.start()
    held_copies = start_all(
        [
            pltpu.make_async_copy(weight, held_ref.at[pl.ds(i * depth, depth), :], held_sems.at[i])
            for i, weight in enumerate((own, other))
        ]
    )
    row_copy.wait()
    share = outs[0].shape[0]
    first = share // 8
    near = rows_ref[:, :first].reshape(share, 2 * depth)
    far = rows_ref[:, first:].reshape(3 * share, 2 * depth)
    wait_all(held_copies)
    for n, size in steps(width):
        columns = held_ref[:, n : n + size]
        product = jnp.dot(far, columns, preferred_element_type=jnp.float32)
        for t in range(3):
            outs[t + 1][:, n : n + size] = product[t * share : (t + 1) * share].astype(outs[t + 1].dtype)
        product = jnp.dot(near, columns, preferred_element_type=jnp.float32)
        outs[0][:, n : n + size] = product.astype(outs[0].dtype)


def down(hidden, weights):
    count = hidden.shape[0] * hidden.shape[1]
    depth, width = weights[0].shape
    return pl.pallas_call(
        down_kernel,
        in_specs=[ANY] * 3,
        out_specs=[VMEM] * 4,
        out_shape=[jax.ShapeDtypeStruct((count // 4, width), jnp.bfloat16)] * 4,
        scratch_shapes=[
            pltpu.VMEM(hidden.shape, jnp.bfloat16),
            pltpu.VMEM((2 * depth, width), jnp.bfloat16),
            pltpu.SemaphoreType.DMA((1,)),
            pltpu.SemaphoreType.DMA((2,)),
        ],
        name="down",
        **params(16, 4 * count * depth * width, 2 * (2 * count * depth + 2 * depth * width + count * width)),
    )(hidden, *weights)


def add_up(pieces):
    total = pieces[0].astype(jnp.float32)
    for piece in pieces[1:]:
        total = total + piece.astype(jnp.float32)
    return total


def exchange(pieces, axis):
    return lax.all_to_all(pieces, axis, split_axis=0, concat_axis=0, tiled=True)


def scatter_sum(partial, axis):
    parts = lax.axis_size(axis)
    pieces = partial.reshape(parts, partial.shape[0] // parts, partial.shape[1])
    return jnp.sum(exchange(pieces, axis).astype(jnp.float32), axis=0)


def gather(rows, axis):
    return exchange(jnp.broadcast_to(rows[None], (lax.axis_size(axis),) + rows.shape), axis)


def body(
    hidden_in,
    queries,
    cache_key,
    cache_value,
    new_key,
    new_value,
    lengths,
    out_weight,
    norm_gain,
    w_gate,
    w_up,
    w_down,
):
    device = lax.axis_index(GRP + ATT)
    place = lax.dynamic_slice_in_dim(jnp.asarray(places()), device, 1, 0)[0]
    out_own = [out_weight] + [ring_from(out_weight, "y", t) for t in (1, 2, 3)]
    out_other = swap(out_weight, "core")

    attended = attend(queries, cache_key, cache_value, new_key, new_value, lengths)
    count = attended.shape[0]
    slots = attended.reshape(count, 4, 4, -1).transpose(2, 0, 1, 3).reshape(4, count, -1)
    block = exchange(slots, "z").reshape(4 * count, -1)
    block = jnp.concatenate([block, swap(block, "l")], axis=0)
    block, *out_own[1:] = lax.optimization_barrier((block, *out_own[1:]))
    out_others = swap(jnp.concatenate(out_own[1:], axis=0), "core")
    pieces = [spread(block, step) for step in range(4)]
    partial = project(place, pieces, out_own, out_other, out_others)
    partial, *late = lax.optimization_barrier((partial, w_gate, w_up))
    gate_other, up_other = [swap(w, "core") for w in late]

    share = hidden_in.shape[0] // 32
    own_in = lax.dynamic_slice_in_dim(hidden_in, (device & 31) * share, share, 0)
    own_in = own_in.reshape(4, 2, count, -1).transpose(1, 0, 2, 3).reshape(share, -1)
    mixed = own_in.astype(jnp.float32) + scatter_sum(partial, "z")
    normed = (mixed * norm_gain).astype(jnp.bfloat16)
    normed, gate_other, up_other = lax.optimization_barrier((normed, gate_other, up_other))

    block = jnp.concatenate([normed] + [ring_from(normed, "z", t) for t in (1, 2, 3)], axis=0)
    block, late = lax.optimization_barrier((block, w_down))
    down_other = swap(late, "core")
    pieces = [ring_from(block, "y", t) for t in (1, 2, 3)]
    weights = [w_gate, w_up, gate_other, up_other]
    summed = [scatter_sum(gate_up(norm_gain[None, :], part, weights), GRP) for part in ([block], pieces)]
    summed = jnp.concatenate(summed, axis=0)
    width = w_gate.shape[1]
    square_sum = summed[:, 4 * width] + summed[:, 4 * width + 1]
    hidden = jnp.concatenate(
        [
            activate(summed[:, i * width : (i + 1) * width], summed[:, (i + 1) * width : (i + 2) * width], square_sum)
            for i in (0, 2)
        ],
        axis=1,
    )
    parts = down(gather(hidden, GRP), [w_down, down_other])
    total = add_up([parts[0]] + [ring_to(parts[t], "y", t) for t in (1, 2, 3)])
    parts = [total[t * share : (t + 1) * share] for t in range(4)]
    total = add_up([parts[0]] + [ring_to(parts[t].astype(jnp.bfloat16), "z", t) for t in (1, 2, 3)])
    layer_out = (mixed + total).astype(jnp.bfloat16)
    return layer_out.reshape(2, 4, count, -1).transpose(1, 0, 2, 3).reshape(share, -1)


def solution(mesh):
    fine = Mesh(mesh.devices.reshape(SIZES), NAMES)
    rows = P(GRP + ATT)
    in_specs = (
        P(None, GRP),
        rows,
        rows,
        rows,
        rows,
        rows,
        rows,
        P(ATT, GRP),
        P(GRP),
        P(GRP, ATT),
        P(GRP, ATT),
        P(ATT, GRP),
    )
    out_specs = P(ATT, GRP)
    return jax.shard_map(body, mesh=fine, in_specs=in_specs, out_specs=out_specs, check_vma=False)
```

time: 796 us -> 218 us (0.27)
  the two profiles are of different devices: /device:TPU:1 before, /device:TPU:6 now
where the time goes in v1:
time: 218 us; the launch traced here: 217 us
  waiting for transfers between devices  97 us (44%)
  starting transfers between devices  60.1 us (28%)
  Pallas kernels  18.1 us (8%)
  blocking collectives  16.6 us (8%)
  local copies, waits for them, and re-layouts  12.5 us (6%)
  other arithmetic  9.14 us (4%)
  matrix products  3.15 us (1%)
    all_to_all x4, waiting for transfers between devices, exchange(): return lax.all_to_all(pieces, axis, split_axis=0, concat_axis=0, tiled=True)  51 us
    all_to_all x4, starting transfers between devices, exchange(): return lax.all_to_all(pieces, axis, split_axis=0, concat_axis=0, tiled=True)  21.7 us
    all_to_all x1, blocking collectives, exchange(): return lax.all_to_all(pieces, axis, split_axis=0, concat_axis=0, tiled=True)  16.6 us
    ppermute x9, waiting for transfers between devices, ring_from(): return lax.ppermute(block, axis, [((i + shift) % 4, i) for i in range(4)])  16 us
    ppermute x6, waiting for transfers between devices, ring_to(): return lax.ppermute(block, axis, [(i, (i + shift) % 4) for i in range(4)])  15.6 us
    ppermute x9, starting transfers between devices, ring_from(): return lax.ppermute(block, axis, [((i + shift) % 4, i) for i in range(4)])  14.8 us
    ppermute x6, starting transfers between devices, ring_to(): return lax.ppermute(block, axis, [(i, (i + shift) % 4) for i in range(4)])  12 us
    pallas_call x2, Pallas kernels, gate_up(): pl.pallas_call(gate_up_kernel, in_specs=[VMEM] + [ANY] * (len(pieces) + 4...  10.1 us
  transfers between devices with their start and end apart: 29, of which 20 were waited for; matrix products, arithmetic and copies ran while one was open for 4% of the time, Pallas kernels for 3%

profile of v1, /device:TPU:6, one launch (start us, length us, event | category | flops | bytes accessed | tf_op | source)
XLA Modules:
  0.0 216.8 jit_solution(10392577257757417907)
XLA Ops:
  0.0 3.0 %collective-permute-start.1 = (bf16[256,1024]{1,0:T(8,128)(2,1)}, bf16[256,1024]{1,0:T(8,128)(2,1)S(1)}, u32[]{:S(2)}, u32[]{:S(2)}) collective-permute-start(bf16[256,1024]{1,0:T(8,128)(2,1)} %refs_4_.2), channel_id=1, source_target_pairs={{8,0},{16,8},{24,16},{0,24},{9,1},{17,9},{25,17},{1,25},{10,2},{18... | collective-permute-start | bytes 1572872 | tf_op jit(solution)/shard_map/ppermute | solution.py:85
  7.2 1.6 fusion.51
  9.7 16.6 %all_to_all.25 = bf16[4,4,2048]{2,1,0:T(4,128)(2,1)S(1)} all-to-all(bf16[4,4,2048]{2,1,0:T(4,128)(2,1)S(1)} %reshape.67), channel_id=1, replica_groups=mesh['x'=4,'l'=2,'y'=4,'z'=4,'core'=2] {'z'}, dimensions={0} | all-to-all | bytes 131072 | tf_op jit(solution)/shard_map/all_to_all | solution.py:278
  27.4 3.3 %collective-permute-done = bf16[16,2048]{1,0:T(8,128)(2,1)S(1)} collective-permute-done((bf16[16,2048]{1,0:T(8,128)(2,1)S(1)}, bf16[16,2048]{1,0:T(8,128)(2,1)S(1)}, u32[]{:S(2)}, u32[]{:S(2)}) %collective-permute-start) | collective-permute-done | bytes 65568 | tf_op jit(solution)/shard_map/ppermute | solution.py:81
  31.3 2.3 %pad_maximum_fusion = bf16[768,1024]{1,0:T(8,128)(2,1)} fusion(bf16[256,1024]{1,0:T(8,128)(2,1)} %collective-permute-done.3.refs_7_, bf16[256,1024]{1,0:T(8,128)(2,1)S(1)} %collective-permute-done.2.refs_6_, bf16[256,1024]{1,0:T(8,128)(2,1)S(1)} %collective-permute-done.1.refs_5_), kind=kLoop, calls=%fused_computation.13 | loop fusion | flops 4718592 | bytes 3145728 | tf_op jit(solution)/shard_map/concatenate | solution.py:316
  34.1 4.0 %collective-permute-start.4 = (bf16[32,2048]{1,0:T(8,128)(2,1)}, bf16[32,2048]{1,0:T(8,128)(2,1)S(1)}, u32[]{:S(2)}, u32[]{:S(2)}) collective-permute-start(bf16[32,2048]{1,0:T(8,128)(2,1)} %pad_maximum_fusion.4), channel_id=1, source_target_pairs={{0,0},{1,64},{8,1},{9,65},{16,128},{17,192},{24,129},{25,193},{64,... | collective-permute-start | bytes 393224 | tf_op jit(solution)/shard_map/ppermute | solution.py:99
  38.2 3.8 %collective-permute-start.5 = (bf16[32,2048]{1,0:T(8,128)(2,1)}, bf16[32,2048]{1,0:T(8,128)(2,1)S(1)}, u32[]{:S(2)}, u32[]{:S(2)}) collective-permute-start(bf16[32,2048]{1,0:T(8,128)(2,1)} %pad_maximum_fusion.4), channel_id=1, source_target_pairs={{0,64},{1,0},{8,65},{9,1},{16,192},{17,128},{24,193},{25,129},{64,... | collective-permute-start | bytes 393224 | tf_op jit(solution)/shard_map/ppermute | solution.py:99
  42.8 1.5 collective-permute-start.7
  45.0 2.6 %collective-permute-done.4.refs_0_ = bf16[32,2048]{1,0:T(8,128)(2,1)S(1)} collective-permute-done((bf16[32,2048]{1,0:T(8,128)(2,1)}, bf16[32,2048]{1,0:T(8,128)(2,1)S(1)}, u32[]{:S(2)}, u32[]{:S(2)}) %collective-permute-start.4) | collective-permute-done | bytes 131104 | tf_op jit(solution)/shard_map/ppermute | solution.py:99
  47.6 1.6 collective-permute-done.5.refs_1_
  49.2 1.8 collective-permute-done.6.refs_2_
  51.0 1.2 collective-permute-done.7.refs_3_
  54.3 4.3 %project.1 = bf16[128,1024]{1,0:T(8,128)(2,1)} custom-call(s32[13]{0:T(128)S(1)} %dynamic-slice_bitcast_fusion.place_ref, bf16[32,2048]{1,0:T(8,128)(2,1)S(1)} %collective-permute-done.4.refs_0_, bf16[32,2048]{1,0:T(8,128)(2,1)S(1)} %collective-permute-done.5.refs_1_, bf16[32,2048]{1,0:T(8,128)(2,1)S(1)} %collective-permute-done.6.refs_2_, ...), custom_call_target="tpu_custom_call" | custom-call | flops 536870912 | bytes 4980736 | tf_op jit(solution)/shard_map/project/pallas_call | solution.py:159
  59.1 5.1 %all-to-all-start.1 = ((bf16[4,32,1024]{2,1,0:T(8,128)(2,1)}), bf16[4,32,1024]{2,1,0:T(8,128)(2,1)S(1)}, u32[]{:S(2)}, u32[]{:S(2)}) async-start(bf16[4,32,1024]{2,1,0:T(8,128)(2,1)} %bitcast.5), calls=%async_computation.1 | async-start | bytes 524288 | tf_op jit(solution)/shard_map/all_to_all | solution.py:278
  65.2 10.4 %all-to-all-done.1 = bf16[4,32,1024]{2,1,0:T(8,128)(2,1)S(1)} async-done(((bf16[4,32,1024]{2,1,0:T(8,128)(2,1)}), bf16[4,32,1024]{2,1,0:T(8,128)(2,1)S(1)}, u32[]{:S(2)}, u32[]{:S(2)}) %all-to-all-start.1) | async-done | bytes 262176 | tf_op jit(solution)/shard_map/all_to_all | solution.py:278
  75.7 1.3 collective-permute-start.12
  77.0 4.0 %collective-permute-start.13 = (bf16[32,1024]{1,0:T(8,128)(2,1)S(1)}, bf16[32,1024]{1,0:T(8,128)(2,1)S(1)}, u32[]{:S(2)}, u32[]{:S(2)}) collective-permute-start(bf16[32,1024]{1,0:T(8,128)(2,1)S(1)} %get-tuple-element.28), channel_id=1, source_target_pairs={{4,0},{6,2},{0,4},{2,6},{5,1},{7,3},{1,5},{3,7},{12,8},{14,10},{8,... | collective-permute-start | bytes 196616 | tf_op jit(solution)/shard_map/ppermute | solution.py:85
  82.0 4.3 %collective-permute-done.13 = bf16[32,1024]{1,0:T(8,128)(2,1)S(1)} collective-permute-done((bf16[32,1024]{1,0:T(8,128)(2,1)S(1)}, bf16[32,1024]{1,0:T(8,128)(2,1)S(1)}, u32[]{:S(2)}, u32[]{:S(2)}) %collective-permute-start.13) | collective-permute-done | bytes 65568 | tf_op jit(solution)/shard_map/ppermute | solution.py:85
  86.3 1.8 collective-permute-done.14
  88.1 4.6 %gate_up.2 = bf16[128,3712]{1,0:T(8,128)(2,1)} custom-call(f32[1,1024]{1,0:T(1,128)S(1)} %bitcast.57, bf16[128,1024]{1,0:T(8,128)(2,1)S(1)} %pad_maximum_fusion.1.refs_0_, bf16[1024,896]{1,0:T(8,128)(2,1)} %refs_3_.1, bf16[1024,896]{1,0:T(8,128)(2,1)} %refs_4_.3, bf16[1024,896]{1,0:T(8,128)(2,1)} %collective-permute-done.10.refs_3_.refs_5_, ...), custom_call_target="tpu_custom_call" | custom-call | flops 939524096 | bytes 8519680 | tf_op jit(solution)/shard_map/gate_up/pallas_call | solution.py:209
  92.7 4.6 %all-to-all-start.2 = ((bf16[8,16,3712]{2,1,0:T(8,128)(2,1)}), bf16[8,16,3712]{2,1,0:T(8,128)(2,1)}, u32[]{:S(2)}, u32[]{:S(2)}) async-start(bf16[8,16,3712]{2,1,0:T(8,128)(2,1)} %bitcast.7), calls=%async_computation.2 | async-start | bytes 1900544 | tf_op jit(solution)/shard_map/all_to_all | solution.py:278
  97.3 2.2 %collective-permute-start.15 = (bf16[128,1024]{1,0:T(8,128)(2,1)S(1)}, bf16[128,1024]{1,0:T(8,128)(2,1)S(1)}, u32[]{:S(2)}, u32[]{:S(2)}) collective-permute-start(bf16[128,1024]{1,0:T(8,128)(2,1)S(1)} %pad_maximum_fusion.1.refs_0_), channel_id=1, source_target_pairs={{8,0},{16,8},{24,16},{0,24},{9,1},{17,9},{25,17},{1,25},{10,2},{18... | collective-permute-start | bytes 786440 | tf_op jit(solution)/shard_map/ppermute | solution.py:85
  99.5 2.5 %collective-permute-start.16 = (bf16[128,1024]{1,0:T(8,128)(2,1)S(1)}, bf16[128,1024]{1,0:T(8,128)(2,1)S(1)}, u32[]{:S(2)}, u32[]{:S(2)}) collective-permute-start(bf16[128,1024]{1,0:T(8,128)(2,1)S(1)} %pad_maximum_fusion.1.refs_0_), channel_id=1, source_target_pairs={{16,0},{24,8},{0,16},{8,24},{17,1},{25,9},{1,17},{9,25},{18,2},{26... | collective-permute-start | bytes 786440 | tf_op jit(solution)/shard_map/ppermute | solution.py:85
  102.1 3.3 %collective-permute-done.15.refs_0_ = bf16[128,1024]{1,0:T(8,128)(2,1)S(1)} collective-permute-done((bf16[128,1024]{1,0:T(8,128)(2,1)S(1)}, bf16[128,1024]{1,0:T(8,128)(2,1)S(1)}, u32[]{:S(2)}, u32[]{:S(2)}) %collective-permute-start.15) | collective-permute-done | bytes 262176 | tf_op jit(solution)/shard_map/ppermute | solution.py:85
  105.4 2.9 %collective-permute-done.16.refs_1_ = bf16[128,1024]{1,0:T(8,128)(2,1)S(1)} collective-permute-done((bf16[128,1024]{1,0:T(8,128)(2,1)S(1)}, bf16[128,1024]{1,0:T(8,128)(2,1)S(1)}, u32[]{:S(2)}, u32[]{:S(2)}) %collective-permute-start.16) | collective-permute-done | bytes 262176 | tf_op jit(solution)/shard_map/ppermute | solution.py:85
  108.3 2.7 %collective-permute-done.17.refs_2_ = bf16[128,1024]{1,0:T(8,128)(2,1)S(1)} collective-permute-done((bf16[128,1024]{1,0:T(8,128)(2,1)S(1)}, bf16[128,1024]{1,0:T(8,128)(2,1)S(1)}, u32[]{:S(2)}, u32[]{:S(2)}) %collective-permute-start.17) | collective-permute-done | bytes 262176 | tf_op jit(solution)/shard_map/ppermute | solution.py:85
  111.0 5.5 %gate_up.3 = bf16[384,3712]{1,0:T(8,128)(2,1)S(1)} custom-call(f32[1,1024]{1,0:T(1,128)S(1)} %bitcast.58, bf16[128,1024]{1,0:T(8,128)(2,1)S(1)} %collective-permute-done.15.refs_0_, bf16[128,1024]{1,0:T(8,128)(2,1)S(1)} %collective-permute-done.16.refs_1_, bf16[128,1024]{1,0:T(8,128)(2,1)S(1)} %collective-permute-done.17.refs_2_, bf16[1024,896]{1,0:T(8,128)(2,1)} %refs_3_.1, ...), custom_call_target="tpu_custom_call" | custom-call | flops 2818572288 | bytes 10878976 | tf_op jit(solution)/shard_map/gate_up/pallas_call | solution.py:209
  116.6 1.6 copy-done.1
  118.1 5.7 %all-to-all-start.3 = ((bf16[8,48,3712]{2,1,0:T(8,128)(2,1)}), bf16[8,48,3712]{2,1,0:T(8,128)(2,1)}, u32[]{:S(2)}, u32[]{:S(2)}) async-start(bf16[8,48,3712]{2,1,0:T(8,128)(2,1)} %bitcast.56), calls=%async_computation.3 | async-start | bytes 5701632 | tf_op jit(solution)/shard_map/all_to_all | solution.py:278
  123.8 1.3 convert_reduce_fusion.1
  125.2 27.1 %all-to-all-done.3 = bf16[8,48,3712]{2,1,0:T(8,128)(2,1)} async-done(((bf16[8,48,3712]{2,1,0:T(8,128)(2,1)}), bf16[8,48,3712]{2,1,0:T(8,128)(2,1)}, u32[]{:S(2)}, u32[]{:S(2)}) %all-to-all-start.3) | async-done | bytes 2850848 | tf_op jit(solution)/shard_map/all_to_all | solution.py:278
  152.3 2.3 %convert_reduce_fusion = f32[48,3712]{1,0:T(8,128)S(1)} fusion(bf16[8,48,3712]{2,1,0:T(8,128)(2,1)} %all-to-all-done.3), kind=kLoop, calls=%fused_computation | loop fusion | flops 2672640 | bytes 3563520 | tf_op jit(solution)/shard_map/reduce_sum | solution.py:284
  155.0 1.4 broadcast_in_dim.19
  156.4 6.3 %all-to-all-start.4 = ((bf16[8,64,1792]{2,1,0:T(8,128)(2,1)}), bf16[8,64,1792]{2,1,0:T(8,128)(2,1)}, u32[]{:S(2)}, u32[]{:S(2)}) async-start(bf16[8,64,1792]{2,1,0:T(8,128)(2,1)} %broadcast_in_dim.19), calls=%async_computation.4 | async-start | bytes 3670016 | tf_op jit(solution)/shard_map/all_to_all | solution.py:278
  162.7 4.0 %collective-permute-done.18.other = bf16[896,1024]{1,0:T(8,128)(2,1)S(1)} collective-permute-done((bf16[896,1024]{1,0:T(8,128)(2,1)}, bf16[896,1024]{1,0:T(8,128)(2,1)S(1)}, u32[]{:S(2)}, u32[]{:S(2)}) %collective-permute-start.18) | collective-permute-done | bytes 1835040 | tf_op jit(solution)/shard_map/ppermute | solution.py:81
  166.6 1.3 copy-done.8
  167.9 13.6 %all-to-all-done.4.hidden_ref = bf16[8,64,1792]{2,1,0:T(8,128)(2,1)} async-done(((bf16[8,64,1792]{2,1,0:T(8,128)(2,1)}), bf16[8,64,1792]{2,1,0:T(8,128)(2,1)}, u32[]{:S(2)}, u32[]{:S(2)}) %all-to-all-start.4) | async-done | bytes 1835040 | tf_op jit(solution)/shard_map/all_to_all | solution.py:278
  181.5 1.5 copy-done.7
  183.0 1.5 copy-done.9
  184.5 3.7 %down.1 = (bf16[128,1024]{1,0:T(8,128)(2,1)S(1)}, bf16[128,1024]{1,0:T(8,128)(2,1)S(1)}, bf16[128,1024]{1,0:T(8,128)(2,1)S(1)}, bf16[128,1024]{1,0:T(8,128)(2,1)S(1)}) custom-call(bf16[8,64,1792]{2,1,0:T(8,128)(2,1)} %all-to-all-done.4.hidden_ref, bf16[896,1024]{1,0:T(8,128)(2,1)S(1)} %copy-done.7, bf16[896,1024]{1,0:T(8,128)(2,1)S(1)} %copy-done.9), custom_call_target="tpu_custom_call" | custom-call | flops 1879048192 | bytes 6553600 | tf_op jit(solution)/shard_map/down/pallas_call | solution.py:254
  188.3 5.0 %collective-permute-start.20 = (bf16[128,1024]{1,0:T(8,128)(2,1)S(1)}, bf16[128,1024]{1,0:T(8,128)(2,1)S(1)}, u32[]{:S(2)}, u32[]{:S(2)}) collective-permute-start(bf16[128,1024]{1,0:T(8,128)(2,1)S(1)} %get-tuple-element.35), channel_id=1, source_target_pairs={{0,16},{8,24},{16,0},{24,8},{1,17},{9,25},{17,1},{25,9},{2,18},{10... | collective-permute-start | bytes 786440 | tf_op jit(solution)/shard_map/ppermute | solution.py:89
  193.3 2.5 %collective-permute-start.21 = (bf16[128,1024]{1,0:T(8,128)(2,1)S(1)}, bf16[128,1024]{1,0:T(8,128)(2,1)S(1)}, u32[]{:S(2)}, u32[]{:S(2)}) collective-permute-start(bf16[128,1024]{1,0:T(8,128)(2,1)S(1)} %get-tuple-element.36), channel_id=1, source_target_pairs={{0,24},{8,0},{16,8},{24,16},{1,25},{9,1},{17,9},{25,17},{2,26},{10... | collective-permute-start | bytes 786440 | tf_op jit(solution)/shard_map/ppermute | solution.py:89
  195.9 2.7 %collective-permute-done.19 = bf16[128,1024]{1,0:T(8,128)(2,1)S(1)} collective-permute-done((bf16[128,1024]{1,0:T(8,128)(2,1)S(1)}, bf16[128,1024]{1,0:T(8,128)(2,1)S(1)}, u32[]{:S(2)}, u32[]{:S(2)}) %collective-permute-start.19) | collective-permute-done | bytes 262176 | tf_op jit(solution)/shard_map/ppermute | solution.py:89
  198.6 3.9 %collective-permute-done.20 = bf16[128,1024]{1,0:T(8,128)(2,1)S(1)} collective-permute-done((bf16[128,1024]{1,0:T(8,128)(2,1)S(1)}, bf16[128,1024]{1,0:T(8,128)(2,1)S(1)}, u32[]{:S(2)}, u32[]{:S(2)}) %collective-permute-start.20) | collective-permute-done | bytes 262176 | tf_op jit(solution)/shard_map/ppermute | solution.py:89
  202.7 4.2 %collective-permute-start.23 = (bf16[32,1024]{1,0:T(8,128)(2,1)S(1)}, bf16[32,1024]{1,0:T(8,128)(2,1)S(1)}, u32[]{:S(2)}, u32[]{:S(2)}) collective-permute-start(bf16[32,1024]{1,0:T(8,128)(2,1)S(1)} %get-tuple-element.45), channel_id=1, source_target_pairs={{0,4},{2,6},{4,0},{6,2},{1,5},{3,7},{5,1},{7,3},{8,12},{10,14},{12... | collective-permute-start | bytes 196616 | tf_op jit(solution)/shard_map/ppermute | solution.py:89
  207.0 2.1 collective-permute-done.22
  209.2 2.1 collective-permute-done.23
  211.3 4.8 %collective-permute-done.24 = bf16[32,1024]{1,0:T(8,128)(2,1)S(1)} collective-permute-done((bf16[32,1024]{1,0:T(8,128)(2,1)S(1)}, bf16[32,1024]{1,0:T(8,128)(2,1)S(1)}, u32[]{:S(2)}, u32[]{:S(2)}) %collective-permute-start.24) | collective-permute-done | bytes 65568 | tf_op jit(solution)/shard_map/ppermute | solution.py:89
  (75 shorter events, 15.2 us)
Async XLA Ops:
  0.0 7.2 %copy-start = (bf16[4,256,1024]{2,1,0:T(8,128)(2,1)S(1)}, bf16[4,256,1024]{2,1,0:T(8,128)(2,1)}, u32[]{:S(2)}) copy-start(bf16[4,256,1024]{2,1,0:T(8,128)(2,1)} %param.15) | copy-start | bytes 6291460
  0.0 9.0 %copy-start.10 = (bf16[4,1024]{1,0:T(4,128)(2,1)S(1)}, bf16[4,1024]{1,0:T(4,128)(2,1)}, u32[]{:S(2)}) copy-start(bf16[4,1024]{1,0:T(4,128)(2,1)} %param.18) | copy-start | bytes 24580
  0.0 31.3 %collective-permute-start.1 = (bf16[256,1024]{1,0:T(8,128)(2,1)}, bf16[256,1024]{1,0:T(8,128)(2,1)S(1)}, u32[]{:S(2)}, u32[]{:S(2)}) collective-permute-start(bf16[256,1024]{1,0:T(8,128)(2,1)} %refs_4_.2), channel_id=1, source_target_pairs={{8,0},{16,8},{24,16},{0,24},{9,1},{17,9},{25,17},{1,25},{10,2},{18... | collective-permute-start | bytes 1572872 | tf_op jit(solution)/shard_map/ppermute | solution.py:85
  3.0 28.3 %collective-permute-start.2 = (bf16[256,1024]{1,0:T(8,128)(2,1)}, bf16[256,1024]{1,0:T(8,128)(2,1)S(1)}, u32[]{:S(2)}, u32[]{:S(2)}) collective-permute-start(bf16[256,1024]{1,0:T(8,128)(2,1)} %refs_4_.2), channel_id=1, source_target_pairs={{16,0},{24,8},{0,16},{8,24},{17,1},{25,9},{1,17},{9,25},{18,2},{26... | collective-permute-start | bytes 1572872 | tf_op jit(solution)/shard_map/ppermute | solution.py:85
  3.6 27.7 %collective-permute-start.3 = (bf16[256,1024]{1,0:T(8,128)(2,1)}, bf16[256,1024]{1,0:T(8,128)(2,1)}, u32[]{:S(2)}, u32[]{:S(2)}) collective-permute-start(bf16[256,1024]{1,0:T(8,128)(2,1)} %refs_4_.2), channel_id=1, source_target_pairs={{24,0},{0,8},{8,16},{16,24},{25,1},{1,9},{9,17},{17,25},{26,2},{2,... | collective-permute-start | bytes 1572872 | tf_op jit(solution)/shard_map/ppermute | solution.py:85
  6.1 3.0 %copy-start.11 = (bf16[4,256,1024]{2,1,0:T(8,128)(2,1)S(1)}, bf16[4,256,1024]{2,1,0:T(8,128)(2,1)}, u32[]{:S(2)}) copy-start(bf16[4,256,1024]{2,1,0:T(8,128)(2,1)} %param.16) | copy-start | bytes 6291460
  26.3 7.4 %copy-start.2 = (bf16[256,1024]{1,0:T(8,128)(2,1)S(1)}, bf16[256,1024]{1,0:T(8,128)(2,1)}, u32[]{:S(2)}) copy-start(bf16[256,1024]{1,0:T(8,128)(2,1)} %refs_4_.2) | copy-start | bytes 1572868
  26.3 4.4 %collective-permute-start = (bf16[16,2048]{1,0:T(8,128)(2,1)S(1)}, bf16[16,2048]{1,0:T(8,128)(2,1)S(1)}, u32[]{:S(2)}, u32[]{:S(2)}) collective-permute-start(bf16[16,2048]{1,0:T(8,128)(2,1)S(1)} %reshape.68), channel_id=1, source_target_pairs={{0,32},{32,0},{1,33},{33,1},{2,34},{34,2},{3,35},{35,3},{4,36},{36... | collective-permute-start | bytes 196616 | tf_op jit(solution)/shard_map/ppermute | solution.py:81
  33.6 18.5 %collective-permute-start.9 = (bf16[768,1024]{1,0:T(8,128)(2,1)}, bf16[768,1024]{1,0:T(8,128)(2,1)}, u32[]{:S(2)}, u32[]{:S(2)}) collective-permute-start(bf16[768,1024]{1,0:T(8,128)(2,1)} %pad_maximum_fusion), channel_id=1, source_target_pairs={{0,1},{1,0},{2,3},{3,2},{4,5},{5,4},{6,7},{7,6},{8,9},{9,8},{10,11... | collective-permute-start | bytes 4718600 | tf_op jit(solution)/shard_map/ppermute | solution.py:81
  33.6 8.4 %collective-permute-start.8 = (bf16[256,1024]{1,0:T(8,128)(2,1)S(1)}, bf16[256,1024]{1,0:T(8,128)(2,1)S(1)}, u32[]{:S(2)}, u32[]{:S(2)}) collective-permute-start(bf16[256,1024]{1,0:T(8,128)(2,1)S(1)} %copy-done.2), channel_id=1, source_target_pairs={{0,1},{1,0},{2,3},{3,2},{4,5},{5,4},{6,7},{7,6},{8,9},{9,8},{10,11... | collective-permute-start | bytes 1572872 | tf_op jit(solution)/shard_map/ppermute | solution.py:81
  34.1 13.5 %collective-permute-start.4 = (bf16[32,2048]{1,0:T(8,128)(2,1)}, bf16[32,2048]{1,0:T(8,128)(2,1)S(1)}, u32[]{:S(2)}, u32[]{:S(2)}) collective-permute-start(bf16[32,2048]{1,0:T(8,128)(2,1)} %pad_maximum_fusion.4), channel_id=1, source_target_pairs={{0,0},{1,64},{8,1},{9,65},{16,128},{17,192},{24,129},{25,193},{64,... | collective-permute-start | bytes 393224 | tf_op jit(solution)/shard_map/ppermute | solution.py:99
  38.2 11.0 %collective-permute-start.5 = (bf16[32,2048]{1,0:T(8,128)(2,1)}, bf16[32,2048]{1,0:T(8,128)(2,1)S(1)}, u32[]{:S(2)}, u32[]{:S(2)}) collective-permute-start(bf16[32,2048]{1,0:T(8,128)(2,1)} %pad_maximum_fusion.4), channel_id=1, source_target_pairs={{0,64},{1,0},{8,65},{9,1},{16,192},{17,128},{24,193},{25,129},{64,... | collective-permute-start | bytes 393224 | tf_op jit(solution)/shard_map/ppermute | solution.py:99
  42.0 8.9 %collective-permute-start.6 = (bf16[32,2048]{1,0:T(8,128)(2,1)}, bf16[32,2048]{1,0:T(8,128)(2,1)S(1)}, u32[]{:S(2)}, u32[]{:S(2)}) collective-permute-start(bf16[32,2048]{1,0:T(8,128)(2,1)} %pad_maximum_fusion.4), channel_id=1, source_target_pairs={{0,128},{1,192},{8,129},{9,193},{16,0},{17,64},{24,1},{25,65},{64,... | collective-permute-start | bytes 393224 | tf_op jit(solution)/shard_map/ppermute | solution.py:99
  42.0 0.8 copy-start.4
  42.8 9.3 %collective-permute-start.7 = (bf16[32,2048]{1,0:T(8,128)(2,1)}, bf16[32,2048]{1,0:T(8,128)(2,1)}, u32[]{:S(2)}, u32[]{:S(2)}) collective-permute-start(bf16[32,2048]{1,0:T(8,128)(2,1)} %pad_maximum_fusion.4), channel_id=1, source_target_pairs={{0,192},{1,128},{8,193},{9,129},{16,64},{17,0},{24,65},{25,1},{64,... | collective-permute-start | bytes 393224 | tf_op jit(solution)/shard_map/ppermute | solution.py:99
  44.3 31.3 %copy-start.6 = (f32[1024]{0:T(1024)S(1)}, f32[1024]{0:T(1024)}, u32[]{:S(2)}) copy-start(f32[1024]{0:T(1024)} %param.21) | copy-start | bytes 12292
  52.2 1.0 copy-start.3
  53.2 1.0 copy-start.5
  58.5 17.1 %collective-permute-start.10 = (bf16[1024,896]{1,0:T(8,128)(2,1)}, bf16[1024,896]{1,0:T(8,128)(2,1)}, u32[]{:S(2)}, u32[]{:S(2)}) collective-permute-start(bf16[1024,896]{1,0:T(8,128)(2,1)} %refs_3_.1), channel_id=1, source_target_pairs={{0,1},{1,0},{2,3},{3,2},{4,5},{5,4},{6,7},{7,6},{8,9},{9,8},{10,11... | collective-permute-start | bytes 5505032 | tf_op jit(solution)/shard_map/ppermute | solution.py:81
  58.6 17.0 %collective-permute-start.11 = (bf16[1024,896]{1,0:T(8,128)(2,1)}, bf16[1024,896]{1,0:T(8,128)(2,1)}, u32[]{:S(2)}, u32[]{:S(2)}) collective-permute-start(bf16[1024,896]{1,0:T(8,128)(2,1)} %refs_4_.3), channel_id=1, source_target_pairs={{0,1},{1,0},{2,3},{3,2},{4,5},{5,4},{6,7},{7,6},{8,9},{9,8},{10,11... | collective-permute-start | bytes 5505032 | tf_op jit(solution)/shard_map/ppermute | solution.py:81
  59.1 16.4 %all-to-all-start.1 = ((bf16[4,32,1024]{2,1,0:T(8,128)(2,1)}), bf16[4,32,1024]{2,1,0:T(8,128)(2,1)S(1)}, u32[]{:S(2)}, u32[]{:S(2)}) async-start(bf16[4,32,1024]{2,1,0:T(8,128)(2,1)} %bitcast.5), calls=%async_computation.1 | async-start | bytes 524288 | tf_op jit(solution)/shard_map/all_to_all | solution.py:278
  75.7 6.4 %collective-permute-start.12 = (bf16[32,1024]{1,0:T(8,128)(2,1)S(1)}, bf16[32,1024]{1,0:T(8,128)(2,1)S(1)}, u32[]{:S(2)}, u32[]{:S(2)}) collective-permute-start(bf16[32,1024]{1,0:T(8,128)(2,1)S(1)} %get-tuple-element.28), channel_id=1, source_target_pairs={{2,0},{4,2},{6,4},{0,6},{3,1},{5,3},{7,5},{1,7},{10,8},{12,10},{14... | collective-permute-start | bytes 196616 | tf_op jit(solution)/shard_map/ppermute | solution.py:85
  77.0 9.3 %collective-permute-start.13 = (bf16[32,1024]{1,0:T(8,128)(2,1)S(1)}, bf16[32,1024]{1,0:T(8,128)(2,1)S(1)}, u32[]{:S(2)}, u32[]{:S(2)}) collective-permute-start(bf16[32,1024]{1,0:T(8,128)(2,1)S(1)} %get-tuple-element.28), channel_id=1, source_target_pairs={{4,0},{6,2},{0,4},{2,6},{5,1},{7,3},{1,5},{3,7},{12,8},{14,10},{8,... | collective-permute-start | bytes 196616 | tf_op jit(solution)/shard_map/ppermute | solution.py:85
  81.0 7.0 %collective-permute-start.14 = (bf16[32,1024]{1,0:T(8,128)(2,1)S(1)}, bf16[32,1024]{1,0:T(8,128)(2,1)S(1)}, u32[]{:S(2)}, u32[]{:S(2)}) collective-permute-start(bf16[32,1024]{1,0:T(8,128)(2,1)S(1)} %get-tuple-element.28), channel_id=1, source_target_pairs={{6,0},{0,2},{2,4},{4,6},{7,1},{1,3},{3,5},{5,7},{14,8},{8,10},{10,... | collective-permute-start | bytes 196616 | tf_op jit(solution)/shard_map/ppermute | solution.py:85
  92.7 25.4 %all-to-all-start.2 = ((bf16[8,16,3712]{2,1,0:T(8,128)(2,1)}), bf16[8,16,3712]{2,1,0:T(8,128)(2,1)}, u32[]{:S(2)}, u32[]{:S(2)}) async-start(bf16[8,16,3712]{2,1,0:T(8,128)(2,1)} %bitcast.7), calls=%async_computation.2 | async-start | bytes 1900544 | tf_op jit(solution)/shard_map/all_to_all | solution.py:278
  97.3 8.1 %collective-permute-start.15 = (bf16[128,1024]{1,0:T(8,128)(2,1)S(1)}, bf16[128,1024]{1,0:T(8,128)(2,1)S(1)}, u32[]{:S(2)}, u32[]{:S(2)}) collective-permute-start(bf16[128,1024]{1,0:T(8,128)(2,1)S(1)} %pad_maximum_fusion.1.refs_0_), channel_id=1, source_target_pairs={{8,0},{16,8},{24,16},{0,24},{9,1},{17,9},{25,17},{1,25},{10,2},{18... | collective-permute-start | bytes 786440 | tf_op jit(solution)/shard_map/ppermute | solution.py:85
  99.5 8.8 %collective-permute-start.16 = (bf16[128,1024]{1,0:T(8,128)(2,1)S(1)}, bf16[128,1024]{1,0:T(8,128)(2,1)S(1)}, u32[]{:S(2)}, u32[]{:S(2)}) collective-permute-start(bf16[128,1024]{1,0:T(8,128)(2,1)S(1)} %pad_maximum_fusion.1.refs_0_), channel_id=1, source_target_pairs={{16,0},{24,8},{0,16},{8,24},{17,1},{25,9},{1,17},{9,25},{18,2},{26... | collective-permute-start | bytes 786440 | tf_op jit(solution)/shard_map/ppermute | solution.py:85
  102.1 8.9 %collective-permute-start.17 = (bf16[128,1024]{1,0:T(8,128)(2,1)S(1)}, bf16[128,1024]{1,0:T(8,128)(2,1)S(1)}, u32[]{:S(2)}, u32[]{:S(2)}) collective-permute-start(bf16[128,1024]{1,0:T(8,128)(2,1)S(1)} %pad_maximum_fusion.1.refs_0_), channel_id=1, source_target_pairs={{24,0},{0,8},{8,16},{16,24},{25,1},{1,9},{9,17},{17,25},{26,2},{2,... | collective-permute-start | bytes 786440 | tf_op jit(solution)/shard_map/ppermute | solution.py:85
  116.6 1.6 copy-start.1
  118.1 34.1 %all-to-all-start.3 = ((bf16[8,48,3712]{2,1,0:T(8,128)(2,1)}), bf16[8,48,3712]{2,1,0:T(8,128)(2,1)}, u32[]{:S(2)}, u32[]{:S(2)}) async-start(bf16[8,48,3712]{2,1,0:T(8,128)(2,1)} %bitcast.56), calls=%async_computation.3 | async-start | bytes 5701632 | tf_op jit(solution)/shard_map/all_to_all | solution.py:278
  156.4 25.1 %all-to-all-start.4 = ((bf16[8,64,1792]{2,1,0:T(8,128)(2,1)}), bf16[8,64,1792]{2,1,0:T(8,128)(2,1)}, u32[]{:S(2)}, u32[]{:S(2)}) async-start(bf16[8,64,1792]{2,1,0:T(8,128)(2,1)} %broadcast_in_dim.19), calls=%async_computation.4 | async-start | bytes 3670016 | tf_op jit(solution)/shard_map/all_to_all | solution.py:278
  162.6 4.0 %collective-permute-start.18 = (bf16[896,1024]{1,0:T(8,128)(2,1)}, bf16[896,1024]{1,0:T(8,128)(2,1)S(1)}, u32[]{:S(2)}, u32[]{:S(2)}) collective-permute-start(bf16[896,1024]{1,0:T(8,128)(2,1)} %own.1), channel_id=1, source_target_pairs={{0,1},{1,0},{2,3},{3,2},{4,5},{5,4},{6,7},{7,6},{8,9},{9,8},{10,11... | collective-permute-start | bytes 5505032 | tf_op jit(solution)/shard_map/ppermute | solution.py:81
  166.6 1.3 copy-start.8
  181.5 1.5 copy-start.7
  183.0 1.5 copy-start.9
  188.2 10.4 %collective-permute-start.19 = (bf16[128,1024]{1,0:T(8,128)(2,1)S(1)}, bf16[128,1024]{1,0:T(8,128)(2,1)S(1)}, u32[]{:S(2)}, u32[]{:S(2)}) collective-permute-start(bf16[128,1024]{1,0:T(8,128)(2,1)S(1)} %get-tuple-element.34), channel_id=1, source_target_pairs={{0,8},{8,16},{16,24},{24,0},{1,9},{9,17},{17,25},{25,1},{2,10},{10... | collective-permute-start | bytes 786440 | tf_op jit(solution)/shard_map/ppermute | solution.py:89
  188.3 14.1 %collective-permute-start.20 = (bf16[128,1024]{1,0:T(8,128)(2,1)S(1)}, bf16[128,1024]{1,0:T(8,128)(2,1)S(1)}, u32[]{:S(2)}, u32[]{:S(2)}) collective-permute-start(bf16[128,1024]{1,0:T(8,128)(2,1)S(1)} %get-tuple-element.35), channel_id=1, source_target_pairs={{0,16},{8,24},{16,0},{24,8},{1,17},{9,25},{17,1},{25,9},{2,18},{10... | collective-permute-start | bytes 786440 | tf_op jit(solution)/shard_map/ppermute | solution.py:89
  193.3 9.1 %collective-permute-start.21 = (bf16[128,1024]{1,0:T(8,128)(2,1)S(1)}, bf16[128,1024]{1,0:T(8,128)(2,1)S(1)}, u32[]{:S(2)}, u32[]{:S(2)}) collective-permute-start(bf16[128,1024]{1,0:T(8,128)(2,1)S(1)} %get-tuple-element.36), channel_id=1, source_target_pairs={{0,24},{8,0},{16,8},{24,16},{1,25},{9,1},{17,9},{25,17},{2,26},{10... | collective-permute-start | bytes 786440 | tf_op jit(solution)/shard_map/ppermute | solution.py:89
  202.6 6.5 %collective-permute-start.22 = (bf16[32,1024]{1,0:T(8,128)(2,1)S(1)}, bf16[32,1024]{1,0:T(8,128)(2,1)S(1)}, u32[]{:S(2)}, u32[]{:S(2)}) collective-permute-start(bf16[32,1024]{1,0:T(8,128)(2,1)S(1)} %get-tuple-element.43), channel_id=1, source_target_pairs={{0,2},{2,4},{4,6},{6,0},{1,3},{3,5},{5,7},{7,1},{8,10},{10,12},{12... | collective-permute-start | bytes 196616 | tf_op jit(solution)/shard_map/ppermute | solution.py:89
  202.7 8.6 %collective-permute-start.23 = (bf16[32,1024]{1,0:T(8,128)(2,1)S(1)}, bf16[32,1024]{1,0:T(8,128)(2,1)S(1)}, u32[]{:S(2)}, u32[]{:S(2)}) collective-permute-start(bf16[32,1024]{1,0:T(8,128)(2,1)S(1)} %get-tuple-element.45), channel_id=1, source_target_pairs={{0,4},{2,6},{4,0},{6,2},{1,5},{3,7},{5,1},{7,3},{8,12},{10,14},{12... | collective-permute-start | bytes 196616 | tf_op jit(solution)/shard_map/ppermute | solution.py:89
  207.0 9.1 %collective-permute-start.24 = (bf16[32,1024]{1,0:T(8,128)(2,1)S(1)}, bf16[32,1024]{1,0:T(8,128)(2,1)S(1)}, u32[]{:S(2)}, u32[]{:S(2)}) collective-permute-start(bf16[32,1024]{1,0:T(8,128)(2,1)S(1)} %get-tuple-element.44), channel_id=1, source_target_pairs={{0,6},{2,0},{4,2},{6,4},{1,7},{3,1},{5,3},{7,5},{8,14},{10,8},{12,... | collective-permute-start | bytes 196616 | tf_op jit(solution)/shard_map/ppermute | solution.py:89

commit v2 on v1

--- a/solution.py
+++ b/solution.py
@@ -13,6 +13,7 @@
 VMEM = pl.BlockSpec(memory_space=pltpu.VMEM)
 SMEM = pl.BlockSpec(memory_space=pltpu.SMEM)
 ANY = pl.BlockSpec(memory_space=pl.ANY)
+HBM = pl.BlockSpec(memory_space=pltpu.HBM)
 STEP = 256
 
 D = 8192
@@ -68,12 +69,13 @@
 
 
 def places():
-    table = np.zeros((256, 13), np.int32)
+    table = np.zeros((256, 17), np.int32)
     for device in range(256):
         x, l, y, core = device >> 6, (device >> 5) & 1, (device >> 3) & 3, device & 1
         table[device, :8] = [(l ^ b) * 4 + (x ^ j) for j in range(4) for b in range(2)]
         table[device, 8:12] = [(y + t) % 4 for t in range(4)]
         table[device, 12] = core
+        table[device, 13:] = [((device >> 1) + t) % 4 for t in range(4)]
     return table
 
 
@@ -123,7 +125,7 @@
 
 def project_kernel(place_ref, *refs):
     pieces, own, other, others = refs[:4], refs[4:8], refs[8], refs[9]
-    out_ref, rows_ref, held_ref, row_sems, held_sems = refs[10:]
+    outs, rows_ref, held_ref, total_ref, row_sems, held_sems = refs[10:14], *refs[14:]
     step = pieces[0].shape[0] // 2
     row_copies = start_all(
         [
@@ -148,9 +150,13 @@
     wait_all(row_copies)
     wait_all(held_copies)
     for n, size in steps(width):
-        out_ref[:, n : n + size] = jnp.dot(
+        total_ref[:, n : n + size] = jnp.dot(
             rows_ref[...], held_ref[:, n : n + size], preferred_element_type=jnp.float32
-        ).astype(out_ref.dtype)
+        )
+    share = outs[0].shape[0]
+    for t in range(4):
+        start = pl.multiple_of(place_ref[13 + t] * share, share)
+        outs[t][...] = total_ref[pl.ds(start, share), :].astype(outs[t].dtype)
 
 
 def project(place, pieces, own, other, others):
@@ -158,12 +164,15 @@
     width = other.shape[1]
     return pl.pallas_call(
         project_kernel,
-        in_specs=[SMEM] + [ANY] * 10,
-        out_specs=VMEM,
-        out_shape=jax.ShapeDtypeStruct((count, width), jnp.bfloat16),
+        in_specs=[SMEM] + [ANY] * 4 + [HBM] * 6,
+        out_specs=[VMEM] * 4,
+        out_shape=[
+            jax.ShapeDtypeStruct((count // 4, width), jnp.float32 if t == 0 else jnp.bfloat16) for t in range(4)
+        ],
         scratch_shapes=[
             pltpu.VMEM((count, depth), jnp.bfloat16),
             pltpu.VMEM((depth, width), jnp.bfloat16),
+            pltpu.VMEM((count, width), jnp.float32),
             pltpu.SemaphoreType.DMA((8,)),
             pltpu.SemaphoreType.DMA((8,)),
         ],
@@ -173,8 +182,8 @@
 
 
 def gate_up_kernel(gain_ref, *refs):
-    pieces, weights = refs[:-9], refs[-9:-5]
-    out_ref, rows_ref, held_ref, row_sems, held_sems = refs[-5:]
+    pieces, weights = refs[:-11], refs[-11:-7]
+    sent_ref, rows_ref, held_ref, out_ref, row_sems, held_sems, out_sems = refs[-7:]
     step = pieces[0].shape[0]
     width = weights[0].shape[1]
     row_copies = start_all(
@@ -196,11 +205,15 @@
         high = squares.astype(jnp.bfloat16).astype(jnp.float32)
         columns = jnp.where(lane == 0, high, jnp.where(lane == 1, squares - high, 0.0))
         out_ref[t : t + part, 4 * width :] = columns.astype(out_ref.dtype)
+    out_copies = []
     for j in range(4):
         held_copies[j].wait()
         for n, size in steps(width):
             product = jnp.dot(rows_ref[...], held_ref[j, :, n : n + size], preferred_element_type=jnp.float32)
             out_ref[:, j * width + n : j * width + n + size] = product.astype(out_ref.dtype)
+        done = pl.ds(j * width, width if j < 3 else width + 128)
+        out_copies += start_all([pltpu.make_async_copy(out_ref.at[:, done], sent_ref.at[:, done], out_sems.at[j])])
+    wait_all(out_copies)
 
 
 def gate_up(gain, pieces, weights):
@@ -208,13 +221,15 @@
     width = weights[0].shape[1]
     return pl.pallas_call(
         gate_up_kernel,
-        in_specs=[VMEM] + [ANY] * (len(pieces) + 4),
-        out_specs=VMEM,
+        in_specs=[VMEM] + [ANY] * len(pieces) + [HBM] * 4,
+        out_specs=HBM,
         out_shape=jax.ShapeDtypeStruct((count, 4 * width + 128), jnp.bfloat16),
         scratch_shapes=[
             pltpu.VMEM((count, depth), jnp.bfloat16),
             pltpu.VMEM((4, depth, width), jnp.bfloat16),
+            pltpu.VMEM((count, 4 * width + 128), jnp.bfloat16),
             pltpu.SemaphoreType.DMA((len(pieces),)),
+            pltpu.SemaphoreType.DMA((4,)),
             pltpu.SemaphoreType.DMA((4,)),
         ],
         name="gate_up",
@@ -235,17 +250,17 @@
     )
     row_copy.wait()
     share = outs[0].shape[0]
-    first = share // 8
-    near = rows_ref[:, :first].reshape(share, 2 * depth)
-    far = rows_ref[:, first:].reshape(3 * share, 2 * depth)
+    first = hidden_ref.shape[1] // 2
+    near = rows_ref[:, :first].reshape(2 * share, 2 * depth)
+    far = rows_ref[:, first:].reshape(2 * share, 2 * depth)
     wait_all(held_copies)
     for n, size in steps(width):
         columns = held_ref[:, n : n + size]
-        product = jnp.dot(far, columns, preferred_element_type=jnp.float32)
-        for t in range(3):
-            outs[t + 1][:, n : n + size] = product[t * share : (t + 1) * share].astype(outs[t + 1].dtype)
-        product = jnp.dot(near, columns, preferred_element_type=jnp.float32)
-        outs[0][:, n : n + size] = product.astype(outs[0].dtype)
+        for i, rows in enumerate((near, far)):
+            product = jnp.dot(rows, columns, preferred_element_type=jnp.float32)
+            for t in range(2):
+                out_ref = outs[2 * i + t]
+                out_ref[:, n : n + size] = product[t * share : (t + 1) * share].astype(out_ref.dtype)
 
 
 def down(hidden, weights):
@@ -253,7 +268,7 @@
     depth, width = weights[0].shape
     return pl.pallas_call(
         down_kernel,
-        in_specs=[ANY] * 3,
+        in_specs=[ANY] + [HBM] * 2,
         out_specs=[VMEM] * 4,
         out_shape=[jax.ShapeDtypeStruct((count // 4, width), jnp.bfloat16)] * 4,
         scratch_shapes=[
@@ -316,22 +331,22 @@
     out_others = swap(jnp.concatenate(out_own[1:], axis=0), "core")
     pieces = [spread(block, step) for step in range(4)]
     partial = project(place, pieces, out_own, out_other, out_others)
-    partial, *late = lax.optimization_barrier((partial, w_gate, w_up))
-    gate_other, up_other = [swap(w, "core") for w in late]
+    *partial, gate_late, up_late = lax.optimization_barrier((*partial, w_gate, w_up))
+    gate_other, up_other = swap(gate_late, "core"), swap(up_late, "core")
 
     share = hidden_in.shape[0] // 32
     own_in = lax.dynamic_slice_in_dim(hidden_in, (device & 31) * share, share, 0)
     own_in = own_in.reshape(4, 2, count, -1).transpose(1, 0, 2, 3).reshape(share, -1)
-    mixed = own_in.astype(jnp.float32) + scatter_sum(partial, "z")
+    mixed = own_in.astype(jnp.float32) + add_up([partial[0]] + [ring_to(partial[t], "z", t) for t in (1, 2, 3)])
     normed = (mixed * norm_gain).astype(jnp.bfloat16)
     normed, gate_other, up_other = lax.optimization_barrier((normed, gate_other, up_other))
 
     block = jnp.concatenate([normed] + [ring_from(normed, "z", t) for t in (1, 2, 3)], axis=0)
     block, late = lax.optimization_barrier((block, w_down))
     down_other = swap(late, "core")
-    pieces = [ring_from(block, "y", t) for t in (1, 2, 3)]
+    pieces = [block] + [ring_from(block, "y", t) for t in (1, 2, 3)]
     weights = [w_gate, w_up, gate_other, up_other]
-    summed = [scatter_sum(gate_up(norm_gain[None, :], part, weights), GRP) for part in ([block], pieces)]
+    summed = [scatter_sum(gate_up(norm_gain[None, :], part, weights), GRP) for part in (pieces[:2], pieces[2:])]
     summed = jnp.concatenate(summed, axis=0)
     width = w_gate.shape[1]
     square_sum = summed[:, 4 * width] + summed[:, 4 * width + 1]

time: 218 us -> 223 us (1.023)
  the two profiles are of different devices: /device:TPU:6 before, /device:TPU:1 now
where the time goes in v2:
time: 223 us; the launch traced here: 221 us
  waiting for transfers between devices  87.8 us (39%)
  starting transfers between devices  71.7 us (32%)
  Pallas kernels  16.6 us (7%)
  local copies, waits for them, and re-layouts  15.9 us (7%)
  blocking collectives  15 us (7%)
  other arithmetic  10.1 us (5%)
  matrix products  3.15 us (1%)
    all_to_all x3, waiting for transfers between devices, exchange(): return lax.all_to_all(pieces, axis, split_axis=0, concat_axis=0, tiled=True)  36.4 us
    ppermute x9, waiting for transfers between devices, ring_from(): return lax.ppermute(block, axis, [((i + shift) % 4, i) for i in range(4)])  21.2 us
    ppermute x9, starting transfers between devices, ring_to(): return lax.ppermute(block, axis, [(i, (i + shift) % 4) for i in range(4)])  19.3 us
    all_to_all x3, starting transfers between devices, exchange(): return lax.all_to_all(pieces, axis, split_axis=0, concat_axis=0, tiled=True)  18.6 us
    ppermute x9, waiting for transfers between devices, ring_to(): return lax.ppermute(block, axis, [(i, (i + shift) % 4) for i in range(4)])  17.9 us
    ppermute x9, starting transfers between devices, ring_from(): return lax.ppermute(block, axis, [((i + shift) % 4, i) for i in range(4)])  16.6 us
    all_to_all x1, blocking collectives, exchange(): return lax.all_to_all(pieces, axis, split_axis=0, concat_axis=0, tiled=True)  15 us
    unnamed x35, local copies, waits for them, and re-layouts  12.2 us
  transfers between devices with their start and end apart: 31, of which 19 were waited for; matrix products, arithmetic and copies ran while one was open for 5% of the time, Pallas kernels for 2%

profile of v2, /device:TPU:1, one launch (start us, length us, event | category | flops | bytes accessed | tf_op | source)
XLA Modules:
  0.0 220.6 jit_solution(17074220660547647692)
XLA Ops:
  0.0 3.6 %collective-permute-start.1 = (bf16[256,1024]{1,0:T(8,128)(2,1)}, bf16[256,1024]{1,0:T(8,128)(2,1)S(1)}, u32[]{:S(2)}, u32[]{:S(2)}) collective-permute-start(bf16[256,1024]{1,0:T(8,128)(2,1)} %refs_4_.1), channel_id=1, source_target_pairs={{8,0},{16,8},{24,16},{0,24},{9,1},{17,9},{25,17},{1,25},{10,2},{18... | collective-permute-start | bytes 1572872 | tf_op jit(solution)/shard_map/ppermute | solution.py:87
  7.2 1.6 fusion.51
  9.7 15.0 %all_to_all.20 = bf16[4,4,2048]{2,1,0:T(4,128)(2,1)S(1)} all-to-all(bf16[4,4,2048]{2,1,0:T(4,128)(2,1)S(1)} %reshape.64), channel_id=1, replica_groups=mesh['x'=4,'l'=2,'y'=4,'z'=4,'core'=2] {'z'}, dimensions={0} | all-to-all | bytes 131072 | tf_op jit(solution)/shard_map/all_to_all | solution.py:293
  25.6 2.8 %collective-permute-done = bf16[16,2048]{1,0:T(8,128)(2,1)S(1)} collective-permute-done((bf16[16,2048]{1,0:T(8,128)(2,1)S(1)}, bf16[16,2048]{1,0:T(8,128)(2,1)S(1)}, u32[]{:S(2)}, u32[]{:S(2)}) %collective-permute-start) | collective-permute-done | bytes 65568 | tf_op jit(solution)/shard_map/ppermute | solution.py:83
  29.0 1.4 collective-permute-done.3.refs_7_
  30.5 2.3 %pad_maximum_fusion = bf16[768,1024]{1,0:T(8,128)(2,1)} fusion(bf16[256,1024]{1,0:T(8,128)(2,1)} %collective-permute-done.3.refs_7_, bf16[256,1024]{1,0:T(8,128)(2,1)S(1)} %collective-permute-done.2.refs_6_, bf16[256,1024]{1,0:T(8,128)(2,1)S(1)} %collective-permute-done.1.refs_5_), kind=kLoop, calls=%fused_computation.18 | loop fusion | flops 4718592 | bytes 3145728 | tf_op jit(solution)/shard_map/concatenate | solution.py:331
  32.8 2.4 %collective-permute-start.9 = (bf16[768,1024]{1,0:T(8,128)(2,1)}, bf16[768,1024]{1,0:T(8,128)(2,1)}, u32[]{:S(2)}, u32[]{:S(2)}) collective-permute-start(bf16[768,1024]{1,0:T(8,128)(2,1)} %pad_maximum_fusion), channel_id=1, source_target_pairs={{0,1},{1,0},{2,3},{3,2},{4,5},{5,4},{6,7},{7,6},{8,9},{9,8},{10,11... | collective-permute-start | bytes 4718600 | tf_op jit(solution)/shard_map/ppermute | solution.py:83
  35.2 3.5 %collective-permute-start.4 = (bf16[32,2048]{1,0:T(8,128)(2,1)}, bf16[32,2048]{1,0:T(8,128)(2,1)S(1)}, u32[]{:S(2)}, u32[]{:S(2)}) collective-permute-start(bf16[32,2048]{1,0:T(8,128)(2,1)} %pad_maximum_fusion.4), channel_id=1, source_target_pairs={{0,0},{1,64},{8,1},{9,65},{16,128},{17,192},{24,129},{25,193},{64,... | collective-permute-start | bytes 393224 | tf_op jit(solution)/shard_map/ppermute | solution.py:101
  38.8 7.2 %collective-permute-start.6 = (bf16[32,2048]{1,0:T(8,128)(2,1)}, bf16[32,2048]{1,0:T(8,128)(2,1)S(1)}, u32[]{:S(2)}, u32[]{:S(2)}) collective-permute-start(bf16[32,2048]{1,0:T(8,128)(2,1)} %pad_maximum_fusion.4), channel_id=1, source_target_pairs={{0,128},{1,192},{8,129},{9,193},{16,0},{17,64},{24,1},{25,65},{64,... | collective-permute-start | bytes 393224 | tf_op jit(solution)/shard_map/ppermute | solution.py:101
  47.5 3.7 %collective-permute-done.6.refs_2_ = bf16[32,2048]{1,0:T(8,128)(2,1)S(1)} collective-permute-done((bf16[32,2048]{1,0:T(8,128)(2,1)}, bf16[32,2048]{1,0:T(8,128)(2,1)S(1)}, u32[]{:S(2)}, u32[]{:S(2)}) %collective-permute-start.6) | collective-permute-done | bytes 131104 | tf_op jit(solution)/shard_map/ppermute | solution.py:101
  51.1 2.1 collective-permute-done.7.refs_3_
  55.3 3.6 %project.1 = (f32[32,1024]{1,0:T(8,128)S(1)}, bf16[32,1024]{1,0:T(8,128)(2,1)S(1)}, bf16[32,1024]{1,0:T(8,128)(2,1)S(1)}, bf16[32,1024]{1,0:T(8,128)(2,1)S(1)}) custom-call(s32[17]{0:T(128)S(1)} %dynamic-slice_bitcast_fusion.place_ref, bf16[32,2048]{1,0:T(8,128)(2,1)S(1)} %collective-permute-done.4.refs_0_, ...), custom_call_target="tpu_custom_call" | custom-call | flops 536870912 | bytes 4980736 | tf_op jit(solution)/shard_map/project/pallas_call | solution.py:165
  62.0 1.6 collective-permute-start.12
  63.6 1.7 collective-permute-start.11
  65.3 1.6 collective-permute-start.10
  67.9 3.2 %collective-permute-done.11 = bf16[32,1024]{1,0:T(8,128)(2,1)S(1)} collective-permute-done((bf16[32,1024]{1,0:T(8,128)(2,1)}, bf16[32,1024]{1,0:T(8,128)(2,1)S(1)}, u32[]{:S(2)}, u32[]{:S(2)}) %collective-permute-start.11) | collective-permute-done | bytes 65568 | tf_op jit(solution)/shard_map/ppermute | solution.py:91
  71.1 2.0 collective-permute-done.10
  74.1 3.0 %collective-permute-start.16 = (bf16[32,1024]{1,0:T(8,128)(2,1)S(1)}, bf16[32,1024]{1,0:T(8,128)(2,1)S(1)}, u32[]{:S(2)}, u32[]{:S(2)}) collective-permute-start(bf16[32,1024]{1,0:T(8,128)(2,1)S(1)} %get-tuple-element.42), channel_id=1, source_target_pairs={{4,0},{6,2},{0,4},{2,6},{5,1},{7,3},{1,5},{3,7},{12,8},{14,10},{8,... | collective-permute-start | bytes 196616 | tf_op jit(solution)/shard_map/ppermute | solution.py:87
  77.1 3.0 %collective-permute-start.15 = (bf16[32,1024]{1,0:T(8,128)(2,1)S(1)}, bf16[32,1024]{1,0:T(8,128)(2,1)S(1)}, u32[]{:S(2)}, u32[]{:S(2)}) collective-permute-start(bf16[32,1024]{1,0:T(8,128)(2,1)S(1)} %get-tuple-element.42), channel_id=1, source_target_pairs={{2,0},{4,2},{6,4},{0,6},{3,1},{5,3},{7,5},{1,7},{10,8},{12,10},{14... | collective-permute-start | bytes 196616 | tf_op jit(solution)/shard_map/ppermute | solution.py:87
  80.1 1.5 collective-permute-done.16
  82.0 3.1 %collective-permute-start.18 = (bf16[128,1024]{1,0:T(8,128)(2,1)S(1)}, bf16[128,1024]{1,0:T(8,128)(2,1)S(1)}, u32[]{:S(2)}, u32[]{:S(2)}) collective-permute-start(bf16[128,1024]{1,0:T(8,128)(2,1)S(1)} %pad_maximum_fusion.1.refs_0_), channel_id=1, source_target_pairs={{8,0},{16,8},{24,16},{0,24},{9,1},{17,9},{25,17},{1,25},{10,2},{18... | collective-permute-start | bytes 786440 | tf_op jit(solution)/shard_map/ppermute | solution.py:87
  85.1 5.7 %collective-permute-done.18.refs_1_ = bf16[128,1024]{1,0:T(8,128)(2,1)S(1)} collective-permute-done((bf16[128,1024]{1,0:T(8,128)(2,1)S(1)}, bf16[128,1024]{1,0:T(8,128)(2,1)S(1)}, u32[]{:S(2)}, u32[]{:S(2)}) %collective-permute-start.18) | collective-permute-done | bytes 262176 | tf_op jit(solution)/shard_map/ppermute | solution.py:87
  90.7 4.6 %gate_up.2 = bf16[256,3712]{1,0:T(8,128)(2,1)S(1)} custom-call(f32[1,1024]{1,0:T(1,128)S(1)} %bitcast.57, bf16[128,1024]{1,0:T(8,128)(2,1)S(1)} %pad_maximum_fusion.1.refs_0_, bf16[128,1024]{1,0:T(8,128)(2,1)S(1)} %collective-permute-done.18.refs_1_, bf16[1024,896]{1,0:T(8,128)(2,1)} %refs_2_.3, bf16[1024,896]{1,0:T(8,128)(2,1)} %refs_3_.3, ...), custom_call_target="tpu_custom_call" | custom-call | flops 1879048192 | bytes 9699328 | tf_op jit(solution)/shard_map/gate_up/pallas_call | solution.py:222
  96.6 8.4 %all-to-all-start.1 = ((bf16[8,32,3712]{2,1,0:T(8,128)(2,1)}), bf16[8,32,3712]{2,1,0:T(8,128)(2,1)}, u32[]{:S(2)}, u32[]{:S(2)}) async-start(bf16[8,32,3712]{2,1,0:T(8,128)(2,1)} %bitcast.55), calls=%async_computation.1 | async-start | bytes 3801088 | tf_op jit(solution)/shard_map/all_to_all | solution.py:293
  106.3 1.6 collective-permute-start.20
  107.9 4.5 %collective-permute-done.19.refs_0_ = bf16[128,1024]{1,0:T(8,128)(2,1)S(1)} collective-permute-done((bf16[128,1024]{1,0:T(8,128)(2,1)S(1)}, bf16[128,1024]{1,0:T(8,128)(2,1)S(1)}, u32[]{:S(2)}, u32[]{:S(2)}) %collective-permute-start.19) | collective-permute-done | bytes 262176 | tf_op jit(solution)/shard_map/ppermute | solution.py:87
  112.4 7.7 %collective-permute-done.20.refs_1_ = bf16[128,1024]{1,0:T(8,128)(2,1)S(1)} collective-permute-done((bf16[128,1024]{1,0:T(8,128)(2,1)S(1)}, bf16[128,1024]{1,0:T(8,128)(2,1)S(1)}, u32[]{:S(2)}, u32[]{:S(2)}) %collective-permute-start.20) | collective-permute-done | bytes 262176 | tf_op jit(solution)/shard_map/ppermute | solution.py:87
  120.1 4.6 %gate_up.3 = bf16[256,3712]{1,0:T(8,128)(2,1)S(1)} custom-call(f32[1,1024]{1,0:T(1,128)S(1)} %bitcast.58, bf16[128,1024]{1,0:T(8,128)(2,1)S(1)} %collective-permute-done.19.refs_0_, bf16[128,1024]{1,0:T(8,128)(2,1)S(1)} %collective-permute-done.20.refs_1_, bf16[1024,896]{1,0:T(8,128)(2,1)} %refs_2_.3, bf16[1024,896]{1,0:T(8,128)(2,1)} %refs_3_.3, ...), custom_call_target="tpu_custom_call" | custom-call | flops 1879048192 | bytes 9699328 | tf_op jit(solution)/shard_map/gate_up/pallas_call | solution.py:222
  126.0 2.0 all-to-all-done.1
  128.0 4.8 %all-to-all-start.2 = ((bf16[8,32,3712]{2,1,0:T(8,128)(2,1)}), bf16[8,32,3712]{2,1,0:T(8,128)(2,1)}, u32[]{:S(2)}, u32[]{:S(2)}) async-start(bf16[8,32,3712]{2,1,0:T(8,128)(2,1)} %bitcast.56), calls=%async_computation.2 | async-start | bytes 3801088 | tf_op jit(solution)/shard_map/all_to_all | solution.py:293
  132.9 1.8 convert_reduce_fusion.1
  134.7 20.5 %all-to-all-done.2 = bf16[8,32,3712]{2,1,0:T(8,128)(2,1)} async-done(((bf16[8,32,3712]{2,1,0:T(8,128)(2,1)}), bf16[8,32,3712]{2,1,0:T(8,128)(2,1)}, u32[]{:S(2)}, u32[]{:S(2)}) %all-to-all-start.2) | async-done | bytes 1900576 | tf_op jit(solution)/shard_map/all_to_all | solution.py:293
  155.2 1.8 convert_reduce_fusion
  157.5 1.4 broadcast_in_dim.19
  158.8 5.4 %all-to-all-start.3 = ((bf16[8,64,1792]{2,1,0:T(8,128)(2,1)}), bf16[8,64,1792]{2,1,0:T(8,128)(2,1)}, u32[]{:S(2)}, u32[]{:S(2)}) async-start(bf16[8,64,1792]{2,1,0:T(8,128)(2,1)} %broadcast_in_dim.19), calls=%async_computation.3 | async-start | bytes 3670016 | tf_op jit(solution)/shard_map/all_to_all | solution.py:293
  164.2 2.8 %collective-permute-start.21 = (bf16[896,1024]{1,0:T(8,128)(2,1)}, bf16[896,1024]{1,0:T(8,128)(2,1)S(1)}, u32[]{:S(2)}, u32[]{:S(2)}) collective-permute-start(bf16[896,1024]{1,0:T(8,128)(2,1)} %own.1), channel_id=1, source_target_pairs={{0,1},{1,0},{2,3},{3,2},{4,5},{5,4},{6,7},{7,6},{8,9},{9,8},{10,11... | collective-permute-start | bytes 5505032 | tf_op jit(solution)/shard_map/ppermute | solution.py:83
  167.0 3.6 %collective-permute-done.21.other = bf16[896,1024]{1,0:T(8,128)(2,1)S(1)} collective-permute-done((bf16[896,1024]{1,0:T(8,128)(2,1)}, bf16[896,1024]{1,0:T(8,128)(2,1)S(1)}, u32[]{:S(2)}, u32[]{:S(2)}) %collective-permute-start.21) | collective-permute-done | bytes 1835040 | tf_op jit(solution)/shard_map/ppermute | solution.py:83
  171.9 13.9 %all-to-all-done.3.hidden_ref = bf16[8,64,1792]{2,1,0:T(8,128)(2,1)} async-done(((bf16[8,64,1792]{2,1,0:T(8,128)(2,1)}), bf16[8,64,1792]{2,1,0:T(8,128)(2,1)}, u32[]{:S(2)}, u32[]{:S(2)}) %all-to-all-start.3) | async-done | bytes 1835040 | tf_op jit(solution)/shard_map/all_to_all | solution.py:293
  185.8 1.5 copy-done.9
  187.3 1.5 copy-done.11
  188.8 3.7 %down.1 = (bf16[128,1024]{1,0:T(8,128)(2,1)S(1)}, bf16[128,1024]{1,0:T(8,128)(2,1)S(1)}, bf16[128,1024]{1,0:T(8,128)(2,1)S(1)}, bf16[128,1024]{1,0:T(8,128)(2,1)S(1)}) custom-call(bf16[8,64,1792]{2,1,0:T(8,128)(2,1)} %all-to-all-done.3.hidden_ref, bf16[896,1024]{1,0:T(8,128)(2,1)S(1)} %copy-done.9, bf16[896,1024]{1,0:T(8,128)(2,1)S(1)} %copy-done.11), custom_call_target="tpu_custom_call" | custom-call | flops 1879048192 | bytes 6553600 | tf_op jit(solution)/shard_map/down/pallas_call | solution.py:269
  193.8 2.3 %collective-permute-start.23 = (bf16[128,1024]{1,0:T(8,128)(2,1)S(1)}, bf16[128,1024]{1,0:T(8,128)(2,1)S(1)}, u32[]{:S(2)}, u32[]{:S(2)}) collective-permute-start(bf16[128,1024]{1,0:T(8,128)(2,1)S(1)} %get-tuple-element.49), channel_id=1, source_target_pairs={{0,16},{8,24},{16,0},{24,8},{1,17},{9,25},{17,1},{25,9},{2,18},{10... | collective-permute-start | bytes 786440 | tf_op jit(solution)/shard_map/ppermute | solution.py:91
  196.1 2.0 collective-permute-done.24
  198.0 2.5 %collective-permute-done.23 = bf16[128,1024]{1,0:T(8,128)(2,1)S(1)} collective-permute-done((bf16[128,1024]{1,0:T(8,128)(2,1)S(1)}, bf16[128,1024]{1,0:T(8,128)(2,1)S(1)}, u32[]{:S(2)}, u32[]{:S(2)}) %collective-permute-start.23) | collective-permute-done | bytes 262176 | tf_op jit(solution)/shard_map/ppermute | solution.py:91
  200.6 4.0 %collective-permute-done.22 = bf16[128,1024]{1,0:T(8,128)(2,1)S(1)} collective-permute-done((bf16[128,1024]{1,0:T(8,128)(2,1)S(1)}, bf16[128,1024]{1,0:T(8,128)(2,1)S(1)}, u32[]{:S(2)}, u32[]{:S(2)}) %collective-permute-start.22) | collective-permute-done | bytes 262176 | tf_op jit(solution)/shard_map/ppermute | solution.py:91
  204.9 8.5 %collective-permute-start.26 = (bf16[32,1024]{1,0:T(8,128)(2,1)S(1)}, bf16[32,1024]{1,0:T(8,128)(2,1)S(1)}, u32[]{:S(2)}, u32[]{:S(2)}) collective-permute-start(bf16[32,1024]{1,0:T(8,128)(2,1)S(1)} %get-tuple-element.59), channel_id=1, source_target_pairs={{0,4},{2,6},{4,0},{6,2},{1,5},{3,7},{5,1},{7,3},{8,12},{10,14},{12... | collective-permute-start | bytes 196616 | tf_op jit(solution)/shard_map/ppermute | solution.py:91
  213.3 2.3 %collective-permute-start.25 = (bf16[32,1024]{1,0:T(8,128)(2,1)S(1)}, bf16[32,1024]{1,0:T(8,128)(2,1)S(1)}, u32[]{:S(2)}, u32[]{:S(2)}) collective-permute-start(bf16[32,1024]{1,0:T(8,128)(2,1)S(1)} %get-tuple-element.57), channel_id=1, source_target_pairs={{0,2},{2,4},{4,6},{6,0},{1,3},{3,5},{5,7},{7,1},{8,10},{10,12},{12... | collective-permute-start | bytes 196616 | tf_op jit(solution)/shard_map/ppermute | solution.py:91
  215.6 4.2 %collective-permute-done.25 = bf16[32,1024]{1,0:T(8,128)(2,1)S(1)} collective-permute-done((bf16[32,1024]{1,0:T(8,128)(2,1)S(1)}, bf16[32,1024]{1,0:T(8,128)(2,1)S(1)}, u32[]{:S(2)}, u32[]{:S(2)}) %collective-permute-start.25) | collective-permute-done | bytes 65568 | tf_op jit(solution)/shard_map/ppermute | solution.py:91
  (88 shorter events, 22.9 us)
Async XLA Ops:
  0.0 7.2 %copy-start = (bf16[4,256,1024]{2,1,0:T(8,128)(2,1)S(1)}, bf16[4,256,1024]{2,1,0:T(8,128)(2,1)}, u32[]{:S(2)}) copy-start(bf16[4,256,1024]{2,1,0:T(8,128)(2,1)} %param.15) | copy-start | bytes 6291460
  0.0 9.0 %copy-start.15 = (bf16[4,1024]{1,0:T(4,128)(2,1)S(1)}, bf16[4,1024]{1,0:T(4,128)(2,1)}, u32[]{:S(2)}) copy-start(bf16[4,1024]{1,0:T(4,128)(2,1)} %param.18) | copy-start | bytes 24580
  0.0 29.0 %collective-permute-start.1 = (bf16[256,1024]{1,0:T(8,128)(2,1)}, bf16[256,1024]{1,0:T(8,128)(2,1)S(1)}, u32[]{:S(2)}, u32[]{:S(2)}) collective-permute-start(bf16[256,1024]{1,0:T(8,128)(2,1)} %refs_4_.1), channel_id=1, source_target_pairs={{8,0},{16,8},{24,16},{0,24},{9,1},{17,9},{25,17},{1,25},{10,2},{18... | collective-permute-start | bytes 1572872 | tf_op jit(solution)/shard_map/ppermute | solution.py:87
  3.6 25.5 %collective-permute-start.2 = (bf16[256,1024]{1,0:T(8,128)(2,1)}, bf16[256,1024]{1,0:T(8,128)(2,1)S(1)}, u32[]{:S(2)}, u32[]{:S(2)}) collective-permute-start(bf16[256,1024]{1,0:T(8,128)(2,1)} %refs_4_.1), channel_id=1, source_target_pairs={{16,0},{24,8},{0,16},{8,24},{17,1},{25,9},{1,17},{9,25},{18,2},{26... | collective-permute-start | bytes 1572872 | tf_op jit(solution)/shard_map/ppermute | solution.py:87
  3.9 26.6 %collective-permute-start.3 = (bf16[256,1024]{1,0:T(8,128)(2,1)}, bf16[256,1024]{1,0:T(8,128)(2,1)}, u32[]{:S(2)}, u32[]{:S(2)}) collective-permute-start(bf16[256,1024]{1,0:T(8,128)(2,1)} %refs_4_.1), channel_id=1, source_target_pairs={{24,0},{0,8},{8,16},{16,24},{25,1},{1,9},{9,17},{17,25},{26,2},{2,... | collective-permute-start | bytes 1572872 | tf_op jit(solution)/shard_map/ppermute | solution.py:87
  6.0 3.0 %copy-start.16 = (bf16[4,256,1024]{2,1,0:T(8,128)(2,1)S(1)}, bf16[4,256,1024]{2,1,0:T(8,128)(2,1)}, u32[]{:S(2)}) copy-start(bf16[4,256,1024]{2,1,0:T(8,128)(2,1)} %param.16) | copy-start | bytes 6291460
  24.7 10.4 %copy-start.3 = (bf16[256,1024]{1,0:T(8,128)(2,1)S(1)}, bf16[256,1024]{1,0:T(8,128)(2,1)}, u32[]{:S(2)}) copy-start(bf16[256,1024]{1,0:T(8,128)(2,1)} %refs_4_.1) | copy-start | bytes 1572868
  24.7 3.6 %collective-permute-start = (bf16[16,2048]{1,0:T(8,128)(2,1)S(1)}, bf16[16,2048]{1,0:T(8,128)(2,1)S(1)}, u32[]{:S(2)}, u32[]{:S(2)}) collective-permute-start(bf16[16,2048]{1,0:T(8,128)(2,1)S(1)} %reshape.65), channel_id=1, source_target_pairs={{0,32},{32,0},{1,33},{33,1},{2,34},{34,2},{3,35},{35,3},{4,36},{36... | collective-permute-start | bytes 196616 | tf_op jit(solution)/shard_map/ppermute | solution.py:83
  32.8 20.4 %collective-permute-start.9 = (bf16[768,1024]{1,0:T(8,128)(2,1)}, bf16[768,1024]{1,0:T(8,128)(2,1)}, u32[]{:S(2)}, u32[]{:S(2)}) collective-permute-start(bf16[768,1024]{1,0:T(8,128)(2,1)} %pad_maximum_fusion), channel_id=1, source_target_pairs={{0,1},{1,0},{2,3},{3,2},{4,5},{5,4},{6,7},{7,6},{8,9},{9,8},{10,11... | collective-permute-start | bytes 4718600 | tf_op jit(solution)/shard_map/ppermute | solution.py:83
  35.2 10.8 %collective-permute-start.8 = (bf16[256,1024]{1,0:T(8,128)(2,1)S(1)}, bf16[256,1024]{1,0:T(8,128)(2,1)S(1)}, u32[]{:S(2)}, u32[]{:S(2)}) collective-permute-start(bf16[256,1024]{1,0:T(8,128)(2,1)S(1)} %copy-done.3), channel_id=1, source_target_pairs={{0,1},{1,0},{2,3},{3,2},{4,5},{5,4},{6,7},{7,6},{8,9},{9,8},{10,11... | collective-permute-start | bytes 1572872 | tf_op jit(solution)/shard_map/ppermute | solution.py:83
  35.2 12.3 %collective-permute-start.4 = (bf16[32,2048]{1,0:T(8,128)(2,1)}, bf16[32,2048]{1,0:T(8,128)(2,1)S(1)}, u32[]{:S(2)}, u32[]{:S(2)}) collective-permute-start(bf16[32,2048]{1,0:T(8,128)(2,1)} %pad_maximum_fusion.4), channel_id=1, source_target_pairs={{0,0},{1,64},{8,1},{9,65},{16,128},{17,192},{24,129},{25,193},{64,... | collective-permute-start | bytes 393224 | tf_op jit(solution)/shard_map/ppermute | solution.py:101
  38.7 8.8 %collective-permute-start.5 = (bf16[32,2048]{1,0:T(8,128)(2,1)}, bf16[32,2048]{1,0:T(8,128)(2,1)S(1)}, u32[]{:S(2)}, u32[]{:S(2)}) collective-permute-start(bf16[32,2048]{1,0:T(8,128)(2,1)} %pad_maximum_fusion.4), channel_id=1, source_target_pairs={{0,64},{1,0},{8,65},{9,1},{16,192},{17,128},{24,193},{25,129},{64,... | collective-permute-start | bytes 393224 | tf_op jit(solution)/shard_map/ppermute | solution.py:101
  38.8 12.4 %collective-permute-start.6 = (bf16[32,2048]{1,0:T(8,128)(2,1)}, bf16[32,2048]{1,0:T(8,128)(2,1)S(1)}, u32[]{:S(2)}, u32[]{:S(2)}) collective-permute-start(bf16[32,2048]{1,0:T(8,128)(2,1)} %pad_maximum_fusion.4), channel_id=1, source_target_pairs={{0,128},{1,192},{8,129},{9,193},{16,0},{17,64},{24,1},{25,65},{64,... | collective-permute-start | bytes 393224 | tf_op jit(solution)/shard_map/ppermute | solution.py:101
  45.9 0.8 copy-start.5
  46.7 6.5 %collective-permute-start.7 = (bf16[32,2048]{1,0:T(8,128)(2,1)}, bf16[32,2048]{1,0:T(8,128)(2,1)}, u32[]{:S(2)}, u32[]{:S(2)}) collective-permute-start(bf16[32,2048]{1,0:T(8,128)(2,1)} %pad_maximum_fusion.4), channel_id=1, source_target_pairs={{0,192},{1,128},{8,193},{9,129},{16,64},{17,0},{24,65},{25,1},{64,... | collective-permute-start | bytes 393224 | tf_op jit(solution)/shard_map/ppermute | solution.py:101
  46.7 26.3 %copy-start.8 = (f32[1024]{0:T(1024)S(1)}, f32[1024]{0:T(1024)}, u32[]{:S(2)}) copy-start(f32[1024]{0:T(1024)} %param.21) | copy-start | bytes 12292
  53.2 1.0 copy-start.4
  54.3 1.0 copy-start.6
  58.9 0.7 copy-start.7
  59.6 0.6 copy-start.12
  60.2 0.6 copy-start.13
  60.9 0.6 copy-start.14
  61.5 12.5 %collective-permute-start.13 = (bf16[1024,896]{1,0:T(8,128)(2,1)}, bf16[1024,896]{1,0:T(8,128)(2,1)}, u32[]{:S(2)}, u32[]{:S(2)}) collective-permute-start(bf16[1024,896]{1,0:T(8,128)(2,1)} %refs_2_.3), channel_id=1, source_target_pairs={{0,1},{1,0},{2,3},{3,2},{4,5},{5,4},{6,7},{7,6},{8,9},{9,8},{10,11... | collective-permute-start | bytes 5505032 | tf_op jit(solution)/shard_map/ppermute | solution.py:83
  61.5 12.6 %collective-permute-start.14 = (bf16[1024,896]{1,0:T(8,128)(2,1)}, bf16[1024,896]{1,0:T(8,128)(2,1)}, u32[]{:S(2)}, u32[]{:S(2)}) collective-permute-start(bf16[1024,896]{1,0:T(8,128)(2,1)} %refs_3_.3), channel_id=1, source_target_pairs={{0,1},{1,0},{2,3},{3,2},{4,5},{5,4},{6,7},{7,6},{8,9},{9,8},{10,11... | collective-permute-start | bytes 5505032 | tf_op jit(solution)/shard_map/ppermute | solution.py:83
  62.0 5.9 %collective-permute-start.12 = (bf16[32,1024]{1,0:T(8,128)(2,1)}, bf16[32,1024]{1,0:T(8,128)(2,1)S(1)}, u32[]{:S(2)}, u32[]{:S(2)}) collective-permute-start(bf16[32,1024]{1,0:T(8,128)(2,1)} %copy-done.14), channel_id=1, source_target_pairs={{0,6},{2,0},{4,2},{6,4},{1,7},{3,1},{5,3},{7,5},{8,14},{10,8},{12,... | collective-permute-start | bytes 196616 | tf_op jit(solution)/shard_map/ppermute | solution.py:91
  63.6 7.4 %collective-permute-start.11 = (bf16[32,1024]{1,0:T(8,128)(2,1)}, bf16[32,1024]{1,0:T(8,128)(2,1)S(1)}, u32[]{:S(2)}, u32[]{:S(2)}) collective-permute-start(bf16[32,1024]{1,0:T(8,128)(2,1)} %copy-done.13), channel_id=1, source_target_pairs={{0,4},{2,6},{4,0},{6,2},{1,5},{3,7},{5,1},{7,3},{8,12},{10,14},{12... | collective-permute-start | bytes 196616 | tf_op jit(solution)/shard_map/ppermute | solution.py:91
  65.3 7.8 %collective-permute-start.10 = (bf16[32,1024]{1,0:T(8,128)(2,1)}, bf16[32,1024]{1,0:T(8,128)(2,1)S(1)}, u32[]{:S(2)}, u32[]{:S(2)}) collective-permute-start(bf16[32,1024]{1,0:T(8,128)(2,1)} %copy-done.12), channel_id=1, source_target_pairs={{0,2},{2,4},{4,6},{6,0},{1,3},{3,5},{5,7},{7,1},{8,10},{10,12},{12... | collective-permute-start | bytes 196616 | tf_op jit(solution)/shard_map/ppermute | solution.py:91
  74.0 6.0 %collective-permute-start.17 = (bf16[32,1024]{1,0:T(8,128)(2,1)S(1)}, bf16[32,1024]{1,0:T(8,128)(2,1)S(1)}, u32[]{:S(2)}, u32[]{:S(2)}) collective-permute-start(bf16[32,1024]{1,0:T(8,128)(2,1)S(1)} %get-tuple-element.42), channel_id=1, source_target_pairs={{6,0},{0,2},{2,4},{4,6},{7,1},{1,3},{3,5},{5,7},{14,8},{8,10},{10,... | collective-permute-start | bytes 196616 | tf_op jit(solution)/shard_map/ppermute | solution.py:87
  74.1 7.4 %collective-permute-start.16 = (bf16[32,1024]{1,0:T(8,128)(2,1)S(1)}, bf16[32,1024]{1,0:T(8,128)(2,1)S(1)}, u32[]{:S(2)}, u32[]{:S(2)}) collective-permute-start(bf16[32,1024]{1,0:T(8,128)(2,1)S(1)} %get-tuple-element.42), channel_id=1, source_target_pairs={{4,0},{6,2},{0,4},{2,6},{5,1},{7,3},{1,5},{3,7},{12,8},{14,10},{8,... | collective-permute-start | bytes 196616 | tf_op jit(solution)/shard_map/ppermute | solution.py:87
  77.1 4.9 %collective-permute-start.15 = (bf16[32,1024]{1,0:T(8,128)(2,1)S(1)}, bf16[32,1024]{1,0:T(8,128)(2,1)S(1)}, u32[]{:S(2)}, u32[]{:S(2)}) collective-permute-start(bf16[32,1024]{1,0:T(8,128)(2,1)S(1)} %get-tuple-element.42), channel_id=1, source_target_pairs={{2,0},{4,2},{6,4},{0,6},{3,1},{5,3},{7,5},{1,7},{10,8},{12,10},{14... | collective-permute-start | bytes 196616 | tf_op jit(solution)/shard_map/ppermute | solution.py:87
  82.0 8.7 %collective-permute-start.18 = (bf16[128,1024]{1,0:T(8,128)(2,1)S(1)}, bf16[128,1024]{1,0:T(8,128)(2,1)S(1)}, u32[]{:S(2)}, u32[]{:S(2)}) collective-permute-start(bf16[128,1024]{1,0:T(8,128)(2,1)S(1)} %pad_maximum_fusion.1.refs_0_), channel_id=1, source_target_pairs={{8,0},{16,8},{24,16},{0,24},{9,1},{17,9},{25,17},{1,25},{10,2},{18... | collective-permute-start | bytes 786440 | tf_op jit(solution)/shard_map/ppermute | solution.py:87
  95.4 1.3 copy-start.1
  96.6 31.4 %all-to-all-start.1 = ((bf16[8,32,3712]{2,1,0:T(8,128)(2,1)}), bf16[8,32,3712]{2,1,0:T(8,128)(2,1)}, u32[]{:S(2)}, u32[]{:S(2)}) async-start(bf16[8,32,3712]{2,1,0:T(8,128)(2,1)} %bitcast.55), calls=%async_computation.1 | async-start | bytes 3801088 | tf_op jit(solution)/shard_map/all_to_all | solution.py:293
  105.0 7.4 %collective-permute-start.19 = (bf16[128,1024]{1,0:T(8,128)(2,1)S(1)}, bf16[128,1024]{1,0:T(8,128)(2,1)S(1)}, u32[]{:S(2)}, u32[]{:S(2)}) collective-permute-start(bf16[128,1024]{1,0:T(8,128)(2,1)S(1)} %pad_maximum_fusion.1.refs_0_), channel_id=1, source_target_pairs={{16,0},{24,8},{0,16},{8,24},{17,1},{25,9},{1,17},{9,25},{18,2},{26... | collective-permute-start | bytes 786440 | tf_op jit(solution)/shard_map/ppermute | solution.py:87
  106.3 13.8 %collective-permute-start.20 = (bf16[128,1024]{1,0:T(8,128)(2,1)S(1)}, bf16[128,1024]{1,0:T(8,128)(2,1)S(1)}, u32[]{:S(2)}, u32[]{:S(2)}) collective-permute-start(bf16[128,1024]{1,0:T(8,128)(2,1)S(1)} %pad_maximum_fusion.1.refs_0_), channel_id=1, source_target_pairs={{24,0},{0,8},{8,16},{16,24},{25,1},{1,9},{9,17},{17,25},{26,2},{2,... | collective-permute-start | bytes 786440 | tf_op jit(solution)/shard_map/ppermute | solution.py:87
  124.7 1.3 copy-start.2
  128.0 27.1 %all-to-all-start.2 = ((bf16[8,32,3712]{2,1,0:T(8,128)(2,1)}), bf16[8,32,3712]{2,1,0:T(8,128)(2,1)}, u32[]{:S(2)}, u32[]{:S(2)}) async-start(bf16[8,32,3712]{2,1,0:T(8,128)(2,1)} %bitcast.56), calls=%async_computation.2 | async-start | bytes 3801088 | tf_op jit(solution)/shard_map/all_to_all | solution.py:293
  158.8 27.0 %all-to-all-start.3 = ((bf16[8,64,1792]{2,1,0:T(8,128)(2,1)}), bf16[8,64,1792]{2,1,0:T(8,128)(2,1)}, u32[]{:S(2)}, u32[]{:S(2)}) async-start(bf16[8,64,1792]{2,1,0:T(8,128)(2,1)} %broadcast_in_dim.19), calls=%async_computation.3 | async-start | bytes 3670016 | tf_op jit(solution)/shard_map/all_to_all | solution.py:293
  164.2 6.4 %collective-permute-start.21 = (bf16[896,1024]{1,0:T(8,128)(2,1)}, bf16[896,1024]{1,0:T(8,128)(2,1)S(1)}, u32[]{:S(2)}, u32[]{:S(2)}) collective-permute-start(bf16[896,1024]{1,0:T(8,128)(2,1)} %own.1), channel_id=1, source_target_pairs={{0,1},{1,0},{2,3},{3,2},{4,5},{5,4},{6,7},{7,6},{8,9},{9,8},{10,11... | collective-permute-start | bytes 5505032 | tf_op jit(solution)/shard_map/ppermute | solution.py:83
  170.6 1.3 copy-start.10
  185.8 1.5 copy-start.9
  187.3 1.5 copy-start.11
  192.5 5.5 %collective-permute-start.24 = (bf16[128,1024]{1,0:T(8,128)(2,1)S(1)}, bf16[128,1024]{1,0:T(8,128)(2,1)S(1)}, u32[]{:S(2)}, u32[]{:S(2)}) collective-permute-start(bf16[128,1024]{1,0:T(8,128)(2,1)S(1)} %get-tuple-element.50), channel_id=1, source_target_pairs={{0,24},{8,0},{16,8},{24,16},{1,25},{9,1},{17,9},{25,17},{2,26},{10... | collective-permute-start | bytes 786440 | tf_op jit(solution)/shard_map/ppermute | solution.py:91
  193.8 6.8 %collective-permute-start.23 = (bf16[128,1024]{1,0:T(8,128)(2,1)S(1)}, bf16[128,1024]{1,0:T(8,128)(2,1)S(1)}, u32[]{:S(2)}, u32[]{:S(2)}) collective-permute-start(bf16[128,1024]{1,0:T(8,128)(2,1)S(1)} %get-tuple-element.49), channel_id=1, source_target_pairs={{0,16},{8,24},{16,0},{24,8},{1,17},{9,25},{17,1},{25,9},{2,18},{10... | collective-permute-start | bytes 786440 | tf_op jit(solution)/shard_map/ppermute | solution.py:91
  196.1 8.5 %collective-permute-start.22 = (bf16[128,1024]{1,0:T(8,128)(2,1)S(1)}, bf16[128,1024]{1,0:T(8,128)(2,1)S(1)}, u32[]{:S(2)}, u32[]{:S(2)}) collective-permute-start(bf16[128,1024]{1,0:T(8,128)(2,1)S(1)} %get-tuple-element.48), channel_id=1, source_target_pairs={{0,8},{8,16},{16,24},{24,0},{1,9},{9,17},{17,25},{25,1},{2,10},{10... | collective-permute-start | bytes 786440 | tf_op jit(solution)/shard_map/ppermute | solution.py:91
  204.8 10.8 %collective-permute-start.27 = (bf16[32,1024]{1,0:T(8,128)(2,1)S(1)}, bf16[32,1024]{1,0:T(8,128)(2,1)S(1)}, u32[]{:S(2)}, u32[]{:S(2)}) collective-permute-start(bf16[32,1024]{1,0:T(8,128)(2,1)S(1)} %get-tuple-element.58), channel_id=1, source_target_pairs={{0,6},{2,0},{4,2},{6,4},{1,7},{3,1},{5,3},{7,5},{8,14},{10,8},{12,... | collective-permute-start | bytes 196616 | tf_op jit(solution)/shard_map/ppermute | solution.py:91
  204.9 10.8 %collective-permute-start.26 = (bf16[32,1024]{1,0:T(8,128)(2,1)S(1)}, bf16[32,1024]{1,0:T(8,128)(2,1)S(1)}, u32[]{:S(2)}, u32[]{:S(2)}) collective-permute-start(bf16[32,1024]{1,0:T(8,128)(2,1)S(1)} %get-tuple-element.59), channel_id=1, source_target_pairs={{0,4},{2,6},{4,0},{6,2},{1,5},{3,7},{5,1},{7,3},{8,12},{10,14},{12... | collective-permute-start | bytes 196616 | tf_op jit(solution)/shard_map/ppermute | solution.py:91
  213.3 6.5 %collective-permute-start.25 = (bf16[32,1024]{1,0:T(8,128)(2,1)S(1)}, bf16[32,1024]{1,0:T(8,128)(2,1)S(1)}, u32[]{:S(2)}, u32[]{:S(2)}) collective-permute-start(bf16[32,1024]{1,0:T(8,128)(2,1)S(1)} %get-tuple-element.57), channel_id=1, source_target_pairs={{0,2},{2,4},{4,6},{6,0},{1,3},{3,5},{5,7},{7,1},{8,10},{10,12},{12... | collective-permute-start | bytes 196616 | tf_op jit(solution)/shard_map/ppermute | solution.py:91

commit v3 on v1

--- a/solution.py
+++ b/solution.py
@@ -68,12 +68,16 @@
 
 
 def places():
-    table = np.zeros((256, 13), np.int32)
+    table = np.zeros((256, 29), np.int32)
     for device in range(256):
-        x, l, y, core = device >> 6, (device >> 5) & 1, (device >> 3) & 3, device & 1
-        table[device, :8] = [(l ^ b) * 4 + (x ^ j) for j in range(4) for b in range(2)]
+        x, l, y, z, core = device >> 6, (device >> 5) & 1, (device >> 3) & 3, (device >> 1) & 3, device & 1
+        owners = [(z + t) % 4 for t in range(4)]
+        table[device, :8] = [((x + t) % 4) * 2 + (l ^ b) for t in range(4) for b in range(2)]
         table[device, 8:12] = [(y + t) % 4 for t in range(4)]
         table[device, 12] = core
+        table[device, 13:17] = [(y + t - z) % 4 for t in range(4)]
+        table[device, 17:25] = [(2 * (owner % 2) + source - y) % 4 for owner in owners for source in range(2)]
+        table[device, 25:29] = [owner // 2 for owner in owners]
     return table
 
 
@@ -89,14 +93,14 @@
     return lax.ppermute(block, axis, [(i, (i + shift) % 4) for i in range(4)])
 
 
-def spread(block, step):
+def by_owner_core(block, other):
     perm = []
-    for x in range(4):
+    for l in range(2):
         for y in range(4):
             for core in range(2):
-                target = (((y // 2) * 2 + core) ^ step, x, y % 2)
-                perm.append(((x * 4 + y) * 2 + core, (target[0] * 4 + target[1]) * 2 + target[2]))
-    return lax.ppermute(block, ("x", "y", "core"), perm)
+                target = (((l ^ other) * 4 + (y // 2) * 2 + core) * 2) + y % 2
+                perm.append(((l * 4 + y) * 2 + core, target))
+    return lax.ppermute(block, ("l", "y", "core"), perm)
 
 
 def params(mebibytes, flops, nbytes):
@@ -222,8 +226,8 @@
     )(gain, *pieces, *weights)
 
 
-def down_kernel(hidden_ref, own, other, *refs):
-    outs, rows_ref, held_ref, row_sem, held_sems = refs[:4], refs[4], refs[5], refs[6], refs[7]
+def down_kernel(place_ref, hidden_ref, own, other, mixed_ref, *refs):
+    outs, rows_ref, held_ref, total_ref, row_sem, held_sems = refs[:4], *refs[4:]
     depth, width = own.shape
     row_copy = pltpu.make_async_copy(hidden_ref, rows_ref, row_sem.at[0])
     row_copy.start()
@@ -234,37 +238,46 @@
         ]
     )
     row_copy.wait()
-    share = outs[0].shape[0]
-    first = share // 8
-    near = rows_ref[:, :first].reshape(share, 2 * depth)
-    far = rows_ref[:, first:].reshape(3 * share, 2 * depth)
+    share = mixed_ref.shape[0]
+    first = hidden_ref.shape[1] // 4
+    near = rows_ref[:, :first].reshape(4 * share, 2 * depth)
+    far = rows_ref[:, first:].reshape(12 * share, 2 * depth)
     wait_all(held_copies)
     for n, size in steps(width):
         columns = held_ref[:, n : n + size]
+        product = jnp.dot(near, columns, preferred_element_type=jnp.float32)
+        total_ref[:4, :, n : n + size] = product.reshape(4, share, size)
         product = jnp.dot(far, columns, preferred_element_type=jnp.float32)
-        for t in range(3):
-            outs[t + 1][:, n : n + size] = product[t * share : (t + 1) * share].astype(outs[t + 1].dtype)
-        product = jnp.dot(near, columns, preferred_element_type=jnp.float32)
-        outs[0][:, n : n + size] = product.astype(outs[0].dtype)
-
-
-def down(hidden, weights):
+        total_ref[4:, :, n : n + size] = product.reshape(12, share, size)
+    total_ref[0] += mixed_ref[...]
+    half = share // 2
+    for t in range(4):
+        for u in range(4):
+            inner = pl.ds(pl.multiple_of(place_ref[25 + u] * half, half), half)
+            for source in range(2):
+                holder = place_ref[17 + 2 * u + source] * 4 + place_ref[13 + t]
+                start = (2 * u + source) * half
+                outs[t][start : start + half, :] = total_ref[holder, inner, :].astype(outs[t].dtype)
+
+
+def down(place, hidden, weights, mixed):
     count = hidden.shape[0] * hidden.shape[1]
     depth, width = weights[0].shape
     return pl.pallas_call(
         down_kernel,
-        in_specs=[ANY] * 3,
+        in_specs=[SMEM] + [ANY] * 3 + [VMEM],
         out_specs=[VMEM] * 4,
         out_shape=[jax.ShapeDtypeStruct((count // 4, width), jnp.bfloat16)] * 4,
         scratch_shapes=[
             pltpu.VMEM(hidden.shape, jnp.bfloat16),
             pltpu.VMEM((2 * depth, width), jnp.bfloat16),
+            pltpu.VMEM((16, count // 16, width), jnp.float32),
             pltpu.SemaphoreType.DMA((1,)),
             pltpu.SemaphoreType.DMA((2,)),
         ],
         name="down",
-        **params(16, 4 * count * depth * width, 2 * (2 * count * depth + 2 * depth * width + count * width)),
-    )(hidden, *weights)
+        **params(18, 4 * count * depth * width, 2 * (2 * count * depth + 2 * depth * width + count * width)),
+    )(place, hidden, *weights, mixed)
 
 
 def add_up(pieces):
@@ -309,19 +322,21 @@
 
     attended = attend(queries, cache_key, cache_value, new_key, new_value, lengths)
     count = attended.shape[0]
-    slots = attended.reshape(count, 4, 4, -1).transpose(2, 0, 1, 3).reshape(4, count, -1)
-    block = exchange(slots, "z").reshape(4 * count, -1)
-    block = jnp.concatenate([block, swap(block, "l")], axis=0)
+    slots = jnp.stack([by_owner_core(attended, other) for other in range(2)])
+    slots = slots.reshape(2, count, 4, 4, -1).transpose(3, 0, 1, 2, 4).reshape(4, 2 * count, -1)
+    block = exchange(slots, "z").reshape(4, 2, count, -1).transpose(1, 0, 2, 3).reshape(8 * count, -1)
     block, *out_own[1:] = lax.optimization_barrier((block, *out_own[1:]))
     out_others = swap(jnp.concatenate(out_own[1:], axis=0), "core")
-    pieces = [spread(block, step) for step in range(4)]
+    pieces = [block] + [ring_from(block, "x", t) for t in (1, 2, 3)]
     partial = project(place, pieces, out_own, out_other, out_others)
     partial, *late = lax.optimization_barrier((partial, w_gate, w_up))
     gate_other, up_other = [swap(w, "core") for w in late]
 
     share = hidden_in.shape[0] // 32
-    own_in = lax.dynamic_slice_in_dim(hidden_in, (device & 31) * share, share, 0)
-    own_in = own_in.reshape(4, 2, count, -1).transpose(1, 0, 2, 3).reshape(share, -1)
+    y, z, core = (device >> 3) & 3, (device >> 1) & 3, device & 1
+    start = 256 * z + 32 * (2 * (y >> 1) + core)
+    own_in = jnp.stack([lax.dynamic_slice_in_dim(hidden_in, start + 128 * l, share, 0) for l in range(2)])
+    own_in = lax.dynamic_index_in_dim(own_in.reshape(2, 4, 2, count, -1), y & 1, 2, keepdims=False).reshape(share, -1)
     mixed = own_in.astype(jnp.float32) + scatter_sum(partial, "z")
     normed = (mixed * norm_gain).astype(jnp.bfloat16)
     normed, gate_other, up_other = lax.optimization_barrier((normed, gate_other, up_other))
@@ -342,12 +357,11 @@
         ],
         axis=1,
     )
-    parts = down(gather(hidden, GRP), [w_down, down_other])
+    parts = down(place, gather(hidden, GRP), [w_down, down_other], mixed)
     total = add_up([parts[0]] + [ring_to(parts[t], "y", t) for t in (1, 2, 3)])
     parts = [total[t * share : (t + 1) * share] for t in range(4)]
     total = add_up([parts[0]] + [ring_to(parts[t].astype(jnp.bfloat16), "z", t) for t in (1, 2, 3)])
-    layer_out = (mixed + total).astype(jnp.bfloat16)
-    return layer_out.reshape(2, 4, count, -1).transpose(1, 0, 2, 3).reshape(share, -1)
+    return total.astype(jnp.bfloat16).reshape(2, 4, count, -1).transpose(1, 0, 2, 3).reshape(share, -1)
 
 
 def solution(mesh):

time: 218 us -> 225 us (1.032)
  the two profiles are of different devices: /device:TPU:6 before, /device:TPU:1 now
where the time goes in v3:
time: 225 us; the launch traced here: 222 us
  waiting for transfers between devices  102 us (45%)
  starting transfers between devices  63.6 us (28%)
  Pallas kernels  19 us (8%)
  blocking collectives  15.2 us (7%)
  local copies, waits for them, and re-layouts  10.8 us (5%)
  other arithmetic  7.76 us (3%)
  matrix products  3.15 us (1%)
    all_to_all x4, waiting for transfers between devices, exchange(): return lax.all_to_all(pieces, axis, split_axis=0, concat_axis=0, tiled=True)  50 us
    ppermute x12, waiting for transfers between devices, ring_from(): return lax.ppermute(block, axis, [((i + shift) % 4, i) for i in range(4)])  22.8 us
    all_to_all x4, starting transfers between devices, exchange(): return lax.all_to_all(pieces, axis, split_axis=0, concat_axis=0, tiled=True)  21 us
    ppermute x12, starting transfers between devices, ring_from(): return lax.ppermute(block, axis, [((i + shift) % 4, i) for i in range(4)])  18.7 us
    all_to_all x1, blocking collectives, exchange(): return lax.all_to_all(pieces, axis, split_axis=0, concat_axis=0, tiled=True)  15.2 us
    ppermute x6, waiting for transfers between devices, ring_to(): return lax.ppermute(block, axis, [(i, (i + shift) % 4) for i in range(4)])  13.9 us
    ppermute x6, starting transfers between devices, ring_to(): return lax.ppermute(block, axis, [(i, (i + shift) % 4) for i in range(4)])  12.8 us
    ppermute x2, waiting for transfers between devices, by_owner_core(): return lax.ppermute(block, ('l', 'y', 'core'), perm)  11.8 us
  transfers between devices with their start and end apart: 29, of which 14 were waited for; matrix products, arithmetic and copies ran while one was open for 4% of the time, Pallas kernels for 2%

profile of v3, /device:TPU:1, one launch (start us, length us, event | category | flops | bytes accessed | tf_op | source)
XLA Modules:
  0.0 222.2 jit_solution(4108178753308099898)
XLA Ops:
  0.0 3.6 %collective-permute-start.2 = (bf16[256,1024]{1,0:T(8,128)(2,1)}, bf16[256,1024]{1,0:T(8,128)(2,1)S(1)}, u32[]{:S(2)}, u32[]{:S(2)}) collective-permute-start(bf16[256,1024]{1,0:T(8,128)(2,1)} %refs_4_.2), channel_id=1, source_target_pairs={{8,0},{16,8},{24,16},{0,24},{9,1},{17,9},{25,17},{1,25},{10,2},{18... | collective-permute-start | bytes 1572872 | tf_op jit(solution)/shard_map/ppermute | solution.py:89
  4.6 0.7 iota_compare_fusion
  5.3 0.7 reshape.95
  6.1 1.1 fusion.44
  7.2 1.6 fusion.56
  9.6 4.9 %collective-permute-start = (bf16[4,8192]{1,0:T(4,128)(2,1)S(1)}, bf16[4,8192]{1,0:T(4,128)(2,1)S(1)}, u32[]{:S(2)}, u32[]{:S(2)}) collective-permute-start(bf16[4,8192]{1,0:T(4,128)(2,1)S(1)} %bitcast.72), channel_id=1, source_target_pairs={{0,0},{1,8},{8,1},{9,9},{16,16},{17,24},{24,17},{25,25},{32,32},{3... | collective-permute-start | bytes 196616 | tf_op jit(solution)/shard_map/ppermute | solution.py:103
  14.5 1.5 collective-permute-start.1
  16.0 11.8 %collective-permute-done = bf16[4,8192]{1,0:T(4,128)(2,1)S(1)} collective-permute-done((bf16[4,8192]{1,0:T(4,128)(2,1)S(1)}, bf16[4,8192]{1,0:T(4,128)(2,1)S(1)}, u32[]{:S(2)}, u32[]{:S(2)}) %collective-permute-start) | collective-permute-done | bytes 65568 | tf_op jit(solution)/shard_map/ppermute | solution.py:103
  28.2 15.2 %all_to_all.25 = bf16[4,8,2048]{2,1,0:T(8,128)(2,1)S(1)} all-to-all(bf16[4,8,2048]{2,1,0:T(8,128)(2,1)S(1)} %reshape.82), channel_id=1, replica_groups=mesh['x'=4,'l'=2,'y'=4,'z'=4,'core'=2] {'z'}, dimensions={0} | all-to-all | bytes 262144 | tf_op jit(solution)/shard_map/all_to_all | solution.py:291
  43.7 2.3 %pad_maximum_fusion = bf16[768,1024]{1,0:T(8,128)(2,1)} fusion(bf16[256,1024]{1,0:T(8,128)(2,1)} %collective-permute-done.4.refs_7_, bf16[256,1024]{1,0:T(8,128)(2,1)S(1)} %collective-permute-done.3.refs_6_, bf16[256,1024]{1,0:T(8,128)(2,1)S(1)} %collective-permute-done.2.refs_5_), kind=kLoop, calls=%fused_computation.13 | loop fusion | flops 4718592 | bytes 3145728 | tf_op jit(solution)/shard_map/concatenate | solution.py:329
  46.5 2.5 %collective-permute-start.5 = (bf16[32,2048]{1,0:T(8,128)(2,1)S(1)}, bf16[32,2048]{1,0:T(8,128)(2,1)S(1)}, u32[]{:S(2)}, u32[]{:S(2)}) collective-permute-start(bf16[32,2048]{1,0:T(8,128)(2,1)S(1)} %reshape.84.refs_0_), channel_id=1, source_target_pairs={{64,0},{128,64},{192,128},{0,192},{65,1},{129,65},{193,129},{1,193... | collective-permute-start | bytes 393224 | tf_op jit(solution)/shard_map/ppermute | solution.py:89
  50.1 0.7 fusion.53.place_ref
  50.8 3.8 %collective-permute-done.5.refs_1_ = bf16[32,2048]{1,0:T(8,128)(2,1)S(1)} collective-permute-done((bf16[32,2048]{1,0:T(8,128)(2,1)S(1)}, bf16[32,2048]{1,0:T(8,128)(2,1)S(1)}, u32[]{:S(2)}, u32[]{:S(2)}) %collective-permute-start.5) | collective-permute-done | bytes 131104 | tf_op jit(solution)/shard_map/ppermute | solution.py:89
  54.6 0.8 collective-permute-done.6.refs_2_
  55.3 3.5 %collective-permute-done.7.refs_3_ = bf16[32,2048]{1,0:T(8,128)(2,1)} collective-permute-done((bf16[32,2048]{1,0:T(8,128)(2,1)S(1)}, bf16[32,2048]{1,0:T(8,128)(2,1)}, u32[]{:S(2)}, u32[]{:S(2)}) %collective-permute-start.7) | collective-permute-done | bytes 131104 | tf_op jit(solution)/shard_map/ppermute | solution.py:89
  58.8 4.5 %project.1 = bf16[128,1024]{1,0:T(8,128)(2,1)} custom-call(s32[29]{0:T(128)S(1)} %fusion.53.place_ref, bf16[32,2048]{1,0:T(8,128)(2,1)S(1)} %reshape.84.refs_0_, bf16[32,2048]{1,0:T(8,128)(2,1)S(1)} %collective-permute-done.5.refs_1_, bf16[32,2048]{1,0:T(8,128)(2,1)S(1)} %collective-permute-done.6.refs_2_, bf16[32,2048]{1,0:T(8,128)(2,1)} %collective-permute-done.7.refs_3_, ...), custom_call_target="tpu_custom_call" | custom-call | flops 536870912 | bytes 4980736 | tf_op jit(solution)/shard_map/project/pallas_call | solution.py:163
  64.0 3.4 %all-to-all-start.1 = ((bf16[4,32,1024]{2,1,0:T(8,128)(2,1)}), bf16[4,32,1024]{2,1,0:T(8,128)(2,1)S(1)}, u32[]{:S(2)}, u32[]{:S(2)}) async-start(bf16[4,32,1024]{2,1,0:T(8,128)(2,1)} %bitcast.7), calls=%async_computation.1 | async-start | bytes 524288 | tf_op jit(solution)/shard_map/all_to_all | solution.py:291
  67.5 0.9 constant_dynamic-slice_fusion
  68.5 7.9 %all-to-all-done.1 = bf16[4,32,1024]{2,1,0:T(8,128)(2,1)S(1)} async-done(((bf16[4,32,1024]{2,1,0:T(8,128)(2,1)}), bf16[4,32,1024]{2,1,0:T(8,128)(2,1)S(1)}, u32[]{:S(2)}, u32[]{:S(2)}) %all-to-all-start.1) | async-done | bytes 262176 | tf_op jit(solution)/shard_map/all_to_all | solution.py:291
  76.5 2.3 %collective-permute-start.12 = (bf16[32,1024]{1,0:T(8,128)(2,1)S(1)}, bf16[32,1024]{1,0:T(8,128)(2,1)S(1)}, u32[]{:S(2)}, u32[]{:S(2)}) collective-permute-start(bf16[32,1024]{1,0:T(8,128)(2,1)S(1)} %get-tuple-element.28), channel_id=1, source_target_pairs={{2,0},{4,2},{6,4},{0,6},{3,1},{5,3},{7,5},{1,7},{10,8},{12,10},{14... | collective-permute-start | bytes 196616 | tf_op jit(solution)/shard_map/ppermute | solution.py:89
  78.8 1.5 collective-permute-start.13
  81.0 5.5 %collective-permute-done.13 = bf16[32,1024]{1,0:T(8,128)(2,1)S(1)} collective-permute-done((bf16[32,1024]{1,0:T(8,128)(2,1)S(1)}, bf16[32,1024]{1,0:T(8,128)(2,1)S(1)}, u32[]{:S(2)}, u32[]{:S(2)}) %collective-permute-start.13) | collective-permute-done | bytes 65568 | tf_op jit(solution)/shard_map/ppermute | solution.py:89
  86.5 4.6 %gate_up.2 = bf16[128,3712]{1,0:T(8,128)(2,1)} custom-call(f32[1,1024]{1,0:T(1,128)S(1)} %bitcast.64, bf16[128,1024]{1,0:T(8,128)(2,1)S(1)} %pad_maximum_fusion.1.refs_0_, bf16[1024,896]{1,0:T(8,128)(2,1)} %refs_3_.1, bf16[1024,896]{1,0:T(8,128)(2,1)} %refs_4_.3, bf16[1024,896]{1,0:T(8,128)(2,1)} %collective-permute-done.10.refs_3_.refs_5_, ...), custom_call_target="tpu_custom_call" | custom-call | flops 939524096 | bytes 8519680 | tf_op jit(solution)/shard_map/gate_up/pallas_call | solution.py:213
  91.1 4.2 %all-to-all-start.2 = ((bf16[8,16,3712]{2,1,0:T(8,128)(2,1)}), bf16[8,16,3712]{2,1,0:T(8,128)(2,1)}, u32[]{:S(2)}, u32[]{:S(2)}) async-start(bf16[8,16,3712]{2,1,0:T(8,128)(2,1)} %bitcast.8), calls=%async_computation.2 | async-start | bytes 1900544 | tf_op jit(solution)/shard_map/all_to_all | solution.py:291
  95.4 5.4 %collective-permute-start.15 = (bf16[128,1024]{1,0:T(8,128)(2,1)S(1)}, bf16[128,1024]{1,0:T(8,128)(2,1)S(1)}, u32[]{:S(2)}, u32[]{:S(2)}) collective-permute-start(bf16[128,1024]{1,0:T(8,128)(2,1)S(1)} %pad_maximum_fusion.1.refs_0_), channel_id=1, source_target_pairs={{8,0},{16,8},{24,16},{0,24},{9,1},{17,9},{25,17},{1,25},{10,2},{18... | collective-permute-start | bytes 786440 | tf_op jit(solution)/shard_map/ppermute | solution.py:89
  101.4 5.4 %collective-permute-done.15.refs_0_ = bf16[128,1024]{1,0:T(8,128)(2,1)S(1)} collective-permute-done((bf16[128,1024]{1,0:T(8,128)(2,1)S(1)}, bf16[128,1024]{1,0:T(8,128)(2,1)S(1)}, u32[]{:S(2)}, u32[]{:S(2)}) %collective-permute-start.15) | collective-permute-done | bytes 262176 | tf_op jit(solution)/shard_map/ppermute | solution.py:89
  106.9 1.0 collective-permute-done.16.refs_1_
  107.9 2.8 %collective-permute-done.17.refs_2_ = bf16[128,1024]{1,0:T(8,128)(2,1)S(1)} collective-permute-done((bf16[128,1024]{1,0:T(8,128)(2,1)S(1)}, bf16[128,1024]{1,0:T(8,128)(2,1)S(1)}, u32[]{:S(2)}, u32[]{:S(2)}) %collective-permute-start.17) | collective-permute-done | bytes 262176 | tf_op jit(solution)/shard_map/ppermute | solution.py:89
  110.7 5.5 %gate_up.3 = bf16[384,3712]{1,0:T(8,128)(2,1)S(1)} custom-call(f32[1,1024]{1,0:T(1,128)S(1)} %bitcast.65, bf16[128,1024]{1,0:T(8,128)(2,1)S(1)} %collective-permute-done.15.refs_0_, bf16[128,1024]{1,0:T(8,128)(2,1)S(1)} %collective-permute-done.16.refs_1_, bf16[128,1024]{1,0:T(8,128)(2,1)S(1)} %collective-permute-done.17.refs_2_, bf16[1024,896]{1,0:T(8,128)(2,1)} %refs_3_.1, ...), custom_call_target="tpu_custom_call" | custom-call | flops 2818572288 | bytes 10878976 | tf_op jit(solution)/shard_map/gate_up/pallas_call | solution.py:213
  116.2 1.5 copy-done.1
  117.7 7.2 %all-to-all-start.3 = ((bf16[8,48,3712]{2,1,0:T(8,128)(2,1)}), bf16[8,48,3712]{2,1,0:T(8,128)(2,1)}, u32[]{:S(2)}, u32[]{:S(2)}) async-start(bf16[8,48,3712]{2,1,0:T(8,128)(2,1)} %bitcast.63), calls=%async_computation.3 | async-start | bytes 5701632 | tf_op jit(solution)/shard_map/all_to_all | solution.py:291
  125.0 1.3 convert_reduce_fusion.1
  126.3 29.5 %all-to-all-done.3 = bf16[8,48,3712]{2,1,0:T(8,128)(2,1)} async-done(((bf16[8,48,3712]{2,1,0:T(8,128)(2,1)}), bf16[8,48,3712]{2,1,0:T(8,128)(2,1)}, u32[]{:S(2)}, u32[]{:S(2)}) %all-to-all-start.3) | async-done | bytes 2850848 | tf_op jit(solution)/shard_map/all_to_all | solution.py:291
  155.8 2.3 %convert_reduce_fusion = f32[48,3712]{1,0:T(8,128)S(1)} fusion(bf16[8,48,3712]{2,1,0:T(8,128)(2,1)} %all-to-all-done.3), kind=kLoop, calls=%fused_computation | loop fusion | flops 2672640 | bytes 3563520 | tf_op jit(solution)/shard_map/reduce_sum | solution.py:297
  158.5 1.3 broadcast_in_dim.19
  159.9 6.2 %all-to-all-start.4 = ((bf16[8,64,1792]{2,1,0:T(8,128)(2,1)}), bf16[8,64,1792]{2,1,0:T(8,128)(2,1)}, u32[]{:S(2)}, u32[]{:S(2)}) async-start(bf16[8,64,1792]{2,1,0:T(8,128)(2,1)} %broadcast_in_dim.19), calls=%async_computation.4 | async-start | bytes 3670016 | tf_op jit(solution)/shard_map/all_to_all | solution.py:291
  166.1 3.5 %collective-permute-start.18 = (bf16[896,1024]{1,0:T(8,128)(2,1)}, bf16[896,1024]{1,0:T(8,128)(2,1)S(1)}, u32[]{:S(2)}, u32[]{:S(2)}) collective-permute-start(bf16[896,1024]{1,0:T(8,128)(2,1)} %own.1), channel_id=1, source_target_pairs={{0,1},{1,0},{2,3},{3,2},{4,5},{5,4},{6,7},{7,6},{8,9},{9,8},{10,11... | collective-permute-start | bytes 5505032 | tf_op jit(solution)/shard_map/ppermute | solution.py:85
  169.6 3.6 %collective-permute-done.18.other = bf16[896,1024]{1,0:T(8,128)(2,1)S(1)} collective-permute-done((bf16[896,1024]{1,0:T(8,128)(2,1)}, bf16[896,1024]{1,0:T(8,128)(2,1)S(1)}, u32[]{:S(2)}, u32[]{:S(2)}) %collective-permute-start.18) | collective-permute-done | bytes 1835040 | tf_op jit(solution)/shard_map/ppermute | solution.py:85
  173.2 1.3 copy-done.4
  174.5 12.7 %all-to-all-done.4.hidden_ref = bf16[8,64,1792]{2,1,0:T(8,128)(2,1)} async-done(((bf16[8,64,1792]{2,1,0:T(8,128)(2,1)}), bf16[8,64,1792]{2,1,0:T(8,128)(2,1)}, u32[]{:S(2)}, u32[]{:S(2)}) %all-to-all-start.4) | async-done | bytes 1835040 | tf_op jit(solution)/shard_map/all_to_all | solution.py:291
  187.1 1.5 copy-done.3
  188.6 1.5 copy-done.5
  190.1 4.4 %down.1 = (bf16[128,1024]{1,0:T(8,128)(2,1)S(1)}, bf16[128,1024]{1,0:T(8,128)(2,1)S(1)}, bf16[128,1024]{1,0:T(8,128)(2,1)S(1)}, bf16[128,1024]{1,0:T(8,128)(2,1)S(1)}) custom-call(s32[29]{0:T(128)S(1)} %fusion.53.place_ref, bf16[8,64,1792]{2,1,0:T(8,128)(2,1)} %all-to-all-done.4.hidden_ref, bf16[896,1024]{1,0:T(8,128)(2,1)S(1)} %copy-done.3, ...), custom_call_target="tpu_custom_call" | custom-call | flops 1879048192 | bytes 6553600 | tf_op jit(solution)/shard_map/down/pallas_call | solution.py:266
  194.7 2.6 %collective-permute-start.21 = (bf16[128,1024]{1,0:T(8,128)(2,1)S(1)}, bf16[128,1024]{1,0:T(8,128)(2,1)S(1)}, u32[]{:S(2)}, u32[]{:S(2)}) collective-permute-start(bf16[128,1024]{1,0:T(8,128)(2,1)S(1)} %get-tuple-element.36), channel_id=1, source_target_pairs={{0,24},{8,0},{16,8},{24,16},{1,25},{9,1},{17,9},{25,17},{2,26},{10... | collective-permute-start | bytes 786440 | tf_op jit(solution)/shard_map/ppermute | solution.py:93
  197.2 10.6 %collective-permute-done.19 = bf16[128,1024]{1,0:T(8,128)(2,1)S(1)} collective-permute-done((bf16[128,1024]{1,0:T(8,128)(2,1)S(1)}, bf16[128,1024]{1,0:T(8,128)(2,1)S(1)}, u32[]{:S(2)}, u32[]{:S(2)}) %collective-permute-start.19) | collective-permute-done | bytes 262176 | tf_op jit(solution)/shard_map/ppermute | solution.py:93
  208.1 6.5 %collective-permute-start.23 = (bf16[32,1024]{1,0:T(8,128)(2,1)S(1)}, bf16[32,1024]{1,0:T(8,128)(2,1)S(1)}, u32[]{:S(2)}, u32[]{:S(2)}) collective-permute-start(bf16[32,1024]{1,0:T(8,128)(2,1)S(1)} %get-tuple-element.47), channel_id=1, source_target_pairs={{0,4},{2,6},{4,0},{6,2},{1,5},{3,7},{5,1},{7,3},{8,12},{10,14},{12... | collective-permute-start | bytes 196616 | tf_op jit(solution)/shard_map/ppermute | solution.py:93
  214.6 3.5 %collective-permute-start.24 = (bf16[32,1024]{1,0:T(8,128)(2,1)S(1)}, bf16[32,1024]{1,0:T(8,128)(2,1)S(1)}, u32[]{:S(2)}, u32[]{:S(2)}) collective-permute-start(bf16[32,1024]{1,0:T(8,128)(2,1)S(1)} %get-tuple-element.46), channel_id=1, source_target_pairs={{0,6},{2,0},{4,2},{6,4},{1,7},{3,1},{5,3},{7,5},{8,14},{10,8},{12,... | collective-permute-start | bytes 196616 | tf_op jit(solution)/shard_map/ppermute | solution.py:93
  218.1 3.3 %collective-permute-done.24 = bf16[32,1024]{1,0:T(8,128)(2,1)S(1)} collective-permute-done((bf16[32,1024]{1,0:T(8,128)(2,1)S(1)}, bf16[32,1024]{1,0:T(8,128)(2,1)S(1)}, u32[]{:S(2)}, u32[]{:S(2)}) %collective-permute-start.24) | collective-permute-done | bytes 65568 | tf_op jit(solution)/shard_map/ppermute | solution.py:93
  (72 shorter events, 8.0 us)
Async XLA Ops:
  0.0 7.2 %copy-start = (bf16[4,256,1024]{2,1,0:T(8,128)(2,1)S(1)}, bf16[4,256,1024]{2,1,0:T(8,128)(2,1)}, u32[]{:S(2)}) copy-start(bf16[4,256,1024]{2,1,0:T(8,128)(2,1)} %param.15) | copy-start | bytes 6291460
  0.0 9.0 %copy-start.6 = (bf16[4,1024]{1,0:T(4,128)(2,1)S(1)}, bf16[4,1024]{1,0:T(4,128)(2,1)}, u32[]{:S(2)}) copy-start(bf16[4,1024]{1,0:T(4,128)(2,1)} %param.18) | copy-start | bytes 24580
  0.0 43.6 %collective-permute-start.2 = (bf16[256,1024]{1,0:T(8,128)(2,1)}, bf16[256,1024]{1,0:T(8,128)(2,1)S(1)}, u32[]{:S(2)}, u32[]{:S(2)}) collective-permute-start(bf16[256,1024]{1,0:T(8,128)(2,1)} %refs_4_.2), channel_id=1, source_target_pairs={{8,0},{16,8},{24,16},{0,24},{9,1},{17,9},{25,17},{1,25},{10,2},{18... | collective-permute-start | bytes 1572872 | tf_op jit(solution)/shard_map/ppermute | solution.py:89
  3.6 40.1 %collective-permute-start.3 = (bf16[256,1024]{1,0:T(8,128)(2,1)}, bf16[256,1024]{1,0:T(8,128)(2,1)S(1)}, u32[]{:S(2)}, u32[]{:S(2)}) collective-permute-start(bf16[256,1024]{1,0:T(8,128)(2,1)} %refs_4_.2), channel_id=1, source_target_pairs={{16,0},{24,8},{0,16},{8,24},{17,1},{25,9},{1,17},{9,25},{18,2},{26... | collective-permute-start | bytes 1572872 | tf_op jit(solution)/shard_map/ppermute | solution.py:89
  3.9 39.7 %collective-permute-start.4 = (bf16[256,1024]{1,0:T(8,128)(2,1)}, bf16[256,1024]{1,0:T(8,128)(2,1)}, u32[]{:S(2)}, u32[]{:S(2)}) collective-permute-start(bf16[256,1024]{1,0:T(8,128)(2,1)} %refs_4_.2), channel_id=1, source_target_pairs={{24,0},{0,8},{8,16},{16,24},{25,1},{1,9},{9,17},{17,25},{26,2},{2,... | collective-permute-start | bytes 1572872 | tf_op jit(solution)/shard_map/ppermute | solution.py:89
  6.0 3.0 %copy-start.7 = (bf16[4,256,1024]{2,1,0:T(8,128)(2,1)S(1)}, bf16[4,256,1024]{2,1,0:T(8,128)(2,1)}, u32[]{:S(2)}) copy-start(bf16[4,256,1024]{2,1,0:T(8,128)(2,1)} %param.16) | copy-start | bytes 6291460
  9.6 18.2 %collective-permute-start = (bf16[4,8192]{1,0:T(4,128)(2,1)S(1)}, bf16[4,8192]{1,0:T(4,128)(2,1)S(1)}, u32[]{:S(2)}, u32[]{:S(2)}) collective-permute-start(bf16[4,8192]{1,0:T(4,128)(2,1)S(1)} %bitcast.72), channel_id=1, source_target_pairs={{0,0},{1,8},{8,1},{9,9},{16,16},{17,24},{24,17},{25,25},{32,32},{3... | collective-permute-start | bytes 196616 | tf_op jit(solution)/shard_map/ppermute | solution.py:103
  14.5 13.3 %collective-permute-start.1 = (bf16[4,8192]{1,0:T(4,128)(2,1)S(1)}, bf16[4,8192]{1,0:T(4,128)(2,1)S(1)}, u32[]{:S(2)}, u32[]{:S(2)}) collective-permute-start(bf16[4,8192]{1,0:T(4,128)(2,1)S(1)} %bitcast.73), channel_id=1, source_target_pairs={{0,32},{1,40},{8,33},{9,41},{16,48},{17,56},{24,49},{25,57},{32,0}... | collective-permute-start | bytes 196616 | tf_op jit(solution)/shard_map/ppermute | solution.py:103
  46.0 12.8 %collective-permute-start.9 = (bf16[768,1024]{1,0:T(8,128)(2,1)}, bf16[768,1024]{1,0:T(8,128)(2,1)}, u32[]{:S(2)}, u32[]{:S(2)}) collective-permute-start(bf16[768,1024]{1,0:T(8,128)(2,1)} %pad_maximum_fusion), channel_id=1, source_target_pairs={{0,1},{1,0},{2,3},{3,2},{4,5},{5,4},{6,7},{7,6},{8,9},{9,8},{10,11... | collective-permute-start | bytes 4718600 | tf_op jit(solution)/shard_map/ppermute | solution.py:85
  46.0 4.8 %collective-permute-start.8 = (bf16[256,1024]{1,0:T(8,128)(2,1)}, bf16[256,1024]{1,0:T(8,128)(2,1)}, u32[]{:S(2)}, u32[]{:S(2)}) collective-permute-start(bf16[256,1024]{1,0:T(8,128)(2,1)} %refs_4_.2), channel_id=1, source_target_pairs={{0,1},{1,0},{2,3},{3,2},{4,5},{5,4},{6,7},{7,6},{8,9},{9,8},{10,11... | collective-permute-start | bytes 1572872 | tf_op jit(solution)/shard_map/ppermute | solution.py:85
  46.5 8.1 %collective-permute-start.5 = (bf16[32,2048]{1,0:T(8,128)(2,1)S(1)}, bf16[32,2048]{1,0:T(8,128)(2,1)S(1)}, u32[]{:S(2)}, u32[]{:S(2)}) collective-permute-start(bf16[32,2048]{1,0:T(8,128)(2,1)S(1)} %reshape.84.refs_0_), channel_id=1, source_target_pairs={{64,0},{128,64},{192,128},{0,192},{65,1},{129,65},{193,129},{1,193... | collective-permute-start | bytes 393224 | tf_op jit(solution)/shard_map/ppermute | solution.py:89
  49.0 6.4 %collective-permute-start.6 = (bf16[32,2048]{1,0:T(8,128)(2,1)S(1)}, bf16[32,2048]{1,0:T(8,128)(2,1)S(1)}, u32[]{:S(2)}, u32[]{:S(2)}) collective-permute-start(bf16[32,2048]{1,0:T(8,128)(2,1)S(1)} %reshape.84.refs_0_), channel_id=1, source_target_pairs={{128,0},{192,64},{0,128},{64,192},{129,1},{193,65},{1,129},{65,193... | collective-permute-start | bytes 393224 | tf_op jit(solution)/shard_map/ppermute | solution.py:89
  49.5 9.3 %collective-permute-start.7 = (bf16[32,2048]{1,0:T(8,128)(2,1)S(1)}, bf16[32,2048]{1,0:T(8,128)(2,1)}, u32[]{:S(2)}, u32[]{:S(2)}) collective-permute-start(bf16[32,2048]{1,0:T(8,128)(2,1)S(1)} %reshape.84.refs_0_), channel_id=1, source_target_pairs={{192,0},{0,64},{64,128},{128,192},{193,1},{1,65},{65,129},{129,193... | collective-permute-start | bytes 393224 | tf_op jit(solution)/shard_map/ppermute | solution.py:89
  50.8 25.7 %copy-start.2 = (f32[1024]{0:T(1024)S(1)}, f32[1024]{0:T(1024)}, u32[]{:S(2)}) copy-start(f32[1024]{0:T(1024)} %param.21) | copy-start | bytes 12292
  63.4 13.1 %collective-permute-start.10 = (bf16[1024,896]{1,0:T(8,128)(2,1)}, bf16[1024,896]{1,0:T(8,128)(2,1)}, u32[]{:S(2)}, u32[]{:S(2)}) collective-permute-start(bf16[1024,896]{1,0:T(8,128)(2,1)} %refs_3_.1), channel_id=1, source_target_pairs={{0,1},{1,0},{2,3},{3,2},{4,5},{5,4},{6,7},{7,6},{8,9},{9,8},{10,11... | collective-permute-start | bytes 5505032 | tf_op jit(solution)/shard_map/ppermute | solution.py:85
  63.9 12.6 %collective-permute-start.11 = (bf16[1024,896]{1,0:T(8,128)(2,1)}, bf16[1024,896]{1,0:T(8,128)(2,1)}, u32[]{:S(2)}, u32[]{:S(2)}) collective-permute-start(bf16[1024,896]{1,0:T(8,128)(2,1)} %refs_4_.3), channel_id=1, source_target_pairs={{0,1},{1,0},{2,3},{3,2},{4,5},{5,4},{6,7},{7,6},{8,9},{9,8},{10,11... | collective-permute-start | bytes 5505032 | tf_op jit(solution)/shard_map/ppermute | solution.py:85
  64.0 12.4 %all-to-all-start.1 = ((bf16[4,32,1024]{2,1,0:T(8,128)(2,1)}), bf16[4,32,1024]{2,1,0:T(8,128)(2,1)S(1)}, u32[]{:S(2)}, u32[]{:S(2)}) async-start(bf16[4,32,1024]{2,1,0:T(8,128)(2,1)} %bitcast.7), calls=%async_computation.1 | async-start | bytes 524288 | tf_op jit(solution)/shard_map/all_to_all | solution.py:291
  76.5 4.5 %collective-permute-start.12 = (bf16[32,1024]{1,0:T(8,128)(2,1)S(1)}, bf16[32,1024]{1,0:T(8,128)(2,1)S(1)}, u32[]{:S(2)}, u32[]{:S(2)}) collective-permute-start(bf16[32,1024]{1,0:T(8,128)(2,1)S(1)} %get-tuple-element.28), channel_id=1, source_target_pairs={{2,0},{4,2},{6,4},{0,6},{3,1},{5,3},{7,5},{1,7},{10,8},{12,10},{14... | collective-permute-start | bytes 196616 | tf_op jit(solution)/shard_map/ppermute | solution.py:89
  78.8 7.7 %collective-permute-start.13 = (bf16[32,1024]{1,0:T(8,128)(2,1)S(1)}, bf16[32,1024]{1,0:T(8,128)(2,1)S(1)}, u32[]{:S(2)}, u32[]{:S(2)}) collective-permute-start(bf16[32,1024]{1,0:T(8,128)(2,1)S(1)} %get-tuple-element.28), channel_id=1, source_target_pairs={{4,0},{6,2},{0,4},{2,6},{5,1},{7,3},{1,5},{3,7},{12,8},{14,10},{8,... | collective-permute-start | bytes 196616 | tf_op jit(solution)/shard_map/ppermute | solution.py:89
  80.3 6.2 %collective-permute-start.14 = (bf16[32,1024]{1,0:T(8,128)(2,1)S(1)}, bf16[32,1024]{1,0:T(8,128)(2,1)S(1)}, u32[]{:S(2)}, u32[]{:S(2)}) collective-permute-start(bf16[32,1024]{1,0:T(8,128)(2,1)S(1)} %get-tuple-element.28), channel_id=1, source_target_pairs={{6,0},{0,2},{2,4},{4,6},{7,1},{1,3},{3,5},{5,7},{14,8},{8,10},{10,... | collective-permute-start | bytes 196616 | tf_op jit(solution)/shard_map/ppermute | solution.py:89
  91.1 26.6 %all-to-all-start.2 = ((bf16[8,16,3712]{2,1,0:T(8,128)(2,1)}), bf16[8,16,3712]{2,1,0:T(8,128)(2,1)}, u32[]{:S(2)}, u32[]{:S(2)}) async-start(bf16[8,16,3712]{2,1,0:T(8,128)(2,1)} %bitcast.8), calls=%async_computation.2 | async-start | bytes 1900544 | tf_op jit(solution)/shard_map/all_to_all | solution.py:291
  95.4 11.5 %collective-permute-start.15 = (bf16[128,1024]{1,0:T(8,128)(2,1)S(1)}, bf16[128,1024]{1,0:T(8,128)(2,1)S(1)}, u32[]{:S(2)}, u32[]{:S(2)}) collective-permute-start(bf16[128,1024]{1,0:T(8,128)(2,1)S(1)} %pad_maximum_fusion.1.refs_0_), channel_id=1, source_target_pairs={{8,0},{16,8},{24,16},{0,24},{9,1},{17,9},{25,17},{1,25},{10,2},{18... | collective-permute-start | bytes 786440 | tf_op jit(solution)/shard_map/ppermute | solution.py:89
  100.7 7.2 %collective-permute-start.16 = (bf16[128,1024]{1,0:T(8,128)(2,1)S(1)}, bf16[128,1024]{1,0:T(8,128)(2,1)S(1)}, u32[]{:S(2)}, u32[]{:S(2)}) collective-permute-start(bf16[128,1024]{1,0:T(8,128)(2,1)S(1)} %pad_maximum_fusion.1.refs_0_), channel_id=1, source_target_pairs={{16,0},{24,8},{0,16},{8,24},{17,1},{25,9},{1,17},{9,25},{18,2},{26... | collective-permute-start | bytes 786440 | tf_op jit(solution)/shard_map/ppermute | solution.py:89
  101.1 9.6 %collective-permute-start.17 = (bf16[128,1024]{1,0:T(8,128)(2,1)S(1)}, bf16[128,1024]{1,0:T(8,128)(2,1)S(1)}, u32[]{:S(2)}, u32[]{:S(2)}) collective-permute-start(bf16[128,1024]{1,0:T(8,128)(2,1)S(1)} %pad_maximum_fusion.1.refs_0_), channel_id=1, source_target_pairs={{24,0},{0,8},{8,16},{16,24},{25,1},{1,9},{9,17},{17,25},{26,2},{2,... | collective-permute-start | bytes 786440 | tf_op jit(solution)/shard_map/ppermute | solution.py:89
  116.2 1.5 copy-start.1
  117.7 38.1 %all-to-all-start.3 = ((bf16[8,48,3712]{2,1,0:T(8,128)(2,1)}), bf16[8,48,3712]{2,1,0:T(8,128)(2,1)}, u32[]{:S(2)}, u32[]{:S(2)}) async-start(bf16[8,48,3712]{2,1,0:T(8,128)(2,1)} %bitcast.63), calls=%async_computation.3 | async-start | bytes 5701632 | tf_op jit(solution)/shard_map/all_to_all | solution.py:291
  159.9 27.2 %all-to-all-start.4 = ((bf16[8,64,1792]{2,1,0:T(8,128)(2,1)}), bf16[8,64,1792]{2,1,0:T(8,128)(2,1)}, u32[]{:S(2)}, u32[]{:S(2)}) async-start(bf16[8,64,1792]{2,1,0:T(8,128)(2,1)} %broadcast_in_dim.19), calls=%async_computation.4 | async-start | bytes 3670016 | tf_op jit(solution)/shard_map/all_to_all | solution.py:291
  166.1 7.1 %collective-permute-start.18 = (bf16[896,1024]{1,0:T(8,128)(2,1)}, bf16[896,1024]{1,0:T(8,128)(2,1)S(1)}, u32[]{:S(2)}, u32[]{:S(2)}) collective-permute-start(bf16[896,1024]{1,0:T(8,128)(2,1)} %own.1), channel_id=1, source_target_pairs={{0,1},{1,0},{2,3},{3,2},{4,5},{5,4},{6,7},{7,6},{8,9},{9,8},{10,11... | collective-permute-start | bytes 5505032 | tf_op jit(solution)/shard_map/ppermute | solution.py:85
  173.2 1.3 copy-start.4
  187.1 1.5 copy-start.3
  188.6 1.5 copy-start.5
  194.5 13.3 %collective-permute-start.19 = (bf16[128,1024]{1,0:T(8,128)(2,1)S(1)}, bf16[128,1024]{1,0:T(8,128)(2,1)S(1)}, u32[]{:S(2)}, u32[]{:S(2)}) collective-permute-start(bf16[128,1024]{1,0:T(8,128)(2,1)S(1)} %get-tuple-element.34), channel_id=1, source_target_pairs={{0,8},{8,16},{16,24},{24,0},{1,9},{9,17},{17,25},{25,1},{2,10},{10... | collective-permute-start | bytes 786440 | tf_op jit(solution)/shard_map/ppermute | solution.py:93
  194.6 13.2 %collective-permute-start.20 = (bf16[128,1024]{1,0:T(8,128)(2,1)S(1)}, bf16[128,1024]{1,0:T(8,128)(2,1)S(1)}, u32[]{:S(2)}, u32[]{:S(2)}) collective-permute-start(bf16[128,1024]{1,0:T(8,128)(2,1)S(1)} %get-tuple-element.35), channel_id=1, source_target_pairs={{0,16},{8,24},{16,0},{24,8},{1,17},{9,25},{17,1},{25,9},{2,18},{10... | collective-permute-start | bytes 786440 | tf_op jit(solution)/shard_map/ppermute | solution.py:93
  194.7 13.1 %collective-permute-start.21 = (bf16[128,1024]{1,0:T(8,128)(2,1)S(1)}, bf16[128,1024]{1,0:T(8,128)(2,1)S(1)}, u32[]{:S(2)}, u32[]{:S(2)}) collective-permute-start(bf16[128,1024]{1,0:T(8,128)(2,1)S(1)} %get-tuple-element.36), channel_id=1, source_target_pairs={{0,24},{8,0},{16,8},{24,16},{1,25},{9,1},{17,9},{25,17},{2,26},{10... | collective-permute-start | bytes 786440 | tf_op jit(solution)/shard_map/ppermute | solution.py:93
  208.0 10.1 %collective-permute-start.22 = (bf16[32,1024]{1,0:T(8,128)(2,1)S(1)}, bf16[32,1024]{1,0:T(8,128)(2,1)S(1)}, u32[]{:S(2)}, u32[]{:S(2)}) collective-permute-start(bf16[32,1024]{1,0:T(8,128)(2,1)S(1)} %get-tuple-element.45), channel_id=1, source_target_pairs={{0,2},{2,4},{4,6},{6,0},{1,3},{3,5},{5,7},{7,1},{8,10},{10,12},{12... | collective-permute-start | bytes 196616 | tf_op jit(solution)/shard_map/ppermute | solution.py:93
  208.1 10.0 %collective-permute-start.23 = (bf16[32,1024]{1,0:T(8,128)(2,1)S(1)}, bf16[32,1024]{1,0:T(8,128)(2,1)S(1)}, u32[]{:S(2)}, u32[]{:S(2)}) collective-permute-start(bf16[32,1024]{1,0:T(8,128)(2,1)S(1)} %get-tuple-element.47), channel_id=1, source_target_pairs={{0,4},{2,6},{4,0},{6,2},{1,5},{3,7},{5,1},{7,3},{8,12},{10,14},{12... | collective-permute-start | bytes 196616 | tf_op jit(solution)/shard_map/ppermute | solution.py:93
  214.6 6.8 %collective-permute-start.24 = (bf16[32,1024]{1,0:T(8,128)(2,1)S(1)}, bf16[32,1024]{1,0:T(8,128)(2,1)S(1)}, u32[]{:S(2)}, u32[]{:S(2)}) collective-permute-start(bf16[32,1024]{1,0:T(8,128)(2,1)S(1)} %get-tuple-element.46), channel_id=1, source_target_pairs={{0,6},{2,0},{4,2},{6,4},{1,7},{3,1},{5,3},{7,5},{8,14},{10,8},{12,... | collective-permute-start | bytes 196616 | tf_op jit(solution)/shard_map/ppermute | solution.py:93

commit v4 on v3

--- a/solution.py
+++ b/solution.py
@@ -93,16 +93,6 @@
     return lax.ppermute(block, axis, [(i, (i + shift) % 4) for i in range(4)])
 
 
-def by_owner_core(block, other):
-    perm = []
-    for l in range(2):
-        for y in range(4):
-            for core in range(2):
-                target = (((l ^ other) * 4 + (y // 2) * 2 + core) * 2) + y % 2
-                perm.append(((l * 4 + y) * 2 + core, target))
-    return lax.ppermute(block, ("l", "y", "core"), perm)
-
-
 def params(mebibytes, flops, nbytes):
     return dict(
         compiler_params=pltpu.CompilerParams(vmem_limit_bytes=mebibytes << 20),
@@ -126,8 +116,8 @@
 
 
 def project_kernel(place_ref, *refs):
-    pieces, own, other, others = refs[:4], refs[4:8], refs[8], refs[9]
-    out_ref, rows_ref, held_ref, row_sems, held_sems = refs[10:]
+    pieces, own, other = refs[:4], refs[4:8], refs[8:12]
+    out_ref, rows_ref, held_ref, row_sems, held_sems = refs[12:]
     step = pieces[0].shape[0] // 2
     row_copies = start_all(
         [
@@ -144,7 +134,7 @@
     held_copies = []
     for t in range(4):
         for b in range(2):
-            source = own[t] if b == 0 else (other if t == 0 else others.at[pl.ds((t - 1) * depth, depth), :])
+            source = own[t] if b == 0 else other[t]
             start = (2 * place_ref[8 + t] + (place_ref[12] if b == 0 else 1 - place_ref[12])) * depth
             held = held_ref.at[pl.ds(pl.multiple_of(start, depth), depth), :]
             held_copies.append(pltpu.make_async_copy(source, held, held_sems.at[2 * t + b]))
@@ -157,12 +147,12 @@
         ).astype(out_ref.dtype)
 
 
-def project(place, pieces, own, other, others):
+def project(place, pieces, own, other):
     count, depth = 4 * pieces[0].shape[0], pieces[0].shape[1]
-    width = other.shape[1]
+    width = own[0].shape[1]
     return pl.pallas_call(
         project_kernel,
-        in_specs=[SMEM] + [ANY] * 10,
+        in_specs=[SMEM] + [ANY] * 12,
         out_specs=VMEM,
         out_shape=jax.ShapeDtypeStruct((count, width), jnp.bfloat16),
         scratch_shapes=[
@@ -173,7 +163,7 @@
         ],
         name="project",
         **params(12, 2 * count * depth * width, 2 * (depth * width + count * (depth + width))),
-    )(place, *pieces, *own, other, others)
+    )(place, *pieces, *own, *other)
 
 
 def gate_up_kernel(gain_ref, *refs):
@@ -322,21 +312,22 @@
 
     attended = attend(queries, cache_key, cache_value, new_key, new_value, lengths)
     count = attended.shape[0]
-    slots = jnp.stack([by_owner_core(attended, other) for other in range(2)])
-    slots = slots.reshape(2, count, 4, 4, -1).transpose(3, 0, 1, 2, 4).reshape(4, 2 * count, -1)
-    block = exchange(slots, "z").reshape(4, 2, count, -1).transpose(1, 0, 2, 3).reshape(8 * count, -1)
-    block, *out_own[1:] = lax.optimization_barrier((block, *out_own[1:]))
-    out_others = swap(jnp.concatenate(out_own[1:], axis=0), "core")
+    slots = attended.reshape(count, 4, 4, -1).transpose(2, 0, 1, 3).reshape(4, count, -1)
+    block = exchange(slots, "z").reshape(4 * count, -1)
+    block, out_own[1], out_own[3] = lax.optimization_barrier((block, out_own[1], out_own[3]))
+    out_next, out_last = swap(out_own[1], "core"), swap(out_own[3], "core")
+    block = jnp.concatenate([block, swap(block, "l")], axis=0)
     pieces = [block] + [ring_from(block, "x", t) for t in (1, 2, 3)]
-    partial = project(place, pieces, out_own, out_other, out_others)
+    *pieces, out_own[2] = lax.optimization_barrier((*pieces, out_own[2]))
+    partial = project(place, pieces, out_own, [out_other, out_next, swap(out_own[2], "core"), out_last])
     partial, *late = lax.optimization_barrier((partial, w_gate, w_up))
     gate_other, up_other = [swap(w, "core") for w in late]
 
     share = hidden_in.shape[0] // 32
     y, z, core = (device >> 3) & 3, (device >> 1) & 3, device & 1
-    start = 256 * z + 32 * (2 * (y >> 1) + core)
+    start = 256 * z + 32 * y
     own_in = jnp.stack([lax.dynamic_slice_in_dim(hidden_in, start + 128 * l, share, 0) for l in range(2)])
-    own_in = lax.dynamic_index_in_dim(own_in.reshape(2, 4, 2, count, -1), y & 1, 2, keepdims=False).reshape(share, -1)
+    own_in = lax.dynamic_index_in_dim(own_in.reshape(2, 4, 2, count, -1), core, 2, keepdims=False).reshape(share, -1)
     mixed = own_in.astype(jnp.float32) + scatter_sum(partial, "z")
     normed = (mixed * norm_gain).astype(jnp.bfloat16)
     normed, gate_other, up_other = lax.optimization_barrier((normed, gate_other, up_other))
@@ -361,7 +352,12 @@
     total = add_up([parts[0]] + [ring_to(parts[t], "y", t) for t in (1, 2, 3)])
     parts = [total[t * share : (t + 1) * share] for t in range(4)]
     total = add_up([parts[0]] + [ring_to(parts[t].astype(jnp.bfloat16), "z", t) for t in (1, 2, 3)])
-    return total.astype(jnp.bfloat16).reshape(2, 4, count, -1).transpose(1, 0, 2, 3).reshape(share, -1)
+    total = total.astype(jnp.bfloat16)
+    half = share // 2
+    low, high = total[:half], total[half:]
+    given = swap(jnp.where(core == 0, high, low), "core")
+    rows = jnp.stack([jnp.where(core == 0, low, given), jnp.where(core == 0, given, high)])
+    return rows.reshape(2, 4, count, -1).transpose(1, 0, 2, 3).reshape(share, -1)
 
 
 def solution(mesh):

time: 225 us -> 212 us (0.942)
  starting transfers between devices: 63.6 us -> 79.4 us
  blocking collectives: 15.2 us -> 0 us
  waiting for transfers between devices: 102 us -> 90.3 us
    all_to_all x1 -> x0, blocking collectives: 15.2 us -> none  [exchange(): return lax.all_to_all(pieces, axis, split_axis=0, concat_axis=0, tiled=True)]
    ppermute x5 -> x9, starting transfers between devices: 4.68 us -> 18.6 us  [swap(): return lax.ppermute(block, axis, [(0, 1), (1, 0)])]
    ppermute x2 -> x0, waiting for transfers between devices: 11.8 us -> none  [by_owner_core(): return lax.ppermute(block, ('l', 'y', 'core'), perm)]
    all_to_all x4 -> x5, starting transfers between devices: 21 us -> 29.4 us  [exchange(): return lax.all_to_all(pieces, axis, split_axis=0, concat_axis=0, tiled=True)]
    ppermute x12, waiting for transfers between devices: 22.8 us -> 14.4 us  [ring_from(): return lax.ppermute(block, axis, [((i + shift) % 4, i) for i in range(4)])]
    ppermute x2 -> x0, starting transfers between devices: 6.37 us -> none  [by_owner_core(): return lax.ppermute(block, ('l', 'y', 'core'), perm)]
    all_to_all x4 -> x5, waiting for transfers between devices: 50 us -> 55.9 us  [exchange(): return lax.all_to_all(pieces, axis, split_axis=0, concat_axis=0, tiled=True)]
    ppermute x5 -> x9, waiting for transfers between devices: 3.63 us -> 8.42 us  [swap(): return lax.ppermute(block, axis, [(0, 1), (1, 0)])]
  transfers between devices with their start and end apart: 29 -> 32, of which waited for: 14 -> 16; matrix products, arithmetic and copies ran while one was open for 4% -> 4% of each run, Pallas kernels for 2% -> 3%
where the time goes in v4:
time: 212 us; the launch traced here: 211 us
  waiting for transfers between devices  90.3 us (43%)
  starting transfers between devices  79.4 us (37%)
  Pallas kernels  19.2 us (9%)
  local copies, waits for them, and re-layouts  12.7 us (6%)
  other arithmetic  6.26 us (3%)
  matrix products  3 us (1%)
    all_to_all x5, waiting for transfers between devices, exchange(): return lax.all_to_all(pieces, axis, split_axis=0, concat_axis=0, tiled=True)  55.9 us
    all_to_all x5, starting transfers between devices, exchange(): return lax.all_to_all(pieces, axis, split_axis=0, concat_axis=0, tiled=True)  29.4 us
    ppermute x9, starting transfers between devices, swap(): return lax.ppermute(block, axis, [(0, 1), (1, 0)])  18.6 us
    ppermute x12, starting transfers between devices, ring_from(): return lax.ppermute(block, axis, [((i + shift) % 4, i) for i in range(4)])  16.7 us
    ppermute x6, starting transfers between devices, ring_to(): return lax.ppermute(block, axis, [(i, (i + shift) % 4) for i in range(4)])  14.7 us
    ppermute x12, waiting for transfers between devices, ring_from(): return lax.ppermute(block, axis, [((i + shift) % 4, i) for i in range(4)])  14.4 us
    ppermute x6, waiting for transfers between devices, ring_to(): return lax.ppermute(block, axis, [(i, (i + shift) % 4) for i in range(4)])  11.5 us
    pallas_call x2, Pallas kernels, gate_up(): pl.pallas_call(gate_up_kernel, in_specs=[VMEM] + [ANY] * (len(pieces) + 4...  10.1 us
  transfers between devices with their start and end apart: 32, of which 16 were waited for; matrix products, arithmetic and copies ran while one was open for 4% of the time, Pallas kernels for 3%

profile of v4, /device:TPU:1, one launch (start us, length us, event | category | flops | bytes accessed | tf_op | source)
XLA Modules:
  0.0 211.2 jit_solution(11228052343156577480)
XLA Ops:
  0.0 3.6 %collective-permute-start = (bf16[256,1024]{1,0:T(8,128)(2,1)}, bf16[256,1024]{1,0:T(8,128)(2,1)S(1)}, u32[]{:S(2)}, u32[]{:S(2)}) collective-permute-start(bf16[256,1024]{1,0:T(8,128)(2,1)} %refs_4_.2), channel_id=1, source_target_pairs={{8,0},{16,8},{24,16},{0,24},{9,1},{17,9},{25,17},{1,25},{10,2},{18... | collective-permute-start | bytes 1572872 | tf_op jit(solution)/shard_map/ppermute | solution.py:89
  5.9 1.0 fusion.41
  6.9 1.6 fusion.53
  9.9 8.2 %all-to-all-start = ((bf16[4,4,2048]{2,1,0:T(4,128)(2,1)}), bf16[4,4,2048]{2,1,0:T(4,128)(2,1)S(1)}, u32[]{:S(2)}, u32[]{:S(2)}) async-start(bf16[4,4,2048]{2,1,0:T(4,128)(2,1)} %reshape.72), calls=%async_computation | async-start | bytes 131072 | tf_op jit(solution)/shard_map/all_to_all | solution.py:281
  18.1 1.6 collective-permute-start.6
  19.7 5.4 %all-to-all-done = bf16[4,4,2048]{2,1,0:T(4,128)(2,1)S(1)} async-done(((bf16[4,4,2048]{2,1,0:T(4,128)(2,1)}), bf16[4,4,2048]{2,1,0:T(4,128)(2,1)S(1)}, u32[]{:S(2)}, u32[]{:S(2)}) %all-to-all-start) | async-done | bytes 65568 | tf_op jit(solution)/shard_map/all_to_all | solution.py:281
  26.0 2.8 %collective-permute-done.2 = bf16[16,2048]{1,0:T(8,128)(2,1)S(1)} collective-permute-done((bf16[16,2048]{1,0:T(8,128)(2,1)S(1)}, bf16[16,2048]{1,0:T(8,128)(2,1)S(1)}, u32[]{:S(2)}, u32[]{:S(2)}) %collective-permute-start.2) | collective-permute-done | bytes 65568 | tf_op jit(solution)/shard_map/ppermute | solution.py:85
  28.8 2.5 %collective-permute-start.3 = (bf16[32,2048]{1,0:T(8,128)(2,1)S(1)}, bf16[32,2048]{1,0:T(8,128)(2,1)S(1)}, u32[]{:S(2)}, u32[]{:S(2)}) collective-permute-start(bf16[32,2048]{1,0:T(8,128)(2,1)S(1)} %constant_dynamic-update-slice_fusion.refs_0_), channel_id=1, source_target_pairs={{64,0},{128,64},{192,128},{0,192},{65,1},{129,65},{193,129},{1,193... | collective-permute-start | bytes 393224 | tf_op jit(solution)/shard_map/ppermute | solution.py:89
  32.4 4.0 %collective-permute-start.7 = (bf16[256,1024]{1,0:T(8,128)(2,1)S(1)}, bf16[256,1024]{1,0:T(8,128)(2,1)}, u32[]{:S(2)}, u32[]{:S(2)}) collective-permute-start(bf16[256,1024]{1,0:T(8,128)(2,1)S(1)} %copy-done.2), channel_id=1, source_target_pairs={{0,1},{1,0},{2,3},{3,2},{4,5},{5,4},{6,7},{7,6},{8,9},{9,8},{10,11... | collective-permute-start | bytes 1572872 | tf_op jit(solution)/shard_map/ppermute | solution.py:85
  36.4 2.2 %collective-permute-start.8 = (bf16[256,1024]{1,0:T(8,128)(2,1)S(1)}, bf16[256,1024]{1,0:T(8,128)(2,1)}, u32[]{:S(2)}, u32[]{:S(2)}) collective-permute-start(bf16[256,1024]{1,0:T(8,128)(2,1)S(1)} %collective-permute-done.refs_5_), channel_id=1, source_target_pairs={{0,1},{1,0},{2,3},{3,2},{4,5},{5,4},{6,7},{7,6},{8,9},{9,8},{10,11... | collective-permute-start | bytes 1572872 | tf_op jit(solution)/shard_map/ppermute | solution.py:85
  39.3 4.0 %collective-permute-start.9 = (bf16[256,1024]{1,0:T(8,128)(2,1)}, bf16[256,1024]{1,0:T(8,128)(2,1)}, u32[]{:S(2)}, u32[]{:S(2)}) collective-permute-start(bf16[256,1024]{1,0:T(8,128)(2,1)} %collective-permute-done.6.refs_6_), channel_id=1, source_target_pairs={{0,1},{1,0},{2,3},{3,2},{4,5},{5,4},{6,7},{7,6},{8,9},{9,8},{10,11... | collective-permute-start | bytes 1572872 | tf_op jit(solution)/shard_map/ppermute | solution.py:85
  44.0 1.2 collective-permute-done.9.refs_10_
  45.1 0.9 copy-done.4
  46.0 4.7 %project.1 = bf16[128,1024]{1,0:T(8,128)(2,1)} custom-call(s32[29]{0:T(128)S(1)} %fusion.50.place_ref, bf16[32,2048]{1,0:T(8,128)(2,1)S(1)} %constant_dynamic-update-slice_fusion.refs_0_, bf16[32,2048]{1,0:T(8,128)(2,1)S(1)} %collective-permute-done.3.refs_1_, bf16[32,2048]{1,0:T(8,128)(2,1)S(1)} %collective-permute-done.4.refs_2_, ...), custom_call_target="tpu_custom_call" | custom-call | flops 536870912 | bytes 4980736 | tf_op jit(solution)/shard_map/project/pallas_call | solution.py:153
  51.3 3.4 %all-to-all-start.1 = ((bf16[4,32,1024]{2,1,0:T(8,128)(2,1)}), bf16[4,32,1024]{2,1,0:T(8,128)(2,1)S(1)}, u32[]{:S(2)}, u32[]{:S(2)}) async-start(bf16[4,32,1024]{2,1,0:T(8,128)(2,1)} %bitcast.5), calls=%async_computation.1 | async-start | bytes 524288 | tf_op jit(solution)/shard_map/all_to_all | solution.py:281
  54.7 0.9 constant_dynamic-slice_fusion
  55.8 8.2 %all-to-all-done.1 = bf16[4,32,1024]{2,1,0:T(8,128)(2,1)S(1)} async-done(((bf16[4,32,1024]{2,1,0:T(8,128)(2,1)}), bf16[4,32,1024]{2,1,0:T(8,128)(2,1)S(1)}, u32[]{:S(2)}, u32[]{:S(2)}) %all-to-all-start.1) | async-done | bytes 262176 | tf_op jit(solution)/shard_map/all_to_all | solution.py:281
  64.1 2.0 collective-permute-start.13
  66.1 1.5 collective-permute-start.14
  68.3 5.4 %collective-permute-done.14 = bf16[32,1024]{1,0:T(8,128)(2,1)S(1)} collective-permute-done((bf16[32,1024]{1,0:T(8,128)(2,1)S(1)}, bf16[32,1024]{1,0:T(8,128)(2,1)S(1)}, u32[]{:S(2)}, u32[]{:S(2)}) %collective-permute-start.14) | collective-permute-done | bytes 65568 | tf_op jit(solution)/shard_map/ppermute | solution.py:89
  73.7 4.6 %gate_up.2 = bf16[128,3712]{1,0:T(8,128)(2,1)} custom-call(f32[1,1024]{1,0:T(1,128)S(1)} %bitcast.55, bf16[128,1024]{1,0:T(8,128)(2,1)S(1)} %pad_maximum_fusion.refs_0_, bf16[1024,896]{1,0:T(8,128)(2,1)} %refs_3_.1, bf16[1024,896]{1,0:T(8,128)(2,1)} %refs_4_.3, bf16[1024,896]{1,0:T(8,128)(2,1)} %collective-permute-done.11.refs_3_.refs_5_, ...), custom_call_target="tpu_custom_call" | custom-call | flops 939524096 | bytes 8519680 | tf_op jit(solution)/shard_map/gate_up/pallas_call | solution.py:203
  78.4 4.2 %all-to-all-start.2 = ((bf16[8,16,3712]{2,1,0:T(8,128)(2,1)}), bf16[8,16,3712]{2,1,0:T(8,128)(2,1)}, u32[]{:S(2)}, u32[]{:S(2)}) async-start(bf16[8,16,3712]{2,1,0:T(8,128)(2,1)} %bitcast.6), calls=%async_computation.2 | async-start | bytes 1900544 | tf_op jit(solution)/shard_map/all_to_all | solution.py:281
  82.6 3.1 %collective-permute-start.16 = (bf16[128,1024]{1,0:T(8,128)(2,1)S(1)}, bf16[128,1024]{1,0:T(8,128)(2,1)S(1)}, u32[]{:S(2)}, u32[]{:S(2)}) collective-permute-start(bf16[128,1024]{1,0:T(8,128)(2,1)S(1)} %pad_maximum_fusion.refs_0_), channel_id=1, source_target_pairs={{8,0},{16,8},{24,16},{0,24},{9,1},{17,9},{25,17},{1,25},{10,2},{18... | collective-permute-start | bytes 786440 | tf_op jit(solution)/shard_map/ppermute | solution.py:89
  86.4 5.4 %collective-permute-done.16.refs_0_ = bf16[128,1024]{1,0:T(8,128)(2,1)S(1)} collective-permute-done((bf16[128,1024]{1,0:T(8,128)(2,1)S(1)}, bf16[128,1024]{1,0:T(8,128)(2,1)S(1)}, u32[]{:S(2)}, u32[]{:S(2)}) %collective-permute-start.16) | collective-permute-done | bytes 262176 | tf_op jit(solution)/shard_map/ppermute | solution.py:89
  92.5 2.8 %collective-permute-done.18.refs_2_ = bf16[128,1024]{1,0:T(8,128)(2,1)S(1)} collective-permute-done((bf16[128,1024]{1,0:T(8,128)(2,1)S(1)}, bf16[128,1024]{1,0:T(8,128)(2,1)S(1)}, u32[]{:S(2)}, u32[]{:S(2)}) %collective-permute-start.18) | collective-permute-done | bytes 262176 | tf_op jit(solution)/shard_map/ppermute | solution.py:89
  95.3 5.5 %gate_up.3 = bf16[384,3712]{1,0:T(8,128)(2,1)S(1)} custom-call(f32[1,1024]{1,0:T(1,128)S(1)} %bitcast.56, bf16[128,1024]{1,0:T(8,128)(2,1)S(1)} %collective-permute-done.16.refs_0_, bf16[128,1024]{1,0:T(8,128)(2,1)S(1)} %collective-permute-done.17.refs_1_, bf16[128,1024]{1,0:T(8,128)(2,1)S(1)} %collective-permute-done.18.refs_2_, bf16[1024,896]{1,0:T(8,128)(2,1)} %refs_3_.1, ...), custom_call_target="tpu_custom_call" | custom-call | flops 2818572288 | bytes 10878976 | tf_op jit(solution)/shard_map/gate_up/pallas_call | solution.py:203
  100.9 1.6 copy-done.1
  102.4 7.4 %all-to-all-start.3 = ((bf16[8,48,3712]{2,1,0:T(8,128)(2,1)}), bf16[8,48,3712]{2,1,0:T(8,128)(2,1)}, u32[]{:S(2)}, u32[]{:S(2)}) async-start(bf16[8,48,3712]{2,1,0:T(8,128)(2,1)} %bitcast.54), calls=%async_computation.3 | async-start | bytes 5701632 | tf_op jit(solution)/shard_map/all_to_all | solution.py:281
  109.8 1.3 convert_reduce_fusion.1
  111.1 29.5 %all-to-all-done.3 = bf16[8,48,3712]{2,1,0:T(8,128)(2,1)} async-done(((bf16[8,48,3712]{2,1,0:T(8,128)(2,1)}), bf16[8,48,3712]{2,1,0:T(8,128)(2,1)}, u32[]{:S(2)}, u32[]{:S(2)}) %all-to-all-start.3) | async-done | bytes 2850848 | tf_op jit(solution)/shard_map/all_to_all | solution.py:281
  140.7 2.3 %convert_reduce_fusion = f32[48,3712]{1,0:T(8,128)S(1)} fusion(bf16[8,48,3712]{2,1,0:T(8,128)(2,1)} %all-to-all-done.3), kind=kLoop, calls=%fused_computation | loop fusion | flops 2672640 | bytes 3563520 | tf_op jit(solution)/shard_map/reduce_sum | solution.py:287
  143.4 1.4 broadcast_in_dim.19
  144.8 6.2 %all-to-all-start.4 = ((bf16[8,64,1792]{2,1,0:T(8,128)(2,1)}), bf16[8,64,1792]{2,1,0:T(8,128)(2,1)}, u32[]{:S(2)}, u32[]{:S(2)}) async-start(bf16[8,64,1792]{2,1,0:T(8,128)(2,1)} %broadcast_in_dim.19), calls=%async_computation.4 | async-start | bytes 3670016 | tf_op jit(solution)/shard_map/all_to_all | solution.py:281
  151.0 3.4 %collective-permute-start.19 = (bf16[896,1024]{1,0:T(8,128)(2,1)}, bf16[896,1024]{1,0:T(8,128)(2,1)S(1)}, u32[]{:S(2)}, u32[]{:S(2)}) collective-permute-start(bf16[896,1024]{1,0:T(8,128)(2,1)} %own.1), channel_id=1, source_target_pairs={{0,1},{1,0},{2,3},{3,2},{4,5},{5,4},{6,7},{7,6},{8,9},{9,8},{10,11... | collective-permute-start | bytes 5505032 | tf_op jit(solution)/shard_map/ppermute | solution.py:85
  154.4 3.6 %collective-permute-done.19.other = bf16[896,1024]{1,0:T(8,128)(2,1)S(1)} collective-permute-done((bf16[896,1024]{1,0:T(8,128)(2,1)}, bf16[896,1024]{1,0:T(8,128)(2,1)S(1)}, u32[]{:S(2)}, u32[]{:S(2)}) %collective-permute-start.19) | collective-permute-done | bytes 1835040 | tf_op jit(solution)/shard_map/ppermute | solution.py:85
  158.0 1.3 copy-done.7
  159.3 12.8 %all-to-all-done.4.hidden_ref = bf16[8,64,1792]{2,1,0:T(8,128)(2,1)} async-done(((bf16[8,64,1792]{2,1,0:T(8,128)(2,1)}), bf16[8,64,1792]{2,1,0:T(8,128)(2,1)}, u32[]{:S(2)}, u32[]{:S(2)}) %all-to-all-start.4) | async-done | bytes 1835040 | tf_op jit(solution)/shard_map/all_to_all | solution.py:281
  172.1 1.5 copy-done.6
  173.6 1.5 copy-done.8
  175.1 4.4 %down.1 = (bf16[128,1024]{1,0:T(8,128)(2,1)S(1)}, bf16[128,1024]{1,0:T(8,128)(2,1)S(1)}, bf16[128,1024]{1,0:T(8,128)(2,1)S(1)}, bf16[128,1024]{1,0:T(8,128)(2,1)S(1)}) custom-call(s32[29]{0:T(128)S(1)} %fusion.50.place_ref, bf16[8,64,1792]{2,1,0:T(8,128)(2,1)} %all-to-all-done.4.hidden_ref, bf16[896,1024]{1,0:T(8,128)(2,1)S(1)} %copy-done.6, ...), custom_call_target="tpu_custom_call" | custom-call | flops 1879048192 | bytes 6553600 | tf_op jit(solution)/shard_map/down/pallas_call | solution.py:256
  179.9 2.3 %collective-permute-start.22 = (bf16[128,1024]{1,0:T(8,128)(2,1)S(1)}, bf16[128,1024]{1,0:T(8,128)(2,1)S(1)}, u32[]{:S(2)}, u32[]{:S(2)}) collective-permute-start(bf16[128,1024]{1,0:T(8,128)(2,1)S(1)} %get-tuple-element.44), channel_id=1, source_target_pairs={{0,24},{8,0},{16,8},{24,16},{1,25},{9,1},{17,9},{25,17},{2,26},{10... | collective-permute-start | bytes 786440 | tf_op jit(solution)/shard_map/ppermute | solution.py:93
  182.2 6.5 %collective-permute-done.20 = bf16[128,1024]{1,0:T(8,128)(2,1)S(1)} collective-permute-done((bf16[128,1024]{1,0:T(8,128)(2,1)S(1)}, bf16[128,1024]{1,0:T(8,128)(2,1)S(1)}, u32[]{:S(2)}, u32[]{:S(2)}) %collective-permute-start.20) | collective-permute-done | bytes 262176 | tf_op jit(solution)/shard_map/ppermute | solution.py:93
  188.7 0.9 collective-permute-done.21
  190.7 8.4 %collective-permute-start.24 = (bf16[32,1024]{1,0:T(8,128)(2,1)S(1)}, bf16[32,1024]{1,0:T(8,128)(2,1)S(1)}, u32[]{:S(2)}, u32[]{:S(2)}) collective-permute-start(bf16[32,1024]{1,0:T(8,128)(2,1)S(1)} %get-tuple-element.55), channel_id=1, source_target_pairs={{0,4},{2,6},{4,0},{6,2},{1,5},{3,7},{5,1},{7,3},{8,12},{10,14},{12... | collective-permute-start | bytes 196616 | tf_op jit(solution)/shard_map/ppermute | solution.py:93
  199.1 3.5 %collective-permute-start.25 = (bf16[32,1024]{1,0:T(8,128)(2,1)S(1)}, bf16[32,1024]{1,0:T(8,128)(2,1)S(1)}, u32[]{:S(2)}, u32[]{:S(2)}) collective-permute-start(bf16[32,1024]{1,0:T(8,128)(2,1)S(1)} %get-tuple-element.54), channel_id=1, source_target_pairs={{0,6},{2,0},{4,2},{6,4},{1,7},{3,1},{5,3},{7,5},{8,14},{10,8},{12,... | collective-permute-start | bytes 196616 | tf_op jit(solution)/shard_map/ppermute | solution.py:93
  202.6 3.3 %collective-permute-done.25 = bf16[32,1024]{1,0:T(8,128)(2,1)S(1)} collective-permute-done((bf16[32,1024]{1,0:T(8,128)(2,1)S(1)}, bf16[32,1024]{1,0:T(8,128)(2,1)S(1)}, u32[]{:S(2)}, u32[]{:S(2)}) %collective-permute-start.25) | collective-permute-done | bytes 65568 | tf_op jit(solution)/shard_map/ppermute | solution.py:93
  205.9 3.6 %collective-permute-start.26 = (bf16[16,1024]{1,0:T(8,128)(2,1)S(1)}, bf16[16,1024]{1,0:T(8,128)(2,1)S(1)}, u32[]{:S(2)}, u32[]{:S(2)}) collective-permute-start(bf16[16,1024]{1,0:T(8,128)(2,1)S(1)} %broadcast_select_fusion.2), channel_id=1, source_target_pairs={{0,1},{1,0},{2,3},{3,2},{4,5},{5,4},{6,7},{7,6},{8,9},{9,8},{10,11... | collective-permute-start | bytes 98312 | tf_op jit(solution)/shard_map/ppermute | solution.py:85
  209.5 0.9 collective-permute-done.26
  (81 shorter events, 12.7 us)
Async XLA Ops:
  0.0 6.9 %copy-start = (bf16[4,256,1024]{2,1,0:T(8,128)(2,1)S(1)}, bf16[4,256,1024]{2,1,0:T(8,128)(2,1)}, u32[]{:S(2)}) copy-start(bf16[4,256,1024]{2,1,0:T(8,128)(2,1)} %param.15) | copy-start | bytes 6291460
  0.0 25.2 %collective-permute-start = (bf16[256,1024]{1,0:T(8,128)(2,1)}, bf16[256,1024]{1,0:T(8,128)(2,1)S(1)}, u32[]{:S(2)}, u32[]{:S(2)}) collective-permute-start(bf16[256,1024]{1,0:T(8,128)(2,1)} %refs_4_.2), channel_id=1, source_target_pairs={{8,0},{16,8},{24,16},{0,24},{9,1},{17,9},{25,17},{1,25},{10,2},{18... | collective-permute-start | bytes 1572872 | tf_op jit(solution)/shard_map/ppermute | solution.py:89
  3.6 21.6 %collective-permute-start.1 = (bf16[256,1024]{1,0:T(8,128)(2,1)}, bf16[256,1024]{1,0:T(8,128)(2,1)}, u32[]{:S(2)}, u32[]{:S(2)}) collective-permute-start(bf16[256,1024]{1,0:T(8,128)(2,1)} %refs_4_.2), channel_id=1, source_target_pairs={{24,0},{0,8},{8,16},{16,24},{25,1},{1,9},{9,17},{17,25},{26,2},{2,... | collective-permute-start | bytes 1572872 | tf_op jit(solution)/shard_map/ppermute | solution.py:89
  5.0 3.7 %copy-start.9 = (bf16[4,256,1024]{2,1,0:T(8,128)(2,1)S(1)}, bf16[4,256,1024]{2,1,0:T(8,128)(2,1)}, u32[]{:S(2)}) copy-start(bf16[4,256,1024]{2,1,0:T(8,128)(2,1)} %param.16) | copy-start | bytes 6291460
  8.4 9.7 %copy-start.2 = (bf16[256,1024]{1,0:T(8,128)(2,1)S(1)}, bf16[256,1024]{1,0:T(8,128)(2,1)}, u32[]{:S(2)}) copy-start(bf16[256,1024]{1,0:T(8,128)(2,1)} %refs_4_.2) | copy-start | bytes 1572868
  9.9 15.2 %all-to-all-start = ((bf16[4,4,2048]{2,1,0:T(4,128)(2,1)}), bf16[4,4,2048]{2,1,0:T(4,128)(2,1)S(1)}, u32[]{:S(2)}, u32[]{:S(2)}) async-start(bf16[4,4,2048]{2,1,0:T(4,128)(2,1)} %reshape.72), calls=%async_computation | async-start | bytes 131072 | tf_op jit(solution)/shard_map/all_to_all | solution.py:281
  18.1 18.3 %collective-permute-start.6 = (bf16[256,1024]{1,0:T(8,128)(2,1)S(1)}, bf16[256,1024]{1,0:T(8,128)(2,1)}, u32[]{:S(2)}, u32[]{:S(2)}) collective-permute-start(bf16[256,1024]{1,0:T(8,128)(2,1)S(1)} %copy-done.2), channel_id=1, source_target_pairs={{16,0},{24,8},{0,16},{8,24},{17,1},{25,9},{1,17},{9,25},{18,2},{26... | collective-permute-start | bytes 1572872 | tf_op jit(solution)/shard_map/ppermute | solution.py:89
  25.2 3.6 %collective-permute-start.2 = (bf16[16,2048]{1,0:T(8,128)(2,1)S(1)}, bf16[16,2048]{1,0:T(8,128)(2,1)S(1)}, u32[]{:S(2)}, u32[]{:S(2)}) collective-permute-start(bf16[16,2048]{1,0:T(8,128)(2,1)S(1)} %reshape.73), channel_id=1, source_target_pairs={{0,32},{32,0},{1,33},{33,1},{2,34},{34,2},{3,35},{35,3},{4,36},{36... | collective-permute-start | bytes 196616 | tf_op jit(solution)/shard_map/ppermute | solution.py:85
  28.8 7.6 %collective-permute-start.3 = (bf16[32,2048]{1,0:T(8,128)(2,1)S(1)}, bf16[32,2048]{1,0:T(8,128)(2,1)S(1)}, u32[]{:S(2)}, u32[]{:S(2)}) collective-permute-start(bf16[32,2048]{1,0:T(8,128)(2,1)S(1)} %constant_dynamic-update-slice_fusion.refs_0_), channel_id=1, source_target_pairs={{64,0},{128,64},{192,128},{0,192},{65,1},{129,65},{193,129},{1,193... | collective-permute-start | bytes 393224 | tf_op jit(solution)/shard_map/ppermute | solution.py:89
  31.3 7.3 %collective-permute-start.4 = (bf16[32,2048]{1,0:T(8,128)(2,1)S(1)}, bf16[32,2048]{1,0:T(8,128)(2,1)S(1)}, u32[]{:S(2)}, u32[]{:S(2)}) collective-permute-start(bf16[32,2048]{1,0:T(8,128)(2,1)S(1)} %constant_dynamic-update-slice_fusion.refs_0_), channel_id=1, source_target_pairs={{128,0},{192,64},{0,128},{64,192},{129,1},{193,65},{1,129},{65,193... | collective-permute-start | bytes 393224 | tf_op jit(solution)/shard_map/ppermute | solution.py:89
  31.8 6.8 %collective-permute-start.5 = (bf16[32,2048]{1,0:T(8,128)(2,1)S(1)}, bf16[32,2048]{1,0:T(8,128)(2,1)S(1)}, u32[]{:S(2)}, u32[]{:S(2)}) collective-permute-start(bf16[32,2048]{1,0:T(8,128)(2,1)S(1)} %constant_dynamic-update-slice_fusion.refs_0_), channel_id=1, source_target_pairs={{192,0},{0,64},{64,128},{128,192},{193,1},{1,65},{65,129},{129,193... | collective-permute-start | bytes 393224 | tf_op jit(solution)/shard_map/ppermute | solution.py:89
  32.4 11.5 %collective-permute-start.7 = (bf16[256,1024]{1,0:T(8,128)(2,1)S(1)}, bf16[256,1024]{1,0:T(8,128)(2,1)}, u32[]{:S(2)}, u32[]{:S(2)}) collective-permute-start(bf16[256,1024]{1,0:T(8,128)(2,1)S(1)} %copy-done.2), channel_id=1, source_target_pairs={{0,1},{1,0},{2,3},{3,2},{4,5},{5,4},{6,7},{7,6},{8,9},{9,8},{10,11... | collective-permute-start | bytes 1572872 | tf_op jit(solution)/shard_map/ppermute | solution.py:85
  36.4 7.5 %collective-permute-start.10 = (bf16[256,1024]{1,0:T(8,128)(2,1)}, bf16[256,1024]{1,0:T(8,128)(2,1)}, u32[]{:S(2)}, u32[]{:S(2)}) collective-permute-start(bf16[256,1024]{1,0:T(8,128)(2,1)} %collective-permute-done.1.refs_7_), channel_id=1, source_target_pairs={{0,1},{1,0},{2,3},{3,2},{4,5},{5,4},{6,7},{7,6},{8,9},{9,8},{10,11... | collective-permute-start | bytes 1572872 | tf_op jit(solution)/shard_map/ppermute | solution.py:85
  36.4 7.5 %collective-permute-start.8 = (bf16[256,1024]{1,0:T(8,128)(2,1)S(1)}, bf16[256,1024]{1,0:T(8,128)(2,1)}, u32[]{:S(2)}, u32[]{:S(2)}) collective-permute-start(bf16[256,1024]{1,0:T(8,128)(2,1)S(1)} %collective-permute-done.refs_5_), channel_id=1, source_target_pairs={{0,1},{1,0},{2,3},{3,2},{4,5},{5,4},{6,7},{7,6},{8,9},{9,8},{10,11... | collective-permute-start | bytes 1572872 | tf_op jit(solution)/shard_map/ppermute | solution.py:85
  38.6 0.7 copy-start.3
  39.3 5.8 %collective-permute-start.9 = (bf16[256,1024]{1,0:T(8,128)(2,1)}, bf16[256,1024]{1,0:T(8,128)(2,1)}, u32[]{:S(2)}, u32[]{:S(2)}) collective-permute-start(bf16[256,1024]{1,0:T(8,128)(2,1)} %collective-permute-done.6.refs_6_), channel_id=1, source_target_pairs={{0,1},{1,0},{2,3},{3,2},{4,5},{5,4},{6,7},{7,6},{8,9},{9,8},{10,11... | collective-permute-start | bytes 1572872 | tf_op jit(solution)/shard_map/ppermute | solution.py:85
  43.2 20.8 %copy-start.5 = (f32[1024]{0:T(1024)S(1)}, f32[1024]{0:T(1024)}, u32[]{:S(2)}) copy-start(f32[1024]{0:T(1024)} %param.21) | copy-start | bytes 12292
  45.1 0.9 copy-start.4
  50.7 13.4 %collective-permute-start.11 = (bf16[1024,896]{1,0:T(8,128)(2,1)}, bf16[1024,896]{1,0:T(8,128)(2,1)}, u32[]{:S(2)}, u32[]{:S(2)}) collective-permute-start(bf16[1024,896]{1,0:T(8,128)(2,1)} %refs_3_.1), channel_id=1, source_target_pairs={{0,1},{1,0},{2,3},{3,2},{4,5},{5,4},{6,7},{7,6},{8,9},{9,8},{10,11... | collective-permute-start | bytes 5505032 | tf_op jit(solution)/shard_map/ppermute | solution.py:85
  51.2 12.9 %collective-permute-start.12 = (bf16[1024,896]{1,0:T(8,128)(2,1)}, bf16[1024,896]{1,0:T(8,128)(2,1)}, u32[]{:S(2)}, u32[]{:S(2)}) collective-permute-start(bf16[1024,896]{1,0:T(8,128)(2,1)} %refs_4_.3), channel_id=1, source_target_pairs={{0,1},{1,0},{2,3},{3,2},{4,5},{5,4},{6,7},{7,6},{8,9},{9,8},{10,11... | collective-permute-start | bytes 5505032 | tf_op jit(solution)/shard_map/ppermute | solution.py:85
  51.3 12.7 %all-to-all-start.1 = ((bf16[4,32,1024]{2,1,0:T(8,128)(2,1)}), bf16[4,32,1024]{2,1,0:T(8,128)(2,1)S(1)}, u32[]{:S(2)}, u32[]{:S(2)}) async-start(bf16[4,32,1024]{2,1,0:T(8,128)(2,1)} %bitcast.5), calls=%async_computation.1 | async-start | bytes 524288 | tf_op jit(solution)/shard_map/all_to_all | solution.py:281
  64.1 4.2 %collective-permute-start.13 = (bf16[32,1024]{1,0:T(8,128)(2,1)S(1)}, bf16[32,1024]{1,0:T(8,128)(2,1)S(1)}, u32[]{:S(2)}, u32[]{:S(2)}) collective-permute-start(bf16[32,1024]{1,0:T(8,128)(2,1)S(1)} %get-tuple-element.36), channel_id=1, source_target_pairs={{2,0},{4,2},{6,4},{0,6},{3,1},{5,3},{7,5},{1,7},{10,8},{12,10},{14... | collective-permute-start | bytes 196616 | tf_op jit(solution)/shard_map/ppermute | solution.py:89
  66.1 7.6 %collective-permute-start.14 = (bf16[32,1024]{1,0:T(8,128)(2,1)S(1)}, bf16[32,1024]{1,0:T(8,128)(2,1)S(1)}, u32[]{:S(2)}, u32[]{:S(2)}) collective-permute-start(bf16[32,1024]{1,0:T(8,128)(2,1)S(1)} %get-tuple-element.36), channel_id=1, source_target_pairs={{4,0},{6,2},{0,4},{2,6},{5,1},{7,3},{1,5},{3,7},{12,8},{14,10},{8,... | collective-permute-start | bytes 196616 | tf_op jit(solution)/shard_map/ppermute | solution.py:89
  67.6 6.1 %collective-permute-start.15 = (bf16[32,1024]{1,0:T(8,128)(2,1)S(1)}, bf16[32,1024]{1,0:T(8,128)(2,1)S(1)}, u32[]{:S(2)}, u32[]{:S(2)}) collective-permute-start(bf16[32,1024]{1,0:T(8,128)(2,1)S(1)} %get-tuple-element.36), channel_id=1, source_target_pairs={{6,0},{0,2},{2,4},{4,6},{7,1},{1,3},{3,5},{5,7},{14,8},{8,10},{10,... | collective-permute-start | bytes 196616 | tf_op jit(solution)/shard_map/ppermute | solution.py:89
  78.4 24.1 %all-to-all-start.2 = ((bf16[8,16,3712]{2,1,0:T(8,128)(2,1)}), bf16[8,16,3712]{2,1,0:T(8,128)(2,1)}, u32[]{:S(2)}, u32[]{:S(2)}) async-start(bf16[8,16,3712]{2,1,0:T(8,128)(2,1)} %bitcast.6), calls=%async_computation.2 | async-start | bytes 1900544 | tf_op jit(solution)/shard_map/all_to_all | solution.py:281
  82.6 9.2 %collective-permute-start.16 = (bf16[128,1024]{1,0:T(8,128)(2,1)S(1)}, bf16[128,1024]{1,0:T(8,128)(2,1)S(1)}, u32[]{:S(2)}, u32[]{:S(2)}) collective-permute-start(bf16[128,1024]{1,0:T(8,128)(2,1)S(1)} %pad_maximum_fusion.refs_0_), channel_id=1, source_target_pairs={{8,0},{16,8},{24,16},{0,24},{9,1},{17,9},{25,17},{1,25},{10,2},{18... | collective-permute-start | bytes 786440 | tf_op jit(solution)/shard_map/ppermute | solution.py:89
  85.7 6.8 %collective-permute-start.17 = (bf16[128,1024]{1,0:T(8,128)(2,1)S(1)}, bf16[128,1024]{1,0:T(8,128)(2,1)S(1)}, u32[]{:S(2)}, u32[]{:S(2)}) collective-permute-start(bf16[128,1024]{1,0:T(8,128)(2,1)S(1)} %pad_maximum_fusion.refs_0_), channel_id=1, source_target_pairs={{16,0},{24,8},{0,16},{8,24},{17,1},{25,9},{1,17},{9,25},{18,2},{26... | collective-permute-start | bytes 786440 | tf_op jit(solution)/shard_map/ppermute | solution.py:89
  85.7 9.6 %collective-permute-start.18 = (bf16[128,1024]{1,0:T(8,128)(2,1)S(1)}, bf16[128,1024]{1,0:T(8,128)(2,1)S(1)}, u32[]{:S(2)}, u32[]{:S(2)}) collective-permute-start(bf16[128,1024]{1,0:T(8,128)(2,1)S(1)} %pad_maximum_fusion.refs_0_), channel_id=1, source_target_pairs={{24,0},{0,8},{8,16},{16,24},{25,1},{1,9},{9,17},{17,25},{26,2},{2,... | collective-permute-start | bytes 786440 | tf_op jit(solution)/shard_map/ppermute | solution.py:89
  100.9 1.6 copy-start.1
  102.4 38.2 %all-to-all-start.3 = ((bf16[8,48,3712]{2,1,0:T(8,128)(2,1)}), bf16[8,48,3712]{2,1,0:T(8,128)(2,1)}, u32[]{:S(2)}, u32[]{:S(2)}) async-start(bf16[8,48,3712]{2,1,0:T(8,128)(2,1)} %bitcast.54), calls=%async_computation.3 | async-start | bytes 5701632 | tf_op jit(solution)/shard_map/all_to_all | solution.py:281
  144.8 27.3 %all-to-all-start.4 = ((bf16[8,64,1792]{2,1,0:T(8,128)(2,1)}), bf16[8,64,1792]{2,1,0:T(8,128)(2,1)}, u32[]{:S(2)}, u32[]{:S(2)}) async-start(bf16[8,64,1792]{2,1,0:T(8,128)(2,1)} %broadcast_in_dim.19), calls=%async_computation.4 | async-start | bytes 3670016 | tf_op jit(solution)/shard_map/all_to_all | solution.py:281
  151.0 7.0 %collective-permute-start.19 = (bf16[896,1024]{1,0:T(8,128)(2,1)}, bf16[896,1024]{1,0:T(8,128)(2,1)S(1)}, u32[]{:S(2)}, u32[]{:S(2)}) collective-permute-start(bf16[896,1024]{1,0:T(8,128)(2,1)} %own.1), channel_id=1, source_target_pairs={{0,1},{1,0},{2,3},{3,2},{4,5},{5,4},{6,7},{7,6},{8,9},{9,8},{10,11... | collective-permute-start | bytes 5505032 | tf_op jit(solution)/shard_map/ppermute | solution.py:85
  158.0 1.3 copy-start.7
  172.1 1.5 copy-start.6
  173.6 1.5 copy-start.8
  179.5 9.3 %collective-permute-start.20 = (bf16[128,1024]{1,0:T(8,128)(2,1)S(1)}, bf16[128,1024]{1,0:T(8,128)(2,1)S(1)}, u32[]{:S(2)}, u32[]{:S(2)}) collective-permute-start(bf16[128,1024]{1,0:T(8,128)(2,1)S(1)} %get-tuple-element.42), channel_id=1, source_target_pairs={{0,8},{8,16},{16,24},{24,0},{1,9},{9,17},{17,25},{25,1},{2,10},{10... | collective-permute-start | bytes 786440 | tf_op jit(solution)/shard_map/ppermute | solution.py:93
  179.6 10.1 %collective-permute-start.21 = (bf16[128,1024]{1,0:T(8,128)(2,1)S(1)}, bf16[128,1024]{1,0:T(8,128)(2,1)S(1)}, u32[]{:S(2)}, u32[]{:S(2)}) collective-permute-start(bf16[128,1024]{1,0:T(8,128)(2,1)S(1)} %get-tuple-element.43), channel_id=1, source_target_pairs={{0,16},{8,24},{16,0},{24,8},{1,17},{9,25},{17,1},{25,9},{2,18},{10... | collective-permute-start | bytes 786440 | tf_op jit(solution)/shard_map/ppermute | solution.py:93
  179.9 10.5 %collective-permute-start.22 = (bf16[128,1024]{1,0:T(8,128)(2,1)S(1)}, bf16[128,1024]{1,0:T(8,128)(2,1)S(1)}, u32[]{:S(2)}, u32[]{:S(2)}) collective-permute-start(bf16[128,1024]{1,0:T(8,128)(2,1)S(1)} %get-tuple-element.44), channel_id=1, source_target_pairs={{0,24},{8,0},{16,8},{24,16},{1,25},{9,1},{17,9},{25,17},{2,26},{10... | collective-permute-start | bytes 786440 | tf_op jit(solution)/shard_map/ppermute | solution.py:93
  190.6 11.9 %collective-permute-start.23 = (bf16[32,1024]{1,0:T(8,128)(2,1)S(1)}, bf16[32,1024]{1,0:T(8,128)(2,1)S(1)}, u32[]{:S(2)}, u32[]{:S(2)}) collective-permute-start(bf16[32,1024]{1,0:T(8,128)(2,1)S(1)} %get-tuple-element.53), channel_id=1, source_target_pairs={{0,2},{2,4},{4,6},{6,0},{1,3},{3,5},{5,7},{7,1},{8,10},{10,12},{12... | collective-permute-start | bytes 196616 | tf_op jit(solution)/shard_map/ppermute | solution.py:93
  190.7 11.9 %collective-permute-start.24 = (bf16[32,1024]{1,0:T(8,128)(2,1)S(1)}, bf16[32,1024]{1,0:T(8,128)(2,1)S(1)}, u32[]{:S(2)}, u32[]{:S(2)}) collective-permute-start(bf16[32,1024]{1,0:T(8,128)(2,1)S(1)} %get-tuple-element.55), channel_id=1, source_target_pairs={{0,4},{2,6},{4,0},{6,2},{1,5},{3,7},{5,1},{7,3},{8,12},{10,14},{12... | collective-permute-start | bytes 196616 | tf_op jit(solution)/shard_map/ppermute | solution.py:93
  199.1 6.8 %collective-permute-start.25 = (bf16[32,1024]{1,0:T(8,128)(2,1)S(1)}, bf16[32,1024]{1,0:T(8,128)(2,1)S(1)}, u32[]{:S(2)}, u32[]{:S(2)}) collective-permute-start(bf16[32,1024]{1,0:T(8,128)(2,1)S(1)} %get-tuple-element.54), channel_id=1, source_target_pairs={{0,6},{2,0},{4,2},{6,4},{1,7},{3,1},{5,3},{7,5},{8,14},{10,8},{12,... | collective-permute-start | bytes 196616 | tf_op jit(solution)/shard_map/ppermute | solution.py:93
  205.9 4.4 %collective-permute-start.26 = (bf16[16,1024]{1,0:T(8,128)(2,1)S(1)}, bf16[16,1024]{1,0:T(8,128)(2,1)S(1)}, u32[]{:S(2)}, u32[]{:S(2)}) collective-permute-start(bf16[16,1024]{1,0:T(8,128)(2,1)S(1)} %broadcast_select_fusion.2), channel_id=1, source_target_pairs={{0,1},{1,0},{2,3},{3,2},{4,5},{5,4},{6,7},{7,6},{8,9},{9,8},{10,11... | collective-permute-start | bytes 98312 | tf_op jit(solution)/shard_map/ppermute | solution.py:85

commit v5 on v4

--- a/solution.py
+++ b/solution.py
@@ -197,7 +197,7 @@
             out_ref[:, j * width + n : j * width + n + size] = product.astype(out_ref.dtype)
 
 
-def gate_up(gain, pieces, weights):
+def gate_up(gain, pieces, weights, hidden_us):
     count, depth = len(pieces) * pieces[0].shape[0], pieces[0].shape[1]
     width = weights[0].shape[1]
     return pl.pallas_call(
@@ -212,7 +212,7 @@
             pltpu.SemaphoreType.DMA((4,)),
         ],
         name="gate_up",
-        **params(20, 8 * count * depth * width, 2 * (count * depth + 4 * depth * width + 4 * count * width)),
+        **params(20, hidden_us * 1153500000, 2 * (count * depth + 4 * depth * width + 4 * count * width)),
     )(gain, *pieces, *weights)
 
 
@@ -266,7 +266,7 @@
             pltpu.SemaphoreType.DMA((2,)),
         ],
         name="down",
-        **params(18, 4 * count * depth * width, 2 * (2 * count * depth + 2 * depth * width + count * width)),
+        **params(60, 4 * count * depth * width, 2 * (2 * count * depth + 2 * depth * width + count * width)),
     )(place, hidden, *weights, mixed)
 
 
@@ -337,7 +337,10 @@
     down_other = swap(late, "core")
     pieces = [ring_from(block, "y", t) for t in (1, 2, 3)]
     weights = [w_gate, w_up, gate_other, up_other]
-    summed = [scatter_sum(gate_up(norm_gain[None, :], part, weights), GRP) for part in ([block], pieces)]
+    summed = [
+        scatter_sum(gate_up(norm_gain[None, :], part, weights, hidden_us), GRP)
+        for part, hidden_us in (([block], 15), (pieces, 60))
+    ]
     summed = jnp.concatenate(summed, axis=0)
     width = w_gate.shape[1]
     square_sum = summed[:, 4 * width] + summed[:, 4 * width + 1]

time: 212 us -> 202 us (0.953)
  waiting for transfers between devices: 90.3 us -> 81.3 us
  local copies, waits for them, and re-layouts: 12.7 us -> 8.46 us
  Pallas kernels: 19.2 us -> 21.5 us
    ppermute x12, waiting for transfers between devices: 14.4 us -> 5.45 us  [ring_from(): return lax.ppermute(block, axis, [((i + shift) % 4, i) for i in range(4)])]
    ppermute x6, starting transfers between devices: 14.7 us -> 10 us  [ring_to(): return lax.ppermute(block, axis, [(i, (i + shift) % 4) for i in range(4)])]
    ppermute x9, starting transfers between devices: 18.6 us -> 23.2 us  [swap(): return lax.ppermute(block, axis, [(0, 1), (1, 0)])]
    unnamed x22 -> x18, local copies, waits for them, and re-layouts: 7.4 us -> 3.14 us
    pallas_call x1, Pallas kernels: 4.35 us -> 6.64 us  [down(): pl.pallas_call(down_kernel, in_specs=[SMEM] + [ANY] * 3 + [VMEM], out_spe...]
  transfers between devices with their start and end apart: 32 -> 32, of which waited for: 16 -> 14; matrix products, arithmetic and copies ran while one was open for 4% -> 5% of each run, Pallas kernels for 3% -> 5%
where the time goes in v5:
time: 202 us; the launch traced here: 201 us
  waiting for transfers between devices  81.3 us (40%)
  starting transfers between devices  78.4 us (39%)
  Pallas kernels  21.5 us (11%)
  local copies, waits for them, and re-layouts  8.46 us (4%)
  other arithmetic  7.86 us (4%)
  matrix products  3 us (1%)
    all_to_all x5, waiting for transfers between devices, exchange(): return lax.all_to_all(pieces, axis, split_axis=0, concat_axis=0, tiled=True)  57.7 us
    all_to_all x5, starting transfers between devices, exchange(): return lax.all_to_all(pieces, axis, split_axis=0, concat_axis=0, tiled=True)  28.2 us
    ppermute x9, starting transfers between devices, swap(): return lax.ppermute(block, axis, [(0, 1), (1, 0)])  23.2 us
    ppermute x12, starting transfers between devices, ring_from(): return lax.ppermute(block, axis, [((i + shift) % 4, i) for i in range(4)])  17 us
    pallas_call x2, Pallas kernels, gate_up(): pl.pallas_call(gate_up_kernel, in_specs=[VMEM] + [ANY] * (len(pieces) + 4...  10.1 us
    ppermute x6, starting transfers between devices, ring_to(): return lax.ppermute(block, axis, [(i, (i + shift) % 4) for i in range(4)])  10 us
    ppermute x6, waiting for transfers between devices, ring_to(): return lax.ppermute(block, axis, [(i, (i + shift) % 4) for i in range(4)])  9.62 us
    ppermute x9, waiting for transfers between devices, swap(): return lax.ppermute(block, axis, [(0, 1), (1, 0)])  8.55 us
  transfers between devices with their start and end apart: 32, of which 14 were waited for; matrix products, arithmetic and copies ran while one was open for 5% of the time, Pallas kernels for 5%

profile of v5, /device:TPU:1, one launch (start us, length us, event | category | flops | bytes accessed | tf_op | source)
XLA Modules:
  0.0 200.9 jit_solution(8190210075877338976)
XLA Ops:
  0.0 3.6 %collective-permute-start = (bf16[256,1024]{1,0:T(8,128)(2,1)}, bf16[256,1024]{1,0:T(8,128)(2,1)S(1)}, u32[]{:S(2)}, u32[]{:S(2)}) collective-permute-start(bf16[256,1024]{1,0:T(8,128)(2,1)} %refs_4_.2), channel_id=1, source_target_pairs={{8,0},{16,8},{24,16},{0,24},{9,1},{17,9},{25,17},{1,25},{10,2},{18... | collective-permute-start | bytes 1572872 | tf_op jit(solution)/shard_map/ppermute | solution.py:89
  3.6 0.7 iota_compare_fusion
  4.3 0.7 reshape.83
  5.0 0.9 convert_bitcast_fusion
  5.9 1.0 fusion.41
  6.9 1.6 fusion.53
  9.9 8.2 %all-to-all-start = ((bf16[4,4,2048]{2,1,0:T(4,128)(2,1)}), bf16[4,4,2048]{2,1,0:T(4,128)(2,1)S(1)}, u32[]{:S(2)}, u32[]{:S(2)}) async-start(bf16[4,4,2048]{2,1,0:T(4,128)(2,1)} %reshape.72), calls=%async_computation | async-start | bytes 131072 | tf_op jit(solution)/shard_map/all_to_all | solution.py:281
  18.1 1.6 collective-permute-start.6
  19.7 5.4 %all-to-all-done = bf16[4,4,2048]{2,1,0:T(4,128)(2,1)S(1)} async-done(((bf16[4,4,2048]{2,1,0:T(4,128)(2,1)}), bf16[4,4,2048]{2,1,0:T(4,128)(2,1)S(1)}, u32[]{:S(2)}, u32[]{:S(2)}) %all-to-all-start) | async-done | bytes 65568 | tf_op jit(solution)/shard_map/all_to_all | solution.py:281
  25.2 0.8 collective-permute-start.2
  26.0 2.8 %collective-permute-done.2 = bf16[16,2048]{1,0:T(8,128)(2,1)S(1)} collective-permute-done((bf16[16,2048]{1,0:T(8,128)(2,1)S(1)}, bf16[16,2048]{1,0:T(8,128)(2,1)S(1)}, u32[]{:S(2)}, u32[]{:S(2)}) %collective-permute-start.2) | collective-permute-done | bytes 65568 | tf_op jit(solution)/shard_map/ppermute | solution.py:85
  28.8 2.5 %collective-permute-start.3 = (bf16[32,2048]{1,0:T(8,128)(2,1)S(1)}, bf16[32,2048]{1,0:T(8,128)(2,1)S(1)}, u32[]{:S(2)}, u32[]{:S(2)}) collective-permute-start(bf16[32,2048]{1,0:T(8,128)(2,1)S(1)} %constant_dynamic-update-slice_fusion.refs_0_), channel_id=1, source_target_pairs={{64,0},{128,64},{192,128},{0,192},{65,1},{129,65},{193,129},{1,193... | collective-permute-start | bytes 393224 | tf_op jit(solution)/shard_map/ppermute | solution.py:89
  32.4 4.0 %collective-permute-start.7 = (bf16[256,1024]{1,0:T(8,128)(2,1)S(1)}, bf16[256,1024]{1,0:T(8,128)(2,1)}, u32[]{:S(2)}, u32[]{:S(2)}) collective-permute-start(bf16[256,1024]{1,0:T(8,128)(2,1)S(1)} %copy-done.2), channel_id=1, source_target_pairs={{0,1},{1,0},{2,3},{3,2},{4,5},{5,4},{6,7},{7,6},{8,9},{9,8},{10,11... | collective-permute-start | bytes 1572872 | tf_op jit(solution)/shard_map/ppermute | solution.py:85
  36.4 2.2 %collective-permute-start.8 = (bf16[256,1024]{1,0:T(8,128)(2,1)S(1)}, bf16[256,1024]{1,0:T(8,128)(2,1)}, u32[]{:S(2)}, u32[]{:S(2)}) collective-permute-start(bf16[256,1024]{1,0:T(8,128)(2,1)S(1)} %collective-permute-done.refs_5_), channel_id=1, source_target_pairs={{0,1},{1,0},{2,3},{3,2},{4,5},{5,4},{6,7},{7,6},{8,9},{9,8},{10,11... | collective-permute-start | bytes 1572872 | tf_op jit(solution)/shard_map/ppermute | solution.py:85
  39.3 4.0 %collective-permute-start.9 = (bf16[256,1024]{1,0:T(8,128)(2,1)}, bf16[256,1024]{1,0:T(8,128)(2,1)}, u32[]{:S(2)}, u32[]{:S(2)}) collective-permute-start(bf16[256,1024]{1,0:T(8,128)(2,1)} %collective-permute-done.6.refs_6_), channel_id=1, source_target_pairs={{0,1},{1,0},{2,3},{3,2},{4,5},{5,4},{6,7},{7,6},{8,9},{9,8},{10,11... | collective-permute-start | bytes 1572872 | tf_op jit(solution)/shard_map/ppermute | solution.py:85
  44.0 1.2 collective-permute-done.9.refs_10_
  45.1 0.9 copy-done.4
  46.0 4.7 %project.1 = bf16[128,1024]{1,0:T(8,128)(2,1)} custom-call(s32[29]{0:T(128)S(1)} %fusion.50.place_ref, bf16[32,2048]{1,0:T(8,128)(2,1)S(1)} %constant_dynamic-update-slice_fusion.refs_0_, bf16[32,2048]{1,0:T(8,128)(2,1)S(1)} %collective-permute-done.3.refs_1_, bf16[32,2048]{1,0:T(8,128)(2,1)S(1)} %collective-permute-done.4.refs_2_, ...), custom_call_target="tpu_custom_call" | custom-call | flops 536870912 | bytes 4980736 | tf_op jit(solution)/shard_map/project/pallas_call | solution.py:153
  51.3 3.4 %all-to-all-start.1 = ((bf16[4,32,1024]{2,1,0:T(8,128)(2,1)}), bf16[4,32,1024]{2,1,0:T(8,128)(2,1)S(1)}, u32[]{:S(2)}, u32[]{:S(2)}) async-start(bf16[4,32,1024]{2,1,0:T(8,128)(2,1)} %bitcast.5), calls=%async_computation.1 | async-start | bytes 524288 | tf_op jit(solution)/shard_map/all_to_all | solution.py:281
  54.7 0.9 constant_dynamic-slice_fusion
  55.8 7.9 %all-to-all-done.1 = bf16[4,32,1024]{2,1,0:T(8,128)(2,1)S(1)} async-done(((bf16[4,32,1024]{2,1,0:T(8,128)(2,1)}), bf16[4,32,1024]{2,1,0:T(8,128)(2,1)S(1)}, u32[]{:S(2)}, u32[]{:S(2)}) %all-to-all-start.1) | async-done | bytes 262176 | tf_op jit(solution)/shard_map/all_to_all | solution.py:281
  64.4 2.2 %collective-permute-start.13 = (bf16[32,1024]{1,0:T(8,128)(2,1)S(1)}, bf16[32,1024]{1,0:T(8,128)(2,1)S(1)}, u32[]{:S(2)}, u32[]{:S(2)}) collective-permute-start(bf16[32,1024]{1,0:T(8,128)(2,1)S(1)} %get-tuple-element.36), channel_id=1, source_target_pairs={{2,0},{4,2},{6,4},{0,6},{3,1},{5,3},{7,5},{1,7},{10,8},{12,10},{14... | collective-permute-start | bytes 196616 | tf_op jit(solution)/shard_map/ppermute | solution.py:89
  66.6 1.5 collective-permute-start.14
  68.8 5.4 %collective-permute-done.14 = bf16[32,1024]{1,0:T(8,128)(2,1)S(1)} collective-permute-done((bf16[32,1024]{1,0:T(8,128)(2,1)S(1)}, bf16[32,1024]{1,0:T(8,128)(2,1)S(1)}, u32[]{:S(2)}, u32[]{:S(2)}) %collective-permute-start.14) | collective-permute-done | bytes 65568 | tf_op jit(solution)/shard_map/ppermute | solution.py:89
  74.3 3.1 %collective-permute-start.16 = (bf16[128,1024]{1,0:T(8,128)(2,1)S(1)}, bf16[128,1024]{1,0:T(8,128)(2,1)S(1)}, u32[]{:S(2)}, u32[]{:S(2)}) collective-permute-start(bf16[128,1024]{1,0:T(8,128)(2,1)S(1)} %pad_maximum_fusion.refs_0_), channel_id=1, source_target_pairs={{8,0},{16,8},{24,16},{0,24},{9,1},{17,9},{25,17},{1,25},{10,2},{18... | collective-permute-start | bytes 786440 | tf_op jit(solution)/shard_map/ppermute | solution.py:89
  78.0 4.6 %gate_up.2 = bf16[128,3712]{1,0:T(8,128)(2,1)} custom-call(f32[1,1024]{1,0:T(1,128)S(1)} %bitcast.55, bf16[128,1024]{1,0:T(8,128)(2,1)S(1)} %pad_maximum_fusion.refs_0_, bf16[1024,896]{1,0:T(8,128)(2,1)} %refs_3_.1, bf16[1024,896]{1,0:T(8,128)(2,1)} %refs_4_.3, bf16[1024,896]{1,0:T(8,128)(2,1)} %collective-permute-done.11.refs_3_.refs_5_, ...), custom_call_target="tpu_custom_call" | custom-call | flops 17302499328 | bytes 8519680 | tf_op jit(solution)/shard_map/gate_up/pallas_call | solution.py:203
  82.7 4.2 %all-to-all-start.2 = ((bf16[8,16,3712]{2,1,0:T(8,128)(2,1)}), bf16[8,16,3712]{2,1,0:T(8,128)(2,1)}, u32[]{:S(2)}, u32[]{:S(2)}) async-start(bf16[8,16,3712]{2,1,0:T(8,128)(2,1)} %bitcast.6), calls=%async_computation.2 | async-start | bytes 1900544 | tf_op jit(solution)/shard_map/all_to_all | solution.py:281
  86.9 5.5 %gate_up.3 = bf16[384,3712]{1,0:T(8,128)(2,1)S(1)} custom-call(f32[1,1024]{1,0:T(1,128)S(1)} %bitcast.56, bf16[128,1024]{1,0:T(8,128)(2,1)S(1)} %collective-permute-done.16.refs_0_, bf16[128,1024]{1,0:T(8,128)(2,1)S(1)} %collective-permute-done.17.refs_1_, bf16[128,1024]{1,0:T(8,128)(2,1)S(1)} %collective-permute-done.18.refs_2_, bf16[1024,896]{1,0:T(8,128)(2,1)} %refs_3_.1, ...), custom_call_target="tpu_custom_call" | custom-call | flops 69209997312 | bytes 10878976 | tf_op jit(solution)/shard_map/gate_up/pallas_call | solution.py:203
  92.5 1.5 copy-done.1
  94.0 2.8 %all-to-all-done.2 = bf16[8,16,3712]{2,1,0:T(8,128)(2,1)} async-done(((bf16[8,16,3712]{2,1,0:T(8,128)(2,1)}), bf16[8,16,3712]{2,1,0:T(8,128)(2,1)}, u32[]{:S(2)}, u32[]{:S(2)}) %all-to-all-start.2) | async-done | bytes 950304 | tf_op jit(solution)/shard_map/all_to_all | solution.py:281
  96.8 6.2 %all-to-all-start.3 = ((bf16[8,48,3712]{2,1,0:T(8,128)(2,1)}), bf16[8,48,3712]{2,1,0:T(8,128)(2,1)}, u32[]{:S(2)}, u32[]{:S(2)}) async-start(bf16[8,48,3712]{2,1,0:T(8,128)(2,1)} %bitcast.54), calls=%async_computation.3 | async-start | bytes 5701632 | tf_op jit(solution)/shard_map/all_to_all | solution.py:281
  103.0 1.3 convert_reduce_fusion.1
  104.4 28.9 %all-to-all-done.3 = bf16[8,48,3712]{2,1,0:T(8,128)(2,1)} async-done(((bf16[8,48,3712]{2,1,0:T(8,128)(2,1)}), bf16[8,48,3712]{2,1,0:T(8,128)(2,1)}, u32[]{:S(2)}, u32[]{:S(2)}) %all-to-all-start.3) | async-done | bytes 2850848 | tf_op jit(solution)/shard_map/all_to_all | solution.py:281
  133.3 2.3 %convert_reduce_fusion = f32[48,3712]{1,0:T(8,128)S(1)} fusion(bf16[8,48,3712]{2,1,0:T(8,128)(2,1)} %all-to-all-done.3), kind=kLoop, calls=%fused_computation | loop fusion | flops 2672640 | bytes 3563520 | tf_op jit(solution)/shard_map/reduce_sum | solution.py:287
  136.0 1.4 broadcast_in_dim.19
  137.4 6.2 %all-to-all-start.4 = ((bf16[8,64,1792]{2,1,0:T(8,128)(2,1)}), bf16[8,64,1792]{2,1,0:T(8,128)(2,1)}, u32[]{:S(2)}, u32[]{:S(2)}) async-start(bf16[8,64,1792]{2,1,0:T(8,128)(2,1)} %broadcast_in_dim.19), calls=%async_computation.4 | async-start | bytes 3670016 | tf_op jit(solution)/shard_map/all_to_all | solution.py:281
  143.6 4.1 %collective-permute-start.19 = (bf16[896,1024]{1,0:T(8,128)(2,1)}, bf16[896,1024]{1,0:T(8,128)(2,1)}, u32[]{:S(2)}, u32[]{:S(2)}) collective-permute-start(bf16[896,1024]{1,0:T(8,128)(2,1)} %own.1), channel_id=1, source_target_pairs={{0,1},{1,0},{2,3},{3,2},{4,5},{5,4},{6,7},{7,6},{8,9},{9,8},{10,11... | collective-permute-start | bytes 5505032 | tf_op jit(solution)/shard_map/ppermute | solution.py:85
  147.7 3.8 %collective-permute-done.19.other = bf16[896,1024]{1,0:T(8,128)(2,1)} collective-permute-done((bf16[896,1024]{1,0:T(8,128)(2,1)}, bf16[896,1024]{1,0:T(8,128)(2,1)}, u32[]{:S(2)}, u32[]{:S(2)}) %collective-permute-start.19) | collective-permute-done | bytes 1835040 | tf_op jit(solution)/shard_map/ppermute | solution.py:85
  151.4 12.7 %all-to-all-done.4.hidden_ref = bf16[8,64,1792]{2,1,0:T(8,128)(2,1)} async-done(((bf16[8,64,1792]{2,1,0:T(8,128)(2,1)}), bf16[8,64,1792]{2,1,0:T(8,128)(2,1)}, u32[]{:S(2)}, u32[]{:S(2)}) %all-to-all-start.4) | async-done | bytes 1835040 | tf_op jit(solution)/shard_map/all_to_all | solution.py:281
  164.1 6.6 %down.1 = (bf16[128,1024]{1,0:T(8,128)(2,1)}, bf16[128,1024]{1,0:T(8,128)(2,1)}, bf16[128,1024]{1,0:T(8,128)(2,1)}, bf16[128,1024]{1,0:T(8,128)(2,1)}) custom-call(s32[29]{0:T(128)} %copy-done.6, bf16[8,64,1792]{2,1,0:T(8,128)(2,1)} %all-to-all-done.4.hidden_ref, bf16[896,1024]{1,0:T(8,128)(2,1)} %own.1, bf16[896,1024]{1,0:T(8,128)(2,1)} %collective-permute-done.19.other, ...), custom_call_target="tpu_custom_call" | custom-call | flops 1879048192 | bytes 6553600 | tf_op jit(solution)/shard_map/down/pallas_call | solution.py:256
  170.9 2.6 %collective-permute-start.22 = (bf16[128,1024]{1,0:T(8,128)(2,1)}, bf16[128,1024]{1,0:T(8,128)(2,1)S(1)}, u32[]{:S(2)}, u32[]{:S(2)}) collective-permute-start(bf16[128,1024]{1,0:T(8,128)(2,1)} %get-tuple-element.44), channel_id=1, source_target_pairs={{0,24},{8,0},{16,8},{24,16},{1,25},{9,1},{17,9},{25,17},{2,26},{10... | collective-permute-start | bytes 786440 | tf_op jit(solution)/shard_map/ppermute | solution.py:93
  173.5 7.4 %collective-permute-done.20 = bf16[128,1024]{1,0:T(8,128)(2,1)S(1)} collective-permute-done((bf16[128,1024]{1,0:T(8,128)(2,1)}, bf16[128,1024]{1,0:T(8,128)(2,1)S(1)}, u32[]{:S(2)}, u32[]{:S(2)}) %collective-permute-start.20) | collective-permute-done | bytes 262176 | tf_op jit(solution)/shard_map/ppermute | solution.py:93
  181.3 1.1 fusion.51
  182.5 3.7 %collective-permute-start.24 = (bf16[32,1024]{1,0:T(8,128)(2,1)S(1)}, bf16[32,1024]{1,0:T(8,128)(2,1)S(1)}, u32[]{:S(2)}, u32[]{:S(2)}) collective-permute-start(bf16[32,1024]{1,0:T(8,128)(2,1)S(1)} %get-tuple-element.55), channel_id=1, source_target_pairs={{0,4},{2,6},{4,0},{6,2},{1,5},{3,7},{5,1},{7,3},{8,12},{10,14},{12... | collective-permute-start | bytes 196616 | tf_op jit(solution)/shard_map/ppermute | solution.py:93
  186.3 3.5 %collective-permute-start.25 = (bf16[32,1024]{1,0:T(8,128)(2,1)S(1)}, bf16[32,1024]{1,0:T(8,128)(2,1)S(1)}, u32[]{:S(2)}, u32[]{:S(2)}) collective-permute-start(bf16[32,1024]{1,0:T(8,128)(2,1)S(1)} %get-tuple-element.54), channel_id=1, source_target_pairs={{0,6},{2,0},{4,2},{6,4},{1,7},{3,1},{5,3},{7,5},{8,14},{10,8},{12,... | collective-permute-start | bytes 196616 | tf_op jit(solution)/shard_map/ppermute | solution.py:93
  190.4 1.2 collective-permute-done.25
  191.6 7.6 %collective-permute-start.26 = (bf16[16,1024]{1,0:T(8,128)(2,1)S(1)}, bf16[16,1024]{1,0:T(8,128)(2,1)S(1)}, u32[]{:S(2)}, u32[]{:S(2)}) collective-permute-start(bf16[16,1024]{1,0:T(8,128)(2,1)S(1)} %broadcast_select_fusion.2), channel_id=1, source_target_pairs={{0,1},{1,0},{2,3},{3,2},{4,5},{5,4},{6,7},{7,6},{8,9},{9,8},{10,11... | collective-permute-start | bytes 98312 | tf_op jit(solution)/shard_map/ppermute | solution.py:85
  199.2 0.9 collective-permute-done.26
  (77 shorter events, 9.4 us)
Async XLA Ops:
  0.0 6.9 %copy-start = (bf16[4,256,1024]{2,1,0:T(8,128)(2,1)S(1)}, bf16[4,256,1024]{2,1,0:T(8,128)(2,1)}, u32[]{:S(2)}) copy-start(bf16[4,256,1024]{2,1,0:T(8,128)(2,1)} %param.15) | copy-start | bytes 6291460
  0.0 25.2 %collective-permute-start = (bf16[256,1024]{1,0:T(8,128)(2,1)}, bf16[256,1024]{1,0:T(8,128)(2,1)S(1)}, u32[]{:S(2)}, u32[]{:S(2)}) collective-permute-start(bf16[256,1024]{1,0:T(8,128)(2,1)} %refs_4_.2), channel_id=1, source_target_pairs={{8,0},{16,8},{24,16},{0,24},{9,1},{17,9},{25,17},{1,25},{10,2},{18... | collective-permute-start | bytes 1572872 | tf_op jit(solution)/shard_map/ppermute | solution.py:89
  3.6 21.6 %collective-permute-start.1 = (bf16[256,1024]{1,0:T(8,128)(2,1)}, bf16[256,1024]{1,0:T(8,128)(2,1)}, u32[]{:S(2)}, u32[]{:S(2)}) collective-permute-start(bf16[256,1024]{1,0:T(8,128)(2,1)} %refs_4_.2), channel_id=1, source_target_pairs={{24,0},{0,8},{8,16},{16,24},{25,1},{1,9},{9,17},{17,25},{26,2},{2,... | collective-permute-start | bytes 1572872 | tf_op jit(solution)/shard_map/ppermute | solution.py:89
  5.0 3.7 %copy-start.7 = (bf16[4,256,1024]{2,1,0:T(8,128)(2,1)S(1)}, bf16[4,256,1024]{2,1,0:T(8,128)(2,1)}, u32[]{:S(2)}) copy-start(bf16[4,256,1024]{2,1,0:T(8,128)(2,1)} %param.16) | copy-start | bytes 6291460
  8.4 9.7 %copy-start.2 = (bf16[256,1024]{1,0:T(8,128)(2,1)S(1)}, bf16[256,1024]{1,0:T(8,128)(2,1)}, u32[]{:S(2)}) copy-start(bf16[256,1024]{1,0:T(8,128)(2,1)} %refs_4_.2) | copy-start | bytes 1572868
  9.9 15.2 %all-to-all-start = ((bf16[4,4,2048]{2,1,0:T(4,128)(2,1)}), bf16[4,4,2048]{2,1,0:T(4,128)(2,1)S(1)}, u32[]{:S(2)}, u32[]{:S(2)}) async-start(bf16[4,4,2048]{2,1,0:T(4,128)(2,1)} %reshape.72), calls=%async_computation | async-start | bytes 131072 | tf_op jit(solution)/shard_map/all_to_all | solution.py:281
  18.1 18.3 %collective-permute-start.6 = (bf16[256,1024]{1,0:T(8,128)(2,1)S(1)}, bf16[256,1024]{1,0:T(8,128)(2,1)}, u32[]{:S(2)}, u32[]{:S(2)}) collective-permute-start(bf16[256,1024]{1,0:T(8,128)(2,1)S(1)} %copy-done.2), channel_id=1, source_target_pairs={{16,0},{24,8},{0,16},{8,24},{17,1},{25,9},{1,17},{9,25},{18,2},{26... | collective-permute-start | bytes 1572872 | tf_op jit(solution)/shard_map/ppermute | solution.py:89
  25.2 3.6 %collective-permute-start.2 = (bf16[16,2048]{1,0:T(8,128)(2,1)S(1)}, bf16[16,2048]{1,0:T(8,128)(2,1)S(1)}, u32[]{:S(2)}, u32[]{:S(2)}) collective-permute-start(bf16[16,2048]{1,0:T(8,128)(2,1)S(1)} %reshape.73), channel_id=1, source_target_pairs={{0,32},{32,0},{1,33},{33,1},{2,34},{34,2},{3,35},{35,3},{4,36},{36... | collective-permute-start | bytes 196616 | tf_op jit(solution)/shard_map/ppermute | solution.py:85
  28.8 7.6 %collective-permute-start.3 = (bf16[32,2048]{1,0:T(8,128)(2,1)S(1)}, bf16[32,2048]{1,0:T(8,128)(2,1)S(1)}, u32[]{:S(2)}, u32[]{:S(2)}) collective-permute-start(bf16[32,2048]{1,0:T(8,128)(2,1)S(1)} %constant_dynamic-update-slice_fusion.refs_0_), channel_id=1, source_target_pairs={{64,0},{128,64},{192,128},{0,192},{65,1},{129,65},{193,129},{1,193... | collective-permute-start | bytes 393224 | tf_op jit(solution)/shard_map/ppermute | solution.py:89
  31.3 7.3 %collective-permute-start.4 = (bf16[32,2048]{1,0:T(8,128)(2,1)S(1)}, bf16[32,2048]{1,0:T(8,128)(2,1)S(1)}, u32[]{:S(2)}, u32[]{:S(2)}) collective-permute-start(bf16[32,2048]{1,0:T(8,128)(2,1)S(1)} %constant_dynamic-update-slice_fusion.refs_0_), channel_id=1, source_target_pairs={{128,0},{192,64},{0,128},{64,192},{129,1},{193,65},{1,129},{65,193... | collective-permute-start | bytes 393224 | tf_op jit(solution)/shard_map/ppermute | solution.py:89
  31.8 6.8 %collective-permute-start.5 = (bf16[32,2048]{1,0:T(8,128)(2,1)S(1)}, bf16[32,2048]{1,0:T(8,128)(2,1)S(1)}, u32[]{:S(2)}, u32[]{:S(2)}) collective-permute-start(bf16[32,2048]{1,0:T(8,128)(2,1)S(1)} %constant_dynamic-update-slice_fusion.refs_0_), channel_id=1, source_target_pairs={{192,0},{0,64},{64,128},{128,192},{193,1},{1,65},{65,129},{129,193... | collective-permute-start | bytes 393224 | tf_op jit(solution)/shard_map/ppermute | solution.py:89
  32.4 11.5 %collective-permute-start.7 = (bf16[256,1024]{1,0:T(8,128)(2,1)S(1)}, bf16[256,1024]{1,0:T(8,128)(2,1)}, u32[]{:S(2)}, u32[]{:S(2)}) collective-permute-start(bf16[256,1024]{1,0:T(8,128)(2,1)S(1)} %copy-done.2), channel_id=1, source_target_pairs={{0,1},{1,0},{2,3},{3,2},{4,5},{5,4},{6,7},{7,6},{8,9},{9,8},{10,11... | collective-permute-start | bytes 1572872 | tf_op jit(solution)/shard_map/ppermute | solution.py:85
  36.4 7.6 %collective-permute-start.10 = (bf16[256,1024]{1,0:T(8,128)(2,1)}, bf16[256,1024]{1,0:T(8,128)(2,1)}, u32[]{:S(2)}, u32[]{:S(2)}) collective-permute-start(bf16[256,1024]{1,0:T(8,128)(2,1)} %collective-permute-done.1.refs_7_), channel_id=1, source_target_pairs={{0,1},{1,0},{2,3},{3,2},{4,5},{5,4},{6,7},{7,6},{8,9},{9,8},{10,11... | collective-permute-start | bytes 1572872 | tf_op jit(solution)/shard_map/ppermute | solution.py:85
  36.4 7.6 %collective-permute-start.8 = (bf16[256,1024]{1,0:T(8,128)(2,1)S(1)}, bf16[256,1024]{1,0:T(8,128)(2,1)}, u32[]{:S(2)}, u32[]{:S(2)}) collective-permute-start(bf16[256,1024]{1,0:T(8,128)(2,1)S(1)} %collective-permute-done.refs_5_), channel_id=1, source_target_pairs={{0,1},{1,0},{2,3},{3,2},{4,5},{5,4},{6,7},{7,6},{8,9},{9,8},{10,11... | collective-permute-start | bytes 1572872 | tf_op jit(solution)/shard_map/ppermute | solution.py:85
  38.6 0.7 copy-start.3
  39.3 5.8 %collective-permute-start.9 = (bf16[256,1024]{1,0:T(8,128)(2,1)}, bf16[256,1024]{1,0:T(8,128)(2,1)}, u32[]{:S(2)}, u32[]{:S(2)}) collective-permute-start(bf16[256,1024]{1,0:T(8,128)(2,1)} %collective-permute-done.6.refs_6_), channel_id=1, source_target_pairs={{0,1},{1,0},{2,3},{3,2},{4,5},{5,4},{6,7},{7,6},{8,9},{9,8},{10,11... | collective-permute-start | bytes 1572872 | tf_op jit(solution)/shard_map/ppermute | solution.py:85
  43.2 20.5 %copy-start.5 = (f32[1024]{0:T(1024)S(1)}, f32[1024]{0:T(1024)}, u32[]{:S(2)}) copy-start(f32[1024]{0:T(1024)} %param.21) | copy-start | bytes 12292
  43.9 6.8 %copy-start.6 = (s32[29]{0:T(128)}, s32[29]{0:T(128)S(1)}, u32[]{:S(2)}) copy-start(s32[29]{0:T(128)S(1)} %fusion.50.place_ref) | copy-start | bytes 352
  45.1 0.9 copy-start.4
  50.7 13.7 %collective-permute-start.11 = (bf16[1024,896]{1,0:T(8,128)(2,1)}, bf16[1024,896]{1,0:T(8,128)(2,1)}, u32[]{:S(2)}, u32[]{:S(2)}) collective-permute-start(bf16[1024,896]{1,0:T(8,128)(2,1)} %refs_3_.1), channel_id=1, source_target_pairs={{0,1},{1,0},{2,3},{3,2},{4,5},{5,4},{6,7},{7,6},{8,9},{9,8},{10,11... | collective-permute-start | bytes 5505032 | tf_op jit(solution)/shard_map/ppermute | solution.py:85
  51.2 13.3 %collective-permute-start.12 = (bf16[1024,896]{1,0:T(8,128)(2,1)}, bf16[1024,896]{1,0:T(8,128)(2,1)}, u32[]{:S(2)}, u32[]{:S(2)}) collective-permute-start(bf16[1024,896]{1,0:T(8,128)(2,1)} %refs_4_.3), channel_id=1, source_target_pairs={{0,1},{1,0},{2,3},{3,2},{4,5},{5,4},{6,7},{7,6},{8,9},{9,8},{10,11... | collective-permute-start | bytes 5505032 | tf_op jit(solution)/shard_map/ppermute | solution.py:85
  51.3 12.4 %all-to-all-start.1 = ((bf16[4,32,1024]{2,1,0:T(8,128)(2,1)}), bf16[4,32,1024]{2,1,0:T(8,128)(2,1)S(1)}, u32[]{:S(2)}, u32[]{:S(2)}) async-start(bf16[4,32,1024]{2,1,0:T(8,128)(2,1)} %bitcast.5), calls=%async_computation.1 | async-start | bytes 524288 | tf_op jit(solution)/shard_map/all_to_all | solution.py:281
  64.4 4.4 %collective-permute-start.13 = (bf16[32,1024]{1,0:T(8,128)(2,1)S(1)}, bf16[32,1024]{1,0:T(8,128)(2,1)S(1)}, u32[]{:S(2)}, u32[]{:S(2)}) collective-permute-start(bf16[32,1024]{1,0:T(8,128)(2,1)S(1)} %get-tuple-element.36), channel_id=1, source_target_pairs={{2,0},{4,2},{6,4},{0,6},{3,1},{5,3},{7,5},{1,7},{10,8},{12,10},{14... | collective-permute-start | bytes 196616 | tf_op jit(solution)/shard_map/ppermute | solution.py:89
  66.6 7.6 %collective-permute-start.14 = (bf16[32,1024]{1,0:T(8,128)(2,1)S(1)}, bf16[32,1024]{1,0:T(8,128)(2,1)S(1)}, u32[]{:S(2)}, u32[]{:S(2)}) collective-permute-start(bf16[32,1024]{1,0:T(8,128)(2,1)S(1)} %get-tuple-element.36), channel_id=1, source_target_pairs={{4,0},{6,2},{0,4},{2,6},{5,1},{7,3},{1,5},{3,7},{12,8},{14,10},{8,... | collective-permute-start | bytes 196616 | tf_op jit(solution)/shard_map/ppermute | solution.py:89
  68.2 6.1 %collective-permute-start.15 = (bf16[32,1024]{1,0:T(8,128)(2,1)S(1)}, bf16[32,1024]{1,0:T(8,128)(2,1)S(1)}, u32[]{:S(2)}, u32[]{:S(2)}) collective-permute-start(bf16[32,1024]{1,0:T(8,128)(2,1)S(1)} %get-tuple-element.36), channel_id=1, source_target_pairs={{6,0},{0,2},{2,4},{4,6},{7,1},{1,3},{3,5},{5,7},{14,8},{8,10},{10,... | collective-permute-start | bytes 196616 | tf_op jit(solution)/shard_map/ppermute | solution.py:89
  74.3 12.6 %collective-permute-start.16 = (bf16[128,1024]{1,0:T(8,128)(2,1)S(1)}, bf16[128,1024]{1,0:T(8,128)(2,1)S(1)}, u32[]{:S(2)}, u32[]{:S(2)}) collective-permute-start(bf16[128,1024]{1,0:T(8,128)(2,1)S(1)} %pad_maximum_fusion.refs_0_), channel_id=1, source_target_pairs={{8,0},{16,8},{24,16},{0,24},{9,1},{17,9},{25,17},{1,25},{10,2},{18... | collective-permute-start | bytes 786440 | tf_op jit(solution)/shard_map/ppermute | solution.py:89
  77.4 9.6 %collective-permute-start.17 = (bf16[128,1024]{1,0:T(8,128)(2,1)S(1)}, bf16[128,1024]{1,0:T(8,128)(2,1)S(1)}, u32[]{:S(2)}, u32[]{:S(2)}) collective-permute-start(bf16[128,1024]{1,0:T(8,128)(2,1)S(1)} %pad_maximum_fusion.refs_0_), channel_id=1, source_target_pairs={{16,0},{24,8},{0,16},{8,24},{17,1},{25,9},{1,17},{9,25},{18,2},{26... | collective-permute-start | bytes 786440 | tf_op jit(solution)/shard_map/ppermute | solution.py:89
  77.4 9.6 %collective-permute-start.18 = (bf16[128,1024]{1,0:T(8,128)(2,1)S(1)}, bf16[128,1024]{1,0:T(8,128)(2,1)S(1)}, u32[]{:S(2)}, u32[]{:S(2)}) collective-permute-start(bf16[128,1024]{1,0:T(8,128)(2,1)S(1)} %pad_maximum_fusion.refs_0_), channel_id=1, source_target_pairs={{24,0},{0,8},{8,16},{16,24},{25,1},{1,9},{9,17},{17,25},{26,2},{2,... | collective-permute-start | bytes 786440 | tf_op jit(solution)/shard_map/ppermute | solution.py:89
  82.7 14.2 %all-to-all-start.2 = ((bf16[8,16,3712]{2,1,0:T(8,128)(2,1)}), bf16[8,16,3712]{2,1,0:T(8,128)(2,1)}, u32[]{:S(2)}, u32[]{:S(2)}) async-start(bf16[8,16,3712]{2,1,0:T(8,128)(2,1)} %bitcast.6), calls=%async_computation.2 | async-start | bytes 1900544 | tf_op jit(solution)/shard_map/all_to_all | solution.py:281
  92.5 1.6 copy-start.1
  96.8 36.4 %all-to-all-start.3 = ((bf16[8,48,3712]{2,1,0:T(8,128)(2,1)}), bf16[8,48,3712]{2,1,0:T(8,128)(2,1)}, u32[]{:S(2)}, u32[]{:S(2)}) async-start(bf16[8,48,3712]{2,1,0:T(8,128)(2,1)} %bitcast.54), calls=%async_computation.3 | async-start | bytes 5701632 | tf_op jit(solution)/shard_map/all_to_all | solution.py:281
  137.4 26.7 %all-to-all-start.4 = ((bf16[8,64,1792]{2,1,0:T(8,128)(2,1)}), bf16[8,64,1792]{2,1,0:T(8,128)(2,1)}, u32[]{:S(2)}, u32[]{:S(2)}) async-start(bf16[8,64,1792]{2,1,0:T(8,128)(2,1)} %broadcast_in_dim.19), calls=%async_computation.4 | async-start | bytes 3670016 | tf_op jit(solution)/shard_map/all_to_all | solution.py:281
  143.6 7.8 %collective-permute-start.19 = (bf16[896,1024]{1,0:T(8,128)(2,1)}, bf16[896,1024]{1,0:T(8,128)(2,1)}, u32[]{:S(2)}, u32[]{:S(2)}) collective-permute-start(bf16[896,1024]{1,0:T(8,128)(2,1)} %own.1), channel_id=1, source_target_pairs={{0,1},{1,0},{2,3},{3,2},{4,5},{5,4},{6,7},{7,6},{8,9},{9,8},{10,11... | collective-permute-start | bytes 5505032 | tf_op jit(solution)/shard_map/ppermute | solution.py:85
  170.8 10.2 %collective-permute-start.20 = (bf16[128,1024]{1,0:T(8,128)(2,1)}, bf16[128,1024]{1,0:T(8,128)(2,1)S(1)}, u32[]{:S(2)}, u32[]{:S(2)}) collective-permute-start(bf16[128,1024]{1,0:T(8,128)(2,1)} %get-tuple-element.42), channel_id=1, source_target_pairs={{0,8},{8,16},{16,24},{24,0},{1,9},{9,17},{17,25},{25,1},{2,10},{10... | collective-permute-start | bytes 786440 | tf_op jit(solution)/shard_map/ppermute | solution.py:93
  170.8 10.1 %collective-permute-start.21 = (bf16[128,1024]{1,0:T(8,128)(2,1)}, bf16[128,1024]{1,0:T(8,128)(2,1)S(1)}, u32[]{:S(2)}, u32[]{:S(2)}) collective-permute-start(bf16[128,1024]{1,0:T(8,128)(2,1)} %get-tuple-element.43), channel_id=1, source_target_pairs={{0,16},{8,24},{16,0},{24,8},{1,17},{9,25},{17,1},{25,9},{2,18},{10... | collective-permute-start | bytes 786440 | tf_op jit(solution)/shard_map/ppermute | solution.py:93
  170.9 10.3 %collective-permute-start.22 = (bf16[128,1024]{1,0:T(8,128)(2,1)}, bf16[128,1024]{1,0:T(8,128)(2,1)S(1)}, u32[]{:S(2)}, u32[]{:S(2)}) collective-permute-start(bf16[128,1024]{1,0:T(8,128)(2,1)} %get-tuple-element.44), channel_id=1, source_target_pairs={{0,24},{8,0},{16,8},{24,16},{1,25},{9,1},{17,9},{25,17},{2,26},{10... | collective-permute-start | bytes 786440 | tf_op jit(solution)/shard_map/ppermute | solution.py:93
  182.4 7.3 %collective-permute-start.23 = (bf16[32,1024]{1,0:T(8,128)(2,1)S(1)}, bf16[32,1024]{1,0:T(8,128)(2,1)S(1)}, u32[]{:S(2)}, u32[]{:S(2)}) collective-permute-start(bf16[32,1024]{1,0:T(8,128)(2,1)S(1)} %get-tuple-element.53), channel_id=1, source_target_pairs={{0,2},{2,4},{4,6},{6,0},{1,3},{3,5},{5,7},{7,1},{8,10},{10,12},{12... | collective-permute-start | bytes 196616 | tf_op jit(solution)/shard_map/ppermute | solution.py:93
  182.5 7.8 %collective-permute-start.24 = (bf16[32,1024]{1,0:T(8,128)(2,1)S(1)}, bf16[32,1024]{1,0:T(8,128)(2,1)S(1)}, u32[]{:S(2)}, u32[]{:S(2)}) collective-permute-start(bf16[32,1024]{1,0:T(8,128)(2,1)S(1)} %get-tuple-element.55), channel_id=1, source_target_pairs={{0,4},{2,6},{4,0},{6,2},{1,5},{3,7},{5,1},{7,3},{8,12},{10,14},{12... | collective-permute-start | bytes 196616 | tf_op jit(solution)/shard_map/ppermute | solution.py:93
  186.3 5.3 %collective-permute-start.25 = (bf16[32,1024]{1,0:T(8,128)(2,1)S(1)}, bf16[32,1024]{1,0:T(8,128)(2,1)S(1)}, u32[]{:S(2)}, u32[]{:S(2)}) collective-permute-start(bf16[32,1024]{1,0:T(8,128)(2,1)S(1)} %get-tuple-element.54), channel_id=1, source_target_pairs={{0,6},{2,0},{4,2},{6,4},{1,7},{3,1},{5,3},{7,5},{8,14},{10,8},{12,... | collective-permute-start | bytes 196616 | tf_op jit(solution)/shard_map/ppermute | solution.py:93
  191.6 8.4 %collective-permute-start.26 = (bf16[16,1024]{1,0:T(8,128)(2,1)S(1)}, bf16[16,1024]{1,0:T(8,128)(2,1)S(1)}, u32[]{:S(2)}, u32[]{:S(2)}) collective-permute-start(bf16[16,1024]{1,0:T(8,128)(2,1)S(1)} %broadcast_select_fusion.2), channel_id=1, source_target_pairs={{0,1},{1,0},{2,3},{3,2},{4,5},{5,4},{6,7},{7,6},{8,9},{9,8},{10,11... | collective-permute-start | bytes 98312 | tf_op jit(solution)/shard_map/ppermute | solution.py:85

commit v6 on v5

--- a/solution.py
+++ b/solution.py
@@ -10,6 +10,7 @@
 NAMES = ("x", "l", "y", "z", "core")
 SIZES = (4, 2, 4, 4, 2)
 GRP, ATT = ("x", "l"), ("y", "z", "core")
+BLOCK = pl.BlockSpec()
 VMEM = pl.BlockSpec(memory_space=pltpu.VMEM)
 SMEM = pl.BlockSpec(memory_space=pltpu.SMEM)
 ANY = pl.BlockSpec(memory_space=pl.ANY)
@@ -21,54 +22,8 @@
 HD = 128
 
 
-def attend(queries, cache_key, cache_value, new_key, new_value, lengths):
-    row_count = queries.shape[0]
-    slot_count = cache_key.shape[1]
-    scale_factor = 1.0 / jnp.sqrt(jnp.float32(HD))
-    query_heads = queries.reshape(row_count, KVH, HQ // KVH, HD)
-    key_heads = cache_key.reshape(row_count, slot_count, KVH, HD)
-    value_heads = cache_value.reshape(row_count, slot_count, KVH, HD)
-    scores = (
-        jnp.einsum("rkgd,rpkd->rkgp", query_heads, key_heads, preferred_element_type=jnp.float32)
-        * scale_factor
-    )
-    score_new = (
-        jnp.einsum(
-            "rkgd,rkd->rkg",
-            query_heads,
-            new_key.reshape(row_count, KVH, HD),
-            preferred_element_type=jnp.float32,
-        )
-        * scale_factor
-    )
-    valid = jnp.arange(slot_count, dtype=jnp.int32)[None, :] < lengths[:, None]
-    scores = jnp.where(valid[:, None, None, :], scores, -jnp.inf)
-    top_score = jnp.maximum(jnp.max(scores, axis=-1), score_new)
-    weights = jnp.exp(scores - top_score[..., None])
-    weight_new = jnp.exp(score_new - top_score)
-    total = jnp.sum(weights, axis=-1) + weight_new
-    summed = jnp.einsum(
-        "rkgp,rpkd->rkgd",
-        weights.astype(jnp.bfloat16),
-        value_heads,
-        preferred_element_type=jnp.float32,
-    )
-    new_low = weight_new.astype(jnp.bfloat16).astype(jnp.float32)
-    summed = summed + new_low[..., None] * new_value.astype(jnp.float32).reshape(
-        row_count, KVH, 1, HD
-    )
-    return (summed / total[..., None]).astype(jnp.bfloat16).reshape(row_count, HQ * HD)
-
-
-def activate(gate_sum, up_sum, square_sum):
-    inv_rms = lax.rsqrt(square_sum / D + 1e-05)
-    gate = gate_sum * inv_rms[:, None]
-    up_proj = up_sum * inv_rms[:, None]
-    return (jax.nn.silu(gate) * up_proj).astype(jnp.bfloat16)
-
-
 def places():
-    table = np.zeros((256, 29), np.int32)
+    table = np.zeros((256, 33), np.int32)
     for device in range(256):
         x, l, y, z, core = device >> 6, (device >> 5) & 1, (device >> 3) & 3, (device >> 1) & 3, device & 1
         owners = [(z + t) % 4 for t in range(4)]
@@ -78,6 +33,7 @@
         table[device, 13:17] = [(y + t - z) % 4 for t in range(4)]
         table[device, 17:25] = [(2 * (owner % 2) + source - y) % 4 for owner in owners for source in range(2)]
         table[device, 25:29] = [owner // 2 for owner in owners]
+        table[device, 29:] = owners
     return table
 
 
@@ -115,9 +71,114 @@
         copy.wait()
 
 
+def attend_kernel(lengths_ref, queries_ref, new_key_ref, new_value_ref, keys, values, out_ref):
+    rows, slot_count = keys.shape[:2]
+    group = HQ // KVH
+    scale_factor = 1.0 / jnp.sqrt(jnp.float32(HD))
+    slot = lax.broadcasted_iota(jnp.int32, (HQ, slot_count), 1)
+    for r in range(rows):
+
+        def per_head(ref):
+            spread = jnp.broadcast_to(ref[r].astype(jnp.float32)[:, None, :], (KVH, group, HD))
+            return spread.reshape(HQ, HD)
+
+        query = queries_ref[r]
+        scores = [
+            lax.dot_general(
+                query[k * group : (k + 1) * group],
+                keys[r, :, k * HD : (k + 1) * HD],
+                (((1,), (1,)), ((), ())),
+                preferred_element_type=jnp.float32,
+            )
+            for k in range(KVH)
+        ]
+        scores = jnp.where(slot < lengths_ref[r], jnp.concatenate(scores, axis=0) * scale_factor, -jnp.inf)
+        products = query.astype(jnp.float32) * per_head(new_key_ref)
+        score_new = jnp.sum(products, axis=1, keepdims=True) * scale_factor
+        top_score = jnp.maximum(jnp.max(scores, axis=1, keepdims=True), score_new)
+        weights = jnp.exp(scores - top_score)
+        weight_new = jnp.exp(score_new - top_score)
+        total = jnp.sum(weights, axis=1, keepdims=True) + weight_new
+        weights = weights.astype(jnp.bfloat16)
+        summed = [
+            jnp.dot(
+                weights[k * group : (k + 1) * group],
+                values[r, :, k * HD : (k + 1) * HD],
+                preferred_element_type=jnp.float32,
+            )
+            for k in range(KVH)
+        ]
+        new_low = weight_new.astype(jnp.bfloat16).astype(jnp.float32)
+        summed = jnp.concatenate(summed, axis=0) + new_low * per_head(new_value_ref)
+        out_ref[r] = (summed / total).astype(out_ref.dtype)
+
+
+def attend(queries, cache_key, cache_value, new_key, new_value, lengths):
+    rows, slot_count, width = cache_key.shape
+    return pl.pallas_call(
+        attend_kernel,
+        in_specs=[SMEM] + [VMEM] * 5,
+        out_specs=BLOCK,
+        out_shape=jax.ShapeDtypeStruct((rows, HQ, HD), jnp.bfloat16),
+        name="attend",
+        **params(12, 4 * rows * slot_count * HQ * HD, 4 * rows * slot_count * width),
+    )(
+        lengths,
+        queries.reshape(rows, HQ, HD),
+        new_key.reshape(rows, KVH, HD),
+        new_value.reshape(rows, KVH, HD),
+        cache_key,
+        cache_value,
+    )
+
+
+def activate_kernel(*refs):
+    parts, out_ref, held, hidden_ref, sems = refs[:2], refs[2], refs[3:5], refs[5], refs[6]
+    copies = start_all([pltpu.make_async_copy(parts[i], held[i], sems.at[i]) for i in range(2)])
+    width = hidden_ref.shape[1] // 2
+    start = 0
+    for i in range(2):
+        copies[i].wait()
+        groups, rows = held[i].shape[:2]
+
+        def summed(first, size):
+            return add_up([held[i][g, :, first : first + size] for g in range(groups)])
+
+        square_sum = jnp.sum(summed(4 * width, 128), axis=1, keepdims=True)
+        inv_rms = lax.rsqrt(square_sum / D + 1e-05)
+        for j in range(2):
+            for n, size in steps(width):
+                gate = summed(2 * j * width + n, size) * inv_rms
+                up_proj = summed((2 * j + 1) * width + n, size) * inv_rms
+                hidden = gate / (1.0 + jnp.exp(-gate)) * up_proj
+                hidden_ref[start : start + rows, j * width + n : j * width + n + size] = hidden.astype(jnp.bfloat16)
+        start += rows
+    wait_all(
+        start_all(
+            [pltpu.make_async_copy(hidden_ref, out_ref.at[g], sems.at[2 + g]) for g in range(out_ref.shape[0])]
+        )
+    )
+
+
+def activate(parts):
+    groups, _, width = parts[0].shape
+    width = (width - 128) // 2
+    rows = parts[0].shape[1] + parts[1].shape[1]
+    return pl.pallas_call(
+        activate_kernel,
+        in_specs=[ANY] * 2,
+        out_specs=ANY,
+        out_shape=jax.ShapeDtypeStruct((groups, rows, width), jnp.bfloat16),
+        scratch_shapes=[pltpu.VMEM(part.shape, jnp.bfloat16) for part in parts]
+        + [pltpu.VMEM((rows, width), jnp.bfloat16), pltpu.SemaphoreType.DMA((2 + groups,))],
+        name="activate",
+        **params(12, 0, 6 * groups * rows * width),
+    )(*parts)
+
+
 def project_kernel(place_ref, *refs):
     pieces, own, other = refs[:4], refs[4:8], refs[8:12]
-    out_ref, rows_ref, held_ref, row_sems, held_sems = refs[12:]
+    outs, (rows_ref, held_ref, total_ref, row_sems, held_sems) = refs[12:16], refs[16:]
     step = pieces[0].shape[0] // 2
     row_copies = start_all(
         [
@@ -142,9 +203,13 @@
     wait_all(row_copies)
     wait_all(held_copies)
     for n, size in steps(width):
-        out_ref[:, n : n + size] = jnp.dot(
+        total_ref[:, n : n + size] = jnp.dot(
             rows_ref[...], held_ref[:, n : n + size], preferred_element_type=jnp.float32
-        ).astype(out_ref.dtype)
+        )
+    share = outs[0].shape[0]
+    for t in range(4):
+        start = pl.multiple_of(place_ref[29 + t] * share, share)
+        outs[t][...] = total_ref[pl.ds(start, share), :].astype(outs[t].dtype)
 
 
 def project(place, pieces, own, other):
@@ -153,11 +218,12 @@
     return pl.pallas_call(
         project_kernel,
         in_specs=[SMEM] + [ANY] * 12,
-        out_specs=VMEM,
-        out_shape=jax.ShapeDtypeStruct((count, width), jnp.bfloat16),
+        out_specs=[VMEM] * 4,
+        out_shape=[jax.ShapeDtypeStruct((count // 4, width), jnp.bfloat16)] * 4,
         scratch_shapes=[
             pltpu.VMEM((count, depth), jnp.bfloat16),
             pltpu.VMEM((depth, width), jnp.bfloat16),
+            pltpu.VMEM((count, width), jnp.float32),
             pltpu.SemaphoreType.DMA((8,)),
             pltpu.SemaphoreType.DMA((8,)),
         ],
@@ -281,16 +347,6 @@
     return lax.all_to_all(pieces, axis, split_axis=0, concat_axis=0, tiled=True)
 
 
-def scatter_sum(partial, axis):
-    parts = lax.axis_size(axis)
-    pieces = partial.reshape(parts, partial.shape[0] // parts, partial.shape[1])
-    return jnp.sum(exchange(pieces, axis).astype(jnp.float32), axis=0)
-
-
-def gather(rows, axis):
-    return exchange(jnp.broadcast_to(rows[None], (lax.axis_size(axis),) + rows.shape), axis)
-
-
 def body(
     hidden_in,
     queries,
@@ -311,7 +367,7 @@
     out_other = swap(out_weight, "core")
 
     attended = attend(queries, cache_key, cache_value, new_key, new_value, lengths)
-    count = attended.shape[0]
+    count = queries.shape[0]
     slots = attended.reshape(count, 4, 4, -1).transpose(2, 0, 1, 3).reshape(4, count, -1)
     block = exchange(slots, "z").reshape(4 * count, -1)
     block, out_own[1], out_own[3] = lax.optimization_barrier((block, out_own[1], out_own[3]))
@@ -320,17 +376,16 @@
     pieces = [block] + [ring_from(block, "x", t) for t in (1, 2, 3)]
     *pieces, out_own[2] = lax.optimization_barrier((*pieces, out_own[2]))
     partial = project(place, pieces, out_own, [out_other, out_next, swap(out_own[2], "core"), out_last])
-    partial, *late = lax.optimization_barrier((partial, w_gate, w_up))
-    gate_other, up_other = [swap(w, "core") for w in late]
 
     share = hidden_in.shape[0] // 32
     y, z, core = (device >> 3) & 3, (device >> 1) & 3, device & 1
     start = 256 * z + 32 * y
     own_in = jnp.stack([lax.dynamic_slice_in_dim(hidden_in, start + 128 * l, share, 0) for l in range(2)])
     own_in = lax.dynamic_index_in_dim(own_in.reshape(2, 4, 2, count, -1), core, 2, keepdims=False).reshape(share, -1)
-    mixed = own_in.astype(jnp.float32) + scatter_sum(partial, "z")
+    mixed = own_in.astype(jnp.float32) + add_up([partial[0]] + [ring_to(partial[t], "z", t) for t in (1, 2, 3)])
     normed = (mixed * norm_gain).astype(jnp.bfloat16)
-    normed, gate_other, up_other = lax.optimization_barrier((normed, gate_other, up_other))
+    normed, *late = lax.optimization_barrier((normed, w_gate, w_up))
+    gate_other, up_other = [swap(w, "core") for w in late]
 
     block = jnp.concatenate([normed] + [ring_from(normed, "z", t) for t in (1, 2, 3)], axis=0)
     block, late = lax.optimization_barrier((block, w_down))
@@ -338,20 +393,11 @@
     pieces = [ring_from(block, "y", t) for t in (1, 2, 3)]
     weights = [w_gate, w_up, gate_other, up_other]
     summed = [
-        scatter_sum(gate_up(norm_gain[None, :], part, weights, hidden_us), GRP)
+        exchange(gate_up(norm_gain[None, :], part, weights, hidden_us).reshape(8, -1, 4 * w_gate.shape[1] + 128), GRP)
         for part, hidden_us in (([block], 15), (pieces, 60))
     ]
-    summed = jnp.concatenate(summed, axis=0)
-    width = w_gate.shape[1]
-    square_sum = summed[:, 4 * width] + summed[:, 4 * width + 1]
-    hidden = jnp.concatenate(
-        [
-            activate(summed[:, i * width : (i + 1) * width], summed[:, (i + 1) * width : (i + 2) * width], square_sum)
-            for i in (0, 2)
-        ],
-        axis=1,
-    )
-    parts = down(place, gather(hidden, GRP), [w_down, down_other], mixed)
+    hidden = exchange(activate(summed), GRP)
+    parts = down(place, hidden, [w_down, down_other], mixed)
     total = add_up([parts[0]] + [ring_to(parts[t], "y", t) for t in (1, 2, 3)])
     parts = [total[t * share : (t + 1) * share] for t in range(4)]
     total = add_up([parts[0]] + [ring_to(parts[t].astype(jnp.bfloat16), "z", t) for t in (1, 2, 3)])

time: 202 us -> 215 us (1.064)
  blocking collectives: 0 us -> 37 us
  waiting for transfers between devices: 81.3 us -> 59.1 us
  local copies, waits for them, and re-layouts: 8.46 us -> 26 us
  starting transfers between devices: 78.4 us -> 63.9 us
  other arithmetic: 7.86 us -> 2.83 us
  matrix products: 3 us -> 0 us
  Pallas kernels: 21.5 us -> 24.4 us
    all_to_all x5 -> x3, waiting for transfers between devices: 57.7 us -> 20 us  [exchange(): return lax.all_to_all(pieces, axis, split_axis=0, concat_axis=0, tiled=True)]
    all_to_all x0 -> x1, blocking collectives: none -> 37 us  [exchange(): return lax.all_to_all(pieces, axis, split_axis=0, concat_axis=0, tiled=True)]
    unnamed x18 -> x44, local copies, waits for them, and re-layouts: 3.14 us -> 18.5 us
    ppermute x6 -> x9, waiting for transfers between devices: 9.62 us -> 23.6 us  [ring_to(): return lax.ppermute(block, axis, [(i, (i + shift) % 4) for i in range(4)])]
    all_to_all x5 -> x3, starting transfers between devices: 28.2 us -> 15.7 us  [exchange(): return lax.all_to_all(pieces, axis, split_axis=0, concat_axis=0, tiled=True)]
    pallas_call x1 -> x3, Pallas kernels: 4.68 us -> 8.91 us  [the longest x1 4.19 us: project(): pl.pallas_call(project_kernel, in_specs=[SMEM] + [ANY] * 12, out_specs=[V...]
    reduce_sum x4 -> x0, other arithmetic: 3.87 us -> none  [the longest x3 3.66 us: scatter_sum(): return jnp.sum(exchange(pieces, axis).astype(jnp.float32), axis=0)]
    dot_general x3 -> x0, matrix products: 3 us -> none  [the longest x1 1.56 us: attend(): jnp.einsum('rkgd,rpkd->rkgp', query_heads, key_heads, preferred_element_t...]
  transfers between devices with their start and end apart: 32 -> 33, of which waited for: 14 -> 18; matrix products, arithmetic and copies ran while one was open for 5% -> 4% of each run, Pallas kernels for 5% -> 5%
where the time goes in v6:
time: 215 us; the launch traced here: 214 us
  starting transfers between devices  63.9 us (30%)
  waiting for transfers between devices  59.1 us (27%)
  blocking collectives  37 us (17%)
  local copies, waits for them, and re-layouts  26 us (12%)
  Pallas kernels  24.4 us (11%)
  other arithmetic  2.83 us (1%)
    all_to_all x1, blocking collectives, exchange(): return lax.all_to_all(pieces, axis, split_axis=0, concat_axis=0, tiled=True)  37 us
    ppermute x9, waiting for transfers between devices, ring_to(): return lax.ppermute(block, axis, [(i, (i + shift) % 4) for i in range(4)])  23.6 us
    ppermute x9, starting transfers between devices, swap(): return lax.ppermute(block, axis, [(0, 1), (1, 0)])  22.6 us
    all_to_all x3, waiting for transfers between devices, exchange(): return lax.all_to_all(pieces, axis, split_axis=0, concat_axis=0, tiled=True)  20 us
    unnamed x44, local copies, waits for them, and re-layouts  18.5 us
    ppermute x12, starting transfers between devices, ring_from(): return lax.ppermute(block, axis, [((i + shift) % 4, i) for i in range(4)])  17.1 us
    all_to_all x3, starting transfers between devices, exchange(): return lax.all_to_all(pieces, axis, split_axis=0, concat_axis=0, tiled=True)  15.7 us
    pallas_call x2, Pallas kernels, gate_up(): pl.pallas_call(gate_up_kernel, in_specs=[VMEM] + [ANY] * (len(pieces) + 4...  8.8 us
  transfers between devices with their start and end apart: 33, of which 18 were waited for; matrix products, arithmetic and copies ran while one was open for 4% of the time, Pallas kernels for 5%

profile of v6, /device:TPU:1, one launch (start us, length us, event | category | flops | bytes accessed | tf_op | source)
XLA Modules:
  0.0 213.6 jit_solution(513408777078499169)
XLA Ops:
  0.0 3.6 %collective-permute-start = (bf16[256,1024]{1,0:T(8,128)(2,1)}, bf16[256,1024]{1,0:T(8,128)(2,1)S(1)}, u32[]{:S(2)}, u32[]{:S(2)}) collective-permute-start(bf16[256,1024]{1,0:T(8,128)(2,1)} %refs_4_.2), channel_id=1, source_target_pairs={{8,0},{16,8},{24,16},{0,24},{9,1},{17,9},{25,17},{1,25},{10,2},{18... | collective-permute-start | bytes 1572872 | tf_op jit(solution)/shard_map/ppermute | solution.py:45
  5.1 1.6 copy-done.1
  6.7 1.6 copy-done.2
  9.0 2.0 attend.1
  11.8 8.2 %all-to-all-start = ((bf16[4,4,2048]{2,1,0:T(4,128)(2,1)}), bf16[4,4,2048]{2,1,0:T(4,128)(2,1)S(1)}, u32[]{:S(2)}, u32[]{:S(2)}) async-start(bf16[4,4,2048]{2,1,0:T(4,128)(2,1)} %reshape.46), calls=%async_computation | async-start | bytes 131072 | tf_op jit(solution)/shard_map/all_to_all | solution.py:347
  19.9 1.6 collective-permute-start.6
  21.6 5.4 %all-to-all-done = bf16[4,4,2048]{2,1,0:T(4,128)(2,1)S(1)} async-done(((bf16[4,4,2048]{2,1,0:T(4,128)(2,1)}), bf16[4,4,2048]{2,1,0:T(4,128)(2,1)S(1)}, u32[]{:S(2)}, u32[]{:S(2)}) %all-to-all-start) | async-done | bytes 65568 | tf_op jit(solution)/shard_map/all_to_all | solution.py:347
  27.9 2.7 %collective-permute-done.2 = bf16[16,2048]{1,0:T(8,128)(2,1)S(1)} collective-permute-done((bf16[16,2048]{1,0:T(8,128)(2,1)S(1)}, bf16[16,2048]{1,0:T(8,128)(2,1)S(1)}, u32[]{:S(2)}, u32[]{:S(2)}) %collective-permute-start.2) | collective-permute-done | bytes 65568 | tf_op jit(solution)/shard_map/ppermute | solution.py:41
  30.5 2.5 %collective-permute-start.3 = (bf16[32,2048]{1,0:T(8,128)(2,1)S(1)}, bf16[32,2048]{1,0:T(8,128)(2,1)S(1)}, u32[]{:S(2)}, u32[]{:S(2)}) collective-permute-start(bf16[32,2048]{1,0:T(8,128)(2,1)S(1)} %constant_dynamic-update-slice_fusion.refs_0_), channel_id=1, source_target_pairs={{64,0},{128,64},{192,128},{0,192},{65,1},{129,65},{193,129},{1,193... | collective-permute-start | bytes 393224 | tf_op jit(solution)/shard_map/ppermute | solution.py:45
  34.1 4.1 %collective-permute-start.7 = (bf16[256,1024]{1,0:T(8,128)(2,1)S(1)}, bf16[256,1024]{1,0:T(8,128)(2,1)S(1)}, u32[]{:S(2)}, u32[]{:S(2)}) collective-permute-start(bf16[256,1024]{1,0:T(8,128)(2,1)S(1)} %copy-done.3), channel_id=1, source_target_pairs={{0,1},{1,0},{2,3},{3,2},{4,5},{5,4},{6,7},{7,6},{8,9},{9,8},{10,11... | collective-permute-start | bytes 1572872 | tf_op jit(solution)/shard_map/ppermute | solution.py:41
  38.2 2.2 %collective-permute-start.10 = (bf16[256,1024]{1,0:T(8,128)(2,1)S(1)}, bf16[256,1024]{1,0:T(8,128)(2,1)}, u32[]{:S(2)}, u32[]{:S(2)}) collective-permute-start(bf16[256,1024]{1,0:T(8,128)(2,1)S(1)} %collective-permute-done.1.refs_7_), channel_id=1, source_target_pairs={{0,1},{1,0},{2,3},{3,2},{4,5},{5,4},{6,7},{7,6},{8,9},{9,8},{10,11... | collective-permute-start | bytes 1572872 | tf_op jit(solution)/shard_map/ppermute | solution.py:41
  41.1 4.0 %collective-permute-start.9 = (bf16[256,1024]{1,0:T(8,128)(2,1)S(1)}, bf16[256,1024]{1,0:T(8,128)(2,1)}, u32[]{:S(2)}, u32[]{:S(2)}) collective-permute-start(bf16[256,1024]{1,0:T(8,128)(2,1)S(1)} %collective-permute-done.6.refs_6_), channel_id=1, source_target_pairs={{0,1},{1,0},{2,3},{3,2},{4,5},{5,4},{6,7},{7,6},{8,9},{9,8},{10,11... | collective-permute-start | bytes 1572872 | tf_op jit(solution)/shard_map/ppermute | solution.py:41
  45.1 1.5 constant_dynamic-slice_fusion
  51.2 4.2 %project.1 = (bf16[32,1024]{1,0:T(8,128)(2,1)S(1)}, bf16[32,1024]{1,0:T(8,128)(2,1)}, bf16[32,1024]{1,0:T(8,128)(2,1)}, bf16[32,1024]{1,0:T(8,128)(2,1)}) custom-call(s32[33]{0:T(128)S(1)} %fusion.5.place_ref, bf16[32,2048]{1,0:T(8,128)(2,1)S(1)} %constant_dynamic-update-slice_fusion.refs_0_, bf16[32,2048]{1,0:T(8,128)(2,1)S(1)} %collective-permute-done.3.refs_1_, ...), custom_call_target="tpu_custom_call" | custom-call | flops 536870912 | bytes 4980736 | tf_op jit(solution)/shard_map/project/pallas_call | solution.py:218
  56.3 3.2 %collective-permute-start.12 = (bf16[32,1024]{1,0:T(8,128)(2,1)}, bf16[32,1024]{1,0:T(8,128)(2,1)S(1)}, u32[]{:S(2)}, u32[]{:S(2)}) collective-permute-start(bf16[32,1024]{1,0:T(8,128)(2,1)} %get-tuple-element.36), channel_id=1, source_target_pairs={{0,4},{2,6},{4,0},{6,2},{1,5},{3,7},{5,1},{7,3},{8,12},{10,14},{12... | collective-permute-start | bytes 196616 | tf_op jit(solution)/shard_map/ppermute | solution.py:49
  59.6 2.0 collective-permute-done.13
  61.6 4.1 %collective-permute-done.12 = bf16[32,1024]{1,0:T(8,128)(2,1)S(1)} collective-permute-done((bf16[32,1024]{1,0:T(8,128)(2,1)}, bf16[32,1024]{1,0:T(8,128)(2,1)S(1)}, u32[]{:S(2)}, u32[]{:S(2)}) %collective-permute-start.12) | collective-permute-done | bytes 65568 | tf_op jit(solution)/shard_map/ppermute | solution.py:49
  65.7 1.7 collective-permute-done.11
  67.4 1.5 multiply_convert_fusion
  68.9 1.8 collective-permute-start.17
  71.8 3.5 %collective-permute-start.14 = (bf16[32,1024]{1,0:T(8,128)(2,1)S(1)}, bf16[32,1024]{1,0:T(8,128)(2,1)S(1)}, u32[]{:S(2)}, u32[]{:S(2)}) collective-permute-start(bf16[32,1024]{1,0:T(8,128)(2,1)S(1)} %get-tuple-element.38), channel_id=1, source_target_pairs={{2,0},{4,2},{6,4},{0,6},{3,1},{5,3},{7,5},{1,7},{10,8},{12,10},{14... | collective-permute-start | bytes 196616 | tf_op jit(solution)/shard_map/ppermute | solution.py:45
  75.3 1.8 collective-permute-done.16
  77.0 1.6 collective-permute-done.15
  78.6 2.6 %collective-permute-done.14 = bf16[32,1024]{1,0:T(8,128)(2,1)S(1)} collective-permute-done((bf16[32,1024]{1,0:T(8,128)(2,1)S(1)}, bf16[32,1024]{1,0:T(8,128)(2,1)S(1)}, u32[]{:S(2)}, u32[]{:S(2)}) %collective-permute-start.14) | collective-permute-done | bytes 65568 | tf_op jit(solution)/shard_map/ppermute | solution.py:45
  81.2 3.1 %collective-permute-start.19 = (bf16[128,1024]{1,0:T(8,128)(2,1)S(1)}, bf16[128,1024]{1,0:T(8,128)(2,1)S(1)}, u32[]{:S(2)}, u32[]{:S(2)}) collective-permute-start(bf16[128,1024]{1,0:T(8,128)(2,1)S(1)} %pad_maximum_fusion.refs_0_), channel_id=1, source_target_pairs={{8,0},{16,8},{24,16},{0,24},{9,1},{17,9},{25,17},{1,25},{10,2},{18... | collective-permute-start | bytes 786440 | tf_op jit(solution)/shard_map/ppermute | solution.py:45
  85.0 2.8 %copy-done.10 = bf16[1024,896]{1,0:T(8,128)(2,1)S(1)} copy-done((bf16[1024,896]{1,0:T(8,128)(2,1)S(1)}, bf16[1024,896]{1,0:T(8,128)(2,1)}, u32[]{:S(2)}) %copy-start.10) | copy-done | bytes 1835032
  87.9 1.5 copy-done.12
  89.4 3.5 %gate_up.2 = bf16[128,3712]{1,0:T(8,128)(2,1)} custom-call(f32[1,1024]{1,0:T(1,128)S(1)} %bitcast.20, bf16[128,1024]{1,0:T(8,128)(2,1)S(1)} %pad_maximum_fusion.refs_0_, bf16[1024,896]{1,0:T(8,128)(2,1)S(1)} %copy-done.10, bf16[1024,896]{1,0:T(8,128)(2,1)S(1)} %copy-done.12, bf16[1024,896]{1,0:T(8,128)(2,1)S(1)} %collective-permute-done.17.refs_3_.refs_5_, ...), custom_call_target="tpu_custom_call" | custom-call | flops 17302499328 | bytes 8519680 | tf_op jit(solution)/shard_map/gate_up/pallas_call | solution.py:269
  92.9 3.9 %all-to-all-start.1 = ((bf16[8,16,3712]{2,1,0:T(8,128)(2,1)}), bf16[8,16,3712]{2,1,0:T(8,128)(2,1)S(1)}, u32[]{:S(2)}, u32[]{:S(2)}) async-start(bf16[8,16,3712]{2,1,0:T(8,128)(2,1)} %bitcast.3), calls=%async_computation.1 | async-start | bytes 1900544 | tf_op jit(solution)/shard_map/all_to_all | solution.py:347
  96.8 2.3 %collective-permute-done.21.refs_2_ = bf16[128,1024]{1,0:T(8,128)(2,1)} collective-permute-done((bf16[128,1024]{1,0:T(8,128)(2,1)S(1)}, bf16[128,1024]{1,0:T(8,128)(2,1)}, u32[]{:S(2)}, u32[]{:S(2)}) %collective-permute-start.21) | collective-permute-done | bytes 262176 | tf_op jit(solution)/shard_map/ppermute | solution.py:45
  99.1 1.5 copy-done.11
  103.6 5.3 %gate_up.3 = bf16[384,3712]{1,0:T(8,128)(2,1)S(1)} custom-call(f32[1,1024]{1,0:T(1,128)S(1)} %bitcast.21, bf16[128,1024]{1,0:T(8,128)(2,1)S(1)} %collective-permute-done.19.refs_0_, bf16[128,1024]{1,0:T(8,128)(2,1)} %collective-permute-done.20.refs_1_, bf16[128,1024]{1,0:T(8,128)(2,1)} %collective-permute-done.21.refs_2_, bf16[1024,896]{1,0:T(8,128)(2,1)S(1)} %copy-done.11, ...), custom_call_target="tpu_custom_call" | custom-call | flops 69209997312 | bytes 10878976 | tf_op jit(solution)/shard_map/gate_up/pallas_call | solution.py:269
  109.0 1.5 copy-done
  110.5 37.0 %all_to_all.20.refs_1_ = bf16[8,48,3712]{2,1,0:T(8,128)(2,1)S(1)} all-to-all(bf16[8,48,3712]{2,1,0:T(8,128)(2,1)} %bitcast.18), channel_id=1, replica_groups=mesh['x'=4,'l'=2,'y'=4,'z'=4,'core'=2] {'x','l'}, dimensions={0} | all-to-all | bytes 5701632 | tf_op jit(solution)/shard_map/all_to_all | solution.py:347
  147.5 2.7 %activate.1 = bf16[8,64,1792]{2,1,0:T(8,128)(2,1)} custom-call(bf16[8,16,3712]{2,1,0:T(8,128)(2,1)S(1)} %all-to-all-done.1.refs_0_, bf16[8,48,3712]{2,1,0:T(8,128)(2,1)S(1)} %all_to_all.20.refs_1_), custom_call_target="tpu_custom_call" | custom-call | bytes 5505024 | tf_op jit(solution)/shard_map/activate/pallas_call | solution.py:167
  150.2 3.6 %all-to-all-start.3 = ((bf16[8,64,1792]{2,1,0:T(8,128)(2,1)}), bf16[8,64,1792]{2,1,0:T(8,128)(2,1)S(1)}, u32[]{:S(2)}, u32[]{:S(2)}) async-start(bf16[8,64,1792]{2,1,0:T(8,128)(2,1)} %activate.1), calls=%async_computation.3 | async-start | bytes 3670016 | tf_op jit(solution)/shard_map/all_to_all | solution.py:347
  153.8 3.0 %collective-permute-start.22 = (bf16[896,1024]{1,0:T(8,128)(2,1)}, bf16[896,1024]{1,0:T(8,128)(2,1)}, u32[]{:S(2)}, u32[]{:S(2)}) collective-permute-start(bf16[896,1024]{1,0:T(8,128)(2,1)} %own.1), channel_id=1, source_target_pairs={{0,1},{1,0},{2,3},{3,2},{4,5},{5,4},{6,7},{7,6},{8,9},{9,8},{10,11... | collective-permute-start | bytes 5505032 | tf_op jit(solution)/shard_map/ppermute | solution.py:41
  156.9 3.8 %collective-permute-done.22.other = bf16[896,1024]{1,0:T(8,128)(2,1)} collective-permute-done((bf16[896,1024]{1,0:T(8,128)(2,1)}, bf16[896,1024]{1,0:T(8,128)(2,1)}, u32[]{:S(2)}, u32[]{:S(2)}) %collective-permute-start.22) | collective-permute-done | bytes 1835040 | tf_op jit(solution)/shard_map/ppermute | solution.py:41
  160.6 14.6 %all-to-all-done.3.hidden_ref = bf16[8,64,1792]{2,1,0:T(8,128)(2,1)S(1)} async-done(((bf16[8,64,1792]{2,1,0:T(8,128)(2,1)}), bf16[8,64,1792]{2,1,0:T(8,128)(2,1)S(1)}, u32[]{:S(2)}, u32[]{:S(2)}) %all-to-all-start.3) | async-done | bytes 1835040 | tf_op jit(solution)/shard_map/all_to_all | solution.py:347
  176.5 6.7 %down.1 = (bf16[128,1024]{1,0:T(8,128)(2,1)}, bf16[128,1024]{1,0:T(8,128)(2,1)}, bf16[128,1024]{1,0:T(8,128)(2,1)}, bf16[128,1024]{1,0:T(8,128)(2,1)}) custom-call(s32[33]{0:T(128)} %copy-done.9, bf16[8,64,1792]{2,1,0:T(8,128)(2,1)} %copy-done.18, bf16[896,1024]{1,0:T(8,128)(2,1)} %own.1, bf16[896,1024]{1,0:T(8,128)(2,1)} %collective-permute-done.22.other, ...), custom_call_target="tpu_custom_call" | custom-call | flops 1879048192 | bytes 6553600 | tf_op jit(solution)/shard_map/down/pallas_call | solution.py:322
  185.2 3.4 %collective-permute-done.25 = bf16[128,1024]{1,0:T(8,128)(2,1)S(1)} collective-permute-done((bf16[128,1024]{1,0:T(8,128)(2,1)}, bf16[128,1024]{1,0:T(8,128)(2,1)S(1)}, u32[]{:S(2)}, u32[]{:S(2)}) %collective-permute-start.25) | collective-permute-done | bytes 262176 | tf_op jit(solution)/shard_map/ppermute | solution.py:49
  188.6 2.5 %collective-permute-done.24 = bf16[128,1024]{1,0:T(8,128)(2,1)S(1)} collective-permute-done((bf16[128,1024]{1,0:T(8,128)(2,1)}, bf16[128,1024]{1,0:T(8,128)(2,1)S(1)}, u32[]{:S(2)}, u32[]{:S(2)}) %collective-permute-start.24) | collective-permute-done | bytes 262176 | tf_op jit(solution)/shard_map/ppermute | solution.py:49
  191.1 3.7 %collective-permute-done.23 = bf16[128,1024]{1,0:T(8,128)(2,1)S(1)} collective-permute-done((bf16[128,1024]{1,0:T(8,128)(2,1)}, bf16[128,1024]{1,0:T(8,128)(2,1)S(1)}, u32[]{:S(2)}, u32[]{:S(2)}) %collective-permute-start.23) | collective-permute-done | bytes 262176 | tf_op jit(solution)/shard_map/ppermute | solution.py:49
  197.4 1.6 collective-permute-start.26
  199.0 2.3 %collective-permute-done.28 = bf16[32,1024]{1,0:T(8,128)(2,1)S(1)} collective-permute-done((bf16[32,1024]{1,0:T(8,128)(2,1)S(1)}, bf16[32,1024]{1,0:T(8,128)(2,1)S(1)}, u32[]{:S(2)}, u32[]{:S(2)}) %collective-permute-start.28) | collective-permute-done | bytes 65568 | tf_op jit(solution)/shard_map/ppermute | solution.py:49
  201.3 2.2 %collective-permute-done.27 = bf16[32,1024]{1,0:T(8,128)(2,1)S(1)} collective-permute-done((bf16[32,1024]{1,0:T(8,128)(2,1)S(1)}, bf16[32,1024]{1,0:T(8,128)(2,1)S(1)}, u32[]{:S(2)}, u32[]{:S(2)}) %collective-permute-start.27) | collective-permute-done | bytes 65568 | tf_op jit(solution)/shard_map/ppermute | solution.py:49
  203.5 1.7 collective-permute-done.26
  205.3 6.6 %collective-permute-start.29 = (bf16[16,1024]{1,0:T(8,128)(2,1)S(1)}, bf16[16,1024]{1,0:T(8,128)(2,1)S(1)}, u32[]{:S(2)}, u32[]{:S(2)}) collective-permute-start(bf16[16,1024]{1,0:T(8,128)(2,1)S(1)} %broadcast_select_fusion.2), channel_id=1, source_target_pairs={{0,1},{1,0},{2,3},{3,2},{4,5},{5,4},{6,7},{7,6},{8,9},{9,8},{10,11... | collective-permute-start | bytes 98312 | tf_op jit(solution)/shard_map/ppermute | solution.py:41
  (93 shorter events, 23.6 us)
Async XLA Ops:
  0.0 27.0 %collective-permute-start = (bf16[256,1024]{1,0:T(8,128)(2,1)}, bf16[256,1024]{1,0:T(8,128)(2,1)S(1)}, u32[]{:S(2)}, u32[]{:S(2)}) collective-permute-start(bf16[256,1024]{1,0:T(8,128)(2,1)} %refs_4_.2), channel_id=1, source_target_pairs={{8,0},{16,8},{24,16},{0,24},{9,1},{17,9},{25,17},{1,25},{10,2},{18... | collective-permute-start | bytes 1572872 | tf_op jit(solution)/shard_map/ppermute | solution.py:45
  3.6 23.5 %collective-permute-start.1 = (bf16[256,1024]{1,0:T(8,128)(2,1)}, bf16[256,1024]{1,0:T(8,128)(2,1)S(1)}, u32[]{:S(2)}, u32[]{:S(2)}) collective-permute-start(bf16[256,1024]{1,0:T(8,128)(2,1)} %refs_4_.2), channel_id=1, source_target_pairs={{24,0},{0,8},{8,16},{16,24},{25,1},{1,9},{9,17},{17,25},{26,2},{2,... | collective-permute-start | bytes 1572872 | tf_op jit(solution)/shard_map/ppermute | solution.py:45
  5.1 1.6 copy-start.1
  6.7 1.6 copy-start.2
  9.0 11.0 %copy-start.3 = (bf16[256,1024]{1,0:T(8,128)(2,1)S(1)}, bf16[256,1024]{1,0:T(8,128)(2,1)}, u32[]{:S(2)}) copy-start(bf16[256,1024]{1,0:T(8,128)(2,1)} %refs_4_.2) | copy-start | bytes 1572868
  11.8 15.2 %all-to-all-start = ((bf16[4,4,2048]{2,1,0:T(4,128)(2,1)}), bf16[4,4,2048]{2,1,0:T(4,128)(2,1)S(1)}, u32[]{:S(2)}, u32[]{:S(2)}) async-start(bf16[4,4,2048]{2,1,0:T(4,128)(2,1)} %reshape.46), calls=%async_computation | async-start | bytes 131072 | tf_op jit(solution)/shard_map/all_to_all | solution.py:347
  19.9 18.3 %collective-permute-start.6 = (bf16[256,1024]{1,0:T(8,128)(2,1)S(1)}, bf16[256,1024]{1,0:T(8,128)(2,1)S(1)}, u32[]{:S(2)}, u32[]{:S(2)}) collective-permute-start(bf16[256,1024]{1,0:T(8,128)(2,1)S(1)} %copy-done.3), channel_id=1, source_target_pairs={{16,0},{24,8},{0,16},{8,24},{17,1},{25,9},{1,17},{9,25},{18,2},{26... | collective-permute-start | bytes 1572872 | tf_op jit(solution)/shard_map/ppermute | solution.py:45
  27.0 3.5 %collective-permute-start.2 = (bf16[16,2048]{1,0:T(8,128)(2,1)S(1)}, bf16[16,2048]{1,0:T(8,128)(2,1)S(1)}, u32[]{:S(2)}, u32[]{:S(2)}) collective-permute-start(bf16[16,2048]{1,0:T(8,128)(2,1)S(1)} %reshape.47), channel_id=1, source_target_pairs={{0,32},{32,0},{1,33},{33,1},{2,34},{34,2},{3,35},{35,3},{4,36},{36... | collective-permute-start | bytes 196616 | tf_op jit(solution)/shard_map/ppermute | solution.py:41
  30.5 7.7 %collective-permute-start.3 = (bf16[32,2048]{1,0:T(8,128)(2,1)S(1)}, bf16[32,2048]{1,0:T(8,128)(2,1)S(1)}, u32[]{:S(2)}, u32[]{:S(2)}) collective-permute-start(bf16[32,2048]{1,0:T(8,128)(2,1)S(1)} %constant_dynamic-update-slice_fusion.refs_0_), channel_id=1, source_target_pairs={{64,0},{128,64},{192,128},{0,192},{65,1},{129,65},{193,129},{1,193... | collective-permute-start | bytes 393224 | tf_op jit(solution)/shard_map/ppermute | solution.py:45
  33.0 7.4 %collective-permute-start.4 = (bf16[32,2048]{1,0:T(8,128)(2,1)S(1)}, bf16[32,2048]{1,0:T(8,128)(2,1)S(1)}, u32[]{:S(2)}, u32[]{:S(2)}) collective-permute-start(bf16[32,2048]{1,0:T(8,128)(2,1)S(1)} %constant_dynamic-update-slice_fusion.refs_0_), channel_id=1, source_target_pairs={{128,0},{192,64},{0,128},{64,192},{129,1},{193,65},{1,129},{65,193... | collective-permute-start | bytes 393224 | tf_op jit(solution)/shard_map/ppermute | solution.py:45
  33.5 6.9 %collective-permute-start.5 = (bf16[32,2048]{1,0:T(8,128)(2,1)S(1)}, bf16[32,2048]{1,0:T(8,128)(2,1)S(1)}, u32[]{:S(2)}, u32[]{:S(2)}) collective-permute-start(bf16[32,2048]{1,0:T(8,128)(2,1)S(1)} %constant_dynamic-update-slice_fusion.refs_0_), channel_id=1, source_target_pairs={{192,0},{0,64},{64,128},{128,192},{193,1},{1,65},{65,129},{129,193... | collective-permute-start | bytes 393224 | tf_op jit(solution)/shard_map/ppermute | solution.py:45
  34.1 16.2 %collective-permute-start.7 = (bf16[256,1024]{1,0:T(8,128)(2,1)S(1)}, bf16[256,1024]{1,0:T(8,128)(2,1)S(1)}, u32[]{:S(2)}, u32[]{:S(2)}) collective-permute-start(bf16[256,1024]{1,0:T(8,128)(2,1)S(1)} %copy-done.3), channel_id=1, source_target_pairs={{0,1},{1,0},{2,3},{3,2},{4,5},{5,4},{6,7},{7,6},{8,9},{9,8},{10,11... | collective-permute-start | bytes 1572872 | tf_op jit(solution)/shard_map/ppermute | solution.py:41
  38.2 12.1 %collective-permute-start.8 = (bf16[256,1024]{1,0:T(8,128)(2,1)S(1)}, bf16[256,1024]{1,0:T(8,128)(2,1)S(1)}, u32[]{:S(2)}, u32[]{:S(2)}) collective-permute-start(bf16[256,1024]{1,0:T(8,128)(2,1)S(1)} %collective-permute-done.refs_5_), channel_id=1, source_target_pairs={{0,1},{1,0},{2,3},{3,2},{4,5},{5,4},{6,7},{7,6},{8,9},{9,8},{10,11... | collective-permute-start | bytes 1572872 | tf_op jit(solution)/shard_map/ppermute | solution.py:41
  38.2 12.1 %collective-permute-start.10 = (bf16[256,1024]{1,0:T(8,128)(2,1)S(1)}, bf16[256,1024]{1,0:T(8,128)(2,1)}, u32[]{:S(2)}, u32[]{:S(2)}) collective-permute-start(bf16[256,1024]{1,0:T(8,128)(2,1)S(1)} %collective-permute-done.1.refs_7_), channel_id=1, source_target_pairs={{0,1},{1,0},{2,3},{3,2},{4,5},{5,4},{6,7},{7,6},{8,9},{9,8},{10,11... | collective-permute-start | bytes 1572872 | tf_op jit(solution)/shard_map/ppermute | solution.py:41
  41.1 9.2 %collective-permute-start.9 = (bf16[256,1024]{1,0:T(8,128)(2,1)S(1)}, bf16[256,1024]{1,0:T(8,128)(2,1)}, u32[]{:S(2)}, u32[]{:S(2)}) collective-permute-start(bf16[256,1024]{1,0:T(8,128)(2,1)S(1)} %collective-permute-done.6.refs_6_), channel_id=1, source_target_pairs={{0,1},{1,0},{2,3},{3,2},{4,5},{5,4},{6,7},{7,6},{8,9},{9,8},{10,11... | collective-permute-start | bytes 1572872 | tf_op jit(solution)/shard_map/ppermute | solution.py:41
  49.6 17.8 %copy-start.7 = (f32[1024]{0:T(1024)S(1)}, f32[1024]{0:T(1024)}, u32[]{:S(2)}) copy-start(f32[1024]{0:T(1024)} %param.21) | copy-start | bytes 12292
  50.3 5.1 %copy-start.9 = (s32[33]{0:T(128)}, s32[33]{0:T(128)S(1)}, u32[]{:S(2)}) copy-start(s32[33]{0:T(128)S(1)} %fusion.5.place_ref) | copy-start | bytes 400
  51.2 8.3 %copy-start.19 = (bf16[1,4,2,4,1024]{4,3,2,1,0:T(4,128)(2,1)S(1)}, bf16[1,4,2,4,1024]{4,3,2,1,0:T(4,128)(2,1)}, u32[]{:S(2)}) copy-start(bf16[1,4,2,4,1024]{4,3,2,1,0:T(4,128)(2,1)} %stack.18) | copy-start | bytes 196612
  51.2 8.3 %copy-start.20 = (bf16[1,4,2,4,1024]{4,3,2,1,0:T(4,128)(2,1)S(1)}, bf16[1,4,2,4,1024]{4,3,2,1,0:T(4,128)(2,1)}, u32[]{:S(2)}) copy-start(bf16[1,4,2,4,1024]{4,3,2,1,0:T(4,128)(2,1)} %stack.19) | copy-start | bytes 196612
  56.1 5.5 %collective-permute-start.13 = (bf16[32,1024]{1,0:T(8,128)(2,1)}, bf16[32,1024]{1,0:T(8,128)(2,1)S(1)}, u32[]{:S(2)}, u32[]{:S(2)}) collective-permute-start(bf16[32,1024]{1,0:T(8,128)(2,1)} %get-tuple-element.37), channel_id=1, source_target_pairs={{0,6},{2,0},{4,2},{6,4},{1,7},{3,1},{5,3},{7,5},{8,14},{10,8},{12,... | collective-permute-start | bytes 196616 | tf_op jit(solution)/shard_map/ppermute | solution.py:49
  56.3 9.4 %collective-permute-start.12 = (bf16[32,1024]{1,0:T(8,128)(2,1)}, bf16[32,1024]{1,0:T(8,128)(2,1)S(1)}, u32[]{:S(2)}, u32[]{:S(2)}) collective-permute-start(bf16[32,1024]{1,0:T(8,128)(2,1)} %get-tuple-element.36), channel_id=1, source_target_pairs={{0,4},{2,6},{4,0},{6,2},{1,5},{3,7},{5,1},{7,3},{8,12},{10,14},{12... | collective-permute-start | bytes 196616 | tf_op jit(solution)/shard_map/ppermute | solution.py:49
  59.5 7.9 %collective-permute-start.11 = (bf16[32,1024]{1,0:T(8,128)(2,1)}, bf16[32,1024]{1,0:T(8,128)(2,1)S(1)}, u32[]{:S(2)}, u32[]{:S(2)}) collective-permute-start(bf16[32,1024]{1,0:T(8,128)(2,1)} %get-tuple-element.35), channel_id=1, source_target_pairs={{0,2},{2,4},{4,6},{6,0},{1,3},{3,5},{5,7},{7,1},{8,10},{10,12},{12... | collective-permute-start | bytes 196616 | tf_op jit(solution)/shard_map/ppermute | solution.py:49
  68.9 16.1 %collective-permute-start.17 = (bf16[1024,896]{1,0:T(8,128)(2,1)}, bf16[1024,896]{1,0:T(8,128)(2,1)S(1)}, u32[]{:S(2)}, u32[]{:S(2)}) collective-permute-start(bf16[1024,896]{1,0:T(8,128)(2,1)} %refs_3_.1), channel_id=1, source_target_pairs={{0,1},{1,0},{2,3},{3,2},{4,5},{5,4},{6,7},{7,6},{8,9},{9,8},{10,11... | collective-permute-start | bytes 5505032 | tf_op jit(solution)/shard_map/ppermute | solution.py:41
  70.7 14.3 %collective-permute-start.18 = (bf16[1024,896]{1,0:T(8,128)(2,1)}, bf16[1024,896]{1,0:T(8,128)(2,1)S(1)}, u32[]{:S(2)}, u32[]{:S(2)}) collective-permute-start(bf16[1024,896]{1,0:T(8,128)(2,1)} %refs_4_.3), channel_id=1, source_target_pairs={{0,1},{1,0},{2,3},{3,2},{4,5},{5,4},{6,7},{7,6},{8,9},{9,8},{10,11... | collective-permute-start | bytes 5505032 | tf_op jit(solution)/shard_map/ppermute | solution.py:41
  70.7 6.3 %collective-permute-start.16 = (bf16[32,1024]{1,0:T(8,128)(2,1)S(1)}, bf16[32,1024]{1,0:T(8,128)(2,1)S(1)}, u32[]{:S(2)}, u32[]{:S(2)}) collective-permute-start(bf16[32,1024]{1,0:T(8,128)(2,1)S(1)} %get-tuple-element.38), channel_id=1, source_target_pairs={{6,0},{0,2},{2,4},{4,6},{7,1},{1,3},{3,5},{5,7},{14,8},{8,10},{10,... | collective-permute-start | bytes 196616 | tf_op jit(solution)/shard_map/ppermute | solution.py:45
  70.7 7.9 %collective-permute-start.15 = (bf16[32,1024]{1,0:T(8,128)(2,1)S(1)}, bf16[32,1024]{1,0:T(8,128)(2,1)S(1)}, u32[]{:S(2)}, u32[]{:S(2)}) collective-permute-start(bf16[32,1024]{1,0:T(8,128)(2,1)S(1)} %get-tuple-element.38), channel_id=1, source_target_pairs={{4,0},{6,2},{0,4},{2,6},{5,1},{7,3},{1,5},{3,7},{12,8},{14,10},{8,... | collective-permute-start | bytes 196616 | tf_op jit(solution)/shard_map/ppermute | solution.py:45
  71.8 9.5 %collective-permute-start.14 = (bf16[32,1024]{1,0:T(8,128)(2,1)S(1)}, bf16[32,1024]{1,0:T(8,128)(2,1)S(1)}, u32[]{:S(2)}, u32[]{:S(2)}) collective-permute-start(bf16[32,1024]{1,0:T(8,128)(2,1)S(1)} %get-tuple-element.38), channel_id=1, source_target_pairs={{2,0},{4,2},{6,4},{0,6},{3,1},{5,3},{7,5},{1,7},{10,8},{12,10},{14... | collective-permute-start | bytes 196616 | tf_op jit(solution)/shard_map/ppermute | solution.py:45
  81.2 15.6 %collective-permute-start.19 = (bf16[128,1024]{1,0:T(8,128)(2,1)S(1)}, bf16[128,1024]{1,0:T(8,128)(2,1)S(1)}, u32[]{:S(2)}, u32[]{:S(2)}) collective-permute-start(bf16[128,1024]{1,0:T(8,128)(2,1)S(1)} %pad_maximum_fusion.refs_0_), channel_id=1, source_target_pairs={{8,0},{16,8},{24,16},{0,24},{9,1},{17,9},{25,17},{1,25},{10,2},{18... | collective-permute-start | bytes 786440 | tf_op jit(solution)/shard_map/ppermute | solution.py:45
  84.3 12.5 %collective-permute-start.20 = (bf16[128,1024]{1,0:T(8,128)(2,1)S(1)}, bf16[128,1024]{1,0:T(8,128)(2,1)}, u32[]{:S(2)}, u32[]{:S(2)}) collective-permute-start(bf16[128,1024]{1,0:T(8,128)(2,1)S(1)} %pad_maximum_fusion.refs_0_), channel_id=1, source_target_pairs={{16,0},{24,8},{0,16},{8,24},{17,1},{25,9},{1,17},{9,25},{18,2},{26... | collective-permute-start | bytes 786440 | tf_op jit(solution)/shard_map/ppermute | solution.py:45
  84.3 14.8 %collective-permute-start.21 = (bf16[128,1024]{1,0:T(8,128)(2,1)S(1)}, bf16[128,1024]{1,0:T(8,128)(2,1)}, u32[]{:S(2)}, u32[]{:S(2)}) collective-permute-start(bf16[128,1024]{1,0:T(8,128)(2,1)S(1)} %pad_maximum_fusion.refs_0_), channel_id=1, source_target_pairs={{24,0},{0,8},{8,16},{16,24},{25,1},{1,9},{9,17},{17,25},{26,2},{2,... | collective-permute-start | bytes 786440 | tf_op jit(solution)/shard_map/ppermute | solution.py:45
  85.0 7.9 %copy-start.14 = (bf16[1024,896]{1,0:T(8,128)(2,1)}, bf16[1024,896]{1,0:T(8,128)(2,1)S(1)}, u32[]{:S(2)}) copy-start(bf16[1024,896]{1,0:T(8,128)(2,1)S(1)} %collective-permute-done.17.refs_3_.refs_5_) | copy-start | bytes 5505028
  85.0 7.9 %copy-start.16 = (bf16[1024,896]{1,0:T(8,128)(2,1)}, bf16[1024,896]{1,0:T(8,128)(2,1)S(1)}, u32[]{:S(2)}) copy-start(bf16[1024,896]{1,0:T(8,128)(2,1)S(1)} %collective-permute-done.18.refs_4_.refs_6_) | copy-start | bytes 5505028
  85.0 2.8 %copy-start.10 = (bf16[1024,896]{1,0:T(8,128)(2,1)S(1)}, bf16[1024,896]{1,0:T(8,128)(2,1)}, u32[]{:S(2)}) copy-start(bf16[1024,896]{1,0:T(8,128)(2,1)} %refs_3_.1) | copy-start | bytes 5505028
  87.9 1.5 copy-start.12
  92.9 6.3 %copy-start.15 = (bf16[1024,896]{1,0:T(8,128)(2,1)S(1)}, bf16[1024,896]{1,0:T(8,128)(2,1)}, u32[]{:S(2)}) copy-start(bf16[1024,896]{1,0:T(8,128)(2,1)} %copy-done.14) | copy-start | bytes 5505028
  92.9 17.6 %all-to-all-start.1 = ((bf16[8,16,3712]{2,1,0:T(8,128)(2,1)}), bf16[8,16,3712]{2,1,0:T(8,128)(2,1)S(1)}, u32[]{:S(2)}, u32[]{:S(2)}) async-start(bf16[8,16,3712]{2,1,0:T(8,128)(2,1)} %bitcast.3), calls=%async_computation.1 | async-start | bytes 1900544 | tf_op jit(solution)/shard_map/all_to_all | solution.py:347
  99.1 1.5 copy-start.11
  100.6 1.5 copy-start.13
  109.0 1.6 copy-start
  150.2 25.0 %all-to-all-start.3 = ((bf16[8,64,1792]{2,1,0:T(8,128)(2,1)}), bf16[8,64,1792]{2,1,0:T(8,128)(2,1)S(1)}, u32[]{:S(2)}, u32[]{:S(2)}) async-start(bf16[8,64,1792]{2,1,0:T(8,128)(2,1)} %activate.1), calls=%async_computation.3 | async-start | bytes 3670016 | tf_op jit(solution)/shard_map/all_to_all | solution.py:347
  153.8 6.8 %collective-permute-start.22 = (bf16[896,1024]{1,0:T(8,128)(2,1)}, bf16[896,1024]{1,0:T(8,128)(2,1)}, u32[]{:S(2)}, u32[]{:S(2)}) collective-permute-start(bf16[896,1024]{1,0:T(8,128)(2,1)} %own.1), channel_id=1, source_target_pairs={{0,1},{1,0},{2,3},{3,2},{4,5},{5,4},{6,7},{7,6},{8,9},{9,8},{10,11... | collective-permute-start | bytes 5505032 | tf_op jit(solution)/shard_map/ppermute | solution.py:41
  183.1 5.5 %collective-permute-start.25 = (bf16[128,1024]{1,0:T(8,128)(2,1)}, bf16[128,1024]{1,0:T(8,128)(2,1)S(1)}, u32[]{:S(2)}, u32[]{:S(2)}) collective-permute-start(bf16[128,1024]{1,0:T(8,128)(2,1)} %get-tuple-element.46), channel_id=1, source_target_pairs={{0,24},{8,0},{16,8},{24,16},{1,25},{9,1},{17,9},{25,17},{2,26},{10... | collective-permute-start | bytes 786440 | tf_op jit(solution)/shard_map/ppermute | solution.py:49
  184.1 7.0 %collective-permute-start.24 = (bf16[128,1024]{1,0:T(8,128)(2,1)}, bf16[128,1024]{1,0:T(8,128)(2,1)S(1)}, u32[]{:S(2)}, u32[]{:S(2)}) collective-permute-start(bf16[128,1024]{1,0:T(8,128)(2,1)} %get-tuple-element.45), channel_id=1, source_target_pairs={{0,16},{8,24},{16,0},{24,8},{1,17},{9,25},{17,1},{25,9},{2,18},{10... | collective-permute-start | bytes 786440 | tf_op jit(solution)/shard_map/ppermute | solution.py:49
  185.1 9.6 %collective-permute-start.23 = (bf16[128,1024]{1,0:T(8,128)(2,1)}, bf16[128,1024]{1,0:T(8,128)(2,1)S(1)}, u32[]{:S(2)}, u32[]{:S(2)}) collective-permute-start(bf16[128,1024]{1,0:T(8,128)(2,1)} %get-tuple-element.44), channel_id=1, source_target_pairs={{0,8},{8,16},{16,24},{24,0},{1,9},{9,17},{17,25},{25,1},{2,10},{10... | collective-permute-start | bytes 786440 | tf_op jit(solution)/shard_map/ppermute | solution.py:49
  195.9 5.4 %collective-permute-start.28 = (bf16[32,1024]{1,0:T(8,128)(2,1)S(1)}, bf16[32,1024]{1,0:T(8,128)(2,1)S(1)}, u32[]{:S(2)}, u32[]{:S(2)}) collective-permute-start(bf16[32,1024]{1,0:T(8,128)(2,1)S(1)} %get-tuple-element.54), channel_id=1, source_target_pairs={{0,6},{2,0},{4,2},{6,4},{1,7},{3,1},{5,3},{7,5},{8,14},{10,8},{12,... | collective-permute-start | bytes 196616 | tf_op jit(solution)/shard_map/ppermute | solution.py:49
  196.0 7.5 %collective-permute-start.27 = (bf16[32,1024]{1,0:T(8,128)(2,1)S(1)}, bf16[32,1024]{1,0:T(8,128)(2,1)S(1)}, u32[]{:S(2)}, u32[]{:S(2)}) collective-permute-start(bf16[32,1024]{1,0:T(8,128)(2,1)S(1)} %get-tuple-element.55), channel_id=1, source_target_pairs={{0,4},{2,6},{4,0},{6,2},{1,5},{3,7},{5,1},{7,3},{8,12},{10,14},{12... | collective-permute-start | bytes 196616 | tf_op jit(solution)/shard_map/ppermute | solution.py:49
  197.4 7.9 %collective-permute-start.26 = (bf16[32,1024]{1,0:T(8,128)(2,1)S(1)}, bf16[32,1024]{1,0:T(8,128)(2,1)S(1)}, u32[]{:S(2)}, u32[]{:S(2)}) collective-permute-start(bf16[32,1024]{1,0:T(8,128)(2,1)S(1)} %get-tuple-element.53), channel_id=1, source_target_pairs={{0,2},{2,4},{4,6},{6,0},{1,3},{3,5},{5,7},{7,1},{8,10},{10,12},{12... | collective-permute-start | bytes 196616 | tf_op jit(solution)/shard_map/ppermute | solution.py:49
  205.3 7.5 %collective-permute-start.29 = (bf16[16,1024]{1,0:T(8,128)(2,1)S(1)}, bf16[16,1024]{1,0:T(8,128)(2,1)S(1)}, u32[]{:S(2)}, u32[]{:S(2)}) collective-permute-start(bf16[16,1024]{1,0:T(8,128)(2,1)S(1)} %broadcast_select_fusion.2), channel_id=1, source_target_pairs={{0,1},{1,0},{2,3},{3,2},{4,5},{5,4},{6,7},{7,6},{8,9},{9,8},{10,11... | collective-permute-start | bytes 98312 | tf_op jit(solution)/shard_map/ppermute | solution.py:41
  (6 other events, 5.6 us)

commit v7 on v6

--- a/solution.py
+++ b/solution.py
@@ -23,7 +23,7 @@
 
 
 def places():
-    table = np.zeros((256, 33), np.int32)
+    table = np.zeros((256, 29), np.int32)
     for device in range(256):
         x, l, y, z, core = device >> 6, (device >> 5) & 1, (device >> 3) & 3, (device >> 1) & 3, device & 1
         owners = [(z + t) % 4 for t in range(4)]
@@ -33,7 +33,6 @@
         table[device, 13:17] = [(y + t - z) % 4 for t in range(4)]
         table[device, 17:25] = [(2 * (owner % 2) + source - y) % 4 for owner in owners for source in range(2)]
         table[device, 25:29] = [owner // 2 for owner in owners]
-        table[device, 29:] = owners
     return table
 
 
@@ -71,9 +70,16 @@
         copy.wait()
 
 
-def attend_kernel(lengths_ref, queries_ref, new_key_ref, new_value_ref, keys, values, out_ref):
+def attend_kernel(lengths_ref, queries_ref, new_key_ref, new_value_ref, key_ref, value_ref, out_ref, keys, values, sems):
     rows, slot_count = keys.shape[:2]
     group = HQ // KVH
+    copies = start_all(
+        [
+            pltpu.make_async_copy(source.at[r], held.at[r], sems.at[i, r])
+            for r in range(rows)
+            for i, (source, held) in enumerate(((key_ref, keys), (value_ref, values)))
+        ]
+    )
     scale_factor = 1.0 / jnp.sqrt(jnp.float32(HD))
     slot = lax.broadcasted_iota(jnp.int32, (HQ, slot_count), 1)
     for r in range(rows):
@@ -83,6 +89,7 @@
             return spread.reshape(HQ, HD)
 
         query = queries_ref[r]
+        copies[2 * r].wait()
         scores = [
             lax.dot_general(
                 query[k * group : (k + 1) * group],
@@ -100,6 +107,7 @@
         weight_new = jnp.exp(score_new - top_score)
         total = jnp.sum(weights, axis=1, keepdims=True) + weight_new
         weights = weights.astype(jnp.bfloat16)
+        copies[2 * r + 1].wait()
         summed = [
             jnp.dot(
                 weights[k * group : (k + 1) * group],
@@ -117,11 +125,16 @@
     rows, slot_count, width = cache_key.shape
     return pl.pallas_call(
         attend_kernel,
-        in_specs=[SMEM] + [VMEM] * 5,
+        in_specs=[SMEM] + [BLOCK] * 3 + [ANY] * 2,
         out_specs=BLOCK,
         out_shape=jax.ShapeDtypeStruct((rows, HQ, HD), jnp.bfloat16),
+        scratch_shapes=[
+            pltpu.VMEM((rows, slot_count, width), jnp.bfloat16),
+            pltpu.VMEM((rows, slot_count, width), jnp.bfloat16),
+            pltpu.SemaphoreType.DMA((2, rows)),
+        ],
         name="attend",
-        **params(12, 4 * rows * slot_count * HQ * HD, 4 * rows * slot_count * width),
+        **params(60, 4 * rows * slot_count * HQ * HD, 4 * rows * slot_count * width),
     )(
         lengths,
         queries.reshape(rows, HQ, HD),
@@ -178,7 +191,7 @@
 
 def project_kernel(place_ref, *refs):
     pieces, own, other = refs[:4], refs[4:8], refs[8:12]
-    outs, (rows_ref, held_ref, total_ref, row_sems, held_sems) = refs[12:16], refs[16:]
+    out_ref, rows_ref, held_ref, row_sems, held_sems = refs[12:]
     step = pieces[0].shape[0] // 2
     row_copies = start_all(
         [
@@ -197,19 +210,23 @@
         for b in range(2):
             source = own[t] if b == 0 else other[t]
             start = (2 * place_ref[8 + t] + (place_ref[12] if b == 0 else 1 - place_ref[12])) * depth
-            held = held_ref.at[pl.ds(pl.multiple_of(start, depth), depth), :]
-            held_copies.append(pltpu.make_async_copy(source, held, held_sems.at[2 * t + b]))
-    start_all(held_copies)
+            held_rows = pl.ds(pl.multiple_of(start, depth), depth)
+            for i, (n, size) in enumerate(steps(width)):
+                cols = pl.ds(n, size)
+                held_copies.append(
+                    pltpu.make_async_copy(
+                        source.at[:, cols], held_ref.at[held_rows, cols], held_sems.at[i, 2 * t + b]
+                    )
+                )
+    blocks = len(steps(width))
+    for i in range(blocks):
+        start_all(held_copies[i::blocks])
     wait_all(row_copies)
-    wait_all(held_copies)
-    for n, size in steps(width):
-        total_ref[:, n : n + size] = jnp.dot(
+    for i, (n, size) in enumerate(steps(width)):
+        wait_all(held_copies[i::blocks])
+        out_ref[:, n : n + size] = jnp.dot(
             rows_ref[...], held_ref[:, n : n + size], preferred_element_type=jnp.float32
-        )
-    share = outs[0].shape[0]
-    for t in range(4):
-        start = pl.multiple_of(place_ref[29 + t] * share, share)
-        outs[t][...] = total_ref[pl.ds(start, share), :].astype(outs[t].dtype)
+        ).astype(out_ref.dtype)
 
 
 def project(place, pieces, own, other):
@@ -218,14 +235,13 @@
     return pl.pallas_call(
         project_kernel,
         in_specs=[SMEM] + [ANY] * 12,
-        out_specs=[VMEM] * 4,
-        out_shape=[jax.ShapeDtypeStruct((count // 4, width), jnp.bfloat16)] * 4,
+        out_specs=VMEM,
+        out_shape=jax.ShapeDtypeStruct((count, width), jnp.bfloat16),
         scratch_shapes=[
             pltpu.VMEM((count, depth), jnp.bfloat16),
             pltpu.VMEM((depth, width), jnp.bfloat16),
-            pltpu.VMEM((count, width), jnp.float32),
             pltpu.SemaphoreType.DMA((8,)),
-            pltpu.SemaphoreType.DMA((8,)),
+            pltpu.SemaphoreType.DMA((len(steps(width)), 8)),
         ],
         name="project",
         **params(12, 2 * count * depth * width, 2 * (depth * width + count * (depth + width))),
@@ -289,7 +305,12 @@
     row_copy.start()
     held_copies = start_all(
         [
-            pltpu.make_async_copy(weight, held_ref.at[pl.ds(i * depth, depth), :], held_sems.at[i])
+            pltpu.make_async_copy(
+                weight.at[:, pl.ds(n, size)],
+                held_ref.at[pl.ds(i * depth, depth), pl.ds(n, size)],
+                held_sems.at[j, i],
+            )
+            for j, (n, size) in enumerate(steps(width))
             for i, weight in enumerate((own, other))
         ]
     )
@@ -298,8 +319,8 @@
     first = hidden_ref.shape[1] // 4
     near = rows_ref[:, :first].reshape(4 * share, 2 * depth)
     far = rows_ref[:, first:].reshape(12 * share, 2 * depth)
-    wait_all(held_copies)
-    for n, size in steps(width):
+    for j, (n, size) in enumerate(steps(width)):
+        wait_all(held_copies[2 * j : 2 * j + 2])
         columns = held_ref[:, n : n + size]
         product = jnp.dot(near, columns, preferred_element_type=jnp.float32)
         total_ref[:4, :, n : n + size] = product.reshape(4, share, size)
@@ -329,7 +350,7 @@
             pltpu.VMEM((2 * depth, width), jnp.bfloat16),
             pltpu.VMEM((16, count // 16, width), jnp.float32),
             pltpu.SemaphoreType.DMA((1,)),
-            pltpu.SemaphoreType.DMA((2,)),
+            pltpu.SemaphoreType.DMA((len(steps(width)), 2)),
         ],
         name="down",
         **params(60, 4 * count * depth * width, 2 * (2 * count * depth + 2 * depth * width + count * width)),
@@ -345,6 +366,12 @@
 
 def exchange(pieces, axis):
     return lax.all_to_all(pieces, axis, split_axis=0, concat_axis=0, tiled=True)
+
+
+def scatter_sum(partial, axis):
+    parts = lax.axis_size(axis)
+    pieces = partial.reshape(parts, partial.shape[0] // parts, partial.shape[1])
+    return jnp.sum(exchange(pieces, axis).astype(jnp.float32), axis=0)
 
 
 def body(
@@ -376,16 +403,17 @@
     pieces = [block] + [ring_from(block, "x", t) for t in (1, 2, 3)]
     *pieces, out_own[2] = lax.optimization_barrier((*pieces, out_own[2]))
     partial = project(place, pieces, out_own, [out_other, out_next, swap(out_own[2], "core"), out_last])
+    partial, *late = lax.optimization_barrier((partial, w_gate, w_up))
+    gate_other, up_other = [swap(w, "core") for w in late]
 
     share = hidden_in.shape[0] // 32
     y, z, core = (device >> 3) & 3, (device >> 1) & 3, device & 1
     start = 256 * z + 32 * y
     own_in = jnp.stack([lax.dynamic_slice_in_dim(hidden_in, start + 128 * l, share, 0) for l in range(2)])
     own_in = lax.dynamic_index_in_dim(own_in.reshape(2, 4, 2, count, -1), core, 2, keepdims=False).reshape(share, -1)
-    mixed = own_in.astype(jnp.float32) + add_up([partial[0]] + [ring_to(partial[t], "z", t) for t in (1, 2, 3)])
+    mixed = own_in.astype(jnp.float32) + scatter_sum(partial, "z")
     normed = (mixed * norm_gain).astype(jnp.bfloat16)
-    normed, *late = lax.optimization_barrier((normed, w_gate, w_up))
-    gate_other, up_other = [swap(w, "core") for w in late]
+    normed, gate_other, up_other = lax.optimization_barrier((normed, gate_other, up_other))
 
     block = jnp.concatenate([normed] + [ring_from(normed, "z", t) for t in (1, 2, 3)], axis=0)
     block, late = lax.optimization_barrier((block, w_down))

time: 215 us -> 205 us (0.953)
  starting transfers between devices: 63.9 us -> 81.1 us
  local copies, waits for them, and re-layouts: 26 us -> 11.2 us
  waiting for transfers between devices: 59.1 us -> 45 us
  Pallas kernels: 24.4 us -> 31.6 us
  blocking collectives: 37 us -> 32.8 us
    ppermute x9 -> x6, waiting for transfers between devices: 23.6 us -> 8.55 us  [ring_to(): return lax.ppermute(block, axis, [(i, (i + shift) % 4) for i in range(4)])]
    unnamed x44 -> x16, local copies, waits for them, and re-layouts: 18.5 us -> 5.82 us
    ppermute x9 -> x6, starting transfers between devices: 8.56 us -> 19.8 us  [ring_to(): return lax.ppermute(block, axis, [(i, (i + shift) % 4) for i in range(4)])]
    all_to_all x1, blocking collectives: 37 us -> 32.8 us  [exchange(): return lax.all_to_all(pieces, axis, split_axis=0, concat_axis=0, tiled=True)]
    pallas_call x2, Pallas kernels: 6.2 us -> 10.2 us  [the longest x1 5.09 us: project(): pl.pallas_call(project_kernel, in_specs=[SMEM] + [ANY] * 12, out_specs=VM...]
    all_to_all x3 -> x4, starting transfers between devices: 15.7 us -> 19.7 us  [exchange(): return lax.all_to_all(pieces, axis, split_axis=0, concat_axis=0, tiled=True)]
    another operation x2, local copies, waits for them, and re-layouts: 2.99 us -> 0.07 us  [body(): jnp.stack([lax.dynamic_slice_in_dim(hidden_in, start + 128 * l, share, 0)...]
    ppermute x12, waiting for transfers between devices: 8.25 us -> 5.59 us  [ring_from(): return lax.ppermute(block, axis, [((i + shift) % 4, i) for i in range(4)])]
  transfers between devices with their start and end apart: 33 -> 31, of which waited for: 18 -> 14; matrix products, arithmetic and copies ran while one was open for 4% -> 3% of each run, Pallas kernels for 5% -> 7%
where the time goes in v7:
time: 205 us; the launch traced here: 204 us
  starting transfers between devices  81.1 us (40%)
  waiting for transfers between devices  45 us (22%)
  blocking collectives  32.8 us (16%)
  Pallas kernels  31.6 us (15%)
  local copies, waits for them, and re-layouts  11.2 us (5%)
    all_to_all x1, blocking collectives, exchange(): return lax.all_to_all(pieces, axis, split_axis=0, concat_axis=0, tiled=True)  32.8 us
    ppermute x9, starting transfers between devices, swap(): return lax.ppermute(block, axis, [(0, 1), (1, 0)])  23.8 us
    all_to_all x4, waiting for transfers between devices, exchange(): return lax.all_to_all(pieces, axis, split_axis=0, concat_axis=0, tiled=True)  22.6 us
    ppermute x6, starting transfers between devices, ring_to(): return lax.ppermute(block, axis, [(i, (i + shift) % 4) for i in range(4)])  19.8 us
    all_to_all x4, starting transfers between devices, exchange(): return lax.all_to_all(pieces, axis, split_axis=0, concat_axis=0, tiled=True)  19.7 us
    ppermute x12, starting transfers between devices, ring_from(): return lax.ppermute(block, axis, [((i + shift) % 4, i) for i in range(4)])  17.9 us
    pallas_call x2, Pallas kernels, gate_up(): pl.pallas_call(gate_up_kernel, in_specs=[VMEM] + [ANY] * (len(pieces) + 4...  10.1 us
    pallas_call x1, Pallas kernels, down(): pl.pallas_call(down_kernel, in_specs=[SMEM] + [ANY] * 3 + [VMEM], out_spe...  8.67 us
  transfers between devices with their start and end apart: 31, of which 14 were waited for; matrix products, arithmetic and copies ran while one was open for 3% of the time, Pallas kernels for 7%

profile of v7, /device:TPU:1, one launch (start us, length us, event | category | flops | bytes accessed | tf_op | source)
XLA Modules:
  0.0 204.1 jit_solution(15209326852779406061)
XLA Ops:
  0.0 2.1 %collective-permute-start.1 = (bf16[256,1024]{1,0:T(8,128)(2,1)}, bf16[256,1024]{1,0:T(8,128)(2,1)S(1)}, u32[]{:S(2)}, u32[]{:S(2)}) collective-permute-start(bf16[256,1024]{1,0:T(8,128)(2,1)} %refs_4_.2), channel_id=1, source_target_pairs={{24,0},{0,8},{8,16},{16,24},{25,1},{1,9},{9,17},{17,25},{26,2},{2,... | collective-permute-start | bytes 1572872 | tf_op jit(solution)/shard_map/ppermute | solution.py:44
  2.1 1.4 collective-permute-start
  3.6 1.5 copy.24
  5.0 1.3 copy_bitcast_fusion.1
  6.4 5.1 %attend.1 = bf16[4,64,128]{2,1,0:T(8,128)(2,1)} custom-call(s32[4]{0:T(128)} %lengths_ref.1, bf16[4,64,128]{2,1,0:T(8,128)(2,1)} %bitcast.22, bf16[4,8,128]{2,1,0:T(8,128)(2,1)} %get-tuple-element.57.new_key_ref, bf16[4,8,128]{2,1,0:T(8,128)(2,1)} %get-tuple-element.56.new_value_ref, bf16[4,256,1024]{2,1,0:T(8,128)(2,1)} %key_ref.1, ...), custom_call_target="tpu_custom_call" | custom-call | flops 33554432 | bytes 4194304 | tf_op jit(solution)/shard_map/attend/pallas_call | solution.py:126
  11.5 0.9 reshape.48
  13.1 8.2 %all-to-all-start = ((bf16[4,4,2048]{2,1,0:T(4,128)(2,1)}), bf16[4,4,2048]{2,1,0:T(4,128)(2,1)S(1)}, u32[]{:S(2)}, u32[]{:S(2)}) async-start(bf16[4,4,2048]{2,1,0:T(4,128)(2,1)} %reshape.49), calls=%async_computation | async-start | bytes 131072 | tf_op jit(solution)/shard_map/all_to_all | solution.py:368
  21.2 1.6 collective-permute-start.6
  22.9 5.4 %all-to-all-done = bf16[4,4,2048]{2,1,0:T(4,128)(2,1)S(1)} async-done(((bf16[4,4,2048]{2,1,0:T(4,128)(2,1)}), bf16[4,4,2048]{2,1,0:T(4,128)(2,1)S(1)}, u32[]{:S(2)}, u32[]{:S(2)}) %all-to-all-start) | async-done | bytes 65568 | tf_op jit(solution)/shard_map/all_to_all | solution.py:368
  29.2 2.7 %collective-permute-done.2 = bf16[16,2048]{1,0:T(8,128)(2,1)S(1)} collective-permute-done((bf16[16,2048]{1,0:T(8,128)(2,1)S(1)}, bf16[16,2048]{1,0:T(8,128)(2,1)S(1)}, u32[]{:S(2)}, u32[]{:S(2)}) %collective-permute-start.2) | collective-permute-done | bytes 65568 | tf_op jit(solution)/shard_map/ppermute | solution.py:40
  31.8 1.2 collective-permute-start.5
  33.0 2.5 %collective-permute-start.4 = (bf16[32,2048]{1,0:T(8,128)(2,1)S(1)}, bf16[32,2048]{1,0:T(8,128)(2,1)S(1)}, u32[]{:S(2)}, u32[]{:S(2)}) collective-permute-start(bf16[32,2048]{1,0:T(8,128)(2,1)S(1)} %constant_dynamic-update-slice_fusion.refs_0_), channel_id=1, source_target_pairs={{128,0},{192,64},{0,128},{64,192},{129,1},{193,65},{1,129},{65,193... | collective-permute-start | bytes 393224 | tf_op jit(solution)/shard_map/ppermute | solution.py:44
  35.5 1.2 collective-permute-start.3
  36.7 4.4 %collective-permute-start.7 = (bf16[256,1024]{1,0:T(8,128)(2,1)S(1)}, bf16[256,1024]{1,0:T(8,128)(2,1)S(1)}, u32[]{:S(2)}, u32[]{:S(2)}) collective-permute-start(bf16[256,1024]{1,0:T(8,128)(2,1)S(1)} %copy-done.1), channel_id=1, source_target_pairs={{0,1},{1,0},{2,3},{3,2},{4,5},{5,4},{6,7},{7,6},{8,9},{9,8},{10,11... | collective-permute-start | bytes 1572872 | tf_op jit(solution)/shard_map/ppermute | solution.py:40
  42.2 3.0 %collective-permute-start.9 = (bf16[256,1024]{1,0:T(8,128)(2,1)S(1)}, bf16[256,1024]{1,0:T(8,128)(2,1)}, u32[]{:S(2)}, u32[]{:S(2)}) collective-permute-start(bf16[256,1024]{1,0:T(8,128)(2,1)S(1)} %collective-permute-done.6.refs_6_), channel_id=1, source_target_pairs={{0,1},{1,0},{2,3},{3,2},{4,5},{5,4},{6,7},{7,6},{8,9},{9,8},{10,11... | collective-permute-start | bytes 1572872 | tf_op jit(solution)/shard_map/ppermute | solution.py:40
  45.9 1.0 collective-permute-done.9.refs_10_
  46.9 0.9 copy-done.3
  47.8 5.1 %project.1 = bf16[128,1024]{1,0:T(8,128)(2,1)} custom-call(s32[29]{0:T(128)S(1)} %fusion.5.place_ref, bf16[32,2048]{1,0:T(8,128)(2,1)S(1)} %constant_dynamic-update-slice_fusion.refs_0_, bf16[32,2048]{1,0:T(8,128)(2,1)S(1)} %copy-done.3, bf16[32,2048]{1,0:T(8,128)(2,1)S(1)} %collective-permute-done.4.refs_2_, ...), custom_call_target="tpu_custom_call" | custom-call | flops 536870912 | bytes 4980736 | tf_op jit(solution)/shard_map/project/pallas_call | solution.py:235
  53.5 3.4 %all-to-all-start.1 = ((bf16[4,32,1024]{2,1,0:T(8,128)(2,1)}), bf16[4,32,1024]{2,1,0:T(8,128)(2,1)S(1)}, u32[]{:S(2)}, u32[]{:S(2)}) async-start(bf16[4,32,1024]{2,1,0:T(8,128)(2,1)} %bitcast.3), calls=%async_computation.1 | async-start | bytes 524288 | tf_op jit(solution)/shard_map/all_to_all | solution.py:368
  56.9 0.9 constant_dynamic-slice_fusion
  58.0 8.2 %all-to-all-done.1 = bf16[4,32,1024]{2,1,0:T(8,128)(2,1)S(1)} async-done(((bf16[4,32,1024]{2,1,0:T(8,128)(2,1)}), bf16[4,32,1024]{2,1,0:T(8,128)(2,1)S(1)}, u32[]{:S(2)}, u32[]{:S(2)}) %all-to-all-start.1) | async-done | bytes 262176 | tf_op jit(solution)/shard_map/all_to_all | solution.py:368
  67.1 3.9 %collective-permute-start.14 = (bf16[32,1024]{1,0:T(8,128)(2,1)S(1)}, bf16[32,1024]{1,0:T(8,128)(2,1)S(1)}, u32[]{:S(2)}, u32[]{:S(2)}) collective-permute-start(bf16[32,1024]{1,0:T(8,128)(2,1)S(1)} %get-tuple-element.36), channel_id=1, source_target_pairs={{4,0},{6,2},{0,4},{2,6},{5,1},{7,3},{1,5},{3,7},{12,8},{14,10},{8,... | collective-permute-start | bytes 196616 | tf_op jit(solution)/shard_map/ppermute | solution.py:44
  70.9 1.4 collective-permute-done.15
  72.4 2.1 %collective-permute-done.14 = bf16[32,1024]{1,0:T(8,128)(2,1)S(1)} collective-permute-done((bf16[32,1024]{1,0:T(8,128)(2,1)S(1)}, bf16[32,1024]{1,0:T(8,128)(2,1)S(1)}, u32[]{:S(2)}, u32[]{:S(2)}) %collective-permute-start.14) | collective-permute-done | bytes 65568 | tf_op jit(solution)/shard_map/ppermute | solution.py:44
  74.5 2.0 collective-permute-done.13
  76.6 2.7 %collective-permute-start.17 = (bf16[128,1024]{1,0:T(8,128)(2,1)S(1)}, bf16[128,1024]{1,0:T(8,128)(2,1)}, u32[]{:S(2)}, u32[]{:S(2)}) collective-permute-start(bf16[128,1024]{1,0:T(8,128)(2,1)S(1)} %pad_maximum_fusion.refs_0_), channel_id=1, source_target_pairs={{16,0},{24,8},{0,16},{8,24},{17,1},{25,9},{1,17},{9,25},{18,2},{26... | collective-permute-start | bytes 786440 | tf_op jit(solution)/shard_map/ppermute | solution.py:44
  79.3 1.1 collective-permute-start.16
  80.4 4.4 %gate_up.2 = bf16[128,3712]{1,0:T(8,128)(2,1)} custom-call(f32[1,1024]{1,0:T(1,128)S(1)} %bitcast.20, bf16[128,1024]{1,0:T(8,128)(2,1)S(1)} %pad_maximum_fusion.refs_0_, bf16[1024,896]{1,0:T(8,128)(2,1)} %refs_3_.1, bf16[1024,896]{1,0:T(8,128)(2,1)} %refs_4_.3, bf16[1024,896]{1,0:T(8,128)(2,1)S(1)} %collective-permute-done.11.refs_3_.refs_5_, ...), custom_call_target="tpu_custom_call" | custom-call | flops 17302499328 | bytes 8519680 | tf_op jit(solution)/shard_map/gate_up/pallas_call | solution.py:285
  84.8 4.5 %all-to-all-start.2 = ((bf16[8,16,3712]{2,1,0:T(8,128)(2,1)}), bf16[8,16,3712]{2,1,0:T(8,128)(2,1)S(1)}, u32[]{:S(2)}, u32[]{:S(2)}) async-start(bf16[8,16,3712]{2,1,0:T(8,128)(2,1)} %bitcast.4), calls=%async_computation.2 | async-start | bytes 1900544 | tf_op jit(solution)/shard_map/all_to_all | solution.py:368
  89.3 5.7 %gate_up.3 = bf16[384,3712]{1,0:T(8,128)(2,1)S(1)} custom-call(f32[1,1024]{1,0:T(1,128)S(1)} %bitcast.21, bf16[128,1024]{1,0:T(8,128)(2,1)} %collective-permute-done.16.refs_0_, bf16[128,1024]{1,0:T(8,128)(2,1)} %collective-permute-done.17.refs_1_, bf16[128,1024]{1,0:T(8,128)(2,1)S(1)} %collective-permute-done.18.refs_2_, bf16[1024,896]{1,0:T(8,128)(2,1)} %refs_3_.1, ...), custom_call_target="tpu_custom_call" | custom-call | flops 69209997312 | bytes 10878976 | tf_op jit(solution)/shard_map/gate_up/pallas_call | solution.py:285
  95.0 1.5 copy-done
  96.5 2.7 %all-to-all-done.2.refs_0_ = bf16[8,16,3712]{2,1,0:T(8,128)(2,1)S(1)} async-done(((bf16[8,16,3712]{2,1,0:T(8,128)(2,1)}), bf16[8,16,3712]{2,1,0:T(8,128)(2,1)S(1)}, u32[]{:S(2)}, u32[]{:S(2)}) %all-to-all-start.2) | async-done | bytes 950304 | tf_op jit(solution)/shard_map/all_to_all | solution.py:368
  99.3 32.8 %all_to_all.25.refs_1_ = bf16[8,48,3712]{2,1,0:T(8,128)(2,1)S(1)} all-to-all(bf16[8,48,3712]{2,1,0:T(8,128)(2,1)} %bitcast.19), channel_id=1, replica_groups=mesh['x'=4,'l'=2,'y'=4,'z'=4,'core'=2] {'x','l'}, dimensions={0} | all-to-all | bytes 5701632 | tf_op jit(solution)/shard_map/all_to_all | solution.py:368
  132.1 2.7 %activate.1 = bf16[8,64,1792]{2,1,0:T(8,128)(2,1)} custom-call(bf16[8,16,3712]{2,1,0:T(8,128)(2,1)S(1)} %all-to-all-done.2.refs_0_, bf16[8,48,3712]{2,1,0:T(8,128)(2,1)S(1)} %all_to_all.25.refs_1_), custom_call_target="tpu_custom_call" | custom-call | bytes 5505024 | tf_op jit(solution)/shard_map/activate/pallas_call | solution.py:180
  134.8 3.6 %all-to-all-start.4 = ((bf16[8,64,1792]{2,1,0:T(8,128)(2,1)}), bf16[8,64,1792]{2,1,0:T(8,128)(2,1)S(1)}, u32[]{:S(2)}, u32[]{:S(2)}) async-start(bf16[8,64,1792]{2,1,0:T(8,128)(2,1)} %activate.1), calls=%async_computation.4 | async-start | bytes 3670016 | tf_op jit(solution)/shard_map/all_to_all | solution.py:368
  138.4 7.2 %collective-permute-start.19 = (bf16[896,1024]{1,0:T(8,128)(2,1)}, bf16[896,1024]{1,0:T(8,128)(2,1)}, u32[]{:S(2)}, u32[]{:S(2)}) collective-permute-start(bf16[896,1024]{1,0:T(8,128)(2,1)} %own.1), channel_id=1, source_target_pairs={{0,1},{1,0},{2,3},{3,2},{4,5},{5,4},{6,7},{7,6},{8,9},{9,8},{10,11... | collective-permute-start | bytes 5505032 | tf_op jit(solution)/shard_map/ppermute | solution.py:40
  145.7 3.8 %collective-permute-done.19.other = bf16[896,1024]{1,0:T(8,128)(2,1)} collective-permute-done((bf16[896,1024]{1,0:T(8,128)(2,1)}, bf16[896,1024]{1,0:T(8,128)(2,1)}, u32[]{:S(2)}, u32[]{:S(2)}) %collective-permute-start.19) | collective-permute-done | bytes 1835040 | tf_op jit(solution)/shard_map/ppermute | solution.py:40
  149.4 6.3 %all-to-all-done.4.hidden_ref = bf16[8,64,1792]{2,1,0:T(8,128)(2,1)S(1)} async-done(((bf16[8,64,1792]{2,1,0:T(8,128)(2,1)}), bf16[8,64,1792]{2,1,0:T(8,128)(2,1)S(1)}, u32[]{:S(2)}, u32[]{:S(2)}) %all-to-all-start.4) | async-done | bytes 1835040 | tf_op jit(solution)/shard_map/all_to_all | solution.py:368
  155.7 1.2 copy-done.6
  156.9 8.7 %down.1 = (bf16[128,1024]{1,0:T(8,128)(2,1)}, bf16[128,1024]{1,0:T(8,128)(2,1)}, bf16[128,1024]{1,0:T(8,128)(2,1)}, bf16[128,1024]{1,0:T(8,128)(2,1)}) custom-call(s32[29]{0:T(128)} %copy-done.5, bf16[8,64,1792]{2,1,0:T(8,128)(2,1)} %copy-done.6, bf16[896,1024]{1,0:T(8,128)(2,1)} %own.1, bf16[896,1024]{1,0:T(8,128)(2,1)} %collective-permute-done.19.other, ...), custom_call_target="tpu_custom_call" | custom-call | flops 1879048192 | bytes 6553600 | tf_op jit(solution)/shard_map/down/pallas_call | solution.py:343
  166.2 5.8 %collective-permute-start.21 = (bf16[128,1024]{1,0:T(8,128)(2,1)}, bf16[128,1024]{1,0:T(8,128)(2,1)S(1)}, u32[]{:S(2)}, u32[]{:S(2)}) collective-permute-start(bf16[128,1024]{1,0:T(8,128)(2,1)} %get-tuple-element.43), channel_id=1, source_target_pairs={{0,16},{8,24},{16,0},{24,8},{1,17},{9,25},{17,1},{25,9},{2,18},{10... | collective-permute-start | bytes 786440 | tf_op jit(solution)/shard_map/ppermute | solution.py:48
  172.0 2.8 %collective-permute-done.20 = bf16[128,1024]{1,0:T(8,128)(2,1)S(1)} collective-permute-done((bf16[128,1024]{1,0:T(8,128)(2,1)}, bf16[128,1024]{1,0:T(8,128)(2,1)S(1)}, u32[]{:S(2)}, u32[]{:S(2)}) %collective-permute-start.20) | collective-permute-done | bytes 262176 | tf_op jit(solution)/shard_map/ppermute | solution.py:48
  174.8 4.0 %collective-permute-done.21 = bf16[128,1024]{1,0:T(8,128)(2,1)S(1)} collective-permute-done((bf16[128,1024]{1,0:T(8,128)(2,1)}, bf16[128,1024]{1,0:T(8,128)(2,1)S(1)}, u32[]{:S(2)}, u32[]{:S(2)}) %collective-permute-start.21) | collective-permute-done | bytes 262176 | tf_op jit(solution)/shard_map/ppermute | solution.py:48
  178.9 1.1 fusion.6
  180.0 7.9 %collective-permute-start.23 = (bf16[32,1024]{1,0:T(8,128)(2,1)S(1)}, bf16[32,1024]{1,0:T(8,128)(2,1)S(1)}, u32[]{:S(2)}, u32[]{:S(2)}) collective-permute-start(bf16[32,1024]{1,0:T(8,128)(2,1)S(1)} %get-tuple-element.51), channel_id=1, source_target_pairs={{0,2},{2,4},{4,6},{6,0},{1,3},{3,5},{5,7},{7,1},{8,10},{10,12},{12... | collective-permute-start | bytes 196616 | tf_op jit(solution)/shard_map/ppermute | solution.py:48
  187.9 5.5 %collective-permute-start.24 = (bf16[32,1024]{1,0:T(8,128)(2,1)S(1)}, bf16[32,1024]{1,0:T(8,128)(2,1)S(1)}, u32[]{:S(2)}, u32[]{:S(2)}) collective-permute-start(bf16[32,1024]{1,0:T(8,128)(2,1)S(1)} %get-tuple-element.53), channel_id=1, source_target_pairs={{0,4},{2,6},{4,0},{6,2},{1,5},{3,7},{5,1},{7,3},{8,12},{10,14},{12... | collective-permute-start | bytes 196616 | tf_op jit(solution)/shard_map/ppermute | solution.py:48
  193.4 1.7 collective-permute-done.24
  195.2 7.2 %collective-permute-start.26 = (bf16[16,1024]{1,0:T(8,128)(2,1)S(1)}, bf16[16,1024]{1,0:T(8,128)(2,1)S(1)}, u32[]{:S(2)}, u32[]{:S(2)}) collective-permute-start(bf16[16,1024]{1,0:T(8,128)(2,1)S(1)} %broadcast_select_fusion.2), channel_id=1, source_target_pairs={{0,1},{1,0},{2,3},{3,2},{4,5},{5,4},{6,7},{7,6},{8,9},{9,8},{10,11... | collective-permute-start | bytes 98312 | tf_op jit(solution)/shard_map/ppermute | solution.py:40
  (62 shorter events, 7.5 us)
Async XLA Ops:
  0.0 28.3 %collective-permute-start.1 = (bf16[256,1024]{1,0:T(8,128)(2,1)}, bf16[256,1024]{1,0:T(8,128)(2,1)S(1)}, u32[]{:S(2)}, u32[]{:S(2)}) collective-permute-start(bf16[256,1024]{1,0:T(8,128)(2,1)} %refs_4_.2), channel_id=1, source_target_pairs={{24,0},{0,8},{8,16},{16,24},{25,1},{1,9},{9,17},{17,25},{26,2},{2,... | collective-permute-start | bytes 1572872 | tf_op jit(solution)/shard_map/ppermute | solution.py:44
  2.1 26.2 %collective-permute-start = (bf16[256,1024]{1,0:T(8,128)(2,1)}, bf16[256,1024]{1,0:T(8,128)(2,1)S(1)}, u32[]{:S(2)}, u32[]{:S(2)}) collective-permute-start(bf16[256,1024]{1,0:T(8,128)(2,1)} %refs_4_.2), channel_id=1, source_target_pairs={{8,0},{16,8},{24,16},{0,24},{9,1},{17,9},{25,17},{1,25},{10,2},{18... | collective-permute-start | bytes 1572872 | tf_op jit(solution)/shard_map/ppermute | solution.py:44
  6.4 14.9 %copy-start.1 = (bf16[256,1024]{1,0:T(8,128)(2,1)S(1)}, bf16[256,1024]{1,0:T(8,128)(2,1)}, u32[]{:S(2)}) copy-start(bf16[256,1024]{1,0:T(8,128)(2,1)} %refs_4_.2) | copy-start | bytes 1572868
  13.1 15.2 %all-to-all-start = ((bf16[4,4,2048]{2,1,0:T(4,128)(2,1)}), bf16[4,4,2048]{2,1,0:T(4,128)(2,1)S(1)}, u32[]{:S(2)}, u32[]{:S(2)}) async-start(bf16[4,4,2048]{2,1,0:T(4,128)(2,1)} %reshape.49), calls=%async_computation | async-start | bytes 131072 | tf_op jit(solution)/shard_map/all_to_all | solution.py:368
  21.2 19.8 %collective-permute-start.6 = (bf16[256,1024]{1,0:T(8,128)(2,1)S(1)}, bf16[256,1024]{1,0:T(8,128)(2,1)S(1)}, u32[]{:S(2)}, u32[]{:S(2)}) collective-permute-start(bf16[256,1024]{1,0:T(8,128)(2,1)S(1)} %copy-done.1), channel_id=1, source_target_pairs={{16,0},{24,8},{0,16},{8,24},{17,1},{25,9},{1,17},{9,25},{18,2},{26... | collective-permute-start | bytes 1572872 | tf_op jit(solution)/shard_map/ppermute | solution.py:44
  28.3 3.5 %collective-permute-start.2 = (bf16[16,2048]{1,0:T(8,128)(2,1)S(1)}, bf16[16,2048]{1,0:T(8,128)(2,1)S(1)}, u32[]{:S(2)}, u32[]{:S(2)}) collective-permute-start(bf16[16,2048]{1,0:T(8,128)(2,1)S(1)} %reshape.50), channel_id=1, source_target_pairs={{0,32},{32,0},{1,33},{33,1},{2,34},{34,2},{3,35},{35,3},{4,36},{36... | collective-permute-start | bytes 196616 | tf_op jit(solution)/shard_map/ppermute | solution.py:40
  31.8 9.2 %collective-permute-start.5 = (bf16[32,2048]{1,0:T(8,128)(2,1)S(1)}, bf16[32,2048]{1,0:T(8,128)(2,1)S(1)}, u32[]{:S(2)}, u32[]{:S(2)}) collective-permute-start(bf16[32,2048]{1,0:T(8,128)(2,1)S(1)} %constant_dynamic-update-slice_fusion.refs_0_), channel_id=1, source_target_pairs={{192,0},{0,64},{64,128},{128,192},{193,1},{1,65},{65,129},{129,193... | collective-permute-start | bytes 393224 | tf_op jit(solution)/shard_map/ppermute | solution.py:44
  33.0 8.5 %collective-permute-start.4 = (bf16[32,2048]{1,0:T(8,128)(2,1)S(1)}, bf16[32,2048]{1,0:T(8,128)(2,1)S(1)}, u32[]{:S(2)}, u32[]{:S(2)}) collective-permute-start(bf16[32,2048]{1,0:T(8,128)(2,1)S(1)} %constant_dynamic-update-slice_fusion.refs_0_), channel_id=1, source_target_pairs={{128,0},{192,64},{0,128},{64,192},{129,1},{193,65},{1,129},{65,193... | collective-permute-start | bytes 393224 | tf_op jit(solution)/shard_map/ppermute | solution.py:44
  35.5 6.1 %collective-permute-start.3 = (bf16[32,2048]{1,0:T(8,128)(2,1)S(1)}, bf16[32,2048]{1,0:T(8,128)(2,1)S(1)}, u32[]{:S(2)}, u32[]{:S(2)}) collective-permute-start(bf16[32,2048]{1,0:T(8,128)(2,1)S(1)} %constant_dynamic-update-slice_fusion.refs_0_), channel_id=1, source_target_pairs={{64,0},{128,64},{192,128},{0,192},{65,1},{129,65},{193,129},{1,193... | collective-permute-start | bytes 393224 | tf_op jit(solution)/shard_map/ppermute | solution.py:44
  36.7 9.2 %collective-permute-start.7 = (bf16[256,1024]{1,0:T(8,128)(2,1)S(1)}, bf16[256,1024]{1,0:T(8,128)(2,1)S(1)}, u32[]{:S(2)}, u32[]{:S(2)}) collective-permute-start(bf16[256,1024]{1,0:T(8,128)(2,1)S(1)} %copy-done.1), channel_id=1, source_target_pairs={{0,1},{1,0},{2,3},{3,2},{4,5},{5,4},{6,7},{7,6},{8,9},{9,8},{10,11... | collective-permute-start | bytes 1572872 | tf_op jit(solution)/shard_map/ppermute | solution.py:40
  41.0 4.9 %collective-permute-start.8 = (bf16[256,1024]{1,0:T(8,128)(2,1)S(1)}, bf16[256,1024]{1,0:T(8,128)(2,1)S(1)}, u32[]{:S(2)}, u32[]{:S(2)}) collective-permute-start(bf16[256,1024]{1,0:T(8,128)(2,1)S(1)} %collective-permute-done.refs_5_), channel_id=1, source_target_pairs={{0,1},{1,0},{2,3},{3,2},{4,5},{5,4},{6,7},{7,6},{8,9},{9,8},{10,11... | collective-permute-start | bytes 1572872 | tf_op jit(solution)/shard_map/ppermute | solution.py:40
  41.0 4.9 %collective-permute-start.10 = (bf16[256,1024]{1,0:T(8,128)(2,1)S(1)}, bf16[256,1024]{1,0:T(8,128)(2,1)}, u32[]{:S(2)}, u32[]{:S(2)}) collective-permute-start(bf16[256,1024]{1,0:T(8,128)(2,1)S(1)} %collective-permute-done.1.refs_7_), channel_id=1, source_target_pairs={{0,1},{1,0},{2,3},{3,2},{4,5},{5,4},{6,7},{7,6},{8,9},{9,8},{10,11... | collective-permute-start | bytes 1572872 | tf_op jit(solution)/shard_map/ppermute | solution.py:40
  41.6 0.6 copy-start.2
  42.2 4.7 %collective-permute-start.9 = (bf16[256,1024]{1,0:T(8,128)(2,1)S(1)}, bf16[256,1024]{1,0:T(8,128)(2,1)}, u32[]{:S(2)}, u32[]{:S(2)}) collective-permute-start(bf16[256,1024]{1,0:T(8,128)(2,1)S(1)} %collective-permute-done.6.refs_6_), channel_id=1, source_target_pairs={{0,1},{1,0},{2,3},{3,2},{4,5},{5,4},{6,7},{7,6},{8,9},{9,8},{10,11... | collective-permute-start | bytes 1572872 | tf_op jit(solution)/shard_map/ppermute | solution.py:40
  45.9 7.0 %copy-start.5 = (s32[29]{0:T(128)}, s32[29]{0:T(128)S(1)}, u32[]{:S(2)}) copy-start(s32[29]{0:T(128)S(1)} %fusion.5.place_ref) | copy-start | bytes 352
  46.9 0.9 copy-start.3
  52.9 13.3 %copy-start.4 = (f32[1024]{0:T(1024)S(1)}, f32[1024]{0:T(1024)}, u32[]{:S(2)}) copy-start(f32[1024]{0:T(1024)} %param.21) | copy-start | bytes 12292
  52.9 14.0 %collective-permute-start.11 = (bf16[1024,896]{1,0:T(8,128)(2,1)}, bf16[1024,896]{1,0:T(8,128)(2,1)S(1)}, u32[]{:S(2)}, u32[]{:S(2)}) collective-permute-start(bf16[1024,896]{1,0:T(8,128)(2,1)} %refs_3_.1), channel_id=1, source_target_pairs={{0,1},{1,0},{2,3},{3,2},{4,5},{5,4},{6,7},{7,6},{8,9},{9,8},{10,11... | collective-permute-start | bytes 5505032 | tf_op jit(solution)/shard_map/ppermute | solution.py:40
  53.4 13.6 %collective-permute-start.12 = (bf16[1024,896]{1,0:T(8,128)(2,1)}, bf16[1024,896]{1,0:T(8,128)(2,1)}, u32[]{:S(2)}, u32[]{:S(2)}) collective-permute-start(bf16[1024,896]{1,0:T(8,128)(2,1)} %refs_4_.3), channel_id=1, source_target_pairs={{0,1},{1,0},{2,3},{3,2},{4,5},{5,4},{6,7},{7,6},{8,9},{9,8},{10,11... | collective-permute-start | bytes 5505032 | tf_op jit(solution)/shard_map/ppermute | solution.py:40
  53.5 12.7 %all-to-all-start.1 = ((bf16[4,32,1024]{2,1,0:T(8,128)(2,1)}), bf16[4,32,1024]{2,1,0:T(8,128)(2,1)S(1)}, u32[]{:S(2)}, u32[]{:S(2)}) async-start(bf16[4,32,1024]{2,1,0:T(8,128)(2,1)} %bitcast.3), calls=%async_computation.1 | async-start | bytes 524288 | tf_op jit(solution)/shard_map/all_to_all | solution.py:368
  66.9 5.4 %collective-permute-start.15 = (bf16[32,1024]{1,0:T(8,128)(2,1)S(1)}, bf16[32,1024]{1,0:T(8,128)(2,1)S(1)}, u32[]{:S(2)}, u32[]{:S(2)}) collective-permute-start(bf16[32,1024]{1,0:T(8,128)(2,1)S(1)} %get-tuple-element.36), channel_id=1, source_target_pairs={{6,0},{0,2},{2,4},{4,6},{7,1},{1,3},{3,5},{5,7},{14,8},{8,10},{10,... | collective-permute-start | bytes 196616 | tf_op jit(solution)/shard_map/ppermute | solution.py:44
  67.1 7.4 %collective-permute-start.14 = (bf16[32,1024]{1,0:T(8,128)(2,1)S(1)}, bf16[32,1024]{1,0:T(8,128)(2,1)S(1)}, u32[]{:S(2)}, u32[]{:S(2)}) collective-permute-start(bf16[32,1024]{1,0:T(8,128)(2,1)S(1)} %get-tuple-element.36), channel_id=1, source_target_pairs={{4,0},{6,2},{0,4},{2,6},{5,1},{7,3},{1,5},{3,7},{12,8},{14,10},{8,... | collective-permute-start | bytes 196616 | tf_op jit(solution)/shard_map/ppermute | solution.py:44
  70.9 5.6 %collective-permute-start.13 = (bf16[32,1024]{1,0:T(8,128)(2,1)S(1)}, bf16[32,1024]{1,0:T(8,128)(2,1)S(1)}, u32[]{:S(2)}, u32[]{:S(2)}) collective-permute-start(bf16[32,1024]{1,0:T(8,128)(2,1)S(1)} %get-tuple-element.36), channel_id=1, source_target_pairs={{2,0},{4,2},{6,4},{0,6},{3,1},{5,3},{7,5},{1,7},{10,8},{12,10},{14... | collective-permute-start | bytes 196616 | tf_op jit(solution)/shard_map/ppermute | solution.py:44
  76.5 12.8 %collective-permute-start.18 = (bf16[128,1024]{1,0:T(8,128)(2,1)S(1)}, bf16[128,1024]{1,0:T(8,128)(2,1)S(1)}, u32[]{:S(2)}, u32[]{:S(2)}) collective-permute-start(bf16[128,1024]{1,0:T(8,128)(2,1)S(1)} %pad_maximum_fusion.refs_0_), channel_id=1, source_target_pairs={{24,0},{0,8},{8,16},{16,24},{25,1},{1,9},{9,17},{17,25},{26,2},{2,... | collective-permute-start | bytes 786440 | tf_op jit(solution)/shard_map/ppermute | solution.py:44
  76.6 12.7 %collective-permute-start.17 = (bf16[128,1024]{1,0:T(8,128)(2,1)S(1)}, bf16[128,1024]{1,0:T(8,128)(2,1)}, u32[]{:S(2)}, u32[]{:S(2)}) collective-permute-start(bf16[128,1024]{1,0:T(8,128)(2,1)S(1)} %pad_maximum_fusion.refs_0_), channel_id=1, source_target_pairs={{16,0},{24,8},{0,16},{8,24},{17,1},{25,9},{1,17},{9,25},{18,2},{26... | collective-permute-start | bytes 786440 | tf_op jit(solution)/shard_map/ppermute | solution.py:44
  79.3 10.0 %collective-permute-start.16 = (bf16[128,1024]{1,0:T(8,128)(2,1)S(1)}, bf16[128,1024]{1,0:T(8,128)(2,1)}, u32[]{:S(2)}, u32[]{:S(2)}) collective-permute-start(bf16[128,1024]{1,0:T(8,128)(2,1)S(1)} %pad_maximum_fusion.refs_0_), channel_id=1, source_target_pairs={{8,0},{16,8},{24,16},{0,24},{9,1},{17,9},{25,17},{1,25},{10,2},{18... | collective-permute-start | bytes 786440 | tf_op jit(solution)/shard_map/ppermute | solution.py:44
  84.8 14.5 %all-to-all-start.2 = ((bf16[8,16,3712]{2,1,0:T(8,128)(2,1)}), bf16[8,16,3712]{2,1,0:T(8,128)(2,1)S(1)}, u32[]{:S(2)}, u32[]{:S(2)}) async-start(bf16[8,16,3712]{2,1,0:T(8,128)(2,1)} %bitcast.4), calls=%async_computation.2 | async-start | bytes 1900544 | tf_op jit(solution)/shard_map/all_to_all | solution.py:368
  95.0 1.5 copy-start
  134.8 20.9 %all-to-all-start.4 = ((bf16[8,64,1792]{2,1,0:T(8,128)(2,1)}), bf16[8,64,1792]{2,1,0:T(8,128)(2,1)S(1)}, u32[]{:S(2)}, u32[]{:S(2)}) async-start(bf16[8,64,1792]{2,1,0:T(8,128)(2,1)} %activate.1), calls=%async_computation.4 | async-start | bytes 3670016 | tf_op jit(solution)/shard_map/all_to_all | solution.py:368
  138.4 11.0 %collective-permute-start.19 = (bf16[896,1024]{1,0:T(8,128)(2,1)}, bf16[896,1024]{1,0:T(8,128)(2,1)}, u32[]{:S(2)}, u32[]{:S(2)}) collective-permute-start(bf16[896,1024]{1,0:T(8,128)(2,1)} %own.1), channel_id=1, source_target_pairs={{0,1},{1,0},{2,3},{3,2},{4,5},{5,4},{6,7},{7,6},{8,9},{9,8},{10,11... | collective-permute-start | bytes 5505032 | tf_op jit(solution)/shard_map/ppermute | solution.py:40
  155.7 1.2 copy-start.6
  165.6 9.2 %collective-permute-start.20 = (bf16[128,1024]{1,0:T(8,128)(2,1)}, bf16[128,1024]{1,0:T(8,128)(2,1)S(1)}, u32[]{:S(2)}, u32[]{:S(2)}) collective-permute-start(bf16[128,1024]{1,0:T(8,128)(2,1)} %get-tuple-element.42), channel_id=1, source_target_pairs={{0,8},{8,16},{16,24},{24,0},{1,9},{9,17},{17,25},{25,1},{2,10},{10... | collective-permute-start | bytes 786440 | tf_op jit(solution)/shard_map/ppermute | solution.py:48
  166.2 12.6 %collective-permute-start.21 = (bf16[128,1024]{1,0:T(8,128)(2,1)}, bf16[128,1024]{1,0:T(8,128)(2,1)S(1)}, u32[]{:S(2)}, u32[]{:S(2)}) collective-permute-start(bf16[128,1024]{1,0:T(8,128)(2,1)} %get-tuple-element.43), channel_id=1, source_target_pairs={{0,16},{8,24},{16,0},{24,8},{1,17},{9,25},{17,1},{25,9},{2,18},{10... | collective-permute-start | bytes 786440 | tf_op jit(solution)/shard_map/ppermute | solution.py:48
  172.0 6.8 %collective-permute-start.22 = (bf16[128,1024]{1,0:T(8,128)(2,1)}, bf16[128,1024]{1,0:T(8,128)(2,1)S(1)}, u32[]{:S(2)}, u32[]{:S(2)}) collective-permute-start(bf16[128,1024]{1,0:T(8,128)(2,1)} %get-tuple-element.44), channel_id=1, source_target_pairs={{0,24},{8,0},{16,8},{24,16},{1,25},{9,1},{17,9},{25,17},{2,26},{10... | collective-permute-start | bytes 786440 | tf_op jit(solution)/shard_map/ppermute | solution.py:48
  180.0 13.4 %collective-permute-start.23 = (bf16[32,1024]{1,0:T(8,128)(2,1)S(1)}, bf16[32,1024]{1,0:T(8,128)(2,1)S(1)}, u32[]{:S(2)}, u32[]{:S(2)}) collective-permute-start(bf16[32,1024]{1,0:T(8,128)(2,1)S(1)} %get-tuple-element.51), channel_id=1, source_target_pairs={{0,2},{2,4},{4,6},{6,0},{1,3},{3,5},{5,7},{7,1},{8,10},{10,12},{12... | collective-permute-start | bytes 196616 | tf_op jit(solution)/shard_map/ppermute | solution.py:48
  187.9 5.5 %collective-permute-start.25 = (bf16[32,1024]{1,0:T(8,128)(2,1)S(1)}, bf16[32,1024]{1,0:T(8,128)(2,1)S(1)}, u32[]{:S(2)}, u32[]{:S(2)}) collective-permute-start(bf16[32,1024]{1,0:T(8,128)(2,1)S(1)} %get-tuple-element.52), channel_id=1, source_target_pairs={{0,6},{2,0},{4,2},{6,4},{1,7},{3,1},{5,3},{7,5},{8,14},{10,8},{12,... | collective-permute-start | bytes 196616 | tf_op jit(solution)/shard_map/ppermute | solution.py:48
  187.9 7.2 %collective-permute-start.24 = (bf16[32,1024]{1,0:T(8,128)(2,1)S(1)}, bf16[32,1024]{1,0:T(8,128)(2,1)S(1)}, u32[]{:S(2)}, u32[]{:S(2)}) collective-permute-start(bf16[32,1024]{1,0:T(8,128)(2,1)S(1)} %get-tuple-element.53), channel_id=1, source_target_pairs={{0,4},{2,6},{4,0},{6,2},{1,5},{3,7},{5,1},{7,3},{8,12},{10,14},{12... | collective-permute-start | bytes 196616 | tf_op jit(solution)/shard_map/ppermute | solution.py:48
  195.2 8.1 %collective-permute-start.26 = (bf16[16,1024]{1,0:T(8,128)(2,1)S(1)}, bf16[16,1024]{1,0:T(8,128)(2,1)S(1)}, u32[]{:S(2)}, u32[]{:S(2)}) collective-permute-start(bf16[16,1024]{1,0:T(8,128)(2,1)S(1)} %broadcast_select_fusion.2), channel_id=1, source_target_pairs={{0,1},{1,0},{2,3},{3,2},{4,5},{5,4},{6,7},{7,6},{8,9},{9,8},{10,11... | collective-permute-start | bytes 98312 | tf_op jit(solution)/shard_map/ppermute | solution.py:40

commit v8 on v5

--- a/solution.py
+++ b/solution.py
@@ -58,13 +58,6 @@
         row_count, KVH, 1, HD
     )
     return (summed / total[..., None]).astype(jnp.bfloat16).reshape(row_count, HQ * HD)
-
-
-def activate(gate_sum, up_sum, square_sum):
-    inv_rms = lax.rsqrt(square_sum / D + 1e-05)
-    gate = gate_sum * inv_rms[:, None]
-    up_proj = up_sum * inv_rms[:, None]
-    return (jax.nn.silu(gate) * up_proj).astype(jnp.bfloat16)
 
 
 def places():
@@ -113,6 +106,50 @@
 def wait_all(copies):
     for copy in copies:
         copy.wait()
+
+
+def activate_kernel(*refs):
+    parts, out_ref, held, hidden_ref, sems = refs[:2], refs[2], refs[3:5], refs[5], refs[6]
+    copies = start_all([pltpu.make_async_copy(parts[i], held[i], sems.at[i]) for i in range(2)])
+    width = hidden_ref.shape[1] // 2
+    start = 0
+    for i in range(2):
+        copies[i].wait()
+        groups, rows = held[i].shape[:2]
+
+        def summed(first, size):
+            return add_up([held[i][g, :, first : first + size] for g in range(groups)])
+
+        square_sum = jnp.sum(summed(4 * width, 128), axis=1, keepdims=True)
+        inv_rms = lax.rsqrt(square_sum / D + 1e-05)
+        for j in range(2):
+            for n, size in steps(width):
+                gate = summed(2 * j * width + n, size) * inv_rms
+                up_proj = summed((2 * j + 1) * width + n, size) * inv_rms
+                hidden = gate / (1.0 + jnp.exp(-gate)) * up_proj
+                hidden_ref[start : start + rows, j * width + n : j * width + n + size] = hidden.astype(jnp.bfloat16)
+        start += rows
+    wait_all(
+        start_all(
+            [pltpu.make_async_copy(hidden_ref, out_ref.at[g], sems.at[2 + g]) for g in range(out_ref.shape[0])]
+        )
+    )
+
+
+def activate(parts):
+    groups, _, width = parts[0].shape
+    width = (width - 128) // 2
+    rows = parts[0].shape[1] + parts[1].shape[1]
+    return pl.pallas_call(
+        activate_kernel,
+        in_specs=[ANY] * 2,
+        out_specs=ANY,
+        out_shape=jax.ShapeDtypeStruct((groups, rows, width), jnp.bfloat16),
+        scratch_shapes=[pltpu.VMEM(part.shape, jnp.bfloat16) for part in parts]
+        + [pltpu.VMEM((rows, width), jnp.bfloat16), pltpu.SemaphoreType.DMA((2 + groups,))],
+        name="activate",
+        **params(12, 0, 6 * groups * rows * width),
+    )(*parts)
 
 
 def project_kernel(place_ref, *refs):
@@ -287,10 +324,6 @@
     return jnp.sum(exchange(pieces, axis).astype(jnp.float32), axis=0)
 
 
-def gather(rows, axis):
-    return exchange(jnp.broadcast_to(rows[None], (lax.axis_size(axis),) + rows.shape), axis)
-
-
 def body(
     hidden_in,
     queries,
@@ -338,20 +371,11 @@
     pieces = [ring_from(block, "y", t) for t in (1, 2, 3)]
     weights = [w_gate, w_up, gate_other, up_other]
     summed = [
-        scatter_sum(gate_up(norm_gain[None, :], part, weights, hidden_us), GRP)
+        exchange(gate_up(norm_gain[None, :], part, weights, hidden_us).reshape(8, -1, 4 * w_gate.shape[1] + 128), GRP)
         for part, hidden_us in (([block], 15), (pieces, 60))
     ]
-    summed = jnp.concatenate(summed, axis=0)
-    width = w_gate.shape[1]
-    square_sum = summed[:, 4 * width] + summed[:, 4 * width + 1]
-    hidden = jnp.concatenate(
-        [
-            activate(summed[:, i * width : (i + 1) * width], summed[:, (i + 1) * width : (i + 2) * width], square_sum)
-            for i in (0, 2)
-        ],
-        axis=1,
-    )
-    parts = down(place, gather(hidden, GRP), [w_down, down_other], mixed)
+    hidden = exchange(activate(summed), GRP)
+    parts = down(place, hidden, [w_down, down_other], mixed)
     total = add_up([parts[0]] + [ring_to(parts[t], "y", t) for t in (1, 2, 3)])
     parts = [total[t * share : (t + 1) * share] for t in range(4)]
     total = add_up([parts[0]] + [ring_to(parts[t].astype(jnp.bfloat16), "z", t) for t in (1, 2, 3)])

time: 202 us -> 205 us (1.015)
  waiting for transfers between devices: 81.3 us -> 45.5 us
  blocking collectives: 0 us -> 32.9 us
  starting transfers between devices: 78.4 us -> 83.9 us
  Pallas kernels: 21.5 us -> 25.8 us
  other arithmetic: 7.86 us -> 3.81 us
    all_to_all x5 -> x4, waiting for transfers between devices: 57.7 us -> 21.4 us  [exchange(): return lax.all_to_all(pieces, axis, split_axis=0, concat_axis=0, tiled=True)]
    all_to_all x0 -> x1, blocking collectives: none -> 32.9 us  [exchange(): return lax.all_to_all(pieces, axis, split_axis=0, concat_axis=0, tiled=True)]
    ppermute x6, starting transfers between devices: 10 us -> 23.1 us  [ring_to(): return lax.ppermute(block, axis, [(i, (i + shift) % 4) for i in range(4)])]
    all_to_all x5 -> x4, starting transfers between devices: 28.2 us -> 20.4 us  [exchange(): return lax.all_to_all(pieces, axis, split_axis=0, concat_axis=0, tiled=True)]
    pallas_call x0 -> x1, Pallas kernels: none -> 3.83 us  [activate(): pl.pallas_call(activate_kernel, in_specs=[ANY] * 2, out_specs=ANY, out_sh...]
    reduce_sum x3 -> x1, other arithmetic: 3.66 us -> 0.03 us  [scatter_sum(): return jnp.sum(exchange(pieces, axis).astype(jnp.float32), axis=0)]
    unnamed x18 -> x22, local copies, waits for them, and re-layouts: 3.14 us -> 5.3 us
  transfers between devices with their start and end apart: 32 -> 31, of which waited for: 14 -> 15; matrix products, arithmetic and copies ran while one was open for 5% -> 4% of each run, Pallas kernels for 5% -> 5%
where the time goes in v8:
time: 205 us; the launch traced here: 204 us
  starting transfers between devices  83.9 us (41%)
  waiting for transfers between devices  45.5 us (22%)
  blocking collectives  32.9 us (16%)
  Pallas kernels  25.8 us (13%)
  local copies, waits for them, and re-layouts  9.21 us (4%)
  other arithmetic  3.81 us (2%)
  matrix products  3 us (1%)
    all_to_all x1, blocking collectives, exchange(): return lax.all_to_all(pieces, axis, split_axis=0, concat_axis=0, tiled=True)  32.9 us
    ppermute x6, starting transfers between devices, ring_to(): return lax.ppermute(block, axis, [(i, (i + shift) % 4) for i in range(4)])  23.1 us
    ppermute x9, starting transfers between devices, swap(): return lax.ppermute(block, axis, [(0, 1), (1, 0)])  22.2 us
    all_to_all x4, waiting for transfers between devices, exchange(): return lax.all_to_all(pieces, axis, split_axis=0, concat_axis=0, tiled=True)  21.4 us
    all_to_all x4, starting transfers between devices, exchange(): return lax.all_to_all(pieces, axis, split_axis=0, concat_axis=0, tiled=True)  20.4 us
    ppermute x12, starting transfers between devices, ring_from(): return lax.ppermute(block, axis, [((i + shift) % 4, i) for i in range(4)])  18.2 us
    pallas_call x2, Pallas kernels, gate_up(): pl.pallas_call(gate_up_kernel, in_specs=[VMEM] + [ANY] * (len(pieces) + 4...  10.7 us
    ppermute x6, waiting for transfers between devices, ring_to(): return lax.ppermute(block, axis, [(i, (i + shift) % 4) for i in range(4)])  9.98 us
  transfers between devices with their start and end apart: 31, of which 15 were waited for; matrix products, arithmetic and copies ran while one was open for 4% of the time, Pallas kernels for 5%

profile of v8, /device:TPU:1, one launch (start us, length us, event | category | flops | bytes accessed | tf_op | source)
XLA Modules:
  0.0 204.4 jit_solution(11525342209932230895)
XLA Ops:
  0.0 2.1 %collective-permute-start.1 = (bf16[256,1024]{1,0:T(8,128)(2,1)}, bf16[256,1024]{1,0:T(8,128)(2,1)S(1)}, u32[]{:S(2)}, u32[]{:S(2)}) collective-permute-start(bf16[256,1024]{1,0:T(8,128)(2,1)} %refs_4_.2), channel_id=1, source_target_pairs={{24,0},{0,8},{8,16},{16,24},{25,1},{1,9},{9,17},{17,25},{26,2},{2,... | collective-permute-start | bytes 1572872 | tf_op jit(solution)/shard_map/ppermute | solution.py:82
  2.1 1.5 collective-permute-start
  6.0 1.0 fusion.30
  7.0 1.6 fusion.39
  10.0 8.2 %all-to-all-start = ((bf16[4,4,2048]{2,1,0:T(4,128)(2,1)}), bf16[4,4,2048]{2,1,0:T(4,128)(2,1)S(1)}, u32[]{:S(2)}, u32[]{:S(2)}) async-start(bf16[4,4,2048]{2,1,0:T(4,128)(2,1)} %reshape.71), calls=%async_computation | async-start | bytes 131072 | tf_op jit(solution)/shard_map/all_to_all | solution.py:318
  18.2 1.6 collective-permute-start.6
  19.7 5.5 %all-to-all-done = bf16[4,4,2048]{2,1,0:T(4,128)(2,1)S(1)} async-done(((bf16[4,4,2048]{2,1,0:T(4,128)(2,1)}), bf16[4,4,2048]{2,1,0:T(4,128)(2,1)S(1)}, u32[]{:S(2)}, u32[]{:S(2)}) %all-to-all-start) | async-done | bytes 65568 | tf_op jit(solution)/shard_map/all_to_all | solution.py:318
  26.1 2.8 %collective-permute-done.2 = bf16[16,2048]{1,0:T(8,128)(2,1)S(1)} collective-permute-done((bf16[16,2048]{1,0:T(8,128)(2,1)S(1)}, bf16[16,2048]{1,0:T(8,128)(2,1)S(1)}, u32[]{:S(2)}, u32[]{:S(2)}) %collective-permute-start.2) | collective-permute-done | bytes 65568 | tf_op jit(solution)/shard_map/ppermute | solution.py:78
  28.9 1.2 collective-permute-start.5
  30.1 2.5 %collective-permute-start.4 = (bf16[32,2048]{1,0:T(8,128)(2,1)S(1)}, bf16[32,2048]{1,0:T(8,128)(2,1)S(1)}, u32[]{:S(2)}, u32[]{:S(2)}) collective-permute-start(bf16[32,2048]{1,0:T(8,128)(2,1)S(1)} %constant_dynamic-update-slice_fusion.refs_0_), channel_id=1, source_target_pairs={{128,0},{192,64},{0,128},{64,192},{129,1},{193,65},{1,129},{65,193... | collective-permute-start | bytes 393224 | tf_op jit(solution)/shard_map/ppermute | solution.py:82
  32.6 1.2 collective-permute-start.3
  33.7 4.1 %collective-permute-start.7 = (bf16[256,1024]{1,0:T(8,128)(2,1)S(1)}, bf16[256,1024]{1,0:T(8,128)(2,1)}, u32[]{:S(2)}, u32[]{:S(2)}) collective-permute-start(bf16[256,1024]{1,0:T(8,128)(2,1)S(1)} %copy-done.4), channel_id=1, source_target_pairs={{0,1},{1,0},{2,3},{3,2},{4,5},{5,4},{6,7},{7,6},{8,9},{9,8},{10,11... | collective-permute-start | bytes 1572872 | tf_op jit(solution)/shard_map/ppermute | solution.py:78
  39.1 3.0 %collective-permute-start.9 = (bf16[256,1024]{1,0:T(8,128)(2,1)}, bf16[256,1024]{1,0:T(8,128)(2,1)}, u32[]{:S(2)}, u32[]{:S(2)}) collective-permute-start(bf16[256,1024]{1,0:T(8,128)(2,1)} %collective-permute-done.6.refs_6_), channel_id=1, source_target_pairs={{0,1},{1,0},{2,3},{3,2},{4,5},{5,4},{6,7},{7,6},{8,9},{9,8},{10,11... | collective-permute-start | bytes 1572872 | tf_op jit(solution)/shard_map/ppermute | solution.py:78
  42.7 1.2 collective-permute-done.9.refs_10_
  43.9 0.9 copy-done.6
  44.8 4.7 %project.1 = bf16[128,1024]{1,0:T(8,128)(2,1)} custom-call(s32[29]{0:T(128)S(1)} %fusion.36.place_ref, bf16[32,2048]{1,0:T(8,128)(2,1)S(1)} %constant_dynamic-update-slice_fusion.refs_0_, bf16[32,2048]{1,0:T(8,128)(2,1)S(1)} %copy-done.6, bf16[32,2048]{1,0:T(8,128)(2,1)S(1)} %collective-permute-done.4.refs_2_, ...), custom_call_target="tpu_custom_call" | custom-call | flops 536870912 | bytes 4980736 | tf_op jit(solution)/shard_map/project/pallas_call | solution.py:190
  50.1 3.4 %all-to-all-start.1 = ((bf16[4,32,1024]{2,1,0:T(8,128)(2,1)}), bf16[4,32,1024]{2,1,0:T(8,128)(2,1)S(1)}, u32[]{:S(2)}, u32[]{:S(2)}) async-start(bf16[4,32,1024]{2,1,0:T(8,128)(2,1)} %bitcast.5), calls=%async_computation.1 | async-start | bytes 524288 | tf_op jit(solution)/shard_map/all_to_all | solution.py:318
  54.6 7.9 %all-to-all-done.1 = bf16[4,32,1024]{2,1,0:T(8,128)(2,1)S(1)} async-done(((bf16[4,32,1024]{2,1,0:T(8,128)(2,1)}), bf16[4,32,1024]{2,1,0:T(8,128)(2,1)S(1)}, u32[]{:S(2)}, u32[]{:S(2)}) %all-to-all-start.1) | async-done | bytes 262176 | tf_op jit(solution)/shard_map/all_to_all | solution.py:318
  63.6 3.8 %collective-permute-start.14 = (bf16[32,1024]{1,0:T(8,128)(2,1)S(1)}, bf16[32,1024]{1,0:T(8,128)(2,1)S(1)}, u32[]{:S(2)}, u32[]{:S(2)}) collective-permute-start(bf16[32,1024]{1,0:T(8,128)(2,1)S(1)} %get-tuple-element.36), channel_id=1, source_target_pairs={{4,0},{6,2},{0,4},{2,6},{5,1},{7,3},{1,5},{3,7},{12,8},{14,10},{8,... | collective-permute-start | bytes 196616 | tf_op jit(solution)/shard_map/ppermute | solution.py:82
  67.5 1.5 collective-permute-done.15
  69.0 2.1 %collective-permute-done.14 = bf16[32,1024]{1,0:T(8,128)(2,1)S(1)} collective-permute-done((bf16[32,1024]{1,0:T(8,128)(2,1)S(1)}, bf16[32,1024]{1,0:T(8,128)(2,1)S(1)}, u32[]{:S(2)}, u32[]{:S(2)}) %collective-permute-start.14) | collective-permute-done | bytes 65568 | tf_op jit(solution)/shard_map/ppermute | solution.py:82
  71.1 2.0 collective-permute-done.13
  73.3 2.6 %collective-permute-start.17 = (bf16[128,1024]{1,0:T(8,128)(2,1)S(1)}, bf16[128,1024]{1,0:T(8,128)(2,1)}, u32[]{:S(2)}, u32[]{:S(2)}) collective-permute-start(bf16[128,1024]{1,0:T(8,128)(2,1)S(1)} %pad_maximum_fusion.refs_0_), channel_id=1, source_target_pairs={{16,0},{24,8},{0,16},{8,24},{17,1},{25,9},{1,17},{9,25},{18,2},{26... | collective-permute-start | bytes 786440 | tf_op jit(solution)/shard_map/ppermute | solution.py:82
  75.9 1.1 collective-permute-start.16
  77.0 3.7 %gate_up.2 = bf16[128,3712]{1,0:T(8,128)(2,1)S(1)} custom-call(f32[1,1024]{1,0:T(1,128)S(1)} %bitcast.56, bf16[128,1024]{1,0:T(8,128)(2,1)S(1)} %pad_maximum_fusion.refs_0_, bf16[1024,896]{1,0:T(8,128)(2,1)} %refs_3_.1, bf16[1024,896]{1,0:T(8,128)(2,1)} %refs_4_.3, bf16[1024,896]{1,0:T(8,128)(2,1)} %collective-permute-done.11.refs_3_.refs_5_, ...), custom_call_target="tpu_custom_call" | custom-call | flops 17302499328 | bytes 8519680 | tf_op jit(solution)/shard_map/gate_up/pallas_call | solution.py:240
  80.7 0.9 copy-done.3
  81.6 4.5 %all-to-all-start.2 = ((bf16[8,16,3712]{2,1,0:T(8,128)(2,1)}), bf16[8,16,3712]{2,1,0:T(8,128)(2,1)S(1)}, u32[]{:S(2)}, u32[]{:S(2)}) async-start(bf16[8,16,3712]{2,1,0:T(8,128)(2,1)} %bitcast.55), calls=%async_computation.2 | async-start | bytes 1900544 | tf_op jit(solution)/shard_map/all_to_all | solution.py:318
  86.1 7.0 %gate_up.3 = bf16[384,3712]{1,0:T(8,128)(2,1)S(1)} custom-call(f32[1,1024]{1,0:T(1,128)S(1)} %bitcast.57, bf16[128,1024]{1,0:T(8,128)(2,1)} %collective-permute-done.16.refs_0_, bf16[128,1024]{1,0:T(8,128)(2,1)} %collective-permute-done.17.refs_1_, bf16[128,1024]{1,0:T(8,128)(2,1)} %collective-permute-done.18.refs_2_, bf16[1024,896]{1,0:T(8,128)(2,1)} %refs_3_.1, ...), custom_call_target="tpu_custom_call" | custom-call | flops 69209997312 | bytes 10878976 | tf_op jit(solution)/shard_map/gate_up/pallas_call | solution.py:240
  93.2 1.5 copy-done.2
  94.7 1.4 all-to-all-done.2.refs_0_
  96.1 32.9 %all_to_all.25.refs_1_ = bf16[8,48,3712]{2,1,0:T(8,128)(2,1)S(1)} all-to-all(bf16[8,48,3712]{2,1,0:T(8,128)(2,1)} %bitcast.54), channel_id=1, replica_groups=mesh['x'=4,'l'=2,'y'=4,'z'=4,'core'=2] {'x','l'}, dimensions={0} | all-to-all | bytes 5701632 | tf_op jit(solution)/shard_map/all_to_all | solution.py:318
  128.9 3.8 %activate.1 = bf16[8,64,1792]{2,1,0:T(8,128)(2,1)S(1)} custom-call(bf16[8,16,3712]{2,1,0:T(8,128)(2,1)S(1)} %all-to-all-done.2.refs_0_, bf16[8,48,3712]{2,1,0:T(8,128)(2,1)S(1)} %all_to_all.25.refs_1_), custom_call_target="tpu_custom_call" | custom-call | bytes 5505024 | tf_op jit(solution)/shard_map/activate/pallas_call | solution.py:143
  132.8 1.2 copy-done.1
  134.0 4.3 %all-to-all-start.4 = ((bf16[8,64,1792]{2,1,0:T(8,128)(2,1)}), bf16[8,64,1792]{2,1,0:T(8,128)(2,1)}, u32[]{:S(2)}, u32[]{:S(2)}) async-start(bf16[8,64,1792]{2,1,0:T(8,128)(2,1)} %copy-done.1), calls=%async_computation.4 | async-start | bytes 3670016 | tf_op jit(solution)/shard_map/all_to_all | solution.py:318
  138.4 7.0 %collective-permute-start.19 = (bf16[896,1024]{1,0:T(8,128)(2,1)}, bf16[896,1024]{1,0:T(8,128)(2,1)}, u32[]{:S(2)}, u32[]{:S(2)}) collective-permute-start(bf16[896,1024]{1,0:T(8,128)(2,1)} %own.1), channel_id=1, source_target_pairs={{0,1},{1,0},{2,3},{3,2},{4,5},{5,4},{6,7},{7,6},{8,9},{9,8},{10,11... | collective-permute-start | bytes 5505032 | tf_op jit(solution)/shard_map/ppermute | solution.py:78
  145.3 3.8 %collective-permute-done.19.other = bf16[896,1024]{1,0:T(8,128)(2,1)} collective-permute-done((bf16[896,1024]{1,0:T(8,128)(2,1)}, bf16[896,1024]{1,0:T(8,128)(2,1)}, u32[]{:S(2)}, u32[]{:S(2)}) %collective-permute-start.19) | collective-permute-done | bytes 1835040 | tf_op jit(solution)/shard_map/ppermute | solution.py:78
  149.1 6.6 %all-to-all-done.4.hidden_ref = bf16[8,64,1792]{2,1,0:T(8,128)(2,1)} async-done(((bf16[8,64,1792]{2,1,0:T(8,128)(2,1)}), bf16[8,64,1792]{2,1,0:T(8,128)(2,1)}, u32[]{:S(2)}, u32[]{:S(2)}) %all-to-all-start.4) | async-done | bytes 1835040 | tf_op jit(solution)/shard_map/all_to_all | solution.py:318
  155.7 6.6 %down.1 = (bf16[128,1024]{1,0:T(8,128)(2,1)}, bf16[128,1024]{1,0:T(8,128)(2,1)}, bf16[128,1024]{1,0:T(8,128)(2,1)}, bf16[128,1024]{1,0:T(8,128)(2,1)}) custom-call(s32[29]{0:T(128)} %copy-done.8, bf16[8,64,1792]{2,1,0:T(8,128)(2,1)} %all-to-all-done.4.hidden_ref, bf16[896,1024]{1,0:T(8,128)(2,1)} %own.1, bf16[896,1024]{1,0:T(8,128)(2,1)} %collective-permute-done.19.other, ...), custom_call_target="tpu_custom_call" | custom-call | flops 1879048192 | bytes 6553600 | tf_op jit(solution)/shard_map/down/pallas_call | solution.py:293
  162.3 3.6 %collective-permute-start.20 = (bf16[128,1024]{1,0:T(8,128)(2,1)}, bf16[128,1024]{1,0:T(8,128)(2,1)S(1)}, u32[]{:S(2)}, u32[]{:S(2)}) collective-permute-start(bf16[128,1024]{1,0:T(8,128)(2,1)} %get-tuple-element.42), channel_id=1, source_target_pairs={{0,8},{8,16},{16,24},{24,0},{1,9},{9,17},{17,25},{25,1},{2,10},{10... | collective-permute-start | bytes 786440 | tf_op jit(solution)/shard_map/ppermute | solution.py:86
  166.0 6.3 %collective-permute-start.21 = (bf16[128,1024]{1,0:T(8,128)(2,1)}, bf16[128,1024]{1,0:T(8,128)(2,1)S(1)}, u32[]{:S(2)}, u32[]{:S(2)}) collective-permute-start(bf16[128,1024]{1,0:T(8,128)(2,1)} %get-tuple-element.43), channel_id=1, source_target_pairs={{0,16},{8,24},{16,0},{24,8},{1,17},{9,25},{17,1},{25,9},{2,18},{10... | collective-permute-start | bytes 786440 | tf_op jit(solution)/shard_map/ppermute | solution.py:86
  172.3 2.8 %collective-permute-done.20 = bf16[128,1024]{1,0:T(8,128)(2,1)S(1)} collective-permute-done((bf16[128,1024]{1,0:T(8,128)(2,1)}, bf16[128,1024]{1,0:T(8,128)(2,1)S(1)}, u32[]{:S(2)}, u32[]{:S(2)}) %collective-permute-start.20) | collective-permute-done | bytes 262176 | tf_op jit(solution)/shard_map/ppermute | solution.py:86
  175.1 4.3 %collective-permute-done.21 = bf16[128,1024]{1,0:T(8,128)(2,1)S(1)} collective-permute-done((bf16[128,1024]{1,0:T(8,128)(2,1)}, bf16[128,1024]{1,0:T(8,128)(2,1)S(1)}, u32[]{:S(2)}, u32[]{:S(2)}) %collective-permute-start.21) | collective-permute-done | bytes 262176 | tf_op jit(solution)/shard_map/ppermute | solution.py:86
  179.4 1.1 fusion.37
  180.5 9.0 %collective-permute-start.23 = (bf16[32,1024]{1,0:T(8,128)(2,1)S(1)}, bf16[32,1024]{1,0:T(8,128)(2,1)S(1)}, u32[]{:S(2)}, u32[]{:S(2)}) collective-permute-start(bf16[32,1024]{1,0:T(8,128)(2,1)S(1)} %get-tuple-element.51), channel_id=1, source_target_pairs={{0,2},{2,4},{4,6},{6,0},{1,3},{3,5},{5,7},{7,1},{8,10},{10,12},{12... | collective-permute-start | bytes 196616 | tf_op jit(solution)/shard_map/ppermute | solution.py:86
  189.5 4.2 %collective-permute-start.24 = (bf16[32,1024]{1,0:T(8,128)(2,1)S(1)}, bf16[32,1024]{1,0:T(8,128)(2,1)S(1)}, u32[]{:S(2)}, u32[]{:S(2)}) collective-permute-start(bf16[32,1024]{1,0:T(8,128)(2,1)S(1)} %get-tuple-element.53), channel_id=1, source_target_pairs={{0,4},{2,6},{4,0},{6,2},{1,5},{3,7},{5,1},{7,3},{8,12},{10,14},{12... | collective-permute-start | bytes 196616 | tf_op jit(solution)/shard_map/ppermute | solution.py:86
  193.7 1.3 collective-permute-done.25
  194.9 1.7 collective-permute-done.24
  196.6 6.1 %collective-permute-start.26 = (bf16[16,1024]{1,0:T(8,128)(2,1)S(1)}, bf16[16,1024]{1,0:T(8,128)(2,1)S(1)}, u32[]{:S(2)}, u32[]{:S(2)}) collective-permute-start(bf16[16,1024]{1,0:T(8,128)(2,1)S(1)} %broadcast_select_fusion.2), channel_id=1, source_target_pairs={{0,1},{1,0},{2,3},{3,2},{4,5},{5,4},{6,7},{7,6},{8,9},{9,8},{10,11... | collective-permute-start | bytes 98312 | tf_op jit(solution)/shard_map/ppermute | solution.py:78
  (75 shorter events, 11.2 us)
Async XLA Ops:
  0.0 7.0 %copy-start = (bf16[4,256,1024]{2,1,0:T(8,128)(2,1)S(1)}, bf16[4,256,1024]{2,1,0:T(8,128)(2,1)}, u32[]{:S(2)}) copy-start(bf16[4,256,1024]{2,1,0:T(8,128)(2,1)} %param.15) | copy-start | bytes 6291460
  0.0 25.3 %collective-permute-start.1 = (bf16[256,1024]{1,0:T(8,128)(2,1)}, bf16[256,1024]{1,0:T(8,128)(2,1)S(1)}, u32[]{:S(2)}, u32[]{:S(2)}) collective-permute-start(bf16[256,1024]{1,0:T(8,128)(2,1)} %refs_4_.2), channel_id=1, source_target_pairs={{24,0},{0,8},{8,16},{16,24},{25,1},{1,9},{9,17},{17,25},{26,2},{2,... | collective-permute-start | bytes 1572872 | tf_op jit(solution)/shard_map/ppermute | solution.py:82
  2.1 23.1 %collective-permute-start = (bf16[256,1024]{1,0:T(8,128)(2,1)}, bf16[256,1024]{1,0:T(8,128)(2,1)}, u32[]{:S(2)}, u32[]{:S(2)}) collective-permute-start(bf16[256,1024]{1,0:T(8,128)(2,1)} %refs_4_.2), channel_id=1, source_target_pairs={{8,0},{16,8},{24,16},{0,24},{9,1},{17,9},{25,17},{1,25},{10,2},{18... | collective-permute-start | bytes 1572872 | tf_op jit(solution)/shard_map/ppermute | solution.py:82
  5.1 3.7 %copy-start.9 = (bf16[4,256,1024]{2,1,0:T(8,128)(2,1)S(1)}, bf16[4,256,1024]{2,1,0:T(8,128)(2,1)}, u32[]{:S(2)}) copy-start(bf16[4,256,1024]{2,1,0:T(8,128)(2,1)} %param.16) | copy-start | bytes 6291460
  8.5 9.7 %copy-start.4 = (bf16[256,1024]{1,0:T(8,128)(2,1)S(1)}, bf16[256,1024]{1,0:T(8,128)(2,1)}, u32[]{:S(2)}) copy-start(bf16[256,1024]{1,0:T(8,128)(2,1)} %refs_4_.2) | copy-start | bytes 1572868
  10.0 15.2 %all-to-all-start = ((bf16[4,4,2048]{2,1,0:T(4,128)(2,1)}), bf16[4,4,2048]{2,1,0:T(4,128)(2,1)S(1)}, u32[]{:S(2)}, u32[]{:S(2)}) async-start(bf16[4,4,2048]{2,1,0:T(4,128)(2,1)} %reshape.71), calls=%async_computation | async-start | bytes 131072 | tf_op jit(solution)/shard_map/all_to_all | solution.py:318
  18.2 19.7 %collective-permute-start.6 = (bf16[256,1024]{1,0:T(8,128)(2,1)S(1)}, bf16[256,1024]{1,0:T(8,128)(2,1)}, u32[]{:S(2)}, u32[]{:S(2)}) collective-permute-start(bf16[256,1024]{1,0:T(8,128)(2,1)S(1)} %copy-done.4), channel_id=1, source_target_pairs={{16,0},{24,8},{0,16},{8,24},{17,1},{25,9},{1,17},{9,25},{18,2},{26... | collective-permute-start | bytes 1572872 | tf_op jit(solution)/shard_map/ppermute | solution.py:82
  25.3 3.6 %collective-permute-start.2 = (bf16[16,2048]{1,0:T(8,128)(2,1)S(1)}, bf16[16,2048]{1,0:T(8,128)(2,1)S(1)}, u32[]{:S(2)}, u32[]{:S(2)}) collective-permute-start(bf16[16,2048]{1,0:T(8,128)(2,1)S(1)} %reshape.72), channel_id=1, source_target_pairs={{0,32},{32,0},{1,33},{33,1},{2,34},{34,2},{3,35},{35,3},{4,36},{36... | collective-permute-start | bytes 196616 | tf_op jit(solution)/shard_map/ppermute | solution.py:78
  28.9 9.0 %collective-permute-start.5 = (bf16[32,2048]{1,0:T(8,128)(2,1)S(1)}, bf16[32,2048]{1,0:T(8,128)(2,1)S(1)}, u32[]{:S(2)}, u32[]{:S(2)}) collective-permute-start(bf16[32,2048]{1,0:T(8,128)(2,1)S(1)} %constant_dynamic-update-slice_fusion.refs_0_), channel_id=1, source_target_pairs={{192,0},{0,64},{64,128},{128,192},{193,1},{1,65},{65,129},{129,193... | collective-permute-start | bytes 393224 | tf_op jit(solution)/shard_map/ppermute | solution.py:82
  30.1 8.3 %collective-permute-start.4 = (bf16[32,2048]{1,0:T(8,128)(2,1)S(1)}, bf16[32,2048]{1,0:T(8,128)(2,1)S(1)}, u32[]{:S(2)}, u32[]{:S(2)}) collective-permute-start(bf16[32,2048]{1,0:T(8,128)(2,1)S(1)} %constant_dynamic-update-slice_fusion.refs_0_), channel_id=1, source_target_pairs={{128,0},{192,64},{0,128},{64,192},{129,1},{193,65},{1,129},{65,193... | collective-permute-start | bytes 393224 | tf_op jit(solution)/shard_map/ppermute | solution.py:82
  32.6 5.9 %collective-permute-start.3 = (bf16[32,2048]{1,0:T(8,128)(2,1)S(1)}, bf16[32,2048]{1,0:T(8,128)(2,1)S(1)}, u32[]{:S(2)}, u32[]{:S(2)}) collective-permute-start(bf16[32,2048]{1,0:T(8,128)(2,1)S(1)} %constant_dynamic-update-slice_fusion.refs_0_), channel_id=1, source_target_pairs={{64,0},{128,64},{192,128},{0,192},{65,1},{129,65},{193,129},{1,193... | collective-permute-start | bytes 393224 | tf_op jit(solution)/shard_map/ppermute | solution.py:82
  33.7 9.0 %collective-permute-start.7 = (bf16[256,1024]{1,0:T(8,128)(2,1)S(1)}, bf16[256,1024]{1,0:T(8,128)(2,1)}, u32[]{:S(2)}, u32[]{:S(2)}) collective-permute-start(bf16[256,1024]{1,0:T(8,128)(2,1)S(1)} %copy-done.4), channel_id=1, source_target_pairs={{0,1},{1,0},{2,3},{3,2},{4,5},{5,4},{6,7},{7,6},{8,9},{9,8},{10,11... | collective-permute-start | bytes 1572872 | tf_op jit(solution)/shard_map/ppermute | solution.py:78
  37.8 4.9 %collective-permute-start.8 = (bf16[256,1024]{1,0:T(8,128)(2,1)}, bf16[256,1024]{1,0:T(8,128)(2,1)}, u32[]{:S(2)}, u32[]{:S(2)}) collective-permute-start(bf16[256,1024]{1,0:T(8,128)(2,1)} %collective-permute-done.refs_5_), channel_id=1, source_target_pairs={{0,1},{1,0},{2,3},{3,2},{4,5},{5,4},{6,7},{7,6},{8,9},{9,8},{10,11... | collective-permute-start | bytes 1572872 | tf_op jit(solution)/shard_map/ppermute | solution.py:78
  37.8 4.9 %collective-permute-start.10 = (bf16[256,1024]{1,0:T(8,128)(2,1)S(1)}, bf16[256,1024]{1,0:T(8,128)(2,1)}, u32[]{:S(2)}, u32[]{:S(2)}) collective-permute-start(bf16[256,1024]{1,0:T(8,128)(2,1)S(1)} %collective-permute-done.1.refs_7_), channel_id=1, source_target_pairs={{0,1},{1,0},{2,3},{3,2},{4,5},{5,4},{6,7},{7,6},{8,9},{9,8},{10,11... | collective-permute-start | bytes 1572872 | tf_op jit(solution)/shard_map/ppermute | solution.py:78
  38.4 0.6 copy-start.5
  39.1 4.8 %collective-permute-start.9 = (bf16[256,1024]{1,0:T(8,128)(2,1)}, bf16[256,1024]{1,0:T(8,128)(2,1)}, u32[]{:S(2)}, u32[]{:S(2)}) collective-permute-start(bf16[256,1024]{1,0:T(8,128)(2,1)} %collective-permute-done.6.refs_6_), channel_id=1, source_target_pairs={{0,1},{1,0},{2,3},{3,2},{4,5},{5,4},{6,7},{7,6},{8,9},{9,8},{10,11... | collective-permute-start | bytes 1572872 | tf_op jit(solution)/shard_map/ppermute | solution.py:78
  42.0 20.5 %copy-start.7 = (f32[1024]{0:T(1024)S(1)}, f32[1024]{0:T(1024)}, u32[]{:S(2)}) copy-start(f32[1024]{0:T(1024)} %param.21) | copy-start | bytes 12292
  42.7 6.8 %copy-start.8 = (s32[29]{0:T(128)}, s32[29]{0:T(128)S(1)}, u32[]{:S(2)}) copy-start(s32[29]{0:T(128)S(1)} %fusion.36.place_ref) | copy-start | bytes 352
  43.9 0.9 copy-start.6
  49.5 13.7 %collective-permute-start.11 = (bf16[1024,896]{1,0:T(8,128)(2,1)}, bf16[1024,896]{1,0:T(8,128)(2,1)}, u32[]{:S(2)}, u32[]{:S(2)}) collective-permute-start(bf16[1024,896]{1,0:T(8,128)(2,1)} %refs_3_.1), channel_id=1, source_target_pairs={{0,1},{1,0},{2,3},{3,2},{4,5},{5,4},{6,7},{7,6},{8,9},{9,8},{10,11... | collective-permute-start | bytes 5505032 | tf_op jit(solution)/shard_map/ppermute | solution.py:78
  50.0 13.3 %collective-permute-start.12 = (bf16[1024,896]{1,0:T(8,128)(2,1)}, bf16[1024,896]{1,0:T(8,128)(2,1)}, u32[]{:S(2)}, u32[]{:S(2)}) collective-permute-start(bf16[1024,896]{1,0:T(8,128)(2,1)} %refs_4_.3), channel_id=1, source_target_pairs={{0,1},{1,0},{2,3},{3,2},{4,5},{5,4},{6,7},{7,6},{8,9},{9,8},{10,11... | collective-permute-start | bytes 5505032 | tf_op jit(solution)/shard_map/ppermute | solution.py:78
  50.1 12.4 %all-to-all-start.1 = ((bf16[4,32,1024]{2,1,0:T(8,128)(2,1)}), bf16[4,32,1024]{2,1,0:T(8,128)(2,1)S(1)}, u32[]{:S(2)}, u32[]{:S(2)}) async-start(bf16[4,32,1024]{2,1,0:T(8,128)(2,1)} %bitcast.5), calls=%async_computation.1 | async-start | bytes 524288 | tf_op jit(solution)/shard_map/all_to_all | solution.py:318
  63.2 5.7 %collective-permute-start.15 = (bf16[32,1024]{1,0:T(8,128)(2,1)S(1)}, bf16[32,1024]{1,0:T(8,128)(2,1)S(1)}, u32[]{:S(2)}, u32[]{:S(2)}) collective-permute-start(bf16[32,1024]{1,0:T(8,128)(2,1)S(1)} %get-tuple-element.36), channel_id=1, source_target_pairs={{6,0},{0,2},{2,4},{4,6},{7,1},{1,3},{3,5},{5,7},{14,8},{8,10},{10,... | collective-permute-start | bytes 196616 | tf_op jit(solution)/shard_map/ppermute | solution.py:82
  63.6 7.4 %collective-permute-start.14 = (bf16[32,1024]{1,0:T(8,128)(2,1)S(1)}, bf16[32,1024]{1,0:T(8,128)(2,1)S(1)}, u32[]{:S(2)}, u32[]{:S(2)}) collective-permute-start(bf16[32,1024]{1,0:T(8,128)(2,1)S(1)} %get-tuple-element.36), channel_id=1, source_target_pairs={{4,0},{6,2},{0,4},{2,6},{5,1},{7,3},{1,5},{3,7},{12,8},{14,10},{8,... | collective-permute-start | bytes 196616 | tf_op jit(solution)/shard_map/ppermute | solution.py:82
  67.5 5.6 %collective-permute-start.13 = (bf16[32,1024]{1,0:T(8,128)(2,1)S(1)}, bf16[32,1024]{1,0:T(8,128)(2,1)S(1)}, u32[]{:S(2)}, u32[]{:S(2)}) collective-permute-start(bf16[32,1024]{1,0:T(8,128)(2,1)S(1)} %get-tuple-element.36), channel_id=1, source_target_pairs={{2,0},{4,2},{6,4},{0,6},{3,1},{5,3},{7,5},{1,7},{10,8},{12,10},{14... | collective-permute-start | bytes 196616 | tf_op jit(solution)/shard_map/ppermute | solution.py:82
  73.1 13.0 %collective-permute-start.18 = (bf16[128,1024]{1,0:T(8,128)(2,1)S(1)}, bf16[128,1024]{1,0:T(8,128)(2,1)}, u32[]{:S(2)}, u32[]{:S(2)}) collective-permute-start(bf16[128,1024]{1,0:T(8,128)(2,1)S(1)} %pad_maximum_fusion.refs_0_), channel_id=1, source_target_pairs={{24,0},{0,8},{8,16},{16,24},{25,1},{1,9},{9,17},{17,25},{26,2},{2,... | collective-permute-start | bytes 786440 | tf_op jit(solution)/shard_map/ppermute | solution.py:82
  73.3 12.8 %collective-permute-start.17 = (bf16[128,1024]{1,0:T(8,128)(2,1)S(1)}, bf16[128,1024]{1,0:T(8,128)(2,1)}, u32[]{:S(2)}, u32[]{:S(2)}) collective-permute-start(bf16[128,1024]{1,0:T(8,128)(2,1)S(1)} %pad_maximum_fusion.refs_0_), channel_id=1, source_target_pairs={{16,0},{24,8},{0,16},{8,24},{17,1},{25,9},{1,17},{9,25},{18,2},{26... | collective-permute-start | bytes 786440 | tf_op jit(solution)/shard_map/ppermute | solution.py:82
  75.9 10.2 %collective-permute-start.16 = (bf16[128,1024]{1,0:T(8,128)(2,1)S(1)}, bf16[128,1024]{1,0:T(8,128)(2,1)}, u32[]{:S(2)}, u32[]{:S(2)}) collective-permute-start(bf16[128,1024]{1,0:T(8,128)(2,1)S(1)} %pad_maximum_fusion.refs_0_), channel_id=1, source_target_pairs={{8,0},{16,8},{24,16},{0,24},{9,1},{17,9},{25,17},{1,25},{10,2},{18... | collective-permute-start | bytes 786440 | tf_op jit(solution)/shard_map/ppermute | solution.py:82
  80.7 0.9 copy-start.3
  81.6 14.5 %all-to-all-start.2 = ((bf16[8,16,3712]{2,1,0:T(8,128)(2,1)}), bf16[8,16,3712]{2,1,0:T(8,128)(2,1)S(1)}, u32[]{:S(2)}, u32[]{:S(2)}) async-start(bf16[8,16,3712]{2,1,0:T(8,128)(2,1)} %bitcast.55), calls=%async_computation.2 | async-start | bytes 1900544 | tf_op jit(solution)/shard_map/all_to_all | solution.py:318
  93.1 1.5 copy-start.2
  132.8 1.3 copy-start.1
  134.0 21.7 %all-to-all-start.4 = ((bf16[8,64,1792]{2,1,0:T(8,128)(2,1)}), bf16[8,64,1792]{2,1,0:T(8,128)(2,1)}, u32[]{:S(2)}, u32[]{:S(2)}) async-start(bf16[8,64,1792]{2,1,0:T(8,128)(2,1)} %copy-done.1), calls=%async_computation.4 | async-start | bytes 3670016 | tf_op jit(solution)/shard_map/all_to_all | solution.py:318
  138.4 10.7 %collective-permute-start.19 = (bf16[896,1024]{1,0:T(8,128)(2,1)}, bf16[896,1024]{1,0:T(8,128)(2,1)}, u32[]{:S(2)}, u32[]{:S(2)}) collective-permute-start(bf16[896,1024]{1,0:T(8,128)(2,1)} %own.1), channel_id=1, source_target_pairs={{0,1},{1,0},{2,3},{3,2},{4,5},{5,4},{6,7},{7,6},{8,9},{9,8},{10,11... | collective-permute-start | bytes 5505032 | tf_op jit(solution)/shard_map/ppermute | solution.py:78
  162.3 12.7 %collective-permute-start.20 = (bf16[128,1024]{1,0:T(8,128)(2,1)}, bf16[128,1024]{1,0:T(8,128)(2,1)S(1)}, u32[]{:S(2)}, u32[]{:S(2)}) collective-permute-start(bf16[128,1024]{1,0:T(8,128)(2,1)} %get-tuple-element.42), channel_id=1, source_target_pairs={{0,8},{8,16},{16,24},{24,0},{1,9},{9,17},{17,25},{25,1},{2,10},{10... | collective-permute-start | bytes 786440 | tf_op jit(solution)/shard_map/ppermute | solution.py:86
  166.0 13.4 %collective-permute-start.21 = (bf16[128,1024]{1,0:T(8,128)(2,1)}, bf16[128,1024]{1,0:T(8,128)(2,1)S(1)}, u32[]{:S(2)}, u32[]{:S(2)}) collective-permute-start(bf16[128,1024]{1,0:T(8,128)(2,1)} %get-tuple-element.43), channel_id=1, source_target_pairs={{0,16},{8,24},{16,0},{24,8},{1,17},{9,25},{17,1},{25,9},{2,18},{10... | collective-permute-start | bytes 786440 | tf_op jit(solution)/shard_map/ppermute | solution.py:86
  172.3 7.1 %collective-permute-start.22 = (bf16[128,1024]{1,0:T(8,128)(2,1)}, bf16[128,1024]{1,0:T(8,128)(2,1)S(1)}, u32[]{:S(2)}, u32[]{:S(2)}) collective-permute-start(bf16[128,1024]{1,0:T(8,128)(2,1)} %get-tuple-element.44), channel_id=1, source_target_pairs={{0,24},{8,0},{16,8},{24,16},{1,25},{9,1},{17,9},{25,17},{2,26},{10... | collective-permute-start | bytes 786440 | tf_op jit(solution)/shard_map/ppermute | solution.py:86
  180.5 13.2 %collective-permute-start.23 = (bf16[32,1024]{1,0:T(8,128)(2,1)S(1)}, bf16[32,1024]{1,0:T(8,128)(2,1)S(1)}, u32[]{:S(2)}, u32[]{:S(2)}) collective-permute-start(bf16[32,1024]{1,0:T(8,128)(2,1)S(1)} %get-tuple-element.51), channel_id=1, source_target_pairs={{0,2},{2,4},{4,6},{6,0},{1,3},{3,5},{5,7},{7,1},{8,10},{10,12},{12... | collective-permute-start | bytes 196616 | tf_op jit(solution)/shard_map/ppermute | solution.py:86
  189.5 5.4 %collective-permute-start.25 = (bf16[32,1024]{1,0:T(8,128)(2,1)S(1)}, bf16[32,1024]{1,0:T(8,128)(2,1)S(1)}, u32[]{:S(2)}, u32[]{:S(2)}) collective-permute-start(bf16[32,1024]{1,0:T(8,128)(2,1)S(1)} %get-tuple-element.52), channel_id=1, source_target_pairs={{0,6},{2,0},{4,2},{6,4},{1,7},{3,1},{5,3},{7,5},{8,14},{10,8},{12,... | collective-permute-start | bytes 196616 | tf_op jit(solution)/shard_map/ppermute | solution.py:86
  189.5 7.1 %collective-permute-start.24 = (bf16[32,1024]{1,0:T(8,128)(2,1)S(1)}, bf16[32,1024]{1,0:T(8,128)(2,1)S(1)}, u32[]{:S(2)}, u32[]{:S(2)}) collective-permute-start(bf16[32,1024]{1,0:T(8,128)(2,1)S(1)} %get-tuple-element.53), channel_id=1, source_target_pairs={{0,4},{2,6},{4,0},{6,2},{1,5},{3,7},{5,1},{7,3},{8,12},{10,14},{12... | collective-permute-start | bytes 196616 | tf_op jit(solution)/shard_map/ppermute | solution.py:86
  196.6 7.0 %collective-permute-start.26 = (bf16[16,1024]{1,0:T(8,128)(2,1)S(1)}, bf16[16,1024]{1,0:T(8,128)(2,1)S(1)}, u32[]{:S(2)}, u32[]{:S(2)}) collective-permute-start(bf16[16,1024]{1,0:T(8,128)(2,1)S(1)} %broadcast_select_fusion.2), channel_id=1, source_target_pairs={{0,1},{1,0},{2,3},{3,2},{4,5},{5,4},{6,7},{7,6},{8,9},{9,8},{10,11... | collective-permute-start | bytes 98312 | tf_op jit(solution)/shard_map/ppermute | solution.py:78

commit v9 on v8

--- a/solution.py
+++ b/solution.py
@@ -148,7 +148,7 @@
         scratch_shapes=[pltpu.VMEM(part.shape, jnp.bfloat16) for part in parts]
         + [pltpu.VMEM((rows, width), jnp.bfloat16), pltpu.SemaphoreType.DMA((2 + groups,))],
         name="activate",
-        **params(12, 0, 6 * groups * rows * width),
+        **params(60, 0, 6 * groups * rows * width),
     )(*parts)
 
 

time: 205 us -> 202 us (0.985)
  starting transfers between devices: 83.9 us -> 79.7 us
  waiting for transfers between devices: 45.5 us -> 48.3 us
  local copies, waits for them, and re-layouts: 9.21 us -> 7.08 us
    ppermute x6, starting transfers between devices: 23.1 us -> 16.5 us  [ring_to(): return lax.ppermute(block, axis, [(i, (i + shift) % 4) for i in range(4)])]
    ppermute x9, starting transfers between devices: 22.2 us -> 24.5 us  [swap(): return lax.ppermute(block, axis, [(0, 1), (1, 0)])]
    unnamed x22 -> x18, local copies, waits for them, and re-layouts: 5.3 us -> 3.16 us
  transfers between devices with their start and end apart: 31 -> 31, of which waited for: 15 -> 16; matrix products, arithmetic and copies ran while one was open for 4% -> 4% of each run, Pallas kernels for 5% -> 5%
where the time goes in v9:
time: 202 us; the launch traced here: 201 us
  starting transfers between devices  79.7 us (39%)
  waiting for transfers between devices  48.3 us (24%)
  blocking collectives  33.4 us (17%)
  Pallas kernels  25.3 us (13%)
  local copies, waits for them, and re-layouts  7.08 us (4%)
  other arithmetic  3.82 us (2%)
  matrix products  3 us (1%)
    all_to_all x1, blocking collectives, exchange(): return lax.all_to_all(pieces, axis, split_axis=0, concat_axis=0, tiled=True)  33.4 us
    ppermute x9, starting transfers between devices, swap(): return lax.ppermute(block, axis, [(0, 1), (1, 0)])  24.5 us
    all_to_all x4, waiting for transfers between devices, exchange(): return lax.all_to_all(pieces, axis, split_axis=0, concat_axis=0, tiled=True)  22.2 us
    all_to_all x4, starting transfers between devices, exchange(): return lax.all_to_all(pieces, axis, split_axis=0, concat_axis=0, tiled=True)  20.5 us
    ppermute x12, starting transfers between devices, ring_from(): return lax.ppermute(block, axis, [((i + shift) % 4, i) for i in range(4)])  18.2 us
    ppermute x6, starting transfers between devices, ring_to(): return lax.ppermute(block, axis, [(i, (i + shift) % 4) for i in range(4)])  16.5 us
    ppermute x6, waiting for transfers between devices, ring_to(): return lax.ppermute(block, axis, [(i, (i + shift) % 4) for i in range(4)])  12 us
    pallas_call x2, Pallas kernels, gate_up(): pl.pallas_call(gate_up_kernel, in_specs=[VMEM] + [ANY] * (len(pieces) + 4...  10.1 us
  transfers between devices with their start and end apart: 31, of which 16 were waited for; matrix products, arithmetic and copies ran while one was open for 4% of the time, Pallas kernels for 5%

profile of v9, /device:TPU:1, one launch (start us, length us, event | category | flops | bytes accessed | tf_op | source)
XLA Modules:
  0.0 200.9 jit_solution(16057201992565773347)
XLA Ops:
  0.0 2.1 %collective-permute-start.1 = (bf16[256,1024]{1,0:T(8,128)(2,1)}, bf16[256,1024]{1,0:T(8,128)(2,1)S(1)}, u32[]{:S(2)}, u32[]{:S(2)}) collective-permute-start(bf16[256,1024]{1,0:T(8,128)(2,1)} %refs_4_.2), channel_id=1, source_target_pairs={{24,0},{0,8},{8,16},{16,24},{25,1},{1,9},{9,17},{17,25},{26,2},{2,... | collective-permute-start | bytes 1572872 | tf_op jit(solution)/shard_map/ppermute | solution.py:82
  2.1 1.5 collective-permute-start
  5.1 0.9 convert_bitcast_fusion
  6.0 1.0 fusion.30
  7.0 1.6 fusion.39
  10.0 8.2 %all-to-all-start = ((bf16[4,4,2048]{2,1,0:T(4,128)(2,1)}), bf16[4,4,2048]{2,1,0:T(4,128)(2,1)S(1)}, u32[]{:S(2)}, u32[]{:S(2)}) async-start(bf16[4,4,2048]{2,1,0:T(4,128)(2,1)} %reshape.71), calls=%async_computation | async-start | bytes 131072 | tf_op jit(solution)/shard_map/all_to_all | solution.py:318
  18.2 1.6 collective-permute-start.6
  19.7 5.5 %all-to-all-done = bf16[4,4,2048]{2,1,0:T(4,128)(2,1)S(1)} async-done(((bf16[4,4,2048]{2,1,0:T(4,128)(2,1)}), bf16[4,4,2048]{2,1,0:T(4,128)(2,1)S(1)}, u32[]{:S(2)}, u32[]{:S(2)}) %all-to-all-start) | async-done | bytes 65568 | tf_op jit(solution)/shard_map/all_to_all | solution.py:318
  26.1 2.8 %collective-permute-done.2 = bf16[16,2048]{1,0:T(8,128)(2,1)S(1)} collective-permute-done((bf16[16,2048]{1,0:T(8,128)(2,1)S(1)}, bf16[16,2048]{1,0:T(8,128)(2,1)S(1)}, u32[]{:S(2)}, u32[]{:S(2)}) %collective-permute-start.2) | collective-permute-done | bytes 65568 | tf_op jit(solution)/shard_map/ppermute | solution.py:78
  28.9 1.2 collective-permute-start.5
  30.1 2.5 %collective-permute-start.4 = (bf16[32,2048]{1,0:T(8,128)(2,1)S(1)}, bf16[32,2048]{1,0:T(8,128)(2,1)S(1)}, u32[]{:S(2)}, u32[]{:S(2)}) collective-permute-start(bf16[32,2048]{1,0:T(8,128)(2,1)S(1)} %constant_dynamic-update-slice_fusion.refs_0_), channel_id=1, source_target_pairs={{128,0},{192,64},{0,128},{64,192},{129,1},{193,65},{1,129},{65,193... | collective-permute-start | bytes 393224 | tf_op jit(solution)/shard_map/ppermute | solution.py:82
  32.6 1.2 collective-permute-start.3
  33.7 4.1 %collective-permute-start.7 = (bf16[256,1024]{1,0:T(8,128)(2,1)S(1)}, bf16[256,1024]{1,0:T(8,128)(2,1)}, u32[]{:S(2)}, u32[]{:S(2)}) collective-permute-start(bf16[256,1024]{1,0:T(8,128)(2,1)S(1)} %copy-done.2), channel_id=1, source_target_pairs={{0,1},{1,0},{2,3},{3,2},{4,5},{5,4},{6,7},{7,6},{8,9},{9,8},{10,11... | collective-permute-start | bytes 1572872 | tf_op jit(solution)/shard_map/ppermute | solution.py:78
  39.1 3.0 %collective-permute-start.9 = (bf16[256,1024]{1,0:T(8,128)(2,1)}, bf16[256,1024]{1,0:T(8,128)(2,1)}, u32[]{:S(2)}, u32[]{:S(2)}) collective-permute-start(bf16[256,1024]{1,0:T(8,128)(2,1)} %collective-permute-done.6.refs_6_), channel_id=1, source_target_pairs={{0,1},{1,0},{2,3},{3,2},{4,5},{5,4},{6,7},{7,6},{8,9},{9,8},{10,11... | collective-permute-start | bytes 1572872 | tf_op jit(solution)/shard_map/ppermute | solution.py:78
  42.7 1.2 collective-permute-done.9.refs_10_
  43.9 0.9 copy-done.4
  44.8 4.7 %project.1 = bf16[128,1024]{1,0:T(8,128)(2,1)} custom-call(s32[29]{0:T(128)S(1)} %fusion.36.place_ref, bf16[32,2048]{1,0:T(8,128)(2,1)S(1)} %constant_dynamic-update-slice_fusion.refs_0_, bf16[32,2048]{1,0:T(8,128)(2,1)S(1)} %copy-done.4, bf16[32,2048]{1,0:T(8,128)(2,1)S(1)} %collective-permute-done.4.refs_2_, ...), custom_call_target="tpu_custom_call" | custom-call | flops 536870912 | bytes 4980736 | tf_op jit(solution)/shard_map/project/pallas_call | solution.py:190
  50.1 3.4 %all-to-all-start.1 = ((bf16[4,32,1024]{2,1,0:T(8,128)(2,1)}), bf16[4,32,1024]{2,1,0:T(8,128)(2,1)S(1)}, u32[]{:S(2)}, u32[]{:S(2)}) async-start(bf16[4,32,1024]{2,1,0:T(8,128)(2,1)} %bitcast.5), calls=%async_computation.1 | async-start | bytes 524288 | tf_op jit(solution)/shard_map/all_to_all | solution.py:318
  53.5 0.9 constant_dynamic-slice_fusion
  54.6 7.9 %all-to-all-done.1 = bf16[4,32,1024]{2,1,0:T(8,128)(2,1)S(1)} async-done(((bf16[4,32,1024]{2,1,0:T(8,128)(2,1)}), bf16[4,32,1024]{2,1,0:T(8,128)(2,1)S(1)}, u32[]{:S(2)}, u32[]{:S(2)}) %all-to-all-start.1) | async-done | bytes 262176 | tf_op jit(solution)/shard_map/all_to_all | solution.py:318
  63.7 3.8 %collective-permute-start.14 = (bf16[32,1024]{1,0:T(8,128)(2,1)S(1)}, bf16[32,1024]{1,0:T(8,128)(2,1)S(1)}, u32[]{:S(2)}, u32[]{:S(2)}) collective-permute-start(bf16[32,1024]{1,0:T(8,128)(2,1)S(1)} %get-tuple-element.36), channel_id=1, source_target_pairs={{4,0},{6,2},{0,4},{2,6},{5,1},{7,3},{1,5},{3,7},{12,8},{14,10},{8,... | collective-permute-start | bytes 196616 | tf_op jit(solution)/shard_map/ppermute | solution.py:82
  67.5 1.5 collective-permute-done.15
  69.0 2.2 %collective-permute-done.14 = bf16[32,1024]{1,0:T(8,128)(2,1)S(1)} collective-permute-done((bf16[32,1024]{1,0:T(8,128)(2,1)S(1)}, bf16[32,1024]{1,0:T(8,128)(2,1)S(1)}, u32[]{:S(2)}, u32[]{:S(2)}) %collective-permute-start.14) | collective-permute-done | bytes 65568 | tf_op jit(solution)/shard_map/ppermute | solution.py:82
  71.1 1.9 collective-permute-done.13
  73.3 2.6 %collective-permute-start.17 = (bf16[128,1024]{1,0:T(8,128)(2,1)S(1)}, bf16[128,1024]{1,0:T(8,128)(2,1)S(1)}, u32[]{:S(2)}, u32[]{:S(2)}) collective-permute-start(bf16[128,1024]{1,0:T(8,128)(2,1)S(1)} %pad_maximum_fusion.refs_0_), channel_id=1, source_target_pairs={{16,0},{24,8},{0,16},{8,24},{17,1},{25,9},{1,17},{9,25},{18,2},{26... | collective-permute-start | bytes 786440 | tf_op jit(solution)/shard_map/ppermute | solution.py:82
  75.9 1.1 collective-permute-start.16
  77.0 4.6 %gate_up.2 = bf16[128,3712]{1,0:T(8,128)(2,1)} custom-call(f32[1,1024]{1,0:T(1,128)S(1)} %bitcast.55, bf16[128,1024]{1,0:T(8,128)(2,1)S(1)} %pad_maximum_fusion.refs_0_, bf16[1024,896]{1,0:T(8,128)(2,1)} %refs_3_.1, bf16[1024,896]{1,0:T(8,128)(2,1)} %refs_4_.3, bf16[1024,896]{1,0:T(8,128)(2,1)} %collective-permute-done.11.refs_3_.refs_5_, ...), custom_call_target="tpu_custom_call" | custom-call | flops 17302499328 | bytes 8519680 | tf_op jit(solution)/shard_map/gate_up/pallas_call | solution.py:240
  81.6 4.6 %all-to-all-start.2 = ((bf16[8,16,3712]{2,1,0:T(8,128)(2,1)}), bf16[8,16,3712]{2,1,0:T(8,128)(2,1)}, u32[]{:S(2)}, u32[]{:S(2)}) async-start(bf16[8,16,3712]{2,1,0:T(8,128)(2,1)} %bitcast.6), calls=%async_computation.2 | async-start | bytes 1900544 | tf_op jit(solution)/shard_map/all_to_all | solution.py:318
  86.2 5.5 %gate_up.3 = bf16[384,3712]{1,0:T(8,128)(2,1)S(1)} custom-call(f32[1,1024]{1,0:T(1,128)S(1)} %bitcast.56, bf16[128,1024]{1,0:T(8,128)(2,1)S(1)} %collective-permute-done.16.refs_0_, bf16[128,1024]{1,0:T(8,128)(2,1)S(1)} %collective-permute-done.17.refs_1_, bf16[128,1024]{1,0:T(8,128)(2,1)S(1)} %collective-permute-done.18.refs_2_, bf16[1024,896]{1,0:T(8,128)(2,1)} %refs_3_.1, ...), custom_call_target="tpu_custom_call" | custom-call | flops 69209997312 | bytes 10878976 | tf_op jit(solution)/shard_map/gate_up/pallas_call | solution.py:240
  91.8 1.6 copy-done.1
  93.3 2.9 %all-to-all-done.2.refs_0_ = bf16[8,16,3712]{2,1,0:T(8,128)(2,1)} async-done(((bf16[8,16,3712]{2,1,0:T(8,128)(2,1)}), bf16[8,16,3712]{2,1,0:T(8,128)(2,1)}, u32[]{:S(2)}, u32[]{:S(2)}) %all-to-all-start.2) | async-done | bytes 950304 | tf_op jit(solution)/shard_map/all_to_all | solution.py:318
  96.2 33.4 %all_to_all.25.refs_1_ = bf16[8,48,3712]{2,1,0:T(8,128)(2,1)} all-to-all(bf16[8,48,3712]{2,1,0:T(8,128)(2,1)} %bitcast.54), channel_id=1, replica_groups=mesh['x'=4,'l'=2,'y'=4,'z'=4,'core'=2] {'x','l'}, dimensions={0} | all-to-all | bytes 5701632 | tf_op jit(solution)/shard_map/all_to_all | solution.py:318
  129.6 3.9 %activate.1 = bf16[8,64,1792]{2,1,0:T(8,128)(2,1)} custom-call(bf16[8,16,3712]{2,1,0:T(8,128)(2,1)} %all-to-all-done.2.refs_0_, bf16[8,48,3712]{2,1,0:T(8,128)(2,1)} %all_to_all.25.refs_1_), custom_call_target="tpu_custom_call" | custom-call | bytes 5505024 | tf_op jit(solution)/shard_map/activate/pallas_call | solution.py:143
  133.5 4.3 %all-to-all-start.4 = ((bf16[8,64,1792]{2,1,0:T(8,128)(2,1)}), bf16[8,64,1792]{2,1,0:T(8,128)(2,1)}, u32[]{:S(2)}, u32[]{:S(2)}) async-start(bf16[8,64,1792]{2,1,0:T(8,128)(2,1)} %activate.1), calls=%async_computation.4 | async-start | bytes 3670016 | tf_op jit(solution)/shard_map/all_to_all | solution.py:318
  137.9 7.4 %collective-permute-start.19 = (bf16[896,1024]{1,0:T(8,128)(2,1)}, bf16[896,1024]{1,0:T(8,128)(2,1)}, u32[]{:S(2)}, u32[]{:S(2)}) collective-permute-start(bf16[896,1024]{1,0:T(8,128)(2,1)} %own.1), channel_id=1, source_target_pairs={{0,1},{1,0},{2,3},{3,2},{4,5},{5,4},{6,7},{7,6},{8,9},{9,8},{10,11... | collective-permute-start | bytes 5505032 | tf_op jit(solution)/shard_map/ppermute | solution.py:78
  145.2 3.8 %collective-permute-done.19.other = bf16[896,1024]{1,0:T(8,128)(2,1)} collective-permute-done((bf16[896,1024]{1,0:T(8,128)(2,1)}, bf16[896,1024]{1,0:T(8,128)(2,1)}, u32[]{:S(2)}, u32[]{:S(2)}) %collective-permute-start.19) | collective-permute-done | bytes 1835040 | tf_op jit(solution)/shard_map/ppermute | solution.py:78
  149.0 5.9 %all-to-all-done.4.hidden_ref = bf16[8,64,1792]{2,1,0:T(8,128)(2,1)} async-done(((bf16[8,64,1792]{2,1,0:T(8,128)(2,1)}), bf16[8,64,1792]{2,1,0:T(8,128)(2,1)}, u32[]{:S(2)}, u32[]{:S(2)}) %all-to-all-start.4) | async-done | bytes 1835040 | tf_op jit(solution)/shard_map/all_to_all | solution.py:318
  154.9 6.6 %down.1 = (bf16[128,1024]{1,0:T(8,128)(2,1)}, bf16[128,1024]{1,0:T(8,128)(2,1)}, bf16[128,1024]{1,0:T(8,128)(2,1)}, bf16[128,1024]{1,0:T(8,128)(2,1)}) custom-call(s32[29]{0:T(128)} %copy-done.6, bf16[8,64,1792]{2,1,0:T(8,128)(2,1)} %all-to-all-done.4.hidden_ref, bf16[896,1024]{1,0:T(8,128)(2,1)} %own.1, bf16[896,1024]{1,0:T(8,128)(2,1)} %collective-permute-done.19.other, ...), custom_call_target="tpu_custom_call" | custom-call | flops 1879048192 | bytes 6553600 | tf_op jit(solution)/shard_map/down/pallas_call | solution.py:293
  162.0 2.4 %collective-permute-start.21 = (bf16[128,1024]{1,0:T(8,128)(2,1)}, bf16[128,1024]{1,0:T(8,128)(2,1)S(1)}, u32[]{:S(2)}, u32[]{:S(2)}) collective-permute-start(bf16[128,1024]{1,0:T(8,128)(2,1)} %get-tuple-element.43), channel_id=1, source_target_pairs={{0,16},{8,24},{16,0},{24,8},{1,17},{9,25},{17,1},{25,9},{2,18},{10... | collective-permute-start | bytes 786440 | tf_op jit(solution)/shard_map/ppermute | solution.py:86
  164.8 3.4 %collective-permute-done.20 = bf16[128,1024]{1,0:T(8,128)(2,1)S(1)} collective-permute-done((bf16[128,1024]{1,0:T(8,128)(2,1)}, bf16[128,1024]{1,0:T(8,128)(2,1)S(1)}, u32[]{:S(2)}, u32[]{:S(2)}) %collective-permute-start.20) | collective-permute-done | bytes 262176 | tf_op jit(solution)/shard_map/ppermute | solution.py:86
  168.2 3.0 %collective-permute-done.21 = bf16[128,1024]{1,0:T(8,128)(2,1)S(1)} collective-permute-done((bf16[128,1024]{1,0:T(8,128)(2,1)}, bf16[128,1024]{1,0:T(8,128)(2,1)S(1)}, u32[]{:S(2)}, u32[]{:S(2)}) %collective-permute-start.21) | collective-permute-done | bytes 262176 | tf_op jit(solution)/shard_map/ppermute | solution.py:86
  171.6 1.1 fusion.37
  172.8 9.8 %collective-permute-start.23 = (bf16[32,1024]{1,0:T(8,128)(2,1)S(1)}, bf16[32,1024]{1,0:T(8,128)(2,1)S(1)}, u32[]{:S(2)}, u32[]{:S(2)}) collective-permute-start(bf16[32,1024]{1,0:T(8,128)(2,1)S(1)} %get-tuple-element.51), channel_id=1, source_target_pairs={{0,2},{2,4},{4,6},{6,0},{1,3},{3,5},{5,7},{7,1},{8,10},{10,12},{12... | collective-permute-start | bytes 196616 | tf_op jit(solution)/shard_map/ppermute | solution.py:86
  182.5 3.4 %collective-permute-start.24 = (bf16[32,1024]{1,0:T(8,128)(2,1)S(1)}, bf16[32,1024]{1,0:T(8,128)(2,1)S(1)}, u32[]{:S(2)}, u32[]{:S(2)}) collective-permute-start(bf16[32,1024]{1,0:T(8,128)(2,1)S(1)} %get-tuple-element.53), channel_id=1, source_target_pairs={{0,4},{2,6},{4,0},{6,2},{1,5},{3,7},{5,1},{7,3},{8,12},{10,14},{12... | collective-permute-start | bytes 196616 | tf_op jit(solution)/shard_map/ppermute | solution.py:86
  185.9 2.1 %collective-permute-done.25 = bf16[32,1024]{1,0:T(8,128)(2,1)S(1)} collective-permute-done((bf16[32,1024]{1,0:T(8,128)(2,1)S(1)}, bf16[32,1024]{1,0:T(8,128)(2,1)S(1)}, u32[]{:S(2)}, u32[]{:S(2)}) %collective-permute-start.25) | collective-permute-done | bytes 65568 | tf_op jit(solution)/shard_map/ppermute | solution.py:86
  188.0 3.0 %collective-permute-done.24 = bf16[32,1024]{1,0:T(8,128)(2,1)S(1)} collective-permute-done((bf16[32,1024]{1,0:T(8,128)(2,1)S(1)}, bf16[32,1024]{1,0:T(8,128)(2,1)S(1)}, u32[]{:S(2)}, u32[]{:S(2)}) %collective-permute-start.24) | collective-permute-done | bytes 65568 | tf_op jit(solution)/shard_map/ppermute | solution.py:86
  191.1 8.1 %collective-permute-start.26 = (bf16[16,1024]{1,0:T(8,128)(2,1)S(1)}, bf16[16,1024]{1,0:T(8,128)(2,1)S(1)}, u32[]{:S(2)}, u32[]{:S(2)}) collective-permute-start(bf16[16,1024]{1,0:T(8,128)(2,1)S(1)} %broadcast_select_fusion.2), channel_id=1, source_target_pairs={{0,1},{1,0},{2,3},{3,2},{4,5},{5,4},{6,7},{7,6},{8,9},{9,8},{10,11... | collective-permute-start | bytes 98312 | tf_op jit(solution)/shard_map/ppermute | solution.py:78
  199.2 0.9 collective-permute-done.26
  (71 shorter events, 10.1 us)
Async XLA Ops:
  0.0 7.0 %copy-start = (bf16[4,256,1024]{2,1,0:T(8,128)(2,1)S(1)}, bf16[4,256,1024]{2,1,0:T(8,128)(2,1)}, u32[]{:S(2)}) copy-start(bf16[4,256,1024]{2,1,0:T(8,128)(2,1)} %param.15) | copy-start | bytes 6291460
  0.0 25.3 %collective-permute-start.1 = (bf16[256,1024]{1,0:T(8,128)(2,1)}, bf16[256,1024]{1,0:T(8,128)(2,1)S(1)}, u32[]{:S(2)}, u32[]{:S(2)}) collective-permute-start(bf16[256,1024]{1,0:T(8,128)(2,1)} %refs_4_.2), channel_id=1, source_target_pairs={{24,0},{0,8},{8,16},{16,24},{25,1},{1,9},{9,17},{17,25},{26,2},{2,... | collective-permute-start | bytes 1572872 | tf_op jit(solution)/shard_map/ppermute | solution.py:82
  2.1 23.1 %collective-permute-start = (bf16[256,1024]{1,0:T(8,128)(2,1)}, bf16[256,1024]{1,0:T(8,128)(2,1)}, u32[]{:S(2)}, u32[]{:S(2)}) collective-permute-start(bf16[256,1024]{1,0:T(8,128)(2,1)} %refs_4_.2), channel_id=1, source_target_pairs={{8,0},{16,8},{24,16},{0,24},{9,1},{17,9},{25,17},{1,25},{10,2},{18... | collective-permute-start | bytes 1572872 | tf_op jit(solution)/shard_map/ppermute | solution.py:82
  5.1 3.7 %copy-start.7 = (bf16[4,256,1024]{2,1,0:T(8,128)(2,1)S(1)}, bf16[4,256,1024]{2,1,0:T(8,128)(2,1)}, u32[]{:S(2)}) copy-start(bf16[4,256,1024]{2,1,0:T(8,128)(2,1)} %param.16) | copy-start | bytes 6291460
  8.5 9.7 %copy-start.2 = (bf16[256,1024]{1,0:T(8,128)(2,1)S(1)}, bf16[256,1024]{1,0:T(8,128)(2,1)}, u32[]{:S(2)}) copy-start(bf16[256,1024]{1,0:T(8,128)(2,1)} %refs_4_.2) | copy-start | bytes 1572868
  10.0 15.2 %all-to-all-start = ((bf16[4,4,2048]{2,1,0:T(4,128)(2,1)}), bf16[4,4,2048]{2,1,0:T(4,128)(2,1)S(1)}, u32[]{:S(2)}, u32[]{:S(2)}) async-start(bf16[4,4,2048]{2,1,0:T(4,128)(2,1)} %reshape.71), calls=%async_computation | async-start | bytes 131072 | tf_op jit(solution)/shard_map/all_to_all | solution.py:318
  18.2 19.7 %collective-permute-start.6 = (bf16[256,1024]{1,0:T(8,128)(2,1)S(1)}, bf16[256,1024]{1,0:T(8,128)(2,1)}, u32[]{:S(2)}, u32[]{:S(2)}) collective-permute-start(bf16[256,1024]{1,0:T(8,128)(2,1)S(1)} %copy-done.2), channel_id=1, source_target_pairs={{16,0},{24,8},{0,16},{8,24},{17,1},{25,9},{1,17},{9,25},{18,2},{26... | collective-permute-start | bytes 1572872 | tf_op jit(solution)/shard_map/ppermute | solution.py:82
  25.3 3.6 %collective-permute-start.2 = (bf16[16,2048]{1,0:T(8,128)(2,1)S(1)}, bf16[16,2048]{1,0:T(8,128)(2,1)S(1)}, u32[]{:S(2)}, u32[]{:S(2)}) collective-permute-start(bf16[16,2048]{1,0:T(8,128)(2,1)S(1)} %reshape.72), channel_id=1, source_target_pairs={{0,32},{32,0},{1,33},{33,1},{2,34},{34,2},{3,35},{35,3},{4,36},{36... | collective-permute-start | bytes 196616 | tf_op jit(solution)/shard_map/ppermute | solution.py:78
  28.9 9.0 %collective-permute-start.5 = (bf16[32,2048]{1,0:T(8,128)(2,1)S(1)}, bf16[32,2048]{1,0:T(8,128)(2,1)S(1)}, u32[]{:S(2)}, u32[]{:S(2)}) collective-permute-start(bf16[32,2048]{1,0:T(8,128)(2,1)S(1)} %constant_dynamic-update-slice_fusion.refs_0_), channel_id=1, source_target_pairs={{192,0},{0,64},{64,128},{128,192},{193,1},{1,65},{65,129},{129,193... | collective-permute-start | bytes 393224 | tf_op jit(solution)/shard_map/ppermute | solution.py:82
  30.1 8.3 %collective-permute-start.4 = (bf16[32,2048]{1,0:T(8,128)(2,1)S(1)}, bf16[32,2048]{1,0:T(8,128)(2,1)S(1)}, u32[]{:S(2)}, u32[]{:S(2)}) collective-permute-start(bf16[32,2048]{1,0:T(8,128)(2,1)S(1)} %constant_dynamic-update-slice_fusion.refs_0_), channel_id=1, source_target_pairs={{128,0},{192,64},{0,128},{64,192},{129,1},{193,65},{1,129},{65,193... | collective-permute-start | bytes 393224 | tf_op jit(solution)/shard_map/ppermute | solution.py:82
  32.6 5.9 %collective-permute-start.3 = (bf16[32,2048]{1,0:T(8,128)(2,1)S(1)}, bf16[32,2048]{1,0:T(8,128)(2,1)S(1)}, u32[]{:S(2)}, u32[]{:S(2)}) collective-permute-start(bf16[32,2048]{1,0:T(8,128)(2,1)S(1)} %constant_dynamic-update-slice_fusion.refs_0_), channel_id=1, source_target_pairs={{64,0},{128,64},{192,128},{0,192},{65,1},{129,65},{193,129},{1,193... | collective-permute-start | bytes 393224 | tf_op jit(solution)/shard_map/ppermute | solution.py:82
  33.7 9.0 %collective-permute-start.7 = (bf16[256,1024]{1,0:T(8,128)(2,1)S(1)}, bf16[256,1024]{1,0:T(8,128)(2,1)}, u32[]{:S(2)}, u32[]{:S(2)}) collective-permute-start(bf16[256,1024]{1,0:T(8,128)(2,1)S(1)} %copy-done.2), channel_id=1, source_target_pairs={{0,1},{1,0},{2,3},{3,2},{4,5},{5,4},{6,7},{7,6},{8,9},{9,8},{10,11... | collective-permute-start | bytes 1572872 | tf_op jit(solution)/shard_map/ppermute | solution.py:78
  37.8 4.9 %collective-permute-start.8 = (bf16[256,1024]{1,0:T(8,128)(2,1)}, bf16[256,1024]{1,0:T(8,128)(2,1)}, u32[]{:S(2)}, u32[]{:S(2)}) collective-permute-start(bf16[256,1024]{1,0:T(8,128)(2,1)} %collective-permute-done.refs_5_), channel_id=1, source_target_pairs={{0,1},{1,0},{2,3},{3,2},{4,5},{5,4},{6,7},{7,6},{8,9},{9,8},{10,11... | collective-permute-start | bytes 1572872 | tf_op jit(solution)/shard_map/ppermute | solution.py:78
  37.8 4.9 %collective-permute-start.10 = (bf16[256,1024]{1,0:T(8,128)(2,1)S(1)}, bf16[256,1024]{1,0:T(8,128)(2,1)}, u32[]{:S(2)}, u32[]{:S(2)}) collective-permute-start(bf16[256,1024]{1,0:T(8,128)(2,1)S(1)} %collective-permute-done.1.refs_7_), channel_id=1, source_target_pairs={{0,1},{1,0},{2,3},{3,2},{4,5},{5,4},{6,7},{7,6},{8,9},{9,8},{10,11... | collective-permute-start | bytes 1572872 | tf_op jit(solution)/shard_map/ppermute | solution.py:78
  38.4 0.7 copy-start.3
  39.1 4.8 %collective-permute-start.9 = (bf16[256,1024]{1,0:T(8,128)(2,1)}, bf16[256,1024]{1,0:T(8,128)(2,1)}, u32[]{:S(2)}, u32[]{:S(2)}) collective-permute-start(bf16[256,1024]{1,0:T(8,128)(2,1)} %collective-permute-done.6.refs_6_), channel_id=1, source_target_pairs={{0,1},{1,0},{2,3},{3,2},{4,5},{5,4},{6,7},{7,6},{8,9},{9,8},{10,11... | collective-permute-start | bytes 1572872 | tf_op jit(solution)/shard_map/ppermute | solution.py:78
  42.0 20.5 %copy-start.5 = (f32[1024]{0:T(1024)S(1)}, f32[1024]{0:T(1024)}, u32[]{:S(2)}) copy-start(f32[1024]{0:T(1024)} %param.21) | copy-start | bytes 12292
  42.7 6.8 %copy-start.6 = (s32[29]{0:T(128)}, s32[29]{0:T(128)S(1)}, u32[]{:S(2)}) copy-start(s32[29]{0:T(128)S(1)} %fusion.36.place_ref) | copy-start | bytes 352
  43.9 0.9 copy-start.4
  49.5 13.7 %collective-permute-start.11 = (bf16[1024,896]{1,0:T(8,128)(2,1)}, bf16[1024,896]{1,0:T(8,128)(2,1)}, u32[]{:S(2)}, u32[]{:S(2)}) collective-permute-start(bf16[1024,896]{1,0:T(8,128)(2,1)} %refs_3_.1), channel_id=1, source_target_pairs={{0,1},{1,0},{2,3},{3,2},{4,5},{5,4},{6,7},{7,6},{8,9},{9,8},{10,11... | collective-permute-start | bytes 5505032 | tf_op jit(solution)/shard_map/ppermute | solution.py:78
  50.0 13.3 %collective-permute-start.12 = (bf16[1024,896]{1,0:T(8,128)(2,1)}, bf16[1024,896]{1,0:T(8,128)(2,1)}, u32[]{:S(2)}, u32[]{:S(2)}) collective-permute-start(bf16[1024,896]{1,0:T(8,128)(2,1)} %refs_4_.3), channel_id=1, source_target_pairs={{0,1},{1,0},{2,3},{3,2},{4,5},{5,4},{6,7},{7,6},{8,9},{9,8},{10,11... | collective-permute-start | bytes 5505032 | tf_op jit(solution)/shard_map/ppermute | solution.py:78
  50.1 12.4 %all-to-all-start.1 = ((bf16[4,32,1024]{2,1,0:T(8,128)(2,1)}), bf16[4,32,1024]{2,1,0:T(8,128)(2,1)S(1)}, u32[]{:S(2)}, u32[]{:S(2)}) async-start(bf16[4,32,1024]{2,1,0:T(8,128)(2,1)} %bitcast.5), calls=%async_computation.1 | async-start | bytes 524288 | tf_op jit(solution)/shard_map/all_to_all | solution.py:318
  63.2 5.7 %collective-permute-start.15 = (bf16[32,1024]{1,0:T(8,128)(2,1)S(1)}, bf16[32,1024]{1,0:T(8,128)(2,1)S(1)}, u32[]{:S(2)}, u32[]{:S(2)}) collective-permute-start(bf16[32,1024]{1,0:T(8,128)(2,1)S(1)} %get-tuple-element.36), channel_id=1, source_target_pairs={{6,0},{0,2},{2,4},{4,6},{7,1},{1,3},{3,5},{5,7},{14,8},{8,10},{10,... | collective-permute-start | bytes 196616 | tf_op jit(solution)/shard_map/ppermute | solution.py:82
  63.7 7.5 %collective-permute-start.14 = (bf16[32,1024]{1,0:T(8,128)(2,1)S(1)}, bf16[32,1024]{1,0:T(8,128)(2,1)S(1)}, u32[]{:S(2)}, u32[]{:S(2)}) collective-permute-start(bf16[32,1024]{1,0:T(8,128)(2,1)S(1)} %get-tuple-element.36), channel_id=1, source_target_pairs={{4,0},{6,2},{0,4},{2,6},{5,1},{7,3},{1,5},{3,7},{12,8},{14,10},{8,... | collective-permute-start | bytes 196616 | tf_op jit(solution)/shard_map/ppermute | solution.py:82
  67.5 5.6 %collective-permute-start.13 = (bf16[32,1024]{1,0:T(8,128)(2,1)S(1)}, bf16[32,1024]{1,0:T(8,128)(2,1)S(1)}, u32[]{:S(2)}, u32[]{:S(2)}) collective-permute-start(bf16[32,1024]{1,0:T(8,128)(2,1)S(1)} %get-tuple-element.36), channel_id=1, source_target_pairs={{2,0},{4,2},{6,4},{0,6},{3,1},{5,3},{7,5},{1,7},{10,8},{12,10},{14... | collective-permute-start | bytes 196616 | tf_op jit(solution)/shard_map/ppermute | solution.py:82
  73.1 13.1 %collective-permute-start.18 = (bf16[128,1024]{1,0:T(8,128)(2,1)S(1)}, bf16[128,1024]{1,0:T(8,128)(2,1)S(1)}, u32[]{:S(2)}, u32[]{:S(2)}) collective-permute-start(bf16[128,1024]{1,0:T(8,128)(2,1)S(1)} %pad_maximum_fusion.refs_0_), channel_id=1, source_target_pairs={{24,0},{0,8},{8,16},{16,24},{25,1},{1,9},{9,17},{17,25},{26,2},{2,... | collective-permute-start | bytes 786440 | tf_op jit(solution)/shard_map/ppermute | solution.py:82
  73.3 12.9 %collective-permute-start.17 = (bf16[128,1024]{1,0:T(8,128)(2,1)S(1)}, bf16[128,1024]{1,0:T(8,128)(2,1)S(1)}, u32[]{:S(2)}, u32[]{:S(2)}) collective-permute-start(bf16[128,1024]{1,0:T(8,128)(2,1)S(1)} %pad_maximum_fusion.refs_0_), channel_id=1, source_target_pairs={{16,0},{24,8},{0,16},{8,24},{17,1},{25,9},{1,17},{9,25},{18,2},{26... | collective-permute-start | bytes 786440 | tf_op jit(solution)/shard_map/ppermute | solution.py:82
  75.9 10.3 %collective-permute-start.16 = (bf16[128,1024]{1,0:T(8,128)(2,1)S(1)}, bf16[128,1024]{1,0:T(8,128)(2,1)S(1)}, u32[]{:S(2)}, u32[]{:S(2)}) collective-permute-start(bf16[128,1024]{1,0:T(8,128)(2,1)S(1)} %pad_maximum_fusion.refs_0_), channel_id=1, source_target_pairs={{8,0},{16,8},{24,16},{0,24},{9,1},{17,9},{25,17},{1,25},{10,2},{18... | collective-permute-start | bytes 786440 | tf_op jit(solution)/shard_map/ppermute | solution.py:82
  81.6 14.6 %all-to-all-start.2 = ((bf16[8,16,3712]{2,1,0:T(8,128)(2,1)}), bf16[8,16,3712]{2,1,0:T(8,128)(2,1)}, u32[]{:S(2)}, u32[]{:S(2)}) async-start(bf16[8,16,3712]{2,1,0:T(8,128)(2,1)} %bitcast.6), calls=%async_computation.2 | async-start | bytes 1900544 | tf_op jit(solution)/shard_map/all_to_all | solution.py:318
  91.7 1.6 copy-start.1
  133.5 21.3 %all-to-all-start.4 = ((bf16[8,64,1792]{2,1,0:T(8,128)(2,1)}), bf16[8,64,1792]{2,1,0:T(8,128)(2,1)}, u32[]{:S(2)}, u32[]{:S(2)}) async-start(bf16[8,64,1792]{2,1,0:T(8,128)(2,1)} %activate.1), calls=%async_computation.4 | async-start | bytes 3670016 | tf_op jit(solution)/shard_map/all_to_all | solution.py:318
  137.9 11.1 %collective-permute-start.19 = (bf16[896,1024]{1,0:T(8,128)(2,1)}, bf16[896,1024]{1,0:T(8,128)(2,1)}, u32[]{:S(2)}, u32[]{:S(2)}) collective-permute-start(bf16[896,1024]{1,0:T(8,128)(2,1)} %own.1), channel_id=1, source_target_pairs={{0,1},{1,0},{2,3},{3,2},{4,5},{5,4},{6,7},{7,6},{8,9},{9,8},{10,11... | collective-permute-start | bytes 5505032 | tf_op jit(solution)/shard_map/ppermute | solution.py:78
  161.5 6.7 %collective-permute-start.20 = (bf16[128,1024]{1,0:T(8,128)(2,1)}, bf16[128,1024]{1,0:T(8,128)(2,1)S(1)}, u32[]{:S(2)}, u32[]{:S(2)}) collective-permute-start(bf16[128,1024]{1,0:T(8,128)(2,1)} %get-tuple-element.42), channel_id=1, source_target_pairs={{0,8},{8,16},{16,24},{24,0},{1,9},{9,17},{17,25},{25,1},{2,10},{10... | collective-permute-start | bytes 786440 | tf_op jit(solution)/shard_map/ppermute | solution.py:86
  162.0 9.2 %collective-permute-start.21 = (bf16[128,1024]{1,0:T(8,128)(2,1)}, bf16[128,1024]{1,0:T(8,128)(2,1)S(1)}, u32[]{:S(2)}, u32[]{:S(2)}) collective-permute-start(bf16[128,1024]{1,0:T(8,128)(2,1)} %get-tuple-element.43), channel_id=1, source_target_pairs={{0,16},{8,24},{16,0},{24,8},{1,17},{9,25},{17,1},{25,9},{2,18},{10... | collective-permute-start | bytes 786440 | tf_op jit(solution)/shard_map/ppermute | solution.py:86
  164.4 7.2 %collective-permute-start.22 = (bf16[128,1024]{1,0:T(8,128)(2,1)}, bf16[128,1024]{1,0:T(8,128)(2,1)S(1)}, u32[]{:S(2)}, u32[]{:S(2)}) collective-permute-start(bf16[128,1024]{1,0:T(8,128)(2,1)} %get-tuple-element.44), channel_id=1, source_target_pairs={{0,24},{8,0},{16,8},{24,16},{1,25},{9,1},{17,9},{25,17},{2,26},{10... | collective-permute-start | bytes 786440 | tf_op jit(solution)/shard_map/ppermute | solution.py:86
  172.8 13.1 %collective-permute-start.23 = (bf16[32,1024]{1,0:T(8,128)(2,1)S(1)}, bf16[32,1024]{1,0:T(8,128)(2,1)S(1)}, u32[]{:S(2)}, u32[]{:S(2)}) collective-permute-start(bf16[32,1024]{1,0:T(8,128)(2,1)S(1)} %get-tuple-element.51), channel_id=1, source_target_pairs={{0,2},{2,4},{4,6},{6,0},{1,3},{3,5},{5,7},{7,1},{8,10},{10,12},{12... | collective-permute-start | bytes 196616 | tf_op jit(solution)/shard_map/ppermute | solution.py:86
  182.5 5.5 %collective-permute-start.25 = (bf16[32,1024]{1,0:T(8,128)(2,1)S(1)}, bf16[32,1024]{1,0:T(8,128)(2,1)S(1)}, u32[]{:S(2)}, u32[]{:S(2)}) collective-permute-start(bf16[32,1024]{1,0:T(8,128)(2,1)S(1)} %get-tuple-element.52), channel_id=1, source_target_pairs={{0,6},{2,0},{4,2},{6,4},{1,7},{3,1},{5,3},{7,5},{8,14},{10,8},{12,... | collective-permute-start | bytes 196616 | tf_op jit(solution)/shard_map/ppermute | solution.py:86
  182.5 8.5 %collective-permute-start.24 = (bf16[32,1024]{1,0:T(8,128)(2,1)S(1)}, bf16[32,1024]{1,0:T(8,128)(2,1)S(1)}, u32[]{:S(2)}, u32[]{:S(2)}) collective-permute-start(bf16[32,1024]{1,0:T(8,128)(2,1)S(1)} %get-tuple-element.53), channel_id=1, source_target_pairs={{0,4},{2,6},{4,0},{6,2},{1,5},{3,7},{5,1},{7,3},{8,12},{10,14},{12... | collective-permute-start | bytes 196616 | tf_op jit(solution)/shard_map/ppermute | solution.py:86
  191.1 9.0 %collective-permute-start.26 = (bf16[16,1024]{1,0:T(8,128)(2,1)S(1)}, bf16[16,1024]{1,0:T(8,128)(2,1)S(1)}, u32[]{:S(2)}, u32[]{:S(2)}) collective-permute-start(bf16[16,1024]{1,0:T(8,128)(2,1)S(1)} %broadcast_select_fusion.2), channel_id=1, source_target_pairs={{0,1},{1,0},{2,3},{3,2},{4,5},{5,4},{6,7},{7,6},{8,9},{9,8},{10,11... | collective-permute-start | bytes 98312 | tf_op jit(solution)/shard_map/ppermute | solution.py:78
